TPU v7x, 32 devices: a whole 2x2x4 slice. The times are simulated.
32 devices in a mesh: frag: 2 (over y), pair: 4 (over x, core), aux: 4 (over z).
Axes of the slice: x: 2, y: 2, z: 4, core: 2. Of those that a mesh axis runs over, the one named last changes fastest.
Arguments:
- slabs: bfloat16 [128, 256, 4096], P(('frag', 'pair'), 'aux'), parts along dimension 0, may hold values from -6 to 6
- block_row: int32 [128], P(('frag', 'pair')), parts along dimension 0, may hold values from 0 to 63
- block_col: int32 [128], P(('frag', 'pair')), parts along dimension 0, may hold values from 0 to 63, as said below
- live_count: int32 [8], P(('frag', 'pair')), parts along dimension 0, may hold values from 1 to 16, as said below
- orbitals: bfloat16 [8192, 192], P('frag'), parts along dimension 0, may hold values from -0.09375 to 0.09375
- hcore: float32 [128, 64], P(('frag', 'pair')), parts along dimension 0, may hold values from -6 to 6
Outputs:
- active_vectors: float32 [512, 64, 64], P(('frag', 'aux'), 'pair'), parts along dimension 0
- fock: float32 [128, 64], P(('frag', 'pair')), parts along dimension 0
There are 2 independent parts, one for each index of `frag`. A program takes and returns all parts, laid end to end along the dimension named above; each array names one. Nothing has to cross between parts.
Inputs may be any that keep to these rules, and one draw needn't show every extreme that they name: `block_col`: never above the same slab's block_row; a diagonal block holds half of each integral. `live_count`: a device's live slabs fill its first slots; exactly one device in every draw has all 16 live.
All inputs are finite; a program needn't handle non-finite values.
Results may differ from a plain program's by a relative error of at most 0.0029.
Values may be sent and summed in bfloat16 or wider, within the bound.
No kernel may reach another device: no remote copies, remote signals or barrier semaphores. Data moves between devices by JAX's collectives and lax.ppermute only.
A program may use at most 128 MiB of HBM per device.

v0:
```python
import jax
import jax.numpy as jnp
from jax import lax
from jax.sharding import PartitionSpec as P

BS = 64
NACT = 64
NCOL = 192


def slab_terms(values, left, right):
    half = jnp.einsum("mc,qmn->qnc", left, values, preferred_element_type=jnp.float32).astype(
        jnp.bfloat16
    )
    first = jnp.einsum("qnt,nc->qtc", half[:, :, :NACT], right, preferred_element_type=jnp.float32)
    second = jnp.einsum("qnc,nt->qtc", half, right[:, :NACT], preferred_element_type=jnp.float32)
    trace = 2.0 * jnp.einsum(
        "qni,ni->q", half[:, :, NACT:], right[:, NACT:], preferred_element_type=jnp.float32
    )
    return (first + second, trace)


def add_slab(state, orbitals, values, row_blk, col_blk):
    batch = values.shape[0]
    left = lax.dynamic_slice_in_dim(orbitals, row_blk * BS, BS, 0)
    right = lax.dynamic_slice_in_dim(orbitals, col_blk * BS, BS, 0)
    terms, trace = slab_terms(values.reshape(batch, BS, BS), left, right)
    return (state[0] + terms, state[1] + trace)


def pick_slab(slab_set, rows, cols, slot):
    values = lax.dynamic_index_in_dim(slab_set, slot, 0, keepdims=False)
    return (values, rows[slot], cols[slot])


def body(slabs, block_row, block_col, live_count, orbitals, hcore):
    batch = slabs.shape[1]
    init = (jnp.zeros((batch, NACT, NCOL), jnp.float32), jnp.zeros((batch,), jnp.float32))

    def visit(k, state):
        values, row_blk, col_blk = pick_slab(slabs, block_row, block_col, k)
        return add_slab(state, orbitals, values, row_blk, col_blk)

    vectors, density = lax.fori_loop(0, live_count[0], visit, init)
    density = lax.psum(density, "pair")
    owned = lax.psum_scatter(vectors, "pair", scatter_dimension=1, tiled=True)
    own_active = owned[:, :, :NACT]
    own_inactive = owned[:, :, NACT:]
    exchange = jnp.einsum(
        "qti,qui->tu",
        own_inactive,
        lax.all_gather(own_inactive.astype(jnp.bfloat16), "pair", axis=1, tiled=True).astype(
            jnp.float32
        ),
        precision=lax.Precision.HIGHEST,
    )
    coulomb = jnp.einsum("qtu,q->tu", own_active, density, precision=lax.Precision.HIGHEST)
    partial_fock = 2.0 * coulomb - exchange
    summed = lax.psum(partial_fock, "aux")
    fock = hcore + summed
    return (own_active, fock)


def solution(mesh):
    placed = (
        P(("frag", "pair"), "aux", None),
        P(("frag", "pair")),
        P(("frag", "pair")),
        P(("frag", "pair")),
        P("frag", None),
        P(("frag", "pair"), None),
    )
    return jax.shard_map(
        body,
        mesh=mesh,
        in_specs=placed,
        out_specs=(P(("frag", "aux"), "pair", None), P(("frag", "pair"), None)),
        check_vma=False,
    )
```

profile of v0, /device:TPU:0, one launch (start us, length us, event | category | flops | bytes accessed | tf_op | source)
XLA Modules:
  0.0 322.5 jit_solution(17741122649772247462)
XLA Ops:
  7.2 3.2 copy.14
  10.4 2.5 broadcast_in_dim.6
  12.9 222.1 %while.12 = (s32[]{:T(128)}, f32[64,64,192]{2,1,0:T(8,128)}, f32[64]{0:T(128)S(1)}, s32[]{:T(128)}, bf16[16,64,4096]{2,1,0:T(8,128)(2,1)}, /*index=5*/s32[16]{0:...) while((s32[]{:T(128)}, f32[64,64,192]{2,1,0:T(8,128)}, ...), condition=%wide.region_1.2_spmd, body=%wide.region_0.1_spmd.sunk | while | flops 305397888 | bytes 63046580 | solution.py:44
  24.8 1.9 copy-done.1
  38.6 1.9 copy-done.1
  52.5 1.9 copy-done.1
  66.3 1.9 copy-done.1
  80.1 1.9 copy-done.1
  94.0 1.9 copy-done.1
  107.8 1.9 copy-done.1
  121.6 1.9 copy-done.1
  135.5 1.9 copy-done.1
  149.3 1.9 copy-done.1
  163.2 1.9 copy-done.1
  177.0 1.9 copy-done.1
  190.8 1.9 copy-done.1
  218.5 1.9 copy-done.1
  232.3 1.9 copy-done.1
  235.0 46.8 %reduce-scatter.2.cloned.1.call-done = f32[64,16,192]{2,1,0:T(8,128)} async-done(((f32[64,64,192]{2,1,0:T(8,128)}), f32[64,16,192]{2,1,0:T(8,128)}) %reduce-scatter.2.cloned.1.call-update) | async-done | bytes 786448 | tf_op jit(solution)/shard_map/reduce_scatter | solution.py:46
  281.8 2.2 slice.29
  284.0 5.8 %psum.14 = f32[64]{0:T(128)S(1)} all-reduce(f32[64]{0:T(128)S(1)} %get-tuple-element.47), channel_id=1, replica_groups=mesh['frag'=2,'pair'=4,'aux'=4] {'pair'}, use_global_device_ids=true, to_apply=%region_3.4 | all-reduce | flops 64 | bytes 512 | tf_op jit(solution)/shard_map/psum | solution.py:45
  291.3 9.6 %all-gather.2.cloned.1.call-done = bf16[64,64,128]{2,1,0:T(8,128)(2,1)} async-done(((bf16[64,16,128]{2,1,0:T(8,128)(2,1)}), bf16[64,64,128]{2,1,0:T(8,128)(2,1)}) %all-gather.2.cloned.1.call-update) | async-done | bytes 1048592 | tf_op jit(solution)/shard_map/all_gather | solution.py:52
  301.0 2.2 fusion.14
  303.2 11.8 %psum.15 = f32[16,64]{1,0:T(8,128)S(1)} all-reduce(f32[16,64]{1,0:T(8,128)S(1)} %fusion.14), channel_id=1, replica_groups=mesh['frag'=2,'pair'=4,'aux'=4] {'aux'}, use_global_device_ids=true, to_apply=%region_4.5 | all-reduce | flops 1024 | bytes 8192 | tf_op jit(solution)/shard_map/psum | solution.py:59
  (291 shorter events, 161.5 us)
Async XLA Ops:
  7.2 274.6 %reduce-scatter.2.cloned.1.call-start = ((), (), s32[]{:S(2)}) async-start(), calls=%async_computation.1 | async-start | bytes 5242880 | tf_op jit(solution)/shard_map/reduce_scatter | solution.py:46
  10.4 2.5 copy-start.7
  10.4 2.5 copy-start.8
  13.5 2.6 copy-start.2
  21.6 2.2 copy-start
  27.4 2.6 copy-start.2
  41.2 2.6 copy-start.2
  55.0 2.6 copy-start.2
  68.9 2.6 copy-start.2
  82.7 2.6 copy-start.2
  96.6 2.6 copy-start.2
  110.4 2.6 copy-start.2
  124.2 2.6 copy-start.2
  138.1 2.6 copy-start.2
  151.9 2.6 copy-start.2
  165.8 2.6 copy-start.2
  179.6 2.6 copy-start.2
  193.4 2.6 copy-start.2
  207.3 2.6 copy-start.2
  221.1 2.6 copy-start.2
  235.0 80.1 %copy-start.6 = (f32[16,64]{1,0:T(8,128)S(1)}, f32[16,64]{1,0:T(8,128)}, u32[]{:S(2)}) copy-start(f32[16,64]{1,0:T(8,128)} %param.13) | copy-start | bytes 12292
  235.0 66.0 %all-gather.2.cloned.1.call-start = ((), (), s32[]{:S(2)}) async-start(), calls=%async_computation.2 | async-start | bytes 1310720 | tf_op jit(solution)/shard_map/all_gather | solution.py:52
  281.8 19.2 %copy-start.5 = (f32[64,16,192]{2,1,0:T(8,128)S(1)}, f32[64,16,192]{2,1,0:T(8,128)}, u32[]{:S(2)}) copy-start(f32[64,16,192]{2,1,0:T(8,128)} %reduce-scatter.2.cloned.1.call-done) | copy-start | bytes 2359300
  290.8 24.8 %copy-start.4 = (f32[64,16,64]{2,1,0:T(8,128)}, f32[64,16,64]{2,1,0:T(8,128)S(1)}, u32[]{:S(2)}) copy-start(f32[64,16,64]{2,1,0:T(8,128)S(1)} %slice.22) | copy-start | bytes 786436
  (47 other events, 89.3 us)
Sparse Core Ops, SparseCore 0:
  235.1 46.6 reduce-scatter.1
  284.1 16.8 all-gather.1
where the time goes:
time: 326 us; the launch traced here: 322 us
  local copies, waits for them, and re-layouts  134 us (41%)
  matrix products  65.4 us (20%)
  waiting for transfers between devices  56.4 us (17%)
  loops' own time  34 us (10%)
  blocking collectives  17.6 us (5%)
  between operations  14.1 us (4%)
    while x128, local copies, waits for them, and re-layouts  62 us
    reduce_scatter x1, waiting for transfers between devices, body(): owned = lax.psum_scatter(vectors, 'pair', scatter_dimension=1, tiled=True)  46.8 us
    another operation x1, loops' own time, body(): vectors, density = lax.fori_loop(0, live_count[0], visit, init)  34 us
    dot_general x16, matrix products, slab_terms(): jnp.einsum('mc,qmn->qnc', left, values, preferred_element_type=jnp.float32)  24 us
    dynamic_slice x32, local copies, waits for them, and re-layouts, pick_slab(): return (values, rows[slot], cols[slot])  20.2 us
    reshape x16, local copies, waits for them, and re-layouts, add_slab(): terms, trace = slab_terms(values.reshape(batch, BS, BS), left, right)  18 us
    dynamic_slice x16, local copies, waits for them, and re-layouts, pick_slab(): values = lax.dynamic_index_in_dim(slab_set, slot, 0, keepdims=False)  17.2 us
    dot_general x16, matrix products, slab_terms(): jnp.einsum('qnc,nt->qtc', half, right[:, :NACT], preferred_element_type=j...  16.1 us
  transfers between devices with their start and end apart: 2, of which 2 were waited for; matrix products, arithmetic and copies ran while one was open for 0% of the time, Pallas kernels for 0%

commit v1 on v0

v1 whole, which is shorter than its diff:
```python
import functools

import jax
import jax.numpy as jnp
from jax import lax
from jax.experimental import pallas as pl
from jax.experimental.pallas import tpu as pltpu
from jax.sharding import PartitionSpec as P

BS = 64
NACT = 64
NCOL = 192
NIN = NCOL - NACT
LANES = 128
NBQ = 16
PAIRED = 2 * BS
BF = jnp.bfloat16
F32 = jnp.float32


def low_half(rows):
    return lax.broadcasted_iota(jnp.int32, (rows, LANES), 1) < BS


def orbital_blocks(rows, cols, live, ot_ref, lt_ref, r_ref):
    slabs = lt_ref.shape[0] * 2
    first = low_half(NCOL)

    def window(blk, slot, upper):
        base = pl.multiple_of((blk // 2) * PAIRED, PAIRED)
        w = ot_ref[:, pl.ds(base, PAIRED)].astype(F32)
        w = jnp.concatenate([w[NACT:], w[:NACT]], axis=0)
        moved = lax.rem(blk, 2) != (1 if upper else 0)
        w = jnp.where(moved, pltpu.roll(w, BS, 1), w)
        return jnp.where(slot < live, w, 0.0)

    for k in range(slabs // 2):
        a, b = 2 * k, 2 * k + 1
        left = jnp.where(first, window(rows[a], a, False), window(rows[b], b, True))
        lt_ref[k] = left.astype(BF)
        right = jnp.where(first, window(cols[a], a, False), window(cols[b], b, True))
        right = jnp.concatenate([right, right[NIN:]], axis=0)
        r_ref[pl.ds(k * PAIRED, PAIRED), :] = right.T.astype(BF)


def transform_block(sbuf, lt_ref, r_ref, pair_ref, half_ref, emit_pair):
    slabs = sbuf.shape[0]
    first = low_half(NBQ)
    first_s = low_half(BS)
    zero = jnp.zeros((BS, LANES), BF)

    def half_step(k, wait):
        wait(k)
        for j in range(sbuf.shape[2] // LANES):
            lanes = slice(j * LANES, (j + 1) * LANES)
            a = sbuf[2 * k, :, lanes].astype(F32)
            b = sbuf[2 * k + 1, :, lanes].astype(F32)
            even = jnp.where(first, a, pltpu.roll(b, BS, 1))
            odd = jnp.where(first, pltpu.roll(a, BS, 1), b)
            pair_ref[pl.ds(2 * j, NBQ, stride=BS), :] = even
            pair_ref[pl.ds(2 * j + 1, NBQ, stride=BS), :] = odd
        left = lt_ref[k]
        for q in range(0, NBQ, 2):
            cols = []
            for u in (q, q + 1):
                s = pair_ref[pl.ds(u * BS, BS), :].astype(BF)
                cols.append(
                    jnp.concatenate(
                        [jnp.where(first_s, s, zero), jnp.where(first_s, zero, s)], axis=0
                    )
                )
            half = jnp.dot(
                left, jnp.concatenate(cols, axis=1), preferred_element_type=F32
            ).astype(BF)
            at = pl.ds(pl.multiple_of(k * LANES, LANES), LANES)
            half_ref[q, :, at] = half[:, :LANES]
            half_ref[q + 1, :, at] = half[:, LANES:]

    def second_step(h):
        lhs = half_ref[pl.ds(2 * h, 2)].reshape(2 * NCOL, half_ref.shape[2])
        both = jnp.dot(lhs, r_ref[...], preferred_element_type=F32)
        w0, w1 = both[:NCOL], both[NCOL:]
        side = jnp.where(low_half(NCOL), w0[:, LANES:], w1[:, LANES:])
        across = side[:NIN].T
        in0 = w0[NIN:, :NIN] + across[:NACT]
        in1 = w1[NIN:, :NIN] + across[NACT:]
        square = jnp.concatenate([w0[NIN:, LANES:], w1[NIN:, LANES:]], axis=0).T
        act = side[NIN:] + square[:NACT]
        eye = lax.broadcasted_iota(jnp.int32, (NIN, NIN), 0) == lax.broadcasted_iota(
            jnp.int32, (NIN, NIN), 1
        )
        d0 = jnp.sum(jnp.where(eye, w0[:NIN, :NIN], 0.0), axis=0, keepdims=True)
        d1 = jnp.sum(jnp.where(eye, w1[:NIN, :NIN], 0.0), axis=0, keepdims=True)
        emit_pair(h, in0, in1, act, d0, d1)

    return half_step, second_step


def split_density(diag):
    d = 2.0 * jnp.sum(diag, axis=1, keepdims=True)
    d = jnp.broadcast_to(d, diag.shape)
    hi = d.astype(BF).astype(F32)
    return d, jnp.where(low_half(diag.shape[0]), hi, d - hi).astype(BF)


def load_slabs(slabs_ref, sbuf, sem, block, slot):
    copies = []
    for k in range(slabs_ref.shape[0] // 2):
        copies.append(
            pltpu.make_async_copy(
                slabs_ref.at[pl.ds(2 * k, 2), pl.ds(pl.multiple_of(block * NBQ, NBQ), NBQ), :],
                sbuf.at[slot, pl.ds(2 * k, 2)],
                sem.at[slot, k],
            )
        )
    return copies


def run_block(slabs_ref, sbuf, sem, block, slot, lt_ref, r_ref, pair_ref, half_ref, emit):
    def wait(k):
        pltpu.make_async_copy(
            slabs_ref.at[
                pl.ds(2 * k, 2), pl.ds(pl.multiple_of(block * NBQ, NBQ), NBQ), :
            ],
            sbuf.at[slot, pl.ds(2 * k, 2)],
            sem.at[slot, k],
        ).wait()

    half_step, second_step = transform_block(
        sbuf.at[slot], lt_ref, r_ref, pair_ref, half_ref, emit
    )
    lax.fori_loop(0, slabs_ref.shape[0] // 2, lambda k, c: (half_step(k, wait), c)[1], 0)
    lax.fori_loop(0, NBQ // 2, lambda h, c: (second_step(h), c)[1], 0)


def rows_of(h, first, count):
    return pl.ds(pl.multiple_of(first + h * count, 16), count)


def emit_active(h, act, core, x, send, keep, send_at, keep_at):
    quarter = NACT // 4
    for place in (0, 1):
        xx = (1 - x) if place == 0 else x
        for cc in (0, 1):
            block = act[: quarter]
            for idx in range(4):
                block = jnp.where(
                    2 * xx + cc == idx, act[idx * quarter : (idx + 1) * quarter], block
                ) if idx else act[:quarter]

            @pl.when(core == cc)
            def _():
                keep[place, rows_of(h, keep_at, quarter), :] = block

            @pl.when(core != cc)
            def _():
                send[rows_of(h, send_at[place], quarter), :] = block.astype(BF)


def first_kernel(
    where, rows, cols, live, slabs_ref, ot_ref, lt_out, r_out, msg, act_send, act_keep, dens,
    sbuf, pair_ref, half_ref, diag, sem,
):
    core, x = where[0], where[1]
    block = 2 * (1 - x) + (1 - core)
    for copy in load_slabs(slabs_ref, sbuf, sem, block, 0):
        copy.start()
    orbital_blocks(rows, cols, live[0], ot_ref, lt_out, r_out)

    def emit(h, in0, in1, act, d0, d1):
        msg[2 * h] = in0.astype(BF)
        msg[2 * h + 1] = in1.astype(BF)
        emit_active(h, act, core, x, act_send, act_keep, (0, 128), 0)
        diag[pl.ds(2 * h, 1), :] = d0
        diag[pl.ds(2 * h + 1, 1), :] = d1

    run_block(slabs_ref, sbuf, sem, block, 0, lt_out, r_out, pair_ref, half_ref, emit)
    dens[...] = 2.0 * diag[...]


def second_kernel(
    where, slabs_ref, lt_ref, r_ref, keep_in, act_send, act_keep, dens,
    sbuf, pair_ref, half_ref, diag, sem,
):
    core, x = where[0], where[1]
    block = 2 * (1 - x) + core
    for copy in load_slabs(slabs_ref, sbuf, sem, block, 0):
        copy.start()

    def emit(h, in0, in1, act, d0, d1):
        keep_in[2 * h] = in0
        keep_in[2 * h + 1] = in1
        emit_active(h, act, core, x, act_send, act_keep, (0, 128), 0)
        diag[pl.ds(2 * h, 1), :] = d0
        diag[pl.ds(2 * h + 1, 1), :] = d1

    run_block(slabs_ref, sbuf, sem, block, 0, lt_ref, r_ref, pair_ref, half_ref, emit)
    dens[...] = 2.0 * diag[...]


def third_kernel(
    where, slabs_ref, lt_ref, r_ref, send1, keep1, dens1, send2, keep2, dens2,
    msg, keep_in, act_keep, dens,
    sbuf, pair_ref, half_ref, diag, act_send, sem,
):
    core, x = where[0], where[1]
    blocks = (2 * x + (1 - core), 2 * x + core)
    for slot, block in enumerate(blocks):
        for copy in load_slabs(slabs_ref, sbuf, sem, block, slot):
            copy.start()

    inrows = NBQ * NACT
    per = NBQ // 2 * (NACT // 4)
    for slot, block in enumerate(blocks):

        def emit(h, in0, in1, act, d0, d1, slot=slot):
            if slot == 0:
                msg[rows_of(2 * h, 0, NACT), :] = in0.astype(BF)
                msg[rows_of(2 * h + 1, 0, NACT), :] = in1.astype(BF)
            else:
                keep_in[2 * h] = in0
                keep_in[2 * h + 1] = in1
            emit_active(
                h, act, core, x, msg, act_keep,
                (inrows + (3 - slot) * per, inrows + (7 - slot) * per), (2 + slot) * per,
            )
            diag[pl.ds(slot * NBQ + 2 * h, 1), :] = d0
            diag[pl.ds(slot * NBQ + 2 * h + 1, 1), :] = d1

        run_block(
            slabs_ref, sbuf, sem, block, slot, lt_ref, r_ref, pair_ref, half_ref, emit
        )
    for n, (send, keep) in enumerate(((send1, keep1), (send2, keep2))):
        for place in (0, 1):
            at = inrows + (4 * place + 1 - n) * per
            msg[pl.ds(at, per), :] = send[pl.ds(place * per, per), :]
            act_keep[place, pl.ds(n * per, per), :] = keep[place]
    for n, part in enumerate(
        (dens1[...] * 0.5, dens2[...] * 0.5, diag[:NBQ], diag[NBQ:])
    ):
        d, wire = split_density(part)
        dens[pl.ds(n * NBQ, NBQ), :] = d
        msg[pl.ds(inrows + 8 * per + (n ^ 1) * NBQ, NBQ), :] = wire


def exchange_kernel(mine, near, far, out):
    parts = []
    for q in range(NBQ):
        rows = pl.ds(q * NACT, NACT)
        parts.append(
            mine[q] + near[rows, :].astype(F32) + far[rows, :].astype(F32)
        )
    v = jnp.concatenate(parts, axis=1)
    hi = v.astype(BF)
    lo = (v - hi.astype(F32)).astype(BF)
    both = lax.dot_general(
        jnp.concatenate([hi, lo], axis=0), hi, (((1,), (1,)), ((), ())),
        preferred_element_type=F32,
    )
    out[...] = both[:NACT] + both[NACT:] + both[NACT:].T


def final_kernel(where, act, act_far, dens, dens_far, exch, own, partial):
    x = where[1]
    quarter = NACT // 4
    per = act.shape[0] // 4
    far = dens_far[...].astype(F32)
    far = far + pltpu.roll(far, BS, 1)
    d = dens[...] + far
    first = low_half(quarter)
    total = jnp.zeros((quarter, LANES), F32)
    halves = act.shape[0] // 2
    core = where[0]
    for n in range(4):
        xx = (1 - x) if n < 2 else x
        cc = (1 - core) if n % 2 == 0 else core
        base = NBQ * (2 * xx + cc)
        for h in range(NBQ // 2):
            a = act[pl.ds(n * per + h * quarter, quarter), :]
            m = (n + 2) % 4
            a = a + act_far[pl.ds(m * per + h * quarter, quarter), :].astype(F32)
            own[base + 2 * h] = a[:, :BS]
            own[base + 2 * h + 1] = a[:, BS:]
            q = n * NBQ + 2 * h
            scale = jnp.where(first, d[q : q + 1, :], d[q + 1 : q + 2, :])
            total = total + a * scale
    total = 2.0 * (total + pltpu.roll(total, BS, 1))
    partial[...] = -exch[...]
    at = pl.ds(pl.multiple_of((2 * x + core) * quarter, quarter), quarter)
    partial[at, :] = partial[at, :] + total[:, :BS]


VM = pl.BlockSpec(memory_space=pltpu.VMEM)
SM = pl.BlockSpec(memory_space=pltpu.SMEM)
HB = pl.BlockSpec(memory_space=pl.ANY)


def shape(dims, dtype):
    return jax.ShapeDtypeStruct(dims, dtype)


def slab_scratch(slabs, width, blocks):
    return [
        pltpu.VMEM((blocks, slabs, NBQ, width), BF),
        pltpu.VMEM((NBQ * BS, LANES), F32),
        pltpu.VMEM((NBQ, NCOL, slabs * BS), BF),
        pltpu.VMEM((blocks * NBQ, LANES), F32),
    ]


PARAMS = pltpu.CompilerParams(vmem_limit_bytes=48 * 1024 * 1024)


def paired_body(slabs, block_row, block_col, live_count, orbitals, hcore):
    nslab, batch, width = slabs.shape
    index = lax.axis_index("pair")
    core, x = lax.rem(index, 2), index // 2
    where = jnp.stack([core, x])
    swap_core = [(0, 1), (1, 0), (2, 3), (3, 2)]
    swap_x = [(0, 2), (2, 0), (1, 3), (3, 1)]
    inrows = NBQ * NACT
    per = NBQ // 2 * (NACT // 4)
    aos = nslab * BS
    small = (
        shape((2 * per, LANES), BF),
        shape((2, per, LANES), F32),
        shape((NBQ, LANES), F32),
    )
    lt, r, msg1, send1, keep1, dens1 = pl.pallas_call(
        first_kernel,
        name="slabs_first",
        in_specs=[SM, SM, SM, SM, HB, VM],
        out_specs=[VM] * 6,
        out_shape=(
            shape((nslab // 2, NCOL, PAIRED), BF),
            shape((aos, 2 * LANES), BF),
            shape((NBQ, NACT, NIN), BF),
        ) + small,
        scratch_shapes=slab_scratch(nslab, width, 1) + [pltpu.SemaphoreType.DMA((1, nslab // 2))],
        compiler_params=PARAMS,
    )(where, block_row, block_col, live_count, slabs, orbitals.T)
    near1 = lax.ppermute(msg1.reshape(inrows, LANES), "pair", swap_core)
    keep_in2, send2, keep2, dens2 = pl.pallas_call(
        second_kernel,
        name="slabs_second",
        in_specs=[SM, HB, VM, VM],
        out_specs=[VM] * 4,
        out_shape=(shape((NBQ, NACT, NIN), F32),) + small,
        scratch_shapes=slab_scratch(nslab, width, 1) + [pltpu.SemaphoreType.DMA((1, nslab // 2))],
        compiler_params=PARAMS,
        cost_estimate=pl.CostEstimate(flops=4 * 10**9, bytes_accessed=4 * 10**6, transcendentals=0),
    )(where, slabs, lt, r)
    out2 = (keep_in2.reshape(inrows, LANES) + near1.astype(F32)).astype(BF)
    far1 = lax.ppermute(out2, "pair", swap_x)
    msg3, keep_in3, act_keep, dens = pl.pallas_call(
        third_kernel,
        name="slabs_third",
        in_specs=[SM, HB] + [VM] * 8,
        out_specs=[VM] * 4,
        out_shape=(
            shape((inrows + 8 * per + 4 * NBQ, LANES), BF),
            shape((NBQ, NACT, NIN), F32),
            shape((2, 4 * per, LANES), F32),
            shape((4 * NBQ, LANES), F32),
        ),
        scratch_shapes=slab_scratch(nslab, width, 2)
        + [pltpu.VMEM((16, LANES), BF), pltpu.SemaphoreType.DMA((2, nslab // 2))],
        compiler_params=PARAMS,
        cost_estimate=pl.CostEstimate(flops=8 * 10**9, bytes_accessed=8 * 10**6, transcendentals=0),
    )(where, slabs, lt, r, send1, keep1, dens1, send2, keep2, dens2)
    near3 = lax.ppermute(msg3, "pair", swap_core)
    near_dens = near3[inrows + 8 * per :].astype(F32)
    near_dens = near_dens[:, :BS] + near_dens[:, BS:]
    dens = dens + jnp.concatenate([near_dens, near_dens], axis=1)
    act_other = act_keep[0] + near3[inrows : inrows + 4 * per].astype(F32)
    hi = dens.astype(BF).astype(F32)
    wire = jnp.where(lax.broadcasted_iota(jnp.int32, dens.shape, 1) < BS, hi, dens - hi)
    far3 = lax.ppermute(
        jnp.concatenate([act_other, wire], axis=0).astype(BF), "pair", swap_x
    )
    act_own = act_keep[1] + near3[inrows + 4 * per : inrows + 8 * per].astype(F32)
    exch = pl.pallas_call(
        exchange_kernel,
        name="exchange",
        in_specs=[VM] * 3,
        out_specs=VM,
        out_shape=shape((NACT, NACT), F32),
        compiler_params=PARAMS,
    )(keep_in3, near3[:inrows], far1)
    dens_far = far3[4 * per :]
    dens_far = jnp.concatenate([dens_far[2 * NBQ :], dens_far[: 2 * NBQ]], axis=0)
    own, partial = pl.pallas_call(
        final_kernel,
        name="active_and_coulomb",
        in_specs=[SM] + [VM] * 5,
        out_specs=[VM] * 2,
        out_shape=(
            shape((batch, NACT // 4, NACT), F32),
            shape((NACT, NACT), F32),
        ),
        compiler_params=PARAMS,
    )(where, act_own, far3[: 4 * per], dens, dens_far, exch)
    summed = lax.psum(partial, ("pair", "aux"))
    mine = lax.dynamic_slice_in_dim(summed, index * (NACT // 4), NACT // 4, 0)
    return (own, hcore + mine)


def slab_terms(values, left, right):
    half = jnp.einsum("mc,qmn->qnc", left, values, preferred_element_type=F32).astype(BF)
    first = jnp.einsum("qnt,nc->qtc", half[:, :, :NACT], right, preferred_element_type=F32)
    second = jnp.einsum("qnc,nt->qtc", half, right[:, :NACT], preferred_element_type=F32)
    trace = 2.0 * jnp.einsum(
        "qni,ni->q", half[:, :, NACT:], right[:, NACT:], preferred_element_type=F32
    )
    return (first + second, trace)


def general_body(slabs, block_row, block_col, live_count, orbitals, hcore):
    batch = slabs.shape[1]
    init = (jnp.zeros((batch, NACT, NCOL), F32), jnp.zeros((batch,), F32))

    def visit(k, state):
        values = lax.dynamic_index_in_dim(slabs, k, 0, keepdims=False)
        left = lax.dynamic_slice_in_dim(orbitals, block_row[k] * BS, BS, 0)
        right = lax.dynamic_slice_in_dim(orbitals, block_col[k] * BS, BS, 0)
        terms, trace = slab_terms(values.reshape(batch, BS, BS), left, right)
        return (state[0] + terms, state[1] + trace)

    vectors, density = lax.fori_loop(0, live_count[0], visit, init)
    density = lax.psum(density, "pair")
    owned = lax.psum_scatter(vectors, "pair", scatter_dimension=1, tiled=True)
    own_active, own_inactive = owned[:, :, :NACT], owned[:, :, NACT:]
    gathered = lax.all_gather(own_inactive.astype(BF), "pair", axis=1, tiled=True)
    exchange = jnp.einsum(
        "qti,qui->tu", own_inactive, gathered.astype(F32), precision=lax.Precision.HIGHEST
    )
    coulomb = jnp.einsum("qtu,q->tu", own_active, density, precision=lax.Precision.HIGHEST)
    return (own_active, hcore + lax.psum(2.0 * coulomb - exchange, "aux"))


def solution(mesh):
    placed = (
        P(("frag", "pair"), "aux", None),
        P(("frag", "pair")),
        P(("frag", "pair")),
        P(("frag", "pair")),
        P("frag", None),
        P(("frag", "pair"), None),
    )

    def body(slabs, *rest):
        fits = mesh.shape["pair"] == 4 and slabs.shape[1] == 4 * NBQ and slabs.shape[0] % 2 == 0
        return (paired_body if fits else general_body)(slabs, *rest)

    return jax.shard_map(
        body,
        mesh=mesh,
        in_specs=placed,
        out_specs=(P(("frag", "aux"), "pair", None), P(("frag", "pair"), None)),
        check_vma=False,
    )
```

time: 326 us -> 127 us (0.39); the launches traced: 322 us -> 127 us
  local copies, waits for them, and re-layouts: 134 us -> 2.75 us
  matrix products: 65.4 us -> 0 us
  Pallas kernels: 0 us -> 46.1 us
  waiting for transfers between devices: 56.4 us -> 10.9 us
  blocking collectives: 17.6 us -> 61.5 us
  loops' own time: 34 us -> 0 us
  between operations: 14.1 us -> 1.37 us
  starting transfers between devices: 0.08 us -> 3.64 us
    dot_general x66 -> x0, matrix products: 65.4 us -> none  [the longest x16 24 us: slab_terms(): jnp.einsum('mc,qmn->qnc', left, values, preferred_element_type=jnp.float32)]
    while x129 -> x0, local copies, waits for them, and re-layouts: 65.1 us -> none
    reduce_scatter x1 -> x0, waiting for transfers between devices: 46.8 us -> none  [body(): owned = lax.psum_scatter(vectors, 'pair', scatter_dimension=1, tiled=True)]
    pallas_call x0 -> x5, Pallas kernels: none -> 46.1 us  [the longest x1 20.8 us: paired_body(): pl.pallas_call(third_kernel, name='slabs_third', in_specs=[SM, HB] + [VM]...]
    psum x2 -> x1, blocking collectives: 17.6 us -> 61.5 us  [paired_body(): summed = lax.psum(partial, ('pair', 'aux'))]
    dynamic_slice x48 -> x0, local copies, waits for them, and re-layouts: 37.4 us -> none  [the longest x32 20.2 us: pick_slab(): return (values, rows[slot], cols[slot])]
    another operation x1 -> x0, loops' own time: 34 us -> none  [body(): vectors, density = lax.fori_loop(0, live_count[0], visit, init)]
    reshape x16 -> x0, local copies, waits for them, and re-layouts: 18 us -> none  [add_slab(): terms, trace = slab_terms(values.reshape(batch, BS, BS), left, right)]
  transfers between devices with their start and end apart: 2 -> 4, of which waited for: 2 -> 3; matrix products, arithmetic and copies ran while one was open for 0% -> 0% of each run, Pallas kernels for 0% -> 0%
where the time goes in v1:
time: 127 us
  blocking collectives  61.5 us (48%)
  Pallas kernels  46.1 us (36%)
  waiting for transfers between devices  10.9 us (9%)
  starting transfers between devices  3.64 us (3%)
  local copies, waits for them, and re-layouts  2.75 us (2%)
  between operations  1.37 us (1%)
    psum x1, blocking collectives, paired_body(): summed = lax.psum(partial, ('pair', 'aux'))  61.5 us
    pallas_call x1, Pallas kernels, paired_body(): pl.pallas_call(third_kernel, name='slabs_third', in_specs=[SM, HB] + [VM]...  20.8 us
    pallas_call x1, Pallas kernels, paired_body(): pl.pallas_call(first_kernel, name='slabs_first', in_specs=[SM, SM, SM, SM...  12.3 us
    pallas_call x1, Pallas kernels, paired_body(): pl.pallas_call(second_kernel, name='slabs_second', in_specs=[SM, HB, VM,...  11.1 us
    ppermute x1, waiting for transfers between devices, paired_body(): far1 = lax.ppermute(out2, 'pair', swap_x)  6.72 us
    ppermute x1, starting transfers between devices, paired_body(): far1 = lax.ppermute(out2, 'pair', swap_x)  2.95 us
    unnamed x8, local copies, waits for them, and re-layouts  2.72 us
  transfers between devices with their start and end apart: 4, of which 3 were waited for; matrix products, arithmetic and copies ran while one was open for 0% of the time, Pallas kernels for 0%

profile of v1, /device:TPU:0, one launch (start us, length us, event | category | flops | bytes accessed | tf_op | source)
XLA Modules:
  0.0 127.2 jit_solution(15378795696442748590)
XLA Ops:
  1.3 0.1 pad_add_fusion.where
  1.4 1.4 %copy-done = bf16[4096,192]{0,1:T(8,128)(2,1)S(1)} copy-done((bf16[4096,192]{0,1:T(8,128)(2,1)S(1)}, bf16[4096,192]{0,1:T(8,128)(2,1)}, u32[]{:S(2)}) %copy-start) | copy-done | bytes 1572888
  2.8 0.7 copy-done.1
  3.4 0.7 copy-done.2
  4.1 12.3 %slabs_first.1 = (bf16[8,192,128]{2,1,0:T(8,128)(2,1)S(1)}, bf16[1024,256]{1,0:T(8,128)(2,1)S(1)}, bf16[16,64,128]{2,1,0:T(8,128)(2,1)S(1)}, bf16[256,128]{1,0:T...) custom-call(s32[2]{0:T(128)S(1)} %pad_add_fusion.where, s32[16]{0:T(128)S(1)} %copy-done.1, ...), custom_call_target="tpu_custom_call" | custom-call | tf_op jit(solution)/shard_map/slabs_first/pallas_call | solution.py:329
  16.4 11.1 %slabs_second.1 = (f32[16,64,128]{2,1,0:T(8,128)S(1)}, bf16[256,128]{1,0:T(8,128)(2,1)S(1)}, f32[2,128,128]{2,1,0:T(8,128)S(1)}, f32[16,128]{1,0:T(8,128)S(1)}) custom-call(s32[2]{0:T(128)S(1)} %pad_add_fusion.where, bf16[16,64,4096]{2,1,0:T(8,128)(2,1)} %slabs_ref.5, bf16[8,192,128]{2,1,0:T(8,128)(2,1)S(1)} %get-tuple-element.18.lt_ref, ...), custom_call_target="tpu_custom_call" | custom-call | flops 4000000000 | bytes 4000000 | tf_op jit(solution)/shard_map/slabs_second/pallas_call | solution.py:343
  27.5 0.0 copy-start.3
  27.5 20.8 %slabs_third.1 = (bf16[2112,128]{1,0:T(8,128)(2,1)S(1)}, f32[16,64,128]{2,1,0:T(8,128)S(1)}, f32[2,512,128]{2,1,0:T(8,128)S(1)}, f32[64,128]{1,0:T(8,128)S(1)}) custom-call(s32[2]{0:T(128)S(1)} %pad_add_fusion.where, bf16[16,64,4096]{2,1,0:T(8,128)(2,1)} %slabs_ref.5, bf16[8,192,128]{2,1,0:T(8,128)(2,1)S(1)} %get-tuple-element.18.lt_ref, ...), custom_call_target="tpu_custom_call" | custom-call | flops 8000000000 | bytes 8000000 | tf_op jit(solution)/shard_map/slabs_third/pallas_call | solution.py:355
  48.4 0.5 collective-permute-start
  48.9 0.1 collective-permute-start.2
  49.0 1.9 %collective-permute-done.2 = bf16[1024,128]{1,0:T(8,128)(2,1)S(1)} collective-permute-done((bf16[1024,128]{1,0:T(8,128)(2,1)S(1)}, bf16[1024,128]{1,0:T(8,128)(2,1)S(1)}, u32[]{:S(2)}, u32[]{:S(2)}) %collective-permute-start.2) | collective-permute-done | bytes 262176 | tf_op jit(solution)/shard_map/ppermute | solution.py:342
  50.8 0.1 fusion
  50.9 3.0 %collective-permute-start.3 = (bf16[1024,128]{1,0:T(8,128)(2,1)S(1)}, bf16[1024,128]{1,0:T(8,128)(2,1)S(1)}, u32[]{:S(2)}, u32[]{:S(2)}) collective-permute-start(bf16[1024,128]{1,0:T(8,128)(2,1)S(1)} %fusion), channel_id=1, source_target_pairs={{0,8},{8,0},{4,12},{12,4},{1,9},{9,1},{5,13},{13,5},{2,10},{10,2},... | collective-permute-start | bytes 786440 | tf_op jit(solution)/shard_map/ppermute | solution.py:354
  53.8 0.0 collective-permute-done
  53.8 0.1 slice_add_fusion
  53.9 0.1 fusion.2
  54.1 0.1 collective-permute-start.1
  54.2 6.7 %collective-permute-done.3.far = bf16[1024,128]{1,0:T(8,128)(2,1)S(1)} collective-permute-done((bf16[1024,128]{1,0:T(8,128)(2,1)S(1)}, bf16[1024,128]{1,0:T(8,128)(2,1)S(1)}, u32[]{:S(2)}, u32[]{:S(2)}) %collective-permute-start.3) | collective-permute-done | bytes 262176 | tf_op jit(solution)/shard_map/ppermute | solution.py:354
  60.9 0.4 exchange.1.exch
  61.3 2.3 %collective-permute-done.1 = bf16[576,128]{1,0:T(8,128)(2,1)S(1)} collective-permute-done((bf16[576,128]{1,0:T(8,128)(2,1)S(1)}, bf16[576,128]{1,0:T(8,128)(2,1)S(1)}, u32[]{:S(2)}, u32[]{:S(2)}) %collective-permute-start.1) | collective-permute-done | bytes 147488 | tf_op jit(solution)/shard_map/ppermute | solution.py:378
  63.6 1.5 %active_and_coulomb.1 = (f32[64,16,64]{2,1,0:T(8,128)}, f32[64,64]{1,0:T(8,128)S(1)}) custom-call(s32[2]{0:T(128)S(1)} %pad_add_fusion.where, f32[512,128]{1,0:T(8,128)S(1)} %get-tuple-element.37.act, bf16[512,128]{1,0:T(8,128)(2,1)S(1)} %slice.52.act_far, f32[64,128]{1,0:T(8,128)S(1)} %get-tuple-element.35.dens, ...), custom_call_target="tpu_custom_call" | custom-call | tf_op jit(solution)/shard_map/active_and_coulomb/pallas_call | solution.py:392
  65.1 61.5 %psum.7 = f32[64,64]{1,0:T(8,128)S(1)} all-reduce(f32[64,64]{1,0:T(8,128)S(1)} %get-tuple-element.33), channel_id=1, replica_groups=mesh['frag'=2,'pair'=4,'aux'=4] {'pair','aux'}, use_global_device_ids=true, to_apply=%region_0.1 | all-reduce | flops 4096 | bytes 32768 | tf_op jit(solution)/shard_map/psum | solution.py:403
  126.6 0.0 copy-done.3
  126.6 0.6 dynamic-slice_add_fusion
  (11 shorter events, 0.1 us)
Async XLA Ops:
  1.4 1.4 %copy-start = (bf16[4096,192]{0,1:T(8,128)(2,1)S(1)}, bf16[4096,192]{0,1:T(8,128)(2,1)}, u32[]{:S(2)}) copy-start(bf16[4096,192]{0,1:T(8,128)(2,1)} %param.10) | copy-start | bytes 4718596
  2.8 0.7 copy-start.1
  3.4 0.7 copy-start.2
  27.5 99.1 %copy-start.3 = (f32[16,64]{1,0:T(8,128)S(1)}, f32[16,64]{1,0:T(8,128)}, u32[]{:S(2)}) copy-start(f32[16,64]{1,0:T(8,128)} %param.11) | copy-start | bytes 12292
  48.4 5.5 %collective-permute-start = (bf16[2112,128]{1,0:T(8,128)(2,1)S(1)}, bf16[2112,128]{1,0:T(8,128)(2,1)S(1)}, u32[]{:S(2)}, u32[]{:S(2)}) collective-permute-start(bf16[2112,128]{1,0:T(8,128)(2,1)S(1)} %get-tuple-element.27), channel_id=1, source_target_pairs={{0,4},{4,0},{8,12},{12,8},{1,5},{5,1},{9,13},{13,9},{2,6},{6,2},{1... | collective-permute-start | bytes 1622024 | tf_op jit(solution)/shard_map/ppermute | solution.py:371
  48.9 1.9 %collective-permute-start.2 = (bf16[1024,128]{1,0:T(8,128)(2,1)S(1)}, bf16[1024,128]{1,0:T(8,128)(2,1)S(1)}, u32[]{:S(2)}, u32[]{:S(2)}) collective-permute-start(bf16[1024,128]{1,0:T(8,128)(2,1)S(1)} %bitcast.15), channel_id=1, source_target_pairs={{0,4},{4,0},{8,12},{12,8},{1,5},{5,1},{9,13},{13,9},{2,6},{6,2},{1... | collective-permute-start | bytes 786440 | tf_op jit(solution)/shard_map/ppermute | solution.py:342
  50.9 10.0 %collective-permute-start.3 = (bf16[1024,128]{1,0:T(8,128)(2,1)S(1)}, bf16[1024,128]{1,0:T(8,128)(2,1)S(1)}, u32[]{:S(2)}, u32[]{:S(2)}) collective-permute-start(bf16[1024,128]{1,0:T(8,128)(2,1)S(1)} %fusion), channel_id=1, source_target_pairs={{0,8},{8,0},{4,12},{12,4},{1,9},{9,1},{5,13},{13,5},{2,10},{10,2},... | collective-permute-start | bytes 786440 | tf_op jit(solution)/shard_map/ppermute | solution.py:354
  54.1 9.5 %collective-permute-start.1 = (bf16[576,128]{1,0:T(8,128)(2,1)S(1)}, bf16[576,128]{1,0:T(8,128)(2,1)S(1)}, u32[]{:S(2)}, u32[]{:S(2)}) collective-permute-start(bf16[576,128]{1,0:T(8,128)(2,1)S(1)} %pad_maximum_fusion), channel_id=1, source_target_pairs={{0,8},{8,0},{4,12},{12,4},{1,9},{9,1},{5,13},{13,5},{2,10},{10,2},... | collective-permute-start | bytes 442376 | tf_op jit(solution)/shard_map/ppermute | solution.py:378

commit v2 on v1

--- a/solution.py
+++ b/solution.py
@@ -1,5 +1,3 @@
-import functools
-
 import jax
 import jax.numpy as jnp
 from jax import lax
@@ -14,6 +12,7 @@
 LANES = 128
 NBQ = 16
 PAIRED = 2 * BS
+QSTEP, MSTEP = 3, 49
 BF = jnp.bfloat16
 F32 = jnp.float32
 
@@ -57,13 +56,13 @@
             b = sbuf[2 * k + 1, :, lanes].astype(F32)
             even = jnp.where(first, a, pltpu.roll(b, BS, 1))
             odd = jnp.where(first, pltpu.roll(a, BS, 1), b)
-            pair_ref[pl.ds(2 * j, NBQ, stride=BS), :] = even
-            pair_ref[pl.ds(2 * j + 1, NBQ, stride=BS), :] = odd
+            pair_ref[pl.ds(MSTEP * 2 * j, NBQ, stride=QSTEP), :] = even
+            pair_ref[pl.ds(MSTEP * (2 * j + 1), NBQ, stride=QSTEP), :] = odd
         left = lt_ref[k]
         for q in range(0, NBQ, 2):
             cols = []
             for u in (q, q + 1):
-                s = pair_ref[pl.ds(u * BS, BS), :].astype(BF)
+                s = pair_ref[pl.ds(u * QSTEP, BS, stride=MSTEP), :].astype(BF)
                 cols.append(
                     jnp.concatenate(
                         [jnp.where(first_s, s, zero), jnp.where(first_s, zero, s)], axis=0
@@ -260,7 +259,7 @@
     out[...] = both[:NACT] + both[NACT:] + both[NACT:].T
 
 
-def final_kernel(where, act, act_far, dens, dens_far, exch, own, partial):
+def final_kernel(where, act, act_far, dens, dens_far, exch, e1, e2, e3, own, partial):
     x = where[1]
     quarter = NACT // 4
     per = act.shape[0] // 4
@@ -285,9 +284,8 @@
             scale = jnp.where(first, d[q : q + 1, :], d[q + 1 : q + 2, :])
             total = total + a * scale
     total = 2.0 * (total + pltpu.roll(total, BS, 1))
-    partial[...] = -exch[...]
     at = pl.ds(pl.multiple_of((2 * x + core) * quarter, quarter), quarter)
-    partial[at, :] = partial[at, :] + total[:, :BS]
+    partial[...] = total[:, :BS] - (exch[at, :] + e1[...] + e2[...] + e3[...])
 
 
 VM = pl.BlockSpec(memory_space=pltpu.VMEM)
@@ -302,13 +300,23 @@
 def slab_scratch(slabs, width, blocks):
     return [
         pltpu.VMEM((blocks, slabs, NBQ, width), BF),
-        pltpu.VMEM((NBQ * BS, LANES), F32),
+        pltpu.VMEM((MSTEP * BS, LANES), F32),
         pltpu.VMEM((NBQ, NCOL, slabs * BS), BF),
         pltpu.VMEM((blocks * NBQ, LANES), F32),
     ]
 
 
 PARAMS = pltpu.CompilerParams(vmem_limit_bytes=48 * 1024 * 1024)
+
+
+def sum_over_aux(part):
+    n = lax.axis_size("aux")
+    if n != 4:
+        return lax.psum(part, "aux")
+    one, two, three = (
+        lax.ppermute(part, "aux", [(z, (z + k) % n) for z in range(n)]) for k in (1, 2, 3)
+    )
+    return (part + two) + (one + three)
 
 
 def paired_body(slabs, block_row, block_col, live_count, orbitals, hcore):
@@ -387,22 +395,27 @@
         out_shape=shape((NACT, NACT), F32),
         compiler_params=PARAMS,
     )(keep_in3, near3[:inrows], far1)
+    def rows_for(peer):
+        return lax.dynamic_slice_in_dim(exch, peer * (NACT // 4), NACT // 4, 0)
+
+    parts = [
+        lax.ppermute(rows_for(index ^ k), "pair", [(p, p ^ k) for p in range(4)])
+        for k in (1, 2, 3)
+    ]
     dens_far = far3[4 * per :]
     dens_far = jnp.concatenate([dens_far[2 * NBQ :], dens_far[: 2 * NBQ]], axis=0)
     own, partial = pl.pallas_call(
         final_kernel,
         name="active_and_coulomb",
-        in_specs=[SM] + [VM] * 5,
+        in_specs=[SM] + [VM] * 8,
         out_specs=[VM] * 2,
         out_shape=(
             shape((batch, NACT // 4, NACT), F32),
-            shape((NACT, NACT), F32),
+            shape((NACT // 4, NACT), F32),
         ),
         compiler_params=PARAMS,
-    )(where, act_own, far3[: 4 * per], dens, dens_far, exch)
-    summed = lax.psum(partial, ("pair", "aux"))
-    mine = lax.dynamic_slice_in_dim(summed, index * (NACT // 4), NACT // 4, 0)
-    return (own, hcore + mine)
+    )(where, act_own, far3[: 4 * per], dens, dens_far, exch, *parts)
+    return (own, hcore + sum_over_aux(partial))
 
 
 def slab_terms(values, left, right):

time: 127 us -> 70.3 us (0.55)
  blocking collectives: 61.5 us -> 0 us
  starting transfers between devices: 3.64 us -> 11 us
  Pallas kernels: 46.1 us -> 39.4 us
  waiting for transfers between devices: 10.9 us -> 14.6 us
    psum x1 -> x0, blocking collectives: 61.5 us -> none  [paired_body(): summed = lax.psum(partial, ('pair', 'aux'))]
    ppermute x0 -> x6, starting transfers between devices: none -> 7.35 us  [the longest x3 5.1 us: sum_over_aux(): lax.ppermute(part, 'aux', [(z, (z + k) % n) for z in range(n)])]
    ppermute x0 -> x6, waiting for transfers between devices: none -> 6.02 us  [the longest x3 4.44 us: sum_over_aux(): lax.ppermute(part, 'aux', [(z, (z + k) % n) for z in range(n)])]
    pallas_call x1, Pallas kernels: 20.8 us -> 17.5 us  [paired_body(): pl.pallas_call(third_kernel, name='slabs_third', in_specs=[SM, HB] + [VM]...]
    ppermute x1, waiting for transfers between devices: 2.31 us -> 0.04 us  [paired_body(): lax.ppermute(jnp.concatenate([act_other, wire], axis=0).astype(BF), 'pair...]
    pallas_call x1, Pallas kernels: 12.3 us -> 10.5 us  [paired_body(): pl.pallas_call(first_kernel, name='slabs_first', in_specs=[SM, SM, SM, SM...]
    pallas_call x1, Pallas kernels: 11.1 us -> 9.52 us  [paired_body(): pl.pallas_call(second_kernel, name='slabs_second', in_specs=[SM, HB, VM,...]
  transfers between devices with their start and end apart: 4 -> 10, of which waited for: 3 -> 6; matrix products, arithmetic and copies ran while one was open for 0% -> 0% of each run, Pallas kernels for 0% -> 1%
where the time goes in v2:
time: 70.3 us; the launch traced here: 70.1 us
  Pallas kernels  39.4 us (56%)
  waiting for transfers between devices  14.6 us (21%)
  starting transfers between devices  11 us (16%)
  local copies, waits for them, and re-layouts  2.77 us (4%)
  between operations  1.39 us (2%)
  other arithmetic  0.97 us (1%)
    pallas_call x1, Pallas kernels, paired_body(): pl.pallas_call(third_kernel, name='slabs_third', in_specs=[SM, HB] + [VM]...  17.5 us
    pallas_call x1, Pallas kernels, paired_body(): pl.pallas_call(first_kernel, name='slabs_first', in_specs=[SM, SM, SM, SM...  10.5 us
    pallas_call x1, Pallas kernels, paired_body(): pl.pallas_call(second_kernel, name='slabs_second', in_specs=[SM, HB, VM,...  9.52 us
    ppermute x1, waiting for transfers between devices, paired_body(): far1 = lax.ppermute(out2, 'pair', swap_x)  6.71 us
    ppermute x3, starting transfers between devices, sum_over_aux(): lax.ppermute(part, 'aux', [(z, (z + k) % n) for z in range(n)])  5.1 us
    ppermute x3, waiting for transfers between devices, sum_over_aux(): lax.ppermute(part, 'aux', [(z, (z + k) % n) for z in range(n)])  4.44 us
    ppermute x1, starting transfers between devices, paired_body(): far1 = lax.ppermute(out2, 'pair', swap_x)  2.93 us
    unnamed x8, local copies, waits for them, and re-layouts  2.72 us
  transfers between devices with their start and end apart: 10, of which 6 were waited for; matrix products, arithmetic and copies ran while one was open for 0% of the time, Pallas kernels for 1%

profile of v2, /device:TPU:0, one launch (start us, length us, event | category | flops | bytes accessed | tf_op | source)
XLA Modules:
  0.0 70.1 jit_solution(16793080012796812281)
XLA Ops:
  1.4 1.4 %copy-done = bf16[4096,192]{0,1:T(8,128)(2,1)S(1)} copy-done((bf16[4096,192]{0,1:T(8,128)(2,1)S(1)}, bf16[4096,192]{0,1:T(8,128)(2,1)}, u32[]{:S(2)}) %copy-start) | copy-done | bytes 1572888
  2.8 0.7 copy-done.1
  3.4 0.7 copy-done.2
  4.1 10.5 %slabs_first.1 = (bf16[8,192,128]{2,1,0:T(8,128)(2,1)S(1)}, bf16[1024,256]{1,0:T(8,128)(2,1)S(1)}, bf16[16,64,128]{2,1,0:T(8,128)(2,1)S(1)}, bf16[256,128]{1,0:T...) custom-call(s32[2]{0:T(128)S(1)} %pad_add_fusion.where, s32[16]{0:T(128)S(1)} %copy-done.1, ...), custom_call_target="tpu_custom_call" | custom-call | tf_op jit(solution)/shard_map/slabs_first/pallas_call | solution.py:337
  14.6 9.5 %slabs_second.1 = (f32[16,64,128]{2,1,0:T(8,128)S(1)}, bf16[256,128]{1,0:T(8,128)(2,1)S(1)}, f32[2,128,128]{2,1,0:T(8,128)S(1)}, f32[16,128]{1,0:T(8,128)S(1)}) custom-call(s32[2]{0:T(128)S(1)} %pad_add_fusion.where, bf16[16,64,4096]{2,1,0:T(8,128)(2,1)} %slabs_ref.5, bf16[8,192,128]{2,1,0:T(8,128)(2,1)S(1)} %get-tuple-element.18.lt_ref, ...), custom_call_target="tpu_custom_call" | custom-call | flops 4000000000 | bytes 4000000 | tf_op jit(solution)/shard_map/slabs_second/pallas_call | solution.py:351
  24.1 17.5 %slabs_third.1 = (bf16[2112,128]{1,0:T(8,128)(2,1)S(1)}, f32[16,64,128]{2,1,0:T(8,128)S(1)}, f32[2,512,128]{2,1,0:T(8,128)S(1)}, f32[64,128]{1,0:T(8,128)S(1)}) custom-call(s32[2]{0:T(128)S(1)} %pad_add_fusion.where, bf16[16,64,4096]{2,1,0:T(8,128)(2,1)} %slabs_ref.5, bf16[8,192,128]{2,1,0:T(8,128)(2,1)S(1)} %get-tuple-element.18.lt_ref, ...), custom_call_target="tpu_custom_call" | custom-call | flops 8000000000 | bytes 8000000 | tf_op jit(solution)/shard_map/slabs_third/pallas_call | solution.py:363
  41.6 0.5 collective-permute-start
  42.1 0.1 collective-permute-start.2
  42.2 1.9 %collective-permute-done.2 = bf16[1024,128]{1,0:T(8,128)(2,1)S(1)} collective-permute-done((bf16[1024,128]{1,0:T(8,128)(2,1)S(1)}, bf16[1024,128]{1,0:T(8,128)(2,1)S(1)}, u32[]{:S(2)}, u32[]{:S(2)}) %collective-permute-start.2) | collective-permute-done | bytes 262176 | tf_op jit(solution)/shard_map/ppermute | solution.py:350
  44.1 2.9 %collective-permute-start.3 = (bf16[1024,128]{1,0:T(8,128)(2,1)S(1)}, bf16[1024,128]{1,0:T(8,128)(2,1)S(1)}, u32[]{:S(2)}, u32[]{:S(2)}) collective-permute-start(bf16[1024,128]{1,0:T(8,128)(2,1)S(1)} %fusion), channel_id=1, source_target_pairs={{0,8},{8,0},{4,12},{12,4},{1,9},{9,1},{5,13},{13,5},{2,10},{10,2},... | collective-permute-start | bytes 786440 | tf_op jit(solution)/shard_map/ppermute | solution.py:362
  47.2 0.1 fusion.2
  47.3 0.1 collective-permute-start.1
  47.4 6.7 %collective-permute-done.3.far = bf16[1024,128]{1,0:T(8,128)(2,1)S(1)} collective-permute-done((bf16[1024,128]{1,0:T(8,128)(2,1)S(1)}, bf16[1024,128]{1,0:T(8,128)(2,1)S(1)}, u32[]{:S(2)}, u32[]{:S(2)}) %collective-permute-start.3) | collective-permute-done | bytes 262176 | tf_op jit(solution)/shard_map/ppermute | solution.py:362
  54.1 0.4 exchange.1.exch
  54.5 0.2 collective-permute-start.6
  54.8 2.0 %collective-permute-start.5 = (f32[16,64]{1,0:T(8,128)S(1)}, f32[16,64]{1,0:T(8,128)S(1)}, u32[]{:S(2)}, u32[]{:S(2)}) collective-permute-start(f32[16,64]{1,0:T(8,128)S(1)} %get-tuple-element.41), channel_id=1, source_target_pairs={{0,8},{4,12},{8,0},{12,4},{1,9},{5,13},{9,1},{13,5},{2,10},{6,14},... | collective-permute-start | bytes 12296 | tf_op jit(solution)/shard_map/ppermute | solution.py:402
  56.8 0.8 %collective-permute-done.6.e3 = f32[16,64]{1,0:T(8,128)S(1)} collective-permute-done((f32[16,64]{1,0:T(8,128)S(1)}, f32[16,64]{1,0:T(8,128)S(1)}, u32[]{:S(2)}, u32[]{:S(2)}) %collective-permute-start.6) | collective-permute-done | bytes 4128 | tf_op jit(solution)/shard_map/ppermute | solution.py:402
  57.7 0.7 %collective-permute-done.5.e2 = f32[16,64]{1,0:T(8,128)S(1)} collective-permute-done((f32[16,64]{1,0:T(8,128)S(1)}, f32[16,64]{1,0:T(8,128)S(1)}, u32[]{:S(2)}, u32[]{:S(2)}) %collective-permute-start.5) | collective-permute-done | bytes 4128 | tf_op jit(solution)/shard_map/ppermute | solution.py:402
  58.4 1.5 %active_and_coulomb.1 = (f32[64,16,64]{2,1,0:T(8,128)}, f32[16,64]{1,0:T(8,128)S(1)}) custom-call(s32[2]{0:T(128)S(1)} %pad_add_fusion.where, f32[512,128]{1,0:T(8,128)S(1)} %get-tuple-element.37.act, bf16[512,128]{1,0:T(8,128)(2,1)S(1)} %slice.52.act_far, f32[64,128]{1,0:T(8,128)S(1)} %get-tuple-element.35.dens, ...), custom_call_target="tpu_custom_call" | custom-call | tf_op jit(solution)/shard_map/active_and_coulomb/pallas_call | solution.py:407
  60.0 4.1 %collective-permute-start.9 = (f32[16,64]{1,0:T(8,128)S(1)}, f32[16,64]{1,0:T(8,128)S(1)}, u32[]{:S(2)}, u32[]{:S(2)}) collective-permute-start(f32[16,64]{1,0:T(8,128)S(1)} %get-tuple-element.33), channel_id=1, source_target_pairs={{0,3},{1,0},{2,1},{3,2},{4,7},{5,4},{6,5},{7,6},{8,11},{9,8},{10,9... | collective-permute-start | bytes 12296 | tf_op jit(solution)/shard_map/ppermute | solution.py:317
  64.1 1.0 %collective-permute-start.7 = (f32[16,64]{1,0:T(8,128)S(1)}, f32[16,64]{1,0:T(8,128)S(1)}, u32[]{:S(2)}, u32[]{:S(2)}) collective-permute-start(f32[16,64]{1,0:T(8,128)S(1)} %get-tuple-element.33), channel_id=1, source_target_pairs={{0,2},{1,3},{2,0},{3,1},{4,6},{5,7},{6,4},{7,5},{8,10},{9,11},{10,... | collective-permute-start | bytes 12296 | tf_op jit(solution)/shard_map/ppermute | solution.py:317
  65.1 0.4 collective-permute-done.9
  65.4 4.1 %collective-permute-done.8 = f32[16,64]{1,0:T(8,128)S(1)} collective-permute-done((f32[16,64]{1,0:T(8,128)S(1)}, f32[16,64]{1,0:T(8,128)S(1)}, u32[]{:S(2)}, u32[]{:S(2)}) %collective-permute-start.8) | collective-permute-done | bytes 4128 | tf_op jit(solution)/shard_map/ppermute | solution.py:317
  69.5 0.6 add_add_fusion
  (23 shorter events, 0.4 us)
Async XLA Ops:
  1.4 1.4 %copy-start = (bf16[4096,192]{0,1:T(8,128)(2,1)S(1)}, bf16[4096,192]{0,1:T(8,128)(2,1)}, u32[]{:S(2)}) copy-start(bf16[4096,192]{0,1:T(8,128)(2,1)} %param.10) | copy-start | bytes 4718596
  2.8 0.7 copy-start.1
  3.4 0.7 copy-start.2
  24.1 45.4 %copy-start.3 = (f32[16,64]{1,0:T(8,128)S(1)}, f32[16,64]{1,0:T(8,128)}, u32[]{:S(2)}) copy-start(f32[16,64]{1,0:T(8,128)} %param.11) | copy-start | bytes 12292
  41.6 5.4 %collective-permute-start = (bf16[2112,128]{1,0:T(8,128)(2,1)S(1)}, bf16[2112,128]{1,0:T(8,128)(2,1)S(1)}, u32[]{:S(2)}, u32[]{:S(2)}) collective-permute-start(bf16[2112,128]{1,0:T(8,128)(2,1)S(1)} %get-tuple-element.27), channel_id=1, source_target_pairs={{0,4},{4,0},{8,12},{12,8},{1,5},{5,1},{9,13},{13,9},{2,6},{6,2},{1... | collective-permute-start | bytes 1622024 | tf_op jit(solution)/shard_map/ppermute | solution.py:379
  42.1 1.9 %collective-permute-start.2 = (bf16[1024,128]{1,0:T(8,128)(2,1)S(1)}, bf16[1024,128]{1,0:T(8,128)(2,1)S(1)}, u32[]{:S(2)}, u32[]{:S(2)}) collective-permute-start(bf16[1024,128]{1,0:T(8,128)(2,1)S(1)} %bitcast.15), channel_id=1, source_target_pairs={{0,4},{4,0},{8,12},{12,8},{1,5},{5,1},{9,13},{13,9},{2,6},{6,2},{1... | collective-permute-start | bytes 786440 | tf_op jit(solution)/shard_map/ppermute | solution.py:350
  44.1 10.0 %collective-permute-start.3 = (bf16[1024,128]{1,0:T(8,128)(2,1)S(1)}, bf16[1024,128]{1,0:T(8,128)(2,1)S(1)}, u32[]{:S(2)}, u32[]{:S(2)}) collective-permute-start(bf16[1024,128]{1,0:T(8,128)(2,1)S(1)} %fusion), channel_id=1, source_target_pairs={{0,8},{8,0},{4,12},{12,4},{1,9},{9,1},{5,13},{13,5},{2,10},{10,2},... | collective-permute-start | bytes 786440 | tf_op jit(solution)/shard_map/ppermute | solution.py:362
  47.3 9.5 %collective-permute-start.1 = (bf16[576,128]{1,0:T(8,128)(2,1)S(1)}, bf16[576,128]{1,0:T(8,128)(2,1)S(1)}, u32[]{:S(2)}, u32[]{:S(2)}) collective-permute-start(bf16[576,128]{1,0:T(8,128)(2,1)S(1)} %pad_maximum_fusion), channel_id=1, source_target_pairs={{0,8},{8,0},{4,12},{12,4},{1,9},{9,1},{5,13},{13,5},{2,10},{10,2},... | collective-permute-start | bytes 442376 | tf_op jit(solution)/shard_map/ppermute | solution.py:386
  54.5 3.1 %collective-permute-start.6 = (f32[16,64]{1,0:T(8,128)S(1)}, f32[16,64]{1,0:T(8,128)S(1)}, u32[]{:S(2)}, u32[]{:S(2)}) collective-permute-start(f32[16,64]{1,0:T(8,128)S(1)} %get-tuple-element.40), channel_id=1, source_target_pairs={{0,12},{4,8},{8,4},{12,0},{1,13},{5,9},{9,5},{13,1},{2,14},{6,10},... | collective-permute-start | bytes 12296 | tf_op jit(solution)/shard_map/ppermute | solution.py:402
  54.8 3.7 %collective-permute-start.5 = (f32[16,64]{1,0:T(8,128)S(1)}, f32[16,64]{1,0:T(8,128)S(1)}, u32[]{:S(2)}, u32[]{:S(2)}) collective-permute-start(f32[16,64]{1,0:T(8,128)S(1)} %get-tuple-element.41), channel_id=1, source_target_pairs={{0,8},{4,12},{8,0},{12,4},{1,9},{5,13},{9,1},{13,5},{2,10},{6,14},... | collective-permute-start | bytes 12296 | tf_op jit(solution)/shard_map/ppermute | solution.py:402
  56.7 1.7 %collective-permute-start.4 = (f32[16,64]{1,0:T(8,128)S(1)}, f32[16,64]{1,0:T(8,128)S(1)}, u32[]{:S(2)}, u32[]{:S(2)}) collective-permute-start(f32[16,64]{1,0:T(8,128)S(1)} %get-tuple-element.42), channel_id=1, source_target_pairs={{0,4},{4,0},{8,12},{12,8},{1,5},{5,1},{9,13},{13,9},{2,6},{6,2},{1... | collective-permute-start | bytes 12296 | tf_op jit(solution)/shard_map/ppermute | solution.py:402
  60.0 5.5 %collective-permute-start.9 = (f32[16,64]{1,0:T(8,128)S(1)}, f32[16,64]{1,0:T(8,128)S(1)}, u32[]{:S(2)}, u32[]{:S(2)}) collective-permute-start(f32[16,64]{1,0:T(8,128)S(1)} %get-tuple-element.33), channel_id=1, source_target_pairs={{0,3},{1,0},{2,1},{3,2},{4,7},{5,4},{6,5},{7,6},{8,11},{9,8},{10,9... | collective-permute-start | bytes 12296 | tf_op jit(solution)/shard_map/ppermute | solution.py:317
  64.1 5.4 %collective-permute-start.8 = (f32[16,64]{1,0:T(8,128)S(1)}, f32[16,64]{1,0:T(8,128)S(1)}, u32[]{:S(2)}, u32[]{:S(2)}) collective-permute-start(f32[16,64]{1,0:T(8,128)S(1)} %get-tuple-element.33), channel_id=1, source_target_pairs={{0,1},{1,2},{2,3},{3,0},{4,5},{5,6},{6,7},{7,4},{8,9},{9,10},{10,1... | collective-permute-start | bytes 12296 | tf_op jit(solution)/shard_map/ppermute | solution.py:317
  64.1 5.4 %collective-permute-start.7 = (f32[16,64]{1,0:T(8,128)S(1)}, f32[16,64]{1,0:T(8,128)S(1)}, u32[]{:S(2)}, u32[]{:S(2)}) collective-permute-start(f32[16,64]{1,0:T(8,128)S(1)} %get-tuple-element.33), channel_id=1, source_target_pairs={{0,2},{1,3},{2,0},{3,1},{4,6},{5,7},{6,4},{7,5},{8,10},{9,11},{10,... | collective-permute-start | bytes 12296 | tf_op jit(solution)/shard_map/ppermute | solution.py:317

commit v3 on v0

v3 whole, which is shorter than its diff:
```python
import jax
import jax.numpy as jnp
from jax import lax
from jax.experimental import pallas as pl
from jax.experimental.pallas import tpu as pltpu
from jax.sharding import PartitionSpec as P

BS = 64
NACT = 64
NCOL = 192
NIN = NCOL - NACT
LANES = 128
NBQ = 16
PAIRED = 2 * BS
QSTEP, MSTEP = 3, 49
BF = jnp.bfloat16
F32 = jnp.float32


def low_half(rows):
    return lax.broadcasted_iota(jnp.int32, (rows, LANES), 1) < BS


def orbital_blocks(scalars, slabs, windows, lt_ref, r_ref):
    first = low_half(NCOL)
    live = scalars[2 * slabs]

    def window(n, slot, upper):
        w = windows[n].astype(F32)
        w = jnp.concatenate([w[NACT:], w[:NACT]], axis=0)
        moved = lax.rem(scalars[n], 2) != (1 if upper else 0)
        w = jnp.where(moved, pltpu.roll(w, BS, 1), w)
        return jnp.where(slot < live, w, 0.0)

    for k in range(slabs // 2):
        a, b = 2 * k, 2 * k + 1
        left = jnp.where(first, window(a, a, False), window(b, b, True))
        lt_ref[k] = left.astype(BF)
        right = jnp.where(first, window(slabs + a, a, False), window(slabs + b, b, True))
        right = jnp.concatenate([right, right[NIN:]], axis=0)
        r_ref[pl.ds(k * PAIRED, PAIRED), :] = right.T.astype(BF)


def slab_copy(slabs_ref, sbuf, sem, block, k):
    last = slabs_ref.shape[0] // 2 - 1
    pair = min(k, last) if isinstance(k, int) else jnp.minimum(k, last)
    return pltpu.make_async_copy(
        slabs_ref.at[pl.ds(2 * pair, 2), pl.ds(pl.multiple_of(block * NBQ, NBQ), NBQ), :],
        sbuf.at[k],
        sem.at[k],
    )


def start_slabs(slabs_ref, sbuf, sem, block):
    for k in range(slabs_ref.shape[0] // 2 + 1):
        slab_copy(slabs_ref, sbuf, sem, block, k).start()


def run_block(slabs_ref, block, lt_ref, r_ref, scratch, emit):
    sbuf, even_ref, odd_ref, half_ref, diag, sem = scratch
    pairs = slabs_ref.shape[0] // 2
    first = low_half(NBQ)
    first_s = low_half(BS)
    zero = jnp.zeros((BS, LANES), BF)
    group = 4

    def wait(k):
        slab_copy(slabs_ref, sbuf, sem, block, k).wait()

    def relayout(k, out):
        for j in range(sbuf.shape[3] // LANES):
            lanes = slice(j * LANES, (j + 1) * LANES)
            a = sbuf[k, 0, :, lanes].astype(F32)
            b = sbuf[k, 1, :, lanes].astype(F32)
            out[pl.ds(MSTEP * 2 * j, NBQ, stride=QSTEP), :] = jnp.where(
                first, a, pltpu.roll(b, BS, 1)
            )
            out[pl.ds(MSTEP * (2 * j + 1), NBQ, stride=QSTEP), :] = jnp.where(
                first, pltpu.roll(a, BS, 1), b
            )

    def half_transform(k, rows):
        left = lt_ref[k]
        at = pl.ds(pl.multiple_of(k * LANES, LANES), LANES)
        for q in range(0, NBQ, group):
            cols = []
            for u in range(q, q + group):
                s = rows[pl.ds(u * QSTEP, BS, stride=MSTEP), :].astype(BF)
                cols.append(
                    jnp.concatenate(
                        [jnp.where(first_s, s, zero), jnp.where(first_s, zero, s)], axis=0
                    )
                )
            half = jnp.dot(left, jnp.concatenate(cols, axis=1), preferred_element_type=F32)
            half = half.astype(BF)
            for u in range(group):
                half_ref[q + u, :, at] = half[:, u * LANES : (u + 1) * LANES]

    def two_pairs(i, carry):
        wait(2 * i + 1)
        wait(2 * i + 2)
        relayout(2 * i + 1, odd_ref)
        half_transform(2 * i, even_ref)
        relayout(2 * i + 2, even_ref)
        half_transform(2 * i + 1, odd_ref)
        return carry

    def second_transform(g, carry):
        lhs = half_ref[pl.ds(group * g, group)].reshape(group * NCOL, half_ref.shape[2])
        whole = jnp.dot(lhs, r_ref[...], preferred_element_type=F32)
        eye = lax.broadcasted_iota(jnp.int32, (NIN, NIN), 0) == lax.broadcasted_iota(
            jnp.int32, (NIN, NIN), 1
        )
        for p in range(group // 2):
            w0 = whole[2 * p * NCOL : (2 * p + 1) * NCOL]
            w1 = whole[(2 * p + 1) * NCOL : (2 * p + 2) * NCOL]
            side = jnp.where(low_half(NCOL), w0[:, LANES:], w1[:, LANES:])
            across = side[:NIN].T
            square = jnp.concatenate([w0[NIN:, LANES:], w1[NIN:, LANES:]], axis=0).T
            h = group // 2 * g + p
            emit(
                h,
                w0[NIN:, :NIN] + across[:NACT],
                w1[NIN:, :NIN] + across[NACT:],
                side[NIN:] + square[:NACT],
            )
            for n, w in enumerate((w0, w1)):
                diag[pl.ds(2 * h + n, 1), :] = jnp.sum(
                    jnp.where(eye, w[:NIN, :NIN], 0.0), axis=0, keepdims=True
                )
        return carry

    wait(0)
    relayout(0, even_ref)
    lax.fori_loop(0, pairs // 2, two_pairs, 0)
    lax.fori_loop(0, NBQ // group, second_transform, 0)


def split_wire(d):
    hi = d.astype(BF).astype(F32)
    return jnp.where(low_half(d.shape[0]), hi, d - hi).astype(BF)


def joined(wire):
    w = wire.astype(F32)
    return w + pltpu.roll(w, BS, 1)


def density_of(diag):
    d = 2.0 * jnp.sum(diag, axis=1, keepdims=True)
    return jnp.broadcast_to(d, diag.shape)


QUARTER = NACT // 4
PER = NBQ // 2 * QUARTER
INROWS = NBQ * NACT


def emit_active(h, act, core, x, send, keep, send_at):
    for place in (0, 1):
        xx = (1 - x) if place == 0 else x
        for cc in (0, 1):
            block = act[:QUARTER]
            for idx in range(1, 4):
                block = jnp.where(
                    2 * xx + cc == idx, act[idx * QUARTER : (idx + 1) * QUARTER], block
                )
            off = place * PER + h * QUARTER

            @pl.when(core == cc)
            def _():
                keep[pl.ds(pl.multiple_of(off, QUARTER), QUARTER), :] = block

            @pl.when(core != cc)
            def _():
                send[pl.ds(pl.multiple_of(send_at + off, QUARTER), QUARTER), :] = block.astype(BF)


def pair_rows(h, n):
    return pl.ds(pl.multiple_of((2 * h + n) * NACT, NACT), NACT)


def first_kernel(
    scalars, slabs_ref, ot_ref, lt_out, r_out, msg, keep, dens, windows, wsem, *scratch
):
    slabs = slabs_ref.shape[0]
    core, x = scalars[2 * slabs + 1], scalars[2 * slabs + 2]
    block = 2 * (1 - x) + (1 - core)
    copies = []
    for n in range(2 * slabs):
        base = pl.multiple_of((scalars[n] // 2) * PAIRED, PAIRED)
        copies.append(
            pltpu.make_async_copy(ot_ref.at[:, pl.ds(base, PAIRED)], windows.at[n], wsem.at[n])
        )
        copies[-1].start()
    sbuf, sem, diag = scratch[0], scratch[5], scratch[4]
    start_slabs(slabs_ref, sbuf, sem, block)
    for copy in copies:
        copy.wait()
    orbital_blocks(scalars, slabs, windows, lt_out, r_out)

    def emit(h, in0, in1, act):
        msg[pair_rows(h, 0), :] = in0.astype(BF)
        msg[pair_rows(h, 1), :] = in1.astype(BF)
        emit_active(h, act, core, x, msg, keep, INROWS)

    run_block(slabs_ref, block, lt_out, r_out, scratch, emit)
    dens[...] = density_of(diag[...])
    msg[pl.ds(INROWS + 2 * PER, NBQ), :] = split_wire(dens[...])


def second_kernel(
    scalars, slabs_ref, lt_ref, r_ref, keep_in, send, keep, dens, *scratch
):
    slabs = slabs_ref.shape[0]
    core, x = scalars[2 * slabs + 1], scalars[2 * slabs + 2]
    block = 2 * (1 - x) + core
    start_slabs(slabs_ref, scratch[0], scratch[5], block)

    def emit(h, in0, in1, act):
        keep_in[pair_rows(h, 0), :] = in0
        keep_in[pair_rows(h, 1), :] = in1
        emit_active(h, act, core, x, send, keep, 0)

    run_block(slabs_ref, block, lt_ref, r_ref, scratch, emit)
    dens[...] = density_of(scratch[4][...])


def third_kernel(
    scalars, slabs_ref, lt_ref, r_ref, send2, dens2, msg, keep, dens, *scratch
):
    slabs = slabs_ref.shape[0]
    core, x = scalars[2 * slabs + 1], scalars[2 * slabs + 2]
    block = 2 * x + (1 - core)
    start_slabs(slabs_ref, scratch[0], scratch[5], block)

    def emit(h, in0, in1, act):
        msg[pair_rows(h, 0), :] = in0.astype(BF)
        msg[pair_rows(h, 1), :] = in1.astype(BF)
        emit_active(h, act, core, x, msg, keep, INROWS)

    run_block(slabs_ref, block, lt_ref, r_ref, scratch, emit)
    msg[pl.ds(INROWS + 2 * PER, 2 * PER), :] = send2[...]
    dens[...] = density_of(scratch[4][...])
    msg[pl.ds(INROWS + 4 * PER, NBQ), :] = split_wire(dens[...])
    msg[pl.ds(INROWS + 4 * PER + NBQ, NBQ), :] = split_wire(dens2[...])


def fourth_kernel(
    scalars, slabs_ref, lt_ref, r_ref, far1, msg, keep_in, keep, dens, *scratch
):
    slabs = slabs_ref.shape[0]
    core, x = scalars[2 * slabs + 1], scalars[2 * slabs + 2]
    block = 2 * x + core
    start_slabs(slabs_ref, scratch[0], scratch[5], block)

    def emit(h, in0, in1, act):
        for n, v in enumerate((in0, in1)):
            keep_in[pair_rows(h, n), :] = v + far1[pair_rows(h, n), :].astype(F32)
        emit_active(h, act, core, x, msg, keep, 0)

    run_block(slabs_ref, block, lt_ref, r_ref, scratch, emit)
    dens[...] = density_of(scratch[4][...])
    msg[pl.ds(2 * PER, NBQ), :] = split_wire(dens[...])


def exchange_kernel(scalars, mine, near3, own, e1, e2, e3, whole):
    parts = []
    for q in range(NBQ):
        rows = pl.ds(q * NACT, NACT)
        parts.append(mine[rows, :] + near3[rows, :].astype(F32))
    v = jnp.concatenate(parts, axis=1)
    hi = v.astype(BF)
    lo = (v - hi.astype(F32)).astype(BF)
    both = lax.dot_general(
        jnp.concatenate([hi, lo], axis=0), hi, (((1,), (1,)), ((), ())),
        preferred_element_type=F32,
    )
    whole[...] = both[:NACT] + both[NACT:] + both[NACT:].T
    last = scalars.shape[0] - 1
    index = 2 * scalars[last] + scalars[last - 1]
    for k, out in enumerate((own, e1, e2, e3)):
        at = pl.multiple_of((index ^ k) * QUARTER, QUARTER)
        out[...] = whole[pl.ds(at, QUARTER), :]


def gather_kernel(
    keep1, keep2, keep3, keep4, dens1, dens2, dens3, dens4, near1, near3, near4, far1,
    msg, own, dens,
):
    base = INROWS + 2 * PER
    here = (
        (keep1, near3, base, dens1, base + 2 * PER + NBQ),
        (keep2, near1, INROWS, dens2, base),
        (keep3, near4, 0, dens3, 2 * PER),
        (keep4, near3, INROWS, dens4, base + 2 * PER),
    )
    sent = 0
    for n, (keep, near, at, d, dens_at) in enumerate(here):
        if n != 1:
            other = keep[pl.ds(0, PER), :] + near[pl.ds(at, PER), :].astype(F32)
            msg[pl.ds(sent * PER, PER), :] = other.astype(BF)
            sent += 1
        mine = keep[pl.ds(PER, PER), :] + near[pl.ds(at + PER, PER), :].astype(F32)
        if n == 3:
            mine = mine + far1[pl.ds(INROWS, PER), :].astype(F32)
        own[pl.ds(n * PER, PER), :] = mine
        total = d[...] + joined(near[pl.ds(dens_at, NBQ), :])
        dens[pl.ds(n * NBQ, NBQ), :] = total
        msg[pl.ds(3 * PER + n * NBQ, NBQ), :] = split_wire(total)


FAR_ACTIVE = (1, 2, 0)


def coulomb_kernel(act, far, dens, own, e1, e2, e3, partial):
    first = low_half(QUARTER)
    total = jnp.zeros((QUARTER, LANES), F32)
    for n in range(4):
        d = dens[pl.ds(n * NBQ, NBQ), :] + joined(
            far[pl.ds(3 * PER + (n ^ 2) * NBQ, NBQ), :]
        )
        for h in range(NBQ // 2):
            a = act[pl.ds(n * PER + h * QUARTER, QUARTER), :]
            if n < 3:
                a = a + far[
                    pl.ds(FAR_ACTIVE[n] * PER + h * QUARTER, QUARTER), :
                ].astype(F32)
            total = total + a * jnp.where(first, d[2 * h : 2 * h + 1], d[2 * h + 1 : 2 * h + 2])
    total = 2.0 * (total + pltpu.roll(total, BS, 1))
    partial[...] = total[:, :BS] - (own[...] + e1[...] + e2[...] + e3[...])


def active_kernel(scalars, act, far, out):
    last = scalars.shape[0] - 1
    core, x = scalars[last - 1], scalars[last]
    for n in range(4):
        xx = (1 - x) if n < 2 else x
        cc = (1 - core) if n % 2 == 0 else core
        base = NBQ * (2 * xx + cc)
        for h in range(NBQ // 2):
            a = act[pl.ds(n * PER + h * QUARTER, QUARTER), :]
            if n < 3:
                a = a + far[
                    pl.ds(FAR_ACTIVE[n] * PER + h * QUARTER, QUARTER), :
                ].astype(F32)
            out[base + 2 * h] = a[:, :BS]
            out[base + 2 * h + 1] = a[:, BS:]


VM = pl.BlockSpec(memory_space=pltpu.VMEM)
SM = pl.BlockSpec(memory_space=pltpu.SMEM)
HB = pl.BlockSpec(memory_space=pl.ANY)
PARAMS = pltpu.CompilerParams(vmem_limit_bytes=48 * 1024 * 1024)


def shape(dims, dtype):
    return jax.ShapeDtypeStruct(dims, dtype)


def sum_over_aux(part):
    n = lax.axis_size("aux")
    if n != 4:
        return lax.psum(part, "aux")
    for k in (1, 2):
        part = part + lax.ppermute(part, "aux", [(z, z ^ k) for z in range(n)])
    return part


def paired_body(slabs, block_row, block_col, live_count, orbitals, hcore):
    nslab, batch, width = slabs.shape
    index = lax.axis_index("pair")
    where = jnp.stack([lax.rem(index, 2), index // 2])
    scalars = jnp.concatenate([block_row, block_col, live_count, where])
    swap_core = [(0, 1), (1, 0), (2, 3), (3, 2)]
    swap_x = [(0, 2), (2, 0), (1, 3), (3, 1)]
    aos = nslab * BS
    scratch = [
        pltpu.VMEM((nslab // 2 + 1, 2, NBQ, width), BF),
        pltpu.VMEM((MSTEP * BS, LANES), F32),
        pltpu.VMEM((MSTEP * BS, LANES), F32),
        pltpu.VMEM((NBQ, NCOL, aos), BF),
        pltpu.VMEM((NBQ, LANES), F32),
        pltpu.SemaphoreType.DMA((nslab // 2 + 1,)),
    ]
    cost = pl.CostEstimate(flops=6 * 10**9, bytes_accessed=10**7, transcendentals=0)
    keep, dens = shape((2 * PER, LANES), F32), shape((NBQ, LANES), F32)
    lt, r, msg1, keep1, dens1 = pl.pallas_call(
        first_kernel,
        name="slabs_first",
        in_specs=[SM, HB, HB],
        out_specs=[VM] * 5,
        out_shape=(
            shape((nslab // 2, NCOL, PAIRED), BF),
            shape((aos, 2 * LANES), BF),
            shape((INROWS + 2 * PER + NBQ, LANES), BF),
            keep,
            dens,
        ),
        scratch_shapes=[
            pltpu.VMEM((2 * nslab, NCOL, PAIRED), BF), pltpu.SemaphoreType.DMA((2 * nslab,)),
        ] + scratch,
        compiler_params=PARAMS,
        cost_estimate=cost,
    )(scalars, slabs, orbitals.T)
    near1 = lax.ppermute(msg1, "pair", swap_core)
    keep_in2, send2, keep2, dens2 = pl.pallas_call(
        second_kernel,
        name="slabs_second",
        in_specs=[SM, HB, VM, VM],
        out_specs=[VM] * 4,
        out_shape=(
            shape((INROWS, LANES), F32), shape((2 * PER, LANES), BF), keep, dens,
        ),
        scratch_shapes=scratch,
        compiler_params=PARAMS,
        cost_estimate=cost,
    )(scalars, slabs, lt, r)
    out2 = jnp.concatenate([keep_in2, keep2[:PER]], axis=0)
    out2 = (out2 + near1[: INROWS + PER].astype(F32)).astype(BF)
    out2, lt, r = lax.optimization_barrier((out2, lt, r))
    far1 = lax.ppermute(out2, "pair", swap_x)
    msg3, keep3, dens3 = pl.pallas_call(
        third_kernel,
        name="slabs_third",
        in_specs=[SM, HB] + [VM] * 4,
        out_specs=[VM] * 3,
        out_shape=(shape((INROWS + 4 * PER + 2 * NBQ, LANES), BF), keep, dens),
        scratch_shapes=scratch,
        compiler_params=PARAMS,
        cost_estimate=cost,
    )(scalars, slabs, lt, r, send2, dens2)
    near3 = lax.ppermute(msg3, "pair", swap_core)
    msg4, keep_in4, keep4, dens4 = pl.pallas_call(
        fourth_kernel,
        name="slabs_fourth",
        in_specs=[SM, HB] + [VM] * 3,
        out_specs=[VM] * 4,
        out_shape=(
            shape((2 * PER + NBQ, LANES), BF), shape((INROWS, LANES), F32), keep, dens,
        ),
        scratch_shapes=scratch,
        compiler_params=PARAMS,
        cost_estimate=cost,
    )(scalars, slabs, lt, r, far1)
    near4 = lax.ppermute(msg4, "pair", swap_core)
    rows = shape((QUARTER, NACT), F32)
    own, e1, e2, e3 = pl.pallas_call(
        exchange_kernel,
        name="exchange",
        in_specs=[SM] + [VM] * 2,
        out_specs=[VM] * 4,
        out_shape=(rows,) * 4,
        scratch_shapes=[pltpu.VMEM((NACT, NACT), F32)],
        compiler_params=PARAMS,
    )(scalars, keep_in4, near3)
    msg5, act, dens = pl.pallas_call(
        gather_kernel,
        name="active_of_chip",
        in_specs=[VM] * 12,
        out_specs=[VM] * 3,
        out_shape=(
            shape((3 * PER + 4 * NBQ, LANES), BF),
            shape((4 * PER, LANES), F32),
            shape((4 * NBQ, LANES), F32),
        ),
        compiler_params=PARAMS,
    )(keep1, keep2, keep3, keep4, dens1, dens2, dens3, dens4, near1, near3, near4, far1)
    far5 = lax.ppermute(msg5, "pair", swap_x)
    e1, e2, e3 = (
        lax.ppermute(e, "pair", [(p, p ^ k) for p in range(4)])
        for k, e in ((1, e1), (2, e2), (3, e3))
    )
    partial = pl.pallas_call(
        coulomb_kernel,
        name="coulomb",
        in_specs=[VM] * 7,
        out_specs=VM,
        out_shape=rows,
        compiler_params=PARAMS,
    )(act, far5, dens, own, e1, e2, e3)
    active = pl.pallas_call(
        active_kernel,
        name="own_active",
        in_specs=[SM, VM, VM],
        out_specs=VM,
        out_shape=shape((batch, QUARTER, NACT), F32),
        compiler_params=PARAMS,
        cost_estimate=pl.CostEstimate(flops=10**6, bytes_accessed=10**6, transcendentals=0),
    )(scalars, act, far5)
    return (active, hcore + sum_over_aux(partial))


def slab_terms(values, left, right):
    half = jnp.einsum("mc,qmn->qnc", left, values, preferred_element_type=F32).astype(BF)
    first = jnp.einsum("qnt,nc->qtc", half[:, :, :NACT], right, preferred_element_type=F32)
    second = jnp.einsum("qnc,nt->qtc", half, right[:, :NACT], preferred_element_type=F32)
    trace = 2.0 * jnp.einsum(
        "qni,ni->q", half[:, :, NACT:], right[:, NACT:], preferred_element_type=F32
    )
    return (first + second, trace)


def general_body(slabs, block_row, block_col, live_count, orbitals, hcore):
    batch = slabs.shape[1]
    init = (jnp.zeros((batch, NACT, NCOL), F32), jnp.zeros((batch,), F32))

    def visit(k, state):
        values = lax.dynamic_index_in_dim(slabs, k, 0, keepdims=False)
        left = lax.dynamic_slice_in_dim(orbitals, block_row[k] * BS, BS, 0)
        right = lax.dynamic_slice_in_dim(orbitals, block_col[k] * BS, BS, 0)
        terms, trace = slab_terms(values.reshape(batch, BS, BS), left, right)
        return (state[0] + terms, state[1] + trace)

    vectors, density = lax.fori_loop(0, live_count[0], visit, init)
    density = lax.psum(density, "pair")
    owned = lax.psum_scatter(vectors, "pair", scatter_dimension=1, tiled=True)
    own_active, own_inactive = owned[:, :, :NACT], owned[:, :, NACT:]
    gathered = lax.all_gather(own_inactive.astype(BF), "pair", axis=1, tiled=True)
    exchange = jnp.einsum(
        "qti,qui->tu", own_inactive, gathered.astype(F32), precision=lax.Precision.HIGHEST
    )
    coulomb = jnp.einsum("qtu,q->tu", own_active, density, precision=lax.Precision.HIGHEST)
    return (own_active, hcore + lax.psum(2.0 * coulomb - exchange, "aux"))


def solution(mesh):
    placed = (
        P(("frag", "pair"), "aux", None),
        P(("frag", "pair")),
        P(("frag", "pair")),
        P(("frag", "pair")),
        P("frag", None),
        P(("frag", "pair"), None),
    )

    def body(slabs, *rest):
        fits = mesh.shape["pair"] == 4 and slabs.shape[1] == 4 * NBQ and slabs.shape[0] % 4 == 0
        return (paired_body if fits else general_body)(slabs, *rest)

    return jax.shard_map(
        body,
        mesh=mesh,
        in_specs=placed,
        out_specs=(P(("frag", "aux"), "pair", None), P(("frag", "pair"), None)),
        check_vma=False,
    )
```

time: 326 us -> 55.7 us (0.17); the launches traced: 322 us -> 55.5 us
  local copies, waits for them, and re-layouts: 134 us -> 2.17 us
  matrix products: 65.4 us -> 0 us
  waiting for transfers between devices: 56.4 us -> 5.47 us
  Pallas kernels: 0 us -> 34.5 us
  loops' own time: 34 us -> 0 us
  blocking collectives: 17.6 us -> 0 us
  between operations: 14.1 us -> 1.38 us
  starting transfers between devices: 0.08 us -> 11.3 us
    dot_general x66 -> x0, matrix products: 65.4 us -> none  [the longest x16 24 us: slab_terms(): jnp.einsum('mc,qmn->qnc', left, values, preferred_element_type=jnp.float32)]
    while x129 -> x0, local copies, waits for them, and re-layouts: 65.1 us -> none
    reduce_scatter x1 -> x0, waiting for transfers between devices: 46.8 us -> none  [body(): owned = lax.psum_scatter(vectors, 'pair', scatter_dimension=1, tiled=True)]
    dynamic_slice x48 -> x0, local copies, waits for them, and re-layouts: 37.4 us -> none  [the longest x32 20.2 us: pick_slab(): return (values, rows[slot], cols[slot])]
    pallas_call x0 -> x8, Pallas kernels: none -> 34.5 us  [the longest x1 8.76 us: paired_body(): pl.pallas_call(first_kernel, name='slabs_first', in_specs=[SM, HB, HB], o...]
    another operation x1 -> x0, loops' own time: 34 us -> none  [body(): vectors, density = lax.fori_loop(0, live_count[0], visit, init)]
    reshape x16 -> x0, local copies, waits for them, and re-layouts: 18 us -> none  [add_slab(): terms, trace = slab_terms(values.reshape(batch, BS, BS), left, right)]
    psum x2 -> x0, blocking collectives: 17.6 us -> none  [the longest x1 11.8 us: body(): summed = lax.psum(partial_fock, 'aux')]
  transfers between devices with their start and end apart: 2 -> 10, of which waited for: 2 -> 4; matrix products, arithmetic and copies ran while one was open for 0% -> 0% of each run, Pallas kernels for 0% -> 46%
where the time goes in v3:
time: 55.7 us; the launch traced here: 55.5 us
  Pallas kernels  34.5 us (62%)
  starting transfers between devices  11.3 us (20%)
  waiting for transfers between devices  5.47 us (10%)
  local copies, waits for them, and re-layouts  2.17 us (4%)
  between operations  1.38 us (2%)
  other arithmetic  0.68 us (1%)
    pallas_call x1, Pallas kernels, paired_body(): pl.pallas_call(first_kernel, name='slabs_first', in_specs=[SM, HB, HB], o...  8.76 us
    pallas_call x1, Pallas kernels, paired_body(): pl.pallas_call(third_kernel, name='slabs_third', in_specs=[SM, HB] + [VM]...  7.68 us
    pallas_call x1, Pallas kernels, paired_body(): pl.pallas_call(fourth_kernel, name='slabs_fourth', in_specs=[SM, HB] + [V...  7.68 us
    pallas_call x1, Pallas kernels, paired_body(): pl.pallas_call(second_kernel, name='slabs_second', in_specs=[SM, HB, VM,...  7.68 us
    ppermute x2, starting transfers between devices, sum_over_aux(): part = part + lax.ppermute(part, 'aux', [(z, z ^ k) for z in range(n)])  4.17 us
    ppermute x1, starting transfers between devices, paired_body(): far1 = lax.ppermute(out2, 'pair', swap_x)  2.57 us
    ppermute x2, waiting for transfers between devices, sum_over_aux(): part = part + lax.ppermute(part, 'aux', [(z, z ^ k) for z in range(n)])  2.56 us
    ppermute x3, waiting for transfers between devices, paired_body(): lax.ppermute(e, 'pair', [(p, p ^ k) for p in range(4)])  1.94 us
  transfers between devices with their start and end apart: 10, of which 4 were waited for; matrix products, arithmetic and copies ran while one was open for 0% of the time, Pallas kernels for 46%

profile of v3, /device:TPU:0, one launch (start us, length us, event | category | flops | bytes accessed | tf_op | source)
XLA Modules:
  0.0 55.5 jit_solution(7604561470392310152)
XLA Ops:
  1.3 0.7 %concatenate.6.scalars = s32[35]{0:T(128)S(1)} concatenate(s32[16]{0:T(128)} %param.7, s32[16]{0:T(128)} %param.8, s32[1]{0:T(128)S(6)} %copy.8, s32[1]{0:T(128)} %bitcast, s32[1]{0:T(128)} %bitcast.1), dimensions={0} | concatenate | bytes 280 | tf_op jit(solution)/shard_map/concatenate | solution.py:374
  2.0 1.4 %copy-done = bf16[4096,192]{0,1:T(8,128)(2,1)S(1)} copy-done((bf16[4096,192]{0,1:T(8,128)(2,1)S(1)}, bf16[4096,192]{0,1:T(8,128)(2,1)}, u32[]{:S(2)}) %copy-start) | copy-done | bytes 1572888
  3.4 8.8 %slabs_first.1 = (bf16[8,192,128]{2,1,0:T(8,128)(2,1)S(1)}, bf16[1024,256]{1,0:T(8,128)(2,1)S(1)}, bf16[1296,128]{1,0:T(8,128)(2,1)S(1)}, f32[256,128]{1,0:T(8,128)S(1)}, f32[16,128]{1,0:T(8,128)S(1)}) custom-call(s32[35]{0:T(128)S(1)} %concatenate.6.scalars, bf16[16,64,4096]{2,1,0:T(8,128)(2,1)} %slabs_ref.7, bf16[192,4096]{1,0:T(8,128)(2,1)S(1)} %bitcast.3), custom_call_target="tpu_custom_call" | custom-call | flops 6000000000 | bytes 10000000 | tf_op jit(solution)/shard_map/slabs_first/pallas_call | solution.py:388
  12.2 0.5 collective-permute-start
  12.7 7.7 %slabs_second.1 = (f32[1024,128]{1,0:T(8,128)S(1)}, bf16[256,128]{1,0:T(8,128)(2,1)S(1)}, f32[256,128]{1,0:T(8,128)S(1)}, f32[16,128]{1,0:T(8,128)S(1)}) custom-call(s32[35]{0:T(128)S(1)} %concatenate.6.scalars, bf16[16,64,4096]{2,1,0:T(8,128)(2,1)} %slabs_ref.7, bf16[8,192,128]{2,1,0:T(8,128)(2,1)S(1)} %get-tuple-element.34.lt_ref, ...), custom_call_target="tpu_custom_call" | custom-call | flops 6000000000 | bytes 10000000 | tf_op jit(solution)/shard_map/slabs_second/pallas_call | solution.py:407
  20.5 2.6 %collective-permute-start.1 = (bf16[1152,128]{1,0:T(8,128)(2,1)S(1)}, bf16[1152,128]{1,0:T(8,128)(2,1)S(1)}, u32[]{:S(2)}, u32[]{:S(2)}) collective-permute-start(bf16[1152,128]{1,0:T(8,128)(2,1)S(1)} %fusion), channel_id=1, source_target_pairs={{0,8},{8,0},{4,12},{12,4},{1,9},{9,1},{5,13},{13,5},{2,10},{10,2},... | collective-permute-start | bytes 884744 | tf_op jit(solution)/shard_map/ppermute | solution.py:422
  23.1 7.7 %slabs_third.1 = (bf16[1568,128]{1,0:T(8,128)(2,1)S(1)}, f32[256,128]{1,0:T(8,128)S(1)}, f32[16,128]{1,0:T(8,128)S(1)}) custom-call(s32[35]{0:T(128)S(1)} %concatenate.6.scalars, bf16[16,64,4096]{2,1,0:T(8,128)(2,1)} %slabs_ref.7, bf16[8,192,128]{2,1,0:T(8,128)(2,1)S(1)} %get-tuple-element.34.lt_ref, bf16[1024,256]{1,0:T(8,128)(2,1)S(1)} %get-tuple-element.35.r_ref, ...), custom_call_target="tpu_custom_call" | custom-call | flops 6000000000 | bytes 10000000 | tf_op jit(solution)/shard_map/slabs_third/pallas_call | solution.py:423
  30.8 0.3 collective-permute-start.2
  31.1 7.7 %slabs_fourth.1 = (bf16[272,128]{1,0:T(8,128)(2,1)S(1)}, f32[1024,128]{1,0:T(8,128)S(1)}, f32[256,128]{1,0:T(8,128)S(1)}, f32[16,128]{1,0:T(8,128)S(1)}) custom-call(s32[35]{0:T(128)S(1)} %concatenate.6.scalars, bf16[16,64,4096]{2,1,0:T(8,128)(2,1)} %slabs_ref.7, bf16[8,192,128]{2,1,0:T(8,128)(2,1)S(1)} %get-tuple-element.34.lt_ref, ...), custom_call_target="tpu_custom_call" | custom-call | flops 6000000000 | bytes 10000000 | tf_op jit(solution)/shard_map/slabs_fourth/pallas_call | solution.py:434
  38.8 0.4 collective-permute-start.3
  39.1 1.0 %collective-permute-done.3.near4 = bf16[272,128]{1,0:T(8,128)(2,1)S(1)} collective-permute-done((bf16[272,128]{1,0:T(8,128)(2,1)S(1)}, bf16[272,128]{1,0:T(8,128)(2,1)S(1)}, u32[]{:S(2)}, u32[]{:S(2)}) %collective-permute-start.3) | collective-permute-done | bytes 69664 | tf_op jit(solution)/shard_map/ppermute | solution.py:446
  40.1 0.1 active_of_chip.1
  40.2 1.5 %collective-permute-start.4 = (bf16[448,128]{1,0:T(8,128)(2,1)S(1)}, bf16[448,128]{1,0:T(8,128)(2,1)S(1)}, u32[]{:S(2)}, u32[]{:S(2)}) collective-permute-start(bf16[448,128]{1,0:T(8,128)(2,1)S(1)} %get-tuple-element.47), channel_id=1, source_target_pairs={{0,8},{8,0},{4,12},{12,4},{1,9},{9,1},{5,13},{13,5},{2,10},{10,2},... | collective-permute-start | bytes 344072 | tf_op jit(solution)/shard_map/ppermute | solution.py:469
  41.7 0.9 %exchange.1 = (f32[16,64]{1,0:T(8,128)S(1)}, f32[16,64]{1,0:T(8,128)S(1)}, f32[16,64]{1,0:T(8,128)S(1)}, f32[16,64]{1,0:T(8,128)S(1)}) custom-call(s32[35]{0:T(128)S(1)} %concatenate.6.scalars, f32[1024,128]{1,0:T(8,128)S(1)} %get-tuple-element.49.mine, bf16[1568,128]{1,0:T(8,128)(2,1)S(1)} %collective-permute-done.2.near3), custom_call_target="tpu_custom_call" | custom-call | tf_op jit(solution)/shard_map/exchange/pallas_call | solution.py:448
  42.7 0.7 %collective-permute-start.6 = (f32[16,64]{1,0:T(8,128)S(1)}, f32[16,64]{1,0:T(8,128)S(1)}, u32[]{:S(2)}, u32[]{:S(2)}) collective-permute-start(f32[16,64]{1,0:T(8,128)S(1)} %get-tuple-element.52), channel_id=1, source_target_pairs={{0,8},{4,12},{8,0},{12,4},{1,9},{5,13},{9,1},{13,5},{2,10},{6,14},... | collective-permute-start | bytes 12296 | tf_op jit(solution)/shard_map/ppermute | solution.py:471
  43.3 1.2 %collective-permute-start.7 = (f32[16,64]{1,0:T(8,128)S(1)}, f32[16,64]{1,0:T(8,128)S(1)}, u32[]{:S(2)}, u32[]{:S(2)}) collective-permute-start(f32[16,64]{1,0:T(8,128)S(1)} %get-tuple-element.53), channel_id=1, source_target_pairs={{0,12},{4,8},{8,4},{12,0},{1,13},{5,9},{9,5},{13,1},{2,14},{6,10},... | collective-permute-start | bytes 12296 | tf_op jit(solution)/shard_map/ppermute | solution.py:471
  44.5 1.9 %collective-permute-done.6.e2 = f32[16,64]{1,0:T(8,128)S(1)} collective-permute-done((f32[16,64]{1,0:T(8,128)S(1)}, f32[16,64]{1,0:T(8,128)S(1)}, u32[]{:S(2)}, u32[]{:S(2)}) %collective-permute-start.6) | collective-permute-done | bytes 4128 | tf_op jit(solution)/shard_map/ppermute | solution.py:471
  46.5 0.2 coulomb.1
  46.7 1.6 %collective-permute-start.8 = (f32[16,64]{1,0:T(8,128)S(1)}, f32[16,64]{1,0:T(8,128)S(1)}, u32[]{:S(2)}, u32[]{:S(2)}) collective-permute-start(f32[16,64]{1,0:T(8,128)S(1)} %coulomb.1), channel_id=1, source_target_pairs={{0,1},{1,0},{2,3},{3,2},{4,5},{5,4},{6,7},{7,6},{8,9},{9,8},{10,11... | collective-permute-start | bytes 12296 | tf_op jit(solution)/shard_map/ppermute | solution.py:366
  48.2 2.1 %collective-permute-done.8 = f32[16,64]{1,0:T(8,128)S(1)} collective-permute-done((f32[16,64]{1,0:T(8,128)S(1)}, f32[16,64]{1,0:T(8,128)S(1)}, u32[]{:S(2)}, u32[]{:S(2)}) %collective-permute-start.8) | collective-permute-done | bytes 4128 | tf_op jit(solution)/shard_map/ppermute | solution.py:366
  50.3 2.6 %collective-permute-start.9 = (f32[16,64]{1,0:T(8,128)S(1)}, f32[16,64]{1,0:T(8,128)S(1)}, u32[]{:S(2)}, u32[]{:S(2)}) collective-permute-start(f32[16,64]{1,0:T(8,128)S(1)} %add.14), channel_id=1, source_target_pairs={{0,2},{1,3},{2,0},{3,1},{4,6},{5,7},{6,4},{7,5},{8,10},{9,11},{10,... | collective-permute-start | bytes 12296 | tf_op jit(solution)/shard_map/ppermute | solution.py:366
  52.9 1.5 %own_active.1 = f32[64,16,64]{2,1,0:T(8,128)} custom-call(s32[35]{0:T(128)S(1)} %concatenate.6.scalars, f32[512,128]{1,0:T(8,128)S(1)} %get-tuple-element.46.act, bf16[448,128]{1,0:T(8,128)(2,1)S(1)} %collective-permute-done.4.far), custom_call_target="tpu_custom_call" | custom-call | flops 1000000 | bytes 1000000 | tf_op jit(solution)/shard_map/own_active/pallas_call | solution.py:482
  54.4 0.5 collective-permute-done.9
  54.9 0.6 %add_add_fusion = f32[16,64]{1,0:T(8,128)} fusion(f32[16,64]{1,0:T(8,128)S(1)} %copy-done.1, f32[16,64]{1,0:T(8,128)S(1)} %add.14, f32[16,64]{1,0:T(8,128)S(1)} %collective-permute-done.9), kind=kLoop, calls=%fused_computation.2 | loop fusion | flops 2048 | bytes 16384 | tf_op jit(solution)/shard_map/add | solution.py:491
  (13 shorter events, 0.2 us)
Async XLA Ops:
  2.0 1.4 %copy-start = (bf16[4096,192]{0,1:T(8,128)(2,1)S(1)}, bf16[4096,192]{0,1:T(8,128)(2,1)}, u32[]{:S(2)}) copy-start(bf16[4096,192]{0,1:T(8,128)(2,1)} %param.10) | copy-start | bytes 4718596
  12.2 8.2 %collective-permute-start = (bf16[1296,128]{1,0:T(8,128)(2,1)S(1)}, bf16[1296,128]{1,0:T(8,128)(2,1)S(1)}, u32[]{:S(2)}, u32[]{:S(2)}) collective-permute-start(bf16[1296,128]{1,0:T(8,128)(2,1)S(1)} %get-tuple-element.33), channel_id=1, source_target_pairs={{0,4},{4,0},{8,12},{12,8},{1,5},{5,1},{9,13},{13,9},{2,6},{6,2},{1... | collective-permute-start | bytes 995336 | tf_op jit(solution)/shard_map/ppermute | solution.py:406
  20.5 10.5 %collective-permute-start.1 = (bf16[1152,128]{1,0:T(8,128)(2,1)S(1)}, bf16[1152,128]{1,0:T(8,128)(2,1)S(1)}, u32[]{:S(2)}, u32[]{:S(2)}) collective-permute-start(bf16[1152,128]{1,0:T(8,128)(2,1)S(1)} %fusion), channel_id=1, source_target_pairs={{0,8},{8,0},{4,12},{12,4},{1,9},{9,1},{5,13},{13,5},{2,10},{10,2},... | collective-permute-start | bytes 884744 | tf_op jit(solution)/shard_map/ppermute | solution.py:422
  30.8 24.1 %copy-start.1 = (f32[16,64]{1,0:T(8,128)S(1)}, f32[16,64]{1,0:T(8,128)}, u32[]{:S(2)}) copy-start(f32[16,64]{1,0:T(8,128)} %param.11) | copy-start | bytes 12292
  30.8 9.3 %collective-permute-start.2 = (bf16[1568,128]{1,0:T(8,128)(2,1)S(1)}, bf16[1568,128]{1,0:T(8,128)(2,1)S(1)}, u32[]{:S(2)}, u32[]{:S(2)}) collective-permute-start(bf16[1568,128]{1,0:T(8,128)(2,1)S(1)} %get-tuple-element.44), channel_id=1, source_target_pairs={{0,4},{4,0},{8,12},{12,8},{1,5},{5,1},{9,13},{13,9},{2,6},{6,2},{1... | collective-permute-start | bytes 1204232 | tf_op jit(solution)/shard_map/ppermute | solution.py:433
  38.8 1.3 %collective-permute-start.3 = (bf16[272,128]{1,0:T(8,128)(2,1)S(1)}, bf16[272,128]{1,0:T(8,128)(2,1)S(1)}, u32[]{:S(2)}, u32[]{:S(2)}) collective-permute-start(bf16[272,128]{1,0:T(8,128)(2,1)S(1)} %get-tuple-element.45), channel_id=1, source_target_pairs={{0,4},{4,0},{8,12},{12,8},{1,5},{5,1},{9,13},{13,9},{2,6},{6,2},{1... | collective-permute-start | bytes 208904 | tf_op jit(solution)/shard_map/ppermute | solution.py:446
  40.2 6.3 %collective-permute-start.4 = (bf16[448,128]{1,0:T(8,128)(2,1)S(1)}, bf16[448,128]{1,0:T(8,128)(2,1)S(1)}, u32[]{:S(2)}, u32[]{:S(2)}) collective-permute-start(bf16[448,128]{1,0:T(8,128)(2,1)S(1)} %get-tuple-element.47), channel_id=1, source_target_pairs={{0,8},{8,0},{4,12},{12,4},{1,9},{9,1},{5,13},{13,5},{2,10},{10,2},... | collective-permute-start | bytes 344072 | tf_op jit(solution)/shard_map/ppermute | solution.py:469
  42.6 1.9 %collective-permute-start.5 = (f32[16,64]{1,0:T(8,128)S(1)}, f32[16,64]{1,0:T(8,128)S(1)}, u32[]{:S(2)}, u32[]{:S(2)}) collective-permute-start(f32[16,64]{1,0:T(8,128)S(1)} %get-tuple-element.51), channel_id=1, source_target_pairs={{0,4},{4,0},{8,12},{12,8},{1,5},{5,1},{9,13},{13,9},{2,6},{6,2},{1... | collective-permute-start | bytes 12296 | tf_op jit(solution)/shard_map/ppermute | solution.py:471
  42.7 3.8 %collective-permute-start.6 = (f32[16,64]{1,0:T(8,128)S(1)}, f32[16,64]{1,0:T(8,128)S(1)}, u32[]{:S(2)}, u32[]{:S(2)}) collective-permute-start(f32[16,64]{1,0:T(8,128)S(1)} %get-tuple-element.52), channel_id=1, source_target_pairs={{0,8},{4,12},{8,0},{12,4},{1,9},{5,13},{9,1},{13,5},{2,10},{6,14},... | collective-permute-start | bytes 12296 | tf_op jit(solution)/shard_map/ppermute | solution.py:471
  43.3 3.1 %collective-permute-start.7 = (f32[16,64]{1,0:T(8,128)S(1)}, f32[16,64]{1,0:T(8,128)S(1)}, u32[]{:S(2)}, u32[]{:S(2)}) collective-permute-start(f32[16,64]{1,0:T(8,128)S(1)} %get-tuple-element.53), channel_id=1, source_target_pairs={{0,12},{4,8},{8,4},{12,0},{1,13},{5,9},{9,5},{13,1},{2,14},{6,10},... | collective-permute-start | bytes 12296 | tf_op jit(solution)/shard_map/ppermute | solution.py:471
  46.7 3.7 %collective-permute-start.8 = (f32[16,64]{1,0:T(8,128)S(1)}, f32[16,64]{1,0:T(8,128)S(1)}, u32[]{:S(2)}, u32[]{:S(2)}) collective-permute-start(f32[16,64]{1,0:T(8,128)S(1)} %coulomb.1), channel_id=1, source_target_pairs={{0,1},{1,0},{2,3},{3,2},{4,5},{5,4},{6,7},{7,6},{8,9},{9,8},{10,11... | collective-permute-start | bytes 12296 | tf_op jit(solution)/shard_map/ppermute | solution.py:366
  50.3 4.5 %collective-permute-start.9 = (f32[16,64]{1,0:T(8,128)S(1)}, f32[16,64]{1,0:T(8,128)S(1)}, u32[]{:S(2)}, u32[]{:S(2)}) collective-permute-start(f32[16,64]{1,0:T(8,128)S(1)} %add.14), channel_id=1, source_target_pairs={{0,2},{1,3},{2,0},{3,1},{4,6},{5,7},{6,4},{7,5},{8,10},{9,11},{10,... | collective-permute-start | bytes 12296 | tf_op jit(solution)/shard_map/ppermute | solution.py:366

commit v4 on v3

--- a/solution.py
+++ b/solution.py
@@ -62,7 +62,7 @@
     first = low_half(NBQ)
     first_s = low_half(BS)
     zero = jnp.zeros((BS, LANES), BF)
-    group = 4
+    wide, group = NBQ, 8
 
     def wait(k):
         slab_copy(slabs_ref, sbuf, sem, block, k).wait()
@@ -82,9 +82,9 @@
     def half_transform(k, rows):
         left = lt_ref[k]
         at = pl.ds(pl.multiple_of(k * LANES, LANES), LANES)
-        for q in range(0, NBQ, group):
+        for q in range(0, NBQ, wide):
             cols = []
-            for u in range(q, q + group):
+            for u in range(q, q + wide):
                 s = rows[pl.ds(u * QSTEP, BS, stride=MSTEP), :].astype(BF)
                 cols.append(
                     jnp.concatenate(
@@ -93,7 +93,7 @@
                 )
             half = jnp.dot(left, jnp.concatenate(cols, axis=1), preferred_element_type=F32)
             half = half.astype(BF)
-            for u in range(group):
+            for u in range(wide):
                 half_ref[q + u, :, at] = half[:, u * LANES : (u + 1) * LANES]
 
     def two_pairs(i, carry):
@@ -264,7 +264,7 @@
     msg[pl.ds(2 * PER, NBQ), :] = split_wire(dens[...])
 
 
-def exchange_kernel(scalars, mine, near3, own, e1, e2, e3, whole):
+def exchange_kernel(scalars, mine, near3, msg4, msg, keep, whole):
     parts = []
     for q in range(NBQ):
         rows = pl.ds(q * NACT, NACT)
@@ -276,17 +276,22 @@
         jnp.concatenate([hi, lo], axis=0), hi, (((1,), (1,)), ((), ())),
         preferred_element_type=F32,
     )
-    whole[...] = both[:NACT] + both[NACT:] + both[NACT:].T
+    total = both[:NACT] + both[NACT:] + both[NACT:].T
+    whole[...] = jnp.concatenate([total, total], axis=1)
     last = scalars.shape[0] - 1
-    index = 2 * scalars[last] + scalars[last - 1]
-    for k, out in enumerate((own, e1, e2, e3)):
-        at = pl.multiple_of((index ^ k) * QUARTER, QUARTER)
-        out[...] = whole[pl.ds(at, QUARTER), :]
+    core, x = scalars[last - 1], scalars[last]
+    size = msg4.shape[0]
+    msg[pl.ds(0, size), :] = msg4[...]
+    for place, xx in enumerate((1 - x, x)):
+        there = pl.multiple_of((2 * xx + 1 - core) * QUARTER, QUARTER)
+        here = pl.multiple_of((2 * xx + core) * QUARTER, QUARTER)
+        msg[pl.ds(size + place * QUARTER, QUARTER), :] = split_wire(whole[pl.ds(there, QUARTER), :])
+        keep[pl.ds(place * QUARTER, QUARTER), :] = whole[pl.ds(here, QUARTER), :]
 
 
 def gather_kernel(
-    keep1, keep2, keep3, keep4, dens1, dens2, dens3, dens4, near1, near3, near4, far1,
-    msg, own, dens,
+    keep1, keep2, keep3, keep4, dens1, dens2, dens3, dens4, exch, near1, near3, near4, far1,
+    msg, own, dens, exch_own,
 ):
     base = INROWS + 2 * PER
     here = (
@@ -308,12 +313,15 @@
         total = d[...] + joined(near[pl.ds(dens_at, NBQ), :])
         dens[pl.ds(n * NBQ, NBQ), :] = total
         msg[pl.ds(3 * PER + n * NBQ, NBQ), :] = split_wire(total)
+    rows = exch[...] + joined(near4[pl.ds(2 * PER + NBQ, 2 * QUARTER), :])
+    msg[pl.ds(3 * PER + 4 * NBQ, QUARTER), :] = split_wire(rows[:QUARTER])
+    exch_own[...] = rows[QUARTER:]
 
 
 FAR_ACTIVE = (1, 2, 0)
 
 
-def coulomb_kernel(act, far, dens, own, e1, e2, e3, partial):
+def coulomb_kernel(act, far, dens, exch, partial):
     first = low_half(QUARTER)
     total = jnp.zeros((QUARTER, LANES), F32)
     for n in range(4):
@@ -328,7 +336,8 @@
                 ].astype(F32)
             total = total + a * jnp.where(first, d[2 * h : 2 * h + 1], d[2 * h + 1 : 2 * h + 2])
     total = 2.0 * (total + pltpu.roll(total, BS, 1))
-    partial[...] = total[:, :BS] - (own[...] + e1[...] + e2[...] + e3[...])
+    total = total - exch[...] - joined(far[pl.ds(3 * PER + 4 * NBQ, QUARTER), :])
+    partial[...] = total[:, :BS]
 
 
 def active_kernel(scalars, act, far, out):
@@ -350,7 +359,7 @@
 
 VM = pl.BlockSpec(memory_space=pltpu.VMEM)
 SM = pl.BlockSpec(memory_space=pltpu.SMEM)
-HB = pl.BlockSpec(memory_space=pl.ANY)
+HB = pl.BlockSpec(memory_space=pltpu.HBM)
 PARAMS = pltpu.CompilerParams(vmem_limit_bytes=48 * 1024 * 1024)
 
 
@@ -362,9 +371,10 @@
     n = lax.axis_size("aux")
     if n != 4:
         return lax.psum(part, "aux")
-    for k in (1, 2):
-        part = part + lax.ppermute(part, "aux", [(z, z ^ k) for z in range(n)])
-    return part
+    one, two, three = (
+        lax.ppermute(part, "aux", [(z, z ^ k) for z in range(n)]) for k in (1, 2, 3)
+    )
+    return (part + one) + (two + three)
 
 
 def paired_body(slabs, block_row, block_col, live_count, orbitals, hcore):
@@ -443,42 +453,41 @@
         compiler_params=PARAMS,
         cost_estimate=cost,
     )(scalars, slabs, lt, r, far1)
-    near4 = lax.ppermute(msg4, "pair", swap_core)
-    rows = shape((QUARTER, NACT), F32)
-    own, e1, e2, e3 = pl.pallas_call(
+    msg4, exch = pl.pallas_call(
         exchange_kernel,
         name="exchange",
-        in_specs=[SM] + [VM] * 2,
-        out_specs=[VM] * 4,
-        out_shape=(rows,) * 4,
-        scratch_shapes=[pltpu.VMEM((NACT, NACT), F32)],
-        compiler_params=PARAMS,
-    )(scalars, keep_in4, near3)
-    msg5, act, dens = pl.pallas_call(
+        in_specs=[SM] + [VM] * 3,
+        out_specs=[VM] * 2,
+        out_shape=(
+            shape((2 * PER + NBQ + 2 * QUARTER, LANES), BF),
+            shape((2 * QUARTER, LANES), F32),
+        ),
+        scratch_shapes=[pltpu.VMEM((NACT, LANES), F32)],
+        compiler_params=PARAMS,
+    )(scalars, keep_in4, near3, msg4)
+    near4 = lax.ppermute(msg4, "pair", swap_core)
+    msg5, act, dens, exch = pl.pallas_call(
         gather_kernel,
         name="active_of_chip",
-        in_specs=[VM] * 12,
-        out_specs=[VM] * 3,
+        in_specs=[VM] * 13,
+        out_specs=[VM] * 4,
         out_shape=(
-            shape((3 * PER + 4 * NBQ, LANES), BF),
+            shape((3 * PER + 4 * NBQ + QUARTER, LANES), BF),
             shape((4 * PER, LANES), F32),
             shape((4 * NBQ, LANES), F32),
+            shape((QUARTER, LANES), F32),
         ),
         compiler_params=PARAMS,
-    )(keep1, keep2, keep3, keep4, dens1, dens2, dens3, dens4, near1, near3, near4, far1)
+    )(keep1, keep2, keep3, keep4, dens1, dens2, dens3, dens4, exch, near1, near3, near4, far1)
     far5 = lax.ppermute(msg5, "pair", swap_x)
-    e1, e2, e3 = (
-        lax.ppermute(e, "pair", [(p, p ^ k) for p in range(4)])
-        for k, e in ((1, e1), (2, e2), (3, e3))
-    )
     partial = pl.pallas_call(
         coulomb_kernel,
         name="coulomb",
-        in_specs=[VM] * 7,
+        in_specs=[VM] * 4,
         out_specs=VM,
-        out_shape=rows,
-        compiler_params=PARAMS,
-    )(act, far5, dens, own, e1, e2, e3)
+        out_shape=shape((QUARTER, NACT), F32),
+        compiler_params=PARAMS,
+    )(act, far5, dens, exch)
     active = pl.pallas_call(
         active_kernel,
         name="own_active",

time: 55.7 us -> 55.1 us (0.989)
  waiting for transfers between devices: 5.47 us -> 7.06 us
  starting transfers between devices: 11.3 us -> 9.82 us
  Pallas kernels: 34.5 us -> 33.7 us
    ppermute x1, waiting for transfers between devices: 0.01 us -> 3.8 us  [paired_body(): far5 = lax.ppermute(msg5, 'pair', swap_x)]
    ppermute x5 -> x3, waiting for transfers between devices: 4.5 us -> 2.28 us  [sum_over_aux(): lax.ppermute(part, 'aux', [(z, z ^ k) for z in range(n)])]
    ppermute x5 -> x3, starting transfers between devices: 6.1 us -> 4.39 us  [sum_over_aux(): lax.ppermute(part, 'aux', [(z, z ^ k) for z in range(n)])]
  transfers between devices with their start and end apart: 10 -> 8, of which waited for: 4 -> 3; matrix products, arithmetic and copies ran while one was open for 0% -> 0% of each run, Pallas kernels for 46% -> 44%
where the time goes in v4:
time: 55.1 us; the launch traced here: 54.8 us
  Pallas kernels  33.7 us (61%)
  starting transfers between devices  9.82 us (18%)
  waiting for transfers between devices  7.06 us (13%)
  local copies, waits for them, and re-layouts  2.17 us (4%)
  between operations  1.37 us (2%)
  other arithmetic  0.68 us (1%)
    pallas_call x1, Pallas kernels, paired_body(): pl.pallas_call(first_kernel, name='slabs_first', in_specs=[SM, HB, HB], o...  8.51 us
    pallas_call x1, Pallas kernels, paired_body(): pl.pallas_call(fourth_kernel, name='slabs_fourth', in_specs=[SM, HB] + [V...  7.48 us
    pallas_call x1, Pallas kernels, paired_body(): pl.pallas_call(third_kernel, name='slabs_third', in_specs=[SM, HB] + [VM]...  7.47 us
    pallas_call x1, Pallas kernels, paired_body(): pl.pallas_call(second_kernel, name='slabs_second', in_specs=[SM, HB, VM,...  7.46 us
    ppermute x3, starting transfers between devices, sum_over_aux(): lax.ppermute(part, 'aux', [(z, z ^ k) for z in range(n)])  4.39 us
    ppermute x1, waiting for transfers between devices, paired_body(): far5 = lax.ppermute(msg5, 'pair', swap_x)  3.8 us
    ppermute x1, starting transfers between devices, paired_body(): far1 = lax.ppermute(out2, 'pair', swap_x)  2.6 us
    ppermute x3, waiting for transfers between devices, sum_over_aux(): lax.ppermute(part, 'aux', [(z, z ^ k) for z in range(n)])  2.28 us
  transfers between devices with their start and end apart: 8, of which 3 were waited for; matrix products, arithmetic and copies ran while one was open for 0% of the time, Pallas kernels for 44%

profile of v4, /device:TPU:0, one launch (start us, length us, event | category | flops | bytes accessed | tf_op | source)
XLA Modules:
  0.0 54.8 jit_solution(3913167759810385171)
XLA Ops:
  1.3 0.7 %concatenate.6.scalars = s32[35]{0:T(128)S(1)} concatenate(s32[16]{0:T(128)} %param.7, s32[16]{0:T(128)} %param.8, s32[1]{0:T(128)S(6)} %copy.8, s32[1]{0:T(128)} %bitcast, s32[1]{0:T(128)} %bitcast.1), dimensions={0} | concatenate | bytes 280 | tf_op jit(solution)/shard_map/concatenate | solution.py:384
  2.0 1.4 %copy-done = bf16[4096,192]{0,1:T(8,128)(2,1)S(1)} copy-done((bf16[4096,192]{0,1:T(8,128)(2,1)S(1)}, bf16[4096,192]{0,1:T(8,128)(2,1)}, u32[]{:S(2)}) %copy-start) | copy-done | bytes 1572888
  3.4 8.5 %slabs_first.1 = (bf16[8,192,128]{2,1,0:T(8,128)(2,1)S(1)}, bf16[1024,256]{1,0:T(8,128)(2,1)S(1)}, bf16[1296,128]{1,0:T(8,128)(2,1)S(1)}, f32[256,128]{1,0:T(8,128)S(1)}, f32[16,128]{1,0:T(8,128)S(1)}) custom-call(s32[35]{0:T(128)S(1)} %concatenate.6.scalars, bf16[16,64,4096]{2,1,0:T(8,128)(2,1)} %slabs_ref.7, bf16[192,4096]{1,0:T(8,128)(2,1)S(1)} %bitcast.3), custom_call_target="tpu_custom_call" | custom-call | flops 6000000000 | bytes 10000000 | tf_op jit(solution)/shard_map/slabs_first/pallas_call | solution.py:398
  12.0 0.5 collective-permute-start
  12.5 7.5 %slabs_second.1 = (f32[1024,128]{1,0:T(8,128)S(1)}, bf16[256,128]{1,0:T(8,128)(2,1)S(1)}, f32[256,128]{1,0:T(8,128)S(1)}, f32[16,128]{1,0:T(8,128)S(1)}) custom-call(s32[35]{0:T(128)S(1)} %concatenate.6.scalars, bf16[16,64,4096]{2,1,0:T(8,128)(2,1)} %slabs_ref.7, bf16[8,192,128]{2,1,0:T(8,128)(2,1)S(1)} %get-tuple-element.33.lt_ref, ...), custom_call_target="tpu_custom_call" | custom-call | flops 6000000000 | bytes 10000000 | tf_op jit(solution)/shard_map/slabs_second/pallas_call | solution.py:417
  20.0 0.1 fusion
  20.0 2.6 %collective-permute-start.1 = (bf16[1152,128]{1,0:T(8,128)(2,1)S(1)}, bf16[1152,128]{1,0:T(8,128)(2,1)S(1)}, u32[]{:S(2)}, u32[]{:S(2)}) collective-permute-start(bf16[1152,128]{1,0:T(8,128)(2,1)S(1)} %fusion), channel_id=1, source_target_pairs={{0,8},{8,0},{4,12},{12,4},{1,9},{9,1},{5,13},{13,5},{2,10},{10,2},... | collective-permute-start | bytes 884744 | tf_op jit(solution)/shard_map/ppermute | solution.py:432
  22.6 7.5 %slabs_third.1 = (bf16[1568,128]{1,0:T(8,128)(2,1)S(1)}, f32[256,128]{1,0:T(8,128)S(1)}, f32[16,128]{1,0:T(8,128)S(1)}) custom-call(s32[35]{0:T(128)S(1)} %concatenate.6.scalars, bf16[16,64,4096]{2,1,0:T(8,128)(2,1)} %slabs_ref.7, bf16[8,192,128]{2,1,0:T(8,128)(2,1)S(1)} %get-tuple-element.33.lt_ref, bf16[1024,256]{1,0:T(8,128)(2,1)S(1)} %get-tuple-element.34.r_ref, ...), custom_call_target="tpu_custom_call" | custom-call | flops 6000000000 | bytes 10000000 | tf_op jit(solution)/shard_map/slabs_third/pallas_call | solution.py:433
  30.1 0.0 copy-start.1
  30.1 0.3 collective-permute-start.2
  30.4 7.5 %slabs_fourth.1 = (bf16[272,128]{1,0:T(8,128)(2,1)S(1)}, f32[1024,128]{1,0:T(8,128)S(1)}, f32[256,128]{1,0:T(8,128)S(1)}, f32[16,128]{1,0:T(8,128)S(1)}) custom-call(s32[35]{0:T(128)S(1)} %concatenate.6.scalars, bf16[16,64,4096]{2,1,0:T(8,128)(2,1)} %slabs_ref.7, bf16[8,192,128]{2,1,0:T(8,128)(2,1)S(1)} %get-tuple-element.33.lt_ref, ...), custom_call_target="tpu_custom_call" | custom-call | flops 6000000000 | bytes 10000000 | tf_op jit(solution)/shard_map/slabs_fourth/pallas_call | solution.py:444
  37.9 0.0 collective-permute-done.2.near3
  37.9 1.0 %exchange.1 = (bf16[304,128]{1,0:T(8,128)(2,1)S(1)}, f32[32,128]{1,0:T(8,128)S(1)}) custom-call(s32[35]{0:T(128)S(1)} %concatenate.6.scalars, f32[1024,128]{1,0:T(8,128)S(1)} %get-tuple-element.43.mine, bf16[1568,128]{1,0:T(8,128)(2,1)S(1)} %collective-permute-done.2.near3, bf16[272,128]{1,0:T(8,128)(2,1)S(1)} %get-tuple-element.45.msg4), custom_call_target="tpu_custom_call" | custom-call | tf_op jit(solution)/shard_map/exchange/pallas_call | solution.py:456
  38.9 0.4 collective-permute-start.3
  39.3 1.0 %collective-permute-done.3.near4 = bf16[304,128]{1,0:T(8,128)(2,1)S(1)} collective-permute-done((bf16[304,128]{1,0:T(8,128)(2,1)S(1)}, bf16[304,128]{1,0:T(8,128)(2,1)S(1)}, u32[]{:S(2)}, u32[]{:S(2)}) %collective-permute-start.3) | collective-permute-done | bytes 77856 | tf_op jit(solution)/shard_map/ppermute | solution.py:468
  40.2 0.1 active_of_chip.1
  40.4 1.7 %collective-permute-start.4 = (bf16[464,128]{1,0:T(8,128)(2,1)S(1)}, bf16[464,128]{1,0:T(8,128)(2,1)S(1)}, u32[]{:S(2)}, u32[]{:S(2)}) collective-permute-start(bf16[464,128]{1,0:T(8,128)(2,1)S(1)} %get-tuple-element.49), channel_id=1, source_target_pairs={{0,8},{8,0},{4,12},{12,4},{1,9},{9,1},{5,13},{13,5},{2,10},{10,2},... | collective-permute-start | bytes 356360 | tf_op jit(solution)/shard_map/ppermute | solution.py:482
  42.1 3.8 %collective-permute-done.4.far = bf16[464,128]{1,0:T(8,128)(2,1)S(1)} collective-permute-done((bf16[464,128]{1,0:T(8,128)(2,1)S(1)}, bf16[464,128]{1,0:T(8,128)(2,1)S(1)}, u32[]{:S(2)}, u32[]{:S(2)}) %collective-permute-start.4) | collective-permute-done | bytes 118816 | tf_op jit(solution)/shard_map/ppermute | solution.py:482
  45.9 0.2 coulomb.1
  46.1 3.6 %collective-permute-start.7 = (f32[16,64]{1,0:T(8,128)S(1)}, f32[16,64]{1,0:T(8,128)S(1)}, u32[]{:S(2)}, u32[]{:S(2)}) collective-permute-start(f32[16,64]{1,0:T(8,128)S(1)} %coulomb.1), channel_id=1, source_target_pairs={{0,3},{1,2},{2,1},{3,0},{4,7},{5,6},{6,5},{7,4},{8,11},{9,10},{10,... | collective-permute-start | bytes 12296 | tf_op jit(solution)/shard_map/ppermute | solution.py:375
  49.7 0.8 %collective-permute-start.5 = (f32[16,64]{1,0:T(8,128)S(1)}, f32[16,64]{1,0:T(8,128)S(1)}, u32[]{:S(2)}, u32[]{:S(2)}) collective-permute-start(f32[16,64]{1,0:T(8,128)S(1)} %coulomb.1), channel_id=1, source_target_pairs={{0,1},{1,0},{2,3},{3,2},{4,5},{5,4},{6,7},{7,6},{8,9},{9,8},{10,11... | collective-permute-start | bytes 12296 | tf_op jit(solution)/shard_map/ppermute | solution.py:375
  50.5 1.5 %own_active.1 = f32[64,16,64]{2,1,0:T(8,128)} custom-call(s32[35]{0:T(128)S(1)} %concatenate.6.scalars, f32[512,128]{1,0:T(8,128)S(1)} %get-tuple-element.48.act, bf16[464,128]{1,0:T(8,128)(2,1)S(1)} %collective-permute-done.4.far), custom_call_target="tpu_custom_call" | custom-call | flops 1000000 | bytes 1000000 | tf_op jit(solution)/shard_map/own_active/pallas_call | solution.py:491
  51.9 2.3 %collective-permute-done.6 = f32[16,64]{1,0:T(8,128)S(1)} collective-permute-done((f32[16,64]{1,0:T(8,128)S(1)}, f32[16,64]{1,0:T(8,128)S(1)}, u32[]{:S(2)}, u32[]{:S(2)}) %collective-permute-start.6) | collective-permute-done | bytes 4128 | tf_op jit(solution)/shard_map/ppermute | solution.py:375
  54.2 0.6 %add_add_fusion = f32[16,64]{1,0:T(8,128)} fusion(f32[16,64]{1,0:T(8,128)S(1)} %copy-done.1, f32[16,64]{1,0:T(8,128)S(1)} %collective-permute-done.6, f32[16,64]{1,0:T(8,128)S(1)} %collective-permute-done.7, f32[16,64]{1,0:T(8,128)S(1)} %coulomb.1, f32[16,64]{1,0:T(8,128)S(1)} %collective-permute-done.5), kind=kLoop, calls=%fused_computation.2 | loop fusion | flops 4096 | bytes 24576 | tf_op jit(solution)/shard_map/add | solution.py:500
  (8 shorter events, 0.0 us)
Async XLA Ops:
  2.0 1.4 %copy-start = (bf16[4096,192]{0,1:T(8,128)(2,1)S(1)}, bf16[4096,192]{0,1:T(8,128)(2,1)}, u32[]{:S(2)}) copy-start(bf16[4096,192]{0,1:T(8,128)(2,1)} %param.10) | copy-start | bytes 4718596
  12.0 8.0 %collective-permute-start = (bf16[1296,128]{1,0:T(8,128)(2,1)S(1)}, bf16[1296,128]{1,0:T(8,128)(2,1)S(1)}, u32[]{:S(2)}, u32[]{:S(2)}) collective-permute-start(bf16[1296,128]{1,0:T(8,128)(2,1)S(1)} %get-tuple-element.32), channel_id=1, source_target_pairs={{0,4},{4,0},{8,12},{12,8},{1,5},{5,1},{9,13},{13,9},{2,6},{6,2},{1... | collective-permute-start | bytes 995336 | tf_op jit(solution)/shard_map/ppermute | solution.py:416
  20.0 10.4 %collective-permute-start.1 = (bf16[1152,128]{1,0:T(8,128)(2,1)S(1)}, bf16[1152,128]{1,0:T(8,128)(2,1)S(1)}, u32[]{:S(2)}, u32[]{:S(2)}) collective-permute-start(bf16[1152,128]{1,0:T(8,128)(2,1)S(1)} %fusion), channel_id=1, source_target_pairs={{0,8},{8,0},{4,12},{12,4},{1,9},{9,1},{5,13},{13,5},{2,10},{10,2},... | collective-permute-start | bytes 884744 | tf_op jit(solution)/shard_map/ppermute | solution.py:432
  30.1 24.1 %copy-start.1 = (f32[16,64]{1,0:T(8,128)S(1)}, f32[16,64]{1,0:T(8,128)}, u32[]{:S(2)}) copy-start(f32[16,64]{1,0:T(8,128)} %param.11) | copy-start | bytes 12292
  30.1 7.8 %collective-permute-start.2 = (bf16[1568,128]{1,0:T(8,128)(2,1)S(1)}, bf16[1568,128]{1,0:T(8,128)(2,1)S(1)}, u32[]{:S(2)}, u32[]{:S(2)}) collective-permute-start(bf16[1568,128]{1,0:T(8,128)(2,1)S(1)} %get-tuple-element.44), channel_id=1, source_target_pairs={{0,4},{4,0},{8,12},{12,8},{1,5},{5,1},{9,13},{13,9},{2,6},{6,2},{1... | collective-permute-start | bytes 1204232 | tf_op jit(solution)/shard_map/ppermute | solution.py:443
  38.9 1.3 %collective-permute-start.3 = (bf16[304,128]{1,0:T(8,128)(2,1)S(1)}, bf16[304,128]{1,0:T(8,128)(2,1)S(1)}, u32[]{:S(2)}, u32[]{:S(2)}) collective-permute-start(bf16[304,128]{1,0:T(8,128)(2,1)S(1)} %get-tuple-element.47), channel_id=1, source_target_pairs={{0,4},{4,0},{8,12},{12,8},{1,5},{5,1},{9,13},{13,9},{2,6},{6,2},{1... | collective-permute-start | bytes 233480 | tf_op jit(solution)/shard_map/ppermute | solution.py:468
  40.4 5.5 %collective-permute-start.4 = (bf16[464,128]{1,0:T(8,128)(2,1)S(1)}, bf16[464,128]{1,0:T(8,128)(2,1)S(1)}, u32[]{:S(2)}, u32[]{:S(2)}) collective-permute-start(bf16[464,128]{1,0:T(8,128)(2,1)S(1)} %get-tuple-element.49), channel_id=1, source_target_pairs={{0,8},{8,0},{4,12},{12,4},{1,9},{9,1},{5,13},{13,5},{2,10},{10,2},... | collective-permute-start | bytes 356360 | tf_op jit(solution)/shard_map/ppermute | solution.py:482
  46.1 5.9 %collective-permute-start.7 = (f32[16,64]{1,0:T(8,128)S(1)}, f32[16,64]{1,0:T(8,128)S(1)}, u32[]{:S(2)}, u32[]{:S(2)}) collective-permute-start(f32[16,64]{1,0:T(8,128)S(1)} %coulomb.1), channel_id=1, source_target_pairs={{0,3},{1,2},{2,1},{3,0},{4,7},{5,6},{6,5},{7,4},{8,11},{9,10},{10,... | collective-permute-start | bytes 12296 | tf_op jit(solution)/shard_map/ppermute | solution.py:375
  49.7 4.5 %collective-permute-start.6 = (f32[16,64]{1,0:T(8,128)S(1)}, f32[16,64]{1,0:T(8,128)S(1)}, u32[]{:S(2)}, u32[]{:S(2)}) collective-permute-start(f32[16,64]{1,0:T(8,128)S(1)} %coulomb.1), channel_id=1, source_target_pairs={{0,2},{1,3},{2,0},{3,1},{4,6},{5,7},{6,4},{7,5},{8,10},{9,11},{10,... | collective-permute-start | bytes 12296 | tf_op jit(solution)/shard_map/ppermute | solution.py:375
  49.7 4.5 %collective-permute-start.5 = (f32[16,64]{1,0:T(8,128)S(1)}, f32[16,64]{1,0:T(8,128)S(1)}, u32[]{:S(2)}, u32[]{:S(2)}) collective-permute-start(f32[16,64]{1,0:T(8,128)S(1)} %coulomb.1), channel_id=1, source_target_pairs={{0,1},{1,0},{2,3},{3,2},{4,5},{5,4},{6,7},{7,6},{8,9},{9,8},{10,11... | collective-permute-start | bytes 12296 | tf_op jit(solution)/shard_map/ppermute | solution.py:375

commit v5 on v4

--- a/solution.py
+++ b/solution.py
@@ -21,14 +21,13 @@
     return lax.broadcasted_iota(jnp.int32, (rows, LANES), 1) < BS
 
 
-def orbital_blocks(scalars, slabs, windows, lt_ref, r_ref):
+def orbital_blocks(blocks, live, slabs, windows, lt_ref, r_ref):
     first = low_half(NCOL)
-    live = scalars[2 * slabs]
 
     def window(n, slot, upper):
         w = windows[n].astype(F32)
         w = jnp.concatenate([w[NACT:], w[:NACT]], axis=0)
-        moved = lax.rem(scalars[n], 2) != (1 if upper else 0)
+        moved = lax.rem(blocks[n], 2) != (1 if upper else 0)
         w = jnp.where(moved, pltpu.roll(w, BS, 1), w)
         return jnp.where(slot < live, w, 0.0)
 
@@ -56,13 +55,13 @@
         slab_copy(slabs_ref, sbuf, sem, block, k).start()
 
 
-def run_block(slabs_ref, block, lt_ref, r_ref, scratch, emit):
+def run_block(slabs_ref, block, lt_ref, r_ref, scratch, emit, prepare=None):
     sbuf, even_ref, odd_ref, half_ref, diag, sem = scratch
     pairs = slabs_ref.shape[0] // 2
     first = low_half(NBQ)
     first_s = low_half(BS)
     zero = jnp.zeros((BS, LANES), BF)
-    wide, group = NBQ, 8
+    wide, group = NBQ, 4
 
     def wait(k):
         slab_copy(slabs_ref, sbuf, sem, block, k).wait()
@@ -70,14 +69,14 @@
     def relayout(k, out):
         for j in range(sbuf.shape[3] // LANES):
             lanes = slice(j * LANES, (j + 1) * LANES)
-            a = sbuf[k, 0, :, lanes].astype(F32)
-            b = sbuf[k, 1, :, lanes].astype(F32)
+            a = sbuf[k, 0, :, lanes]
+            b = sbuf[k, 1, :, lanes]
             out[pl.ds(MSTEP * 2 * j, NBQ, stride=QSTEP), :] = jnp.where(
                 first, a, pltpu.roll(b, BS, 1)
-            )
+            ).astype(F32)
             out[pl.ds(MSTEP * (2 * j + 1), NBQ, stride=QSTEP), :] = jnp.where(
                 first, pltpu.roll(a, BS, 1), b
-            )
+            ).astype(F32)
 
     def half_transform(k, rows):
         left = lt_ref[k]
@@ -105,9 +104,11 @@
         half_transform(2 * i + 1, odd_ref)
         return carry
 
-    def second_transform(g, carry):
+    def second_transform(g):
         lhs = half_ref[pl.ds(group * g, group)].reshape(group * NCOL, half_ref.shape[2])
-        whole = jnp.dot(lhs, r_ref[...], preferred_element_type=F32)
+        return jnp.dot(lhs, r_ref[...], preferred_element_type=F32)
+
+    def assemble(g, whole):
         eye = lax.broadcasted_iota(jnp.int32, (NIN, NIN), 0) == lax.broadcasted_iota(
             jnp.int32, (NIN, NIN), 1
         )
@@ -128,12 +129,17 @@
                 diag[pl.ds(2 * h + n, 1), :] = jnp.sum(
                     jnp.where(eye, w[:NIN, :NIN], 0.0), axis=0, keepdims=True
                 )
-        return carry
 
     wait(0)
     relayout(0, even_ref)
+    if prepare is not None:
+        prepare()
     lax.fori_loop(0, pairs // 2, two_pairs, 0)
-    lax.fori_loop(0, NBQ // group, second_transform, 0)
+    whole = second_transform(0)
+    for g in range(NBQ // group):
+        following = second_transform(g + 1) if g + 1 < NBQ // group else None
+        assemble(g, whole)
+        whole = following
 
 
 def split_wire(d):
@@ -157,63 +163,64 @@
 
 
 def emit_active(h, act, core, x, send, keep, send_at):
-    for place in (0, 1):
-        xx = (1 - x) if place == 0 else x
-        for cc in (0, 1):
-            block = act[:QUARTER]
-            for idx in range(1, 4):
-                block = jnp.where(
-                    2 * xx + cc == idx, act[idx * QUARTER : (idx + 1) * QUARTER], block
-                )
-            off = place * PER + h * QUARTER
-
-            @pl.when(core == cc)
-            def _():
-                keep[pl.ds(pl.multiple_of(off, QUARTER), QUARTER), :] = block
-
-            @pl.when(core != cc)
-            def _():
-                send[pl.ds(pl.multiple_of(send_at + off, QUARTER), QUARTER), :] = block.astype(BF)
+    upper, lower = act[: 2 * QUARTER], act[2 * QUARTER :]
+    parts = (jnp.where(x == 0, lower, upper), jnp.where(x == 0, upper, lower))
+    for place, part in enumerate(parts):
+        one, two = part[:QUARTER], part[QUARTER:]
+        off = place * PER + h * QUARTER
+        keep[pl.ds(off, QUARTER), :] = jnp.where(core == 0, one, two)
+        send[pl.ds(send_at + off, QUARTER), :] = jnp.where(core == 0, two, one).astype(BF)
 
 
 def pair_rows(h, n):
-    return pl.ds(pl.multiple_of((2 * h + n) * NACT, NACT), NACT)
+    return pl.ds((2 * h + n) * NACT, NACT)
 
 
 def first_kernel(
-    scalars, slabs_ref, ot_ref, lt_out, r_out, msg, keep, dens, windows, wsem, *scratch
+    where, rows_ref, cols_ref, live, slabs_ref, ot_ref, lt_out, r_out, msg, keep, dens,
+    rows, cols, ssem, windows, wsem, *scratch
 ):
     slabs = slabs_ref.shape[0]
-    core, x = scalars[2 * slabs + 1], scalars[2 * slabs + 2]
+    core, x = where[0], where[1]
     block = 2 * (1 - x) + (1 - core)
+    sbuf, sem, diag = scratch[0], scratch[5], scratch[4]
+    small = [
+        pltpu.make_async_copy(src, dst, ssem.at[n])
+        for n, (src, dst) in enumerate(((rows_ref, rows), (cols_ref, cols)))
+    ]
+    for copy in small:
+        copy.start()
+    start_slabs(slabs_ref, sbuf, sem, block)
+    for copy in small:
+        copy.wait()
+    blocks = [rows[n] for n in range(slabs)] + [cols[n] for n in range(slabs)]
     copies = []
-    for n in range(2 * slabs):
-        base = pl.multiple_of((scalars[n] // 2) * PAIRED, PAIRED)
+    for n, blk in enumerate(blocks):
+        base = pl.multiple_of((blk // 2) * PAIRED, PAIRED)
         copies.append(
             pltpu.make_async_copy(ot_ref.at[:, pl.ds(base, PAIRED)], windows.at[n], wsem.at[n])
         )
         copies[-1].start()
-    sbuf, sem, diag = scratch[0], scratch[5], scratch[4]
-    start_slabs(slabs_ref, sbuf, sem, block)
-    for copy in copies:
-        copy.wait()
-    orbital_blocks(scalars, slabs, windows, lt_out, r_out)
+
+    def prepare():
+        for copy in copies:
+            copy.wait()
+        orbital_blocks(blocks, live[0], slabs, windows, lt_out, r_out)
 
     def emit(h, in0, in1, act):
         msg[pair_rows(h, 0), :] = in0.astype(BF)
         msg[pair_rows(h, 1), :] = in1.astype(BF)
         emit_active(h, act, core, x, msg, keep, INROWS)
 
-    run_block(slabs_ref, block, lt_out, r_out, scratch, emit)
+    run_block(slabs_ref, block, lt_out, r_out, scratch, emit, prepare)
     dens[...] = density_of(diag[...])
     msg[pl.ds(INROWS + 2 * PER, NBQ), :] = split_wire(dens[...])
 
 
 def second_kernel(
-    scalars, slabs_ref, lt_ref, r_ref, keep_in, send, keep, dens, *scratch
+    where, slabs_ref, lt_ref, r_ref, keep_in, send, keep, dens, *scratch
 ):
-    slabs = slabs_ref.shape[0]
-    core, x = scalars[2 * slabs + 1], scalars[2 * slabs + 2]
+    core, x = where[0], where[1]
     block = 2 * (1 - x) + core
     start_slabs(slabs_ref, scratch[0], scratch[5], block)
 
@@ -227,10 +234,9 @@
 
 
 def third_kernel(
-    scalars, slabs_ref, lt_ref, r_ref, send2, dens2, msg, keep, dens, *scratch
+    where, slabs_ref, lt_ref, r_ref, send2, dens2, msg, keep, dens, *scratch
 ):
-    slabs = slabs_ref.shape[0]
-    core, x = scalars[2 * slabs + 1], scalars[2 * slabs + 2]
+    core, x = where[0], where[1]
     block = 2 * x + (1 - core)
     start_slabs(slabs_ref, scratch[0], scratch[5], block)
 
@@ -247,10 +253,9 @@
 
 
 def fourth_kernel(
-    scalars, slabs_ref, lt_ref, r_ref, far1, msg, keep_in, keep, dens, *scratch
+    where, slabs_ref, lt_ref, r_ref, far1, msg, keep_in, keep, dens, *scratch
 ):
-    slabs = slabs_ref.shape[0]
-    core, x = scalars[2 * slabs + 1], scalars[2 * slabs + 2]
+    core, x = where[0], where[1]
     block = 2 * x + core
     start_slabs(slabs_ref, scratch[0], scratch[5], block)
 
@@ -264,7 +269,7 @@
     msg[pl.ds(2 * PER, NBQ), :] = split_wire(dens[...])
 
 
-def exchange_kernel(scalars, mine, near3, msg4, msg, keep, whole):
+def exchange_kernel(where, mine, near3, msg4, msg, keep, whole):
     parts = []
     for q in range(NBQ):
         rows = pl.ds(q * NACT, NACT)
@@ -278,8 +283,7 @@
     )
     total = both[:NACT] + both[NACT:] + both[NACT:].T
     whole[...] = jnp.concatenate([total, total], axis=1)
-    last = scalars.shape[0] - 1
-    core, x = scalars[last - 1], scalars[last]
+    core, x = where[0], where[1]
     size = msg4.shape[0]
     msg[pl.ds(0, size), :] = msg4[...]
     for place, xx in enumerate((1 - x, x)):
@@ -340,9 +344,8 @@
     partial[...] = total[:, :BS]
 
 
-def active_kernel(scalars, act, far, out):
-    last = scalars.shape[0] - 1
-    core, x = scalars[last - 1], scalars[last]
+def active_kernel(where, act, far, out):
+    core, x = where[0], where[1]
     for n in range(4):
         xx = (1 - x) if n < 2 else x
         cc = (1 - core) if n % 2 == 0 else core
@@ -363,6 +366,10 @@
 PARAMS = pltpu.CompilerParams(vmem_limit_bytes=48 * 1024 * 1024)
 
 
+def in_hbm(array):
+    return pltpu.with_memory_space_constraint(array, pltpu.HBM)
+
+
 def shape(dims, dtype):
     return jax.ShapeDtypeStruct(dims, dtype)
 
@@ -381,7 +388,6 @@
     nslab, batch, width = slabs.shape
     index = lax.axis_index("pair")
     where = jnp.stack([lax.rem(index, 2), index // 2])
-    scalars = jnp.concatenate([block_row, block_col, live_count, where])
     swap_core = [(0, 1), (1, 0), (2, 3), (3, 2)]
     swap_x = [(0, 2), (2, 0), (1, 3), (3, 1)]
     aos = nslab * BS
@@ -398,7 +404,7 @@
     lt, r, msg1, keep1, dens1 = pl.pallas_call(
         first_kernel,
         name="slabs_first",
-        in_specs=[SM, HB, HB],
+        in_specs=[SM, HB, HB, SM, HB, HB],
         out_specs=[VM] * 5,
         out_shape=(
             shape((nslab // 2, NCOL, PAIRED), BF),
@@ -408,11 +414,16 @@
             dens,
         ),
         scratch_shapes=[
+            pltpu.SMEM((nslab,), jnp.int32), pltpu.SMEM((nslab,), jnp.int32),
+            pltpu.SemaphoreType.DMA((2,)),
             pltpu.VMEM((2 * nslab, NCOL, PAIRED), BF), pltpu.SemaphoreType.DMA((2 * nslab,)),
         ] + scratch,
         compiler_params=PARAMS,
         cost_estimate=cost,
-    )(scalars, slabs, orbitals.T)
+    )(
+        where, in_hbm(block_row), in_hbm(block_col), live_count, slabs,
+        in_hbm(orbitals.T),
+    )
     near1 = lax.ppermute(msg1, "pair", swap_core)
     keep_in2, send2, keep2, dens2 = pl.pallas_call(
         second_kernel,
@@ -425,7 +436,7 @@
         scratch_shapes=scratch,
         compiler_params=PARAMS,
         cost_estimate=cost,
-    )(scalars, slabs, lt, r)
+    )(where, slabs, lt, r)
     out2 = jnp.concatenate([keep_in2, keep2[:PER]], axis=0)
     out2 = (out2 + near1[: INROWS + PER].astype(F32)).astype(BF)
     out2, lt, r = lax.optimization_barrier((out2, lt, r))
@@ -439,7 +450,7 @@
         scratch_shapes=scratch,
         compiler_params=PARAMS,
         cost_estimate=cost,
-    )(scalars, slabs, lt, r, send2, dens2)
+    )(where, slabs, lt, r, send2, dens2)
     near3 = lax.ppermute(msg3, "pair", swap_core)
     msg4, keep_in4, keep4, dens4 = pl.pallas_call(
         fourth_kernel,
@@ -452,7 +463,7 @@
         scratch_shapes=scratch,
         compiler_params=PARAMS,
         cost_estimate=cost,
-    )(scalars, slabs, lt, r, far1)
+    )(where, slabs, lt, r, far1)
     msg4, exch = pl.pallas_call(
         exchange_kernel,
         name="exchange",
@@ -464,7 +475,7 @@
         ),
         scratch_shapes=[pltpu.VMEM((NACT, LANES), F32)],
         compiler_params=PARAMS,
-    )(scalars, keep_in4, near3, msg4)
+    )(where, keep_in4, near3, msg4)
     near4 = lax.ppermute(msg4, "pair", swap_core)
     msg5, act, dens, exch = pl.pallas_call(
         gather_kernel,
@@ -496,7 +507,7 @@
         out_shape=shape((batch, QUARTER, NACT), F32),
         compiler_params=PARAMS,
         cost_estimate=pl.CostEstimate(flops=10**6, bytes_accessed=10**6, transcendentals=0),
-    )(scalars, act, far5)
+    )(where, act, far5)
     return (active, hcore + sum_over_aux(partial))
 
 

time: 55.1 us -> 51.4 us (0.933)
  Pallas kernels: 33.7 us -> 31.1 us
  local copies, waits for them, and re-layouts: 2.17 us -> 0.01 us
  waiting for transfers between devices: 7.06 us -> 8.14 us
    unnamed x4 -> x2, local copies, waits for them, and re-layouts: 1.42 us -> 0.01 us
    pallas_call x1, Pallas kernels: 7.46 us -> 6.47 us  [paired_body(): pl.pallas_call(second_kernel, name='slabs_second', in_specs=[SM, HB, VM,...]
    pallas_call x1, Pallas kernels: 7.48 us -> 6.5 us  [paired_body(): pl.pallas_call(fourth_kernel, name='slabs_fourth', in_specs=[SM, HB] + [V...]
    pallas_call x1, Pallas kernels: 7.47 us -> 6.5 us  [paired_body(): pl.pallas_call(third_kernel, name='slabs_third', in_specs=[SM, HB] + [VM]...]
    ppermute x1, waiting for transfers between devices: 0.01 us -> 0.89 us  [paired_body(): far1 = lax.ppermute(out2, 'pair', swap_x)]
    concatenate x1 -> x0, local copies, waits for them, and re-layouts: 0.75 us -> none  [paired_body(): scalars = jnp.concatenate([block_row, block_col, live_count, where])]
  transfers between devices with their start and end apart: 8 -> 8, of which waited for: 3 -> 4; matrix products, arithmetic and copies ran while one was open for 0% -> 0% of each run, Pallas kernels for 44% -> 41%
where the time goes in v5:
time: 51.4 us; the launch traced here: 51.1 us
  Pallas kernels  31.1 us (61%)
  starting transfers between devices  9.76 us (19%)
  waiting for transfers between devices  8.14 us (16%)
  between operations  1.37 us (3%)
  other arithmetic  0.75 us (1%)
    pallas_call x1, Pallas kernels, paired_body(): pl.pallas_call(first_kernel, name='slabs_first', in_specs=[SM, HB, HB, SM...  8.83 us
    pallas_call x1, Pallas kernels, paired_body(): pl.pallas_call(third_kernel, name='slabs_third', in_specs=[SM, HB] + [VM]...  6.5 us
    pallas_call x1, Pallas kernels, paired_body(): pl.pallas_call(fourth_kernel, name='slabs_fourth', in_specs=[SM, HB] + [V...  6.5 us
    pallas_call x1, Pallas kernels, paired_body(): pl.pallas_call(second_kernel, name='slabs_second', in_specs=[SM, HB, VM,...  6.47 us
    ppermute x3, starting transfers between devices, sum_over_aux(): lax.ppermute(part, 'aux', [(z, z ^ k) for z in range(n)])  4.49 us
    ppermute x1, waiting for transfers between devices, paired_body(): far5 = lax.ppermute(msg5, 'pair', swap_x)  3.55 us
    ppermute x1, starting transfers between devices, paired_body(): far1 = lax.ppermute(out2, 'pair', swap_x)  2.6 us
    ppermute x3, waiting for transfers between devices, sum_over_aux(): lax.ppermute(part, 'aux', [(z, z ^ k) for z in range(n)])  2.43 us
  transfers between devices with their start and end apart: 8, of which 4 were waited for; matrix products, arithmetic and copies ran while one was open for 0% of the time, Pallas kernels for 41%

profile of v5, /device:TPU:0, one launch (start us, length us, event | category | flops | bytes accessed | tf_op | source)
XLA Modules:
  0.0 51.1 jit_solution(1020113935518012753)
XLA Ops:
  1.3 0.1 pad_add_fusion.where
  1.4 8.8 %slabs_first.1 = (bf16[8,192,128]{2,1,0:T(8,128)(2,1)S(1)}, bf16[1024,256]{1,0:T(8,128)(2,1)S(1)}, bf16[1296,128]{1,0:T(8,128)(2,1)S(1)}, f32[256,128]{1,0:T(8,128)S(1)}, f32[16,128]{1,0:T(8,128)S(1)}) custom-call(s32[2]{0:T(128)S(1)} %pad_add_fusion.where, s32[16]{0:T(128)} %rows_ref.1, s32[16]{0:T(128)} %cols_ref.1, s32[1]{0:T(128)S(6)} %copy.8.live, ...), custom_call_target="tpu_custom_call" | custom-call | flops 6000000000 | bytes 10000000 | tf_op jit(solution)/shard_map/slabs_first/pallas_call | solution.py:404
  10.2 0.5 %collective-permute-start = (bf16[1296,128]{1,0:T(8,128)(2,1)S(1)}, bf16[1296,128]{1,0:T(8,128)(2,1)S(1)}, u32[]{:S(2)}, u32[]{:S(2)}) collective-permute-start(bf16[1296,128]{1,0:T(8,128)(2,1)S(1)} %get-tuple-element.32), channel_id=1, source_target_pairs={{0,4},{4,0},{8,12},{12,8},{1,5},{5,1},{9,13},{13,9},{2,6},{6,2},{1... | collective-permute-start | bytes 995336 | tf_op jit(solution)/shard_map/ppermute | solution.py:427
  10.7 6.5 %slabs_second.1 = (f32[1024,128]{1,0:T(8,128)S(1)}, bf16[256,128]{1,0:T(8,128)(2,1)S(1)}, f32[256,128]{1,0:T(8,128)S(1)}, f32[16,128]{1,0:T(8,128)S(1)}) custom-call(s32[2]{0:T(128)S(1)} %pad_add_fusion.where, bf16[16,64,4096]{2,1,0:T(8,128)(2,1)} %slabs_ref.7, bf16[8,192,128]{2,1,0:T(8,128)(2,1)S(1)} %get-tuple-element.33.lt_ref, ...), custom_call_target="tpu_custom_call" | custom-call | flops 6000000000 | bytes 10000000 | tf_op jit(solution)/shard_map/slabs_second/pallas_call | solution.py:428
  17.2 0.1 fusion
  17.3 2.6 %collective-permute-start.1 = (bf16[1152,128]{1,0:T(8,128)(2,1)S(1)}, bf16[1152,128]{1,0:T(8,128)(2,1)S(1)}, u32[]{:S(2)}, u32[]{:S(2)}) collective-permute-start(bf16[1152,128]{1,0:T(8,128)(2,1)S(1)} %fusion), channel_id=1, source_target_pairs={{0,8},{8,0},{4,12},{12,4},{1,9},{9,1},{5,13},{13,5},{2,10},{10,2},... | collective-permute-start | bytes 884744 | tf_op jit(solution)/shard_map/ppermute | solution.py:443
  19.9 6.5 %slabs_third.1 = (bf16[1568,128]{1,0:T(8,128)(2,1)S(1)}, f32[256,128]{1,0:T(8,128)S(1)}, f32[16,128]{1,0:T(8,128)S(1)}) custom-call(s32[2]{0:T(128)S(1)} %pad_add_fusion.where, bf16[16,64,4096]{2,1,0:T(8,128)(2,1)} %slabs_ref.7, bf16[8,192,128]{2,1,0:T(8,128)(2,1)S(1)} %get-tuple-element.33.lt_ref, bf16[1024,256]{1,0:T(8,128)(2,1)S(1)} %get-tuple-element.34.r_ref, ...), custom_call_target="tpu_custom_call" | custom-call | flops 6000000000 | bytes 10000000 | tf_op jit(solution)/shard_map/slabs_third/pallas_call | solution.py:444
  26.4 0.0 copy-start
  26.4 0.3 collective-permute-start.2
  26.7 0.9 %collective-permute-done.1.far1 = bf16[1152,128]{1,0:T(8,128)(2,1)S(1)} collective-permute-done((bf16[1152,128]{1,0:T(8,128)(2,1)S(1)}, bf16[1152,128]{1,0:T(8,128)(2,1)S(1)}, u32[]{:S(2)}, u32[]{:S(2)}) %collective-permute-start.1) | collective-permute-done | bytes 294944 | tf_op jit(solution)/shard_map/ppermute | solution.py:443
  27.6 6.5 %slabs_fourth.1 = (bf16[272,128]{1,0:T(8,128)(2,1)S(1)}, f32[1024,128]{1,0:T(8,128)S(1)}, f32[256,128]{1,0:T(8,128)S(1)}, f32[16,128]{1,0:T(8,128)S(1)}) custom-call(s32[2]{0:T(128)S(1)} %pad_add_fusion.where, bf16[16,64,4096]{2,1,0:T(8,128)(2,1)} %slabs_ref.7, bf16[8,192,128]{2,1,0:T(8,128)(2,1)S(1)} %get-tuple-element.33.lt_ref, ...), custom_call_target="tpu_custom_call" | custom-call | flops 6000000000 | bytes 10000000 | tf_op jit(solution)/shard_map/slabs_fourth/pallas_call | solution.py:455
  34.1 1.0 %exchange.1 = (bf16[304,128]{1,0:T(8,128)(2,1)S(1)}, f32[32,128]{1,0:T(8,128)S(1)}) custom-call(s32[2]{0:T(128)S(1)} %pad_add_fusion.where, f32[1024,128]{1,0:T(8,128)S(1)} %get-tuple-element.43.mine, bf16[1568,128]{1,0:T(8,128)(2,1)S(1)} %collective-permute-done.2.near3, bf16[272,128]{1,0:T(8,128)(2,1)S(1)} %get-tuple-element.45.msg4), custom_call_target="tpu_custom_call" | custom-call | tf_op jit(solution)/shard_map/exchange/pallas_call | solution.py:467
  35.1 0.1 collective-permute-start.3
  35.2 1.3 %collective-permute-done.3.near4 = bf16[304,128]{1,0:T(8,128)(2,1)S(1)} collective-permute-done((bf16[304,128]{1,0:T(8,128)(2,1)S(1)}, bf16[304,128]{1,0:T(8,128)(2,1)S(1)}, u32[]{:S(2)}, u32[]{:S(2)}) %collective-permute-start.3) | collective-permute-done | bytes 77856 | tf_op jit(solution)/shard_map/ppermute | solution.py:479
  36.4 0.1 active_of_chip.1
  36.6 1.8 %collective-permute-start.4 = (bf16[464,128]{1,0:T(8,128)(2,1)S(1)}, bf16[464,128]{1,0:T(8,128)(2,1)S(1)}, u32[]{:S(2)}, u32[]{:S(2)}) collective-permute-start(bf16[464,128]{1,0:T(8,128)(2,1)S(1)} %get-tuple-element.49), channel_id=1, source_target_pairs={{0,8},{8,0},{4,12},{12,4},{1,9},{9,1},{5,13},{13,5},{2,10},{10,2},... | collective-permute-start | bytes 356360 | tf_op jit(solution)/shard_map/ppermute | solution.py:493
  38.4 3.6 %collective-permute-done.4.far = bf16[464,128]{1,0:T(8,128)(2,1)S(1)} collective-permute-done((bf16[464,128]{1,0:T(8,128)(2,1)S(1)}, bf16[464,128]{1,0:T(8,128)(2,1)S(1)}, u32[]{:S(2)}, u32[]{:S(2)}) %collective-permute-start.4) | collective-permute-done | bytes 118816 | tf_op jit(solution)/shard_map/ppermute | solution.py:493
  41.9 0.2 coulomb.1
  42.1 3.8 %collective-permute-start.7 = (f32[16,64]{1,0:T(8,128)S(1)}, f32[16,64]{1,0:T(8,128)S(1)}, u32[]{:S(2)}, u32[]{:S(2)}) collective-permute-start(f32[16,64]{1,0:T(8,128)S(1)} %coulomb.1), channel_id=1, source_target_pairs={{0,3},{1,2},{2,1},{3,0},{4,7},{5,6},{6,5},{7,4},{8,11},{9,10},{10,... | collective-permute-start | bytes 12296 | tf_op jit(solution)/shard_map/ppermute | solution.py:382
  46.0 0.6 %collective-permute-start.5 = (f32[16,64]{1,0:T(8,128)S(1)}, f32[16,64]{1,0:T(8,128)S(1)}, u32[]{:S(2)}, u32[]{:S(2)}) collective-permute-start(f32[16,64]{1,0:T(8,128)S(1)} %coulomb.1), channel_id=1, source_target_pairs={{0,1},{1,0},{2,3},{3,2},{4,5},{5,4},{6,7},{7,6},{8,9},{9,8},{10,11... | collective-permute-start | bytes 12296 | tf_op jit(solution)/shard_map/ppermute | solution.py:382
  46.6 1.5 %own_active.1 = f32[64,16,64]{2,1,0:T(8,128)} custom-call(s32[2]{0:T(128)S(1)} %pad_add_fusion.where, f32[512,128]{1,0:T(8,128)S(1)} %get-tuple-element.48.act, bf16[464,128]{1,0:T(8,128)(2,1)S(1)} %collective-permute-done.4.far), custom_call_target="tpu_custom_call" | custom-call | flops 1000000 | bytes 1000000 | tf_op jit(solution)/shard_map/own_active/pallas_call | solution.py:502
  48.1 2.4 %collective-permute-done.6 = f32[16,64]{1,0:T(8,128)S(1)} collective-permute-done((f32[16,64]{1,0:T(8,128)S(1)}, f32[16,64]{1,0:T(8,128)S(1)}, u32[]{:S(2)}, u32[]{:S(2)}) %collective-permute-start.6) | collective-permute-done | bytes 4128 | tf_op jit(solution)/shard_map/ppermute | solution.py:382
  50.5 0.0 collective-permute-done.5
  50.5 0.6 %add_add_fusion = f32[16,64]{1,0:T(8,128)} fusion(f32[16,64]{1,0:T(8,128)S(1)} %copy-done, f32[16,64]{1,0:T(8,128)S(1)} %collective-permute-done.6, f32[16,64]{1,0:T(8,128)S(1)} %collective-permute-done.7, f32[16,64]{1,0:T(8,128)S(1)} %coulomb.1, f32[16,64]{1,0:T(8,128)S(1)} %collective-permute-done.5), kind=kLoop, calls=%fused_computation.2 | loop fusion | flops 4096 | bytes 24576 | tf_op jit(solution)/shard_map/add | solution.py:511
  (6 shorter events, 0.0 us)
Async XLA Ops:
  10.2 7.0 %collective-permute-start = (bf16[1296,128]{1,0:T(8,128)(2,1)S(1)}, bf16[1296,128]{1,0:T(8,128)(2,1)S(1)}, u32[]{:S(2)}, u32[]{:S(2)}) collective-permute-start(bf16[1296,128]{1,0:T(8,128)(2,1)S(1)} %get-tuple-element.32), channel_id=1, source_target_pairs={{0,4},{4,0},{8,12},{12,8},{1,5},{5,1},{9,13},{13,9},{2,6},{6,2},{1... | collective-permute-start | bytes 995336 | tf_op jit(solution)/shard_map/ppermute | solution.py:427
  17.3 10.3 %collective-permute-start.1 = (bf16[1152,128]{1,0:T(8,128)(2,1)S(1)}, bf16[1152,128]{1,0:T(8,128)(2,1)S(1)}, u32[]{:S(2)}, u32[]{:S(2)}) collective-permute-start(bf16[1152,128]{1,0:T(8,128)(2,1)S(1)} %fusion), channel_id=1, source_target_pairs={{0,8},{8,0},{4,12},{12,4},{1,9},{9,1},{5,13},{13,5},{2,10},{10,2},... | collective-permute-start | bytes 884744 | tf_op jit(solution)/shard_map/ppermute | solution.py:443
  26.4 24.1 %copy-start = (f32[16,64]{1,0:T(8,128)S(1)}, f32[16,64]{1,0:T(8,128)}, u32[]{:S(2)}) copy-start(f32[16,64]{1,0:T(8,128)} %param.11) | copy-start | bytes 12292
  26.4 7.7 %collective-permute-start.2 = (bf16[1568,128]{1,0:T(8,128)(2,1)S(1)}, bf16[1568,128]{1,0:T(8,128)(2,1)S(1)}, u32[]{:S(2)}, u32[]{:S(2)}) collective-permute-start(bf16[1568,128]{1,0:T(8,128)(2,1)S(1)} %get-tuple-element.44), channel_id=1, source_target_pairs={{0,4},{4,0},{8,12},{12,8},{1,5},{5,1},{9,13},{13,9},{2,6},{6,2},{1... | collective-permute-start | bytes 1204232 | tf_op jit(solution)/shard_map/ppermute | solution.py:454
  35.1 1.3 %collective-permute-start.3 = (bf16[304,128]{1,0:T(8,128)(2,1)S(1)}, bf16[304,128]{1,0:T(8,128)(2,1)S(1)}, u32[]{:S(2)}, u32[]{:S(2)}) collective-permute-start(bf16[304,128]{1,0:T(8,128)(2,1)S(1)} %get-tuple-element.47), channel_id=1, source_target_pairs={{0,4},{4,0},{8,12},{12,8},{1,5},{5,1},{9,13},{13,9},{2,6},{6,2},{1... | collective-permute-start | bytes 233480 | tf_op jit(solution)/shard_map/ppermute | solution.py:479
  36.6 5.4 %collective-permute-start.4 = (bf16[464,128]{1,0:T(8,128)(2,1)S(1)}, bf16[464,128]{1,0:T(8,128)(2,1)S(1)}, u32[]{:S(2)}, u32[]{:S(2)}) collective-permute-start(bf16[464,128]{1,0:T(8,128)(2,1)S(1)} %get-tuple-element.49), channel_id=1, source_target_pairs={{0,8},{8,0},{4,12},{12,4},{1,9},{9,1},{5,13},{13,5},{2,10},{10,2},... | collective-permute-start | bytes 356360 | tf_op jit(solution)/shard_map/ppermute | solution.py:493
  42.1 6.0 %collective-permute-start.7 = (f32[16,64]{1,0:T(8,128)S(1)}, f32[16,64]{1,0:T(8,128)S(1)}, u32[]{:S(2)}, u32[]{:S(2)}) collective-permute-start(f32[16,64]{1,0:T(8,128)S(1)} %coulomb.1), channel_id=1, source_target_pairs={{0,3},{1,2},{2,1},{3,0},{4,7},{5,6},{6,5},{7,4},{8,11},{9,10},{10,... | collective-permute-start | bytes 12296 | tf_op jit(solution)/shard_map/ppermute | solution.py:382
  46.0 4.5 %collective-permute-start.6 = (f32[16,64]{1,0:T(8,128)S(1)}, f32[16,64]{1,0:T(8,128)S(1)}, u32[]{:S(2)}, u32[]{:S(2)}) collective-permute-start(f32[16,64]{1,0:T(8,128)S(1)} %coulomb.1), channel_id=1, source_target_pairs={{0,2},{1,3},{2,0},{3,1},{4,6},{5,7},{6,4},{7,5},{8,10},{9,11},{10,... | collective-permute-start | bytes 12296 | tf_op jit(solution)/shard_map/ppermute | solution.py:382
  46.0 4.5 %collective-permute-start.5 = (f32[16,64]{1,0:T(8,128)S(1)}, f32[16,64]{1,0:T(8,128)S(1)}, u32[]{:S(2)}, u32[]{:S(2)}) collective-permute-start(f32[16,64]{1,0:T(8,128)S(1)} %coulomb.1), channel_id=1, source_target_pairs={{0,1},{1,0},{2,3},{3,2},{4,5},{5,4},{6,7},{7,6},{8,9},{9,8},{10,11... | collective-permute-start | bytes 12296 | tf_op jit(solution)/shard_map/ppermute | solution.py:382

commit v6 on v5

--- a/solution.py
+++ b/solution.py
@@ -21,50 +21,35 @@
     return lax.broadcasted_iota(jnp.int32, (rows, LANES), 1) < BS
 
 
-def orbital_blocks(blocks, live, slabs, windows, lt_ref, r_ref):
-    first = low_half(NCOL)
-
-    def window(n, slot, upper):
-        w = windows[n].astype(F32)
+def orbital_pair(k, blocks, first_window, live, windows):
+    halves = []
+    for n in range(2):
+        slot = 2 * k + n
+        w = windows[first_window + slot]
         w = jnp.concatenate([w[NACT:], w[:NACT]], axis=0)
-        moved = lax.rem(blocks[n], 2) != (1 if upper else 0)
-        w = jnp.where(moved, pltpu.roll(w, BS, 1), w)
-        return jnp.where(slot < live, w, 0.0)
-
-    for k in range(slabs // 2):
-        a, b = 2 * k, 2 * k + 1
-        left = jnp.where(first, window(a, a, False), window(b, b, True))
-        lt_ref[k] = left.astype(BF)
-        right = jnp.where(first, window(slabs + a, a, False), window(slabs + b, b, True))
-        right = jnp.concatenate([right, right[NIN:]], axis=0)
-        r_ref[pl.ds(k * PAIRED, PAIRED), :] = right.T.astype(BF)
-
-
-def slab_copy(slabs_ref, sbuf, sem, block, k):
-    last = slabs_ref.shape[0] // 2 - 1
-    pair = min(k, last) if isinstance(k, int) else jnp.minimum(k, last)
-    return pltpu.make_async_copy(
-        slabs_ref.at[pl.ds(2 * pair, 2), pl.ds(pl.multiple_of(block * NBQ, NBQ), NBQ), :],
-        sbuf.at[k],
-        sem.at[k],
-    )
-
-
-def start_slabs(slabs_ref, sbuf, sem, block):
-    for k in range(slabs_ref.shape[0] // 2 + 1):
-        slab_copy(slabs_ref, sbuf, sem, block, k).start()
-
-
-def run_block(slabs_ref, block, lt_ref, r_ref, scratch, emit, prepare=None):
-    sbuf, even_ref, odd_ref, half_ref, diag, sem = scratch
-    pairs = slabs_ref.shape[0] // 2
+        w = jnp.where(lax.rem(blocks[slot], 2) != n, pltpu.roll(w, BS, 1), w)
+        halves.append(jnp.where(slot < live, w, jnp.zeros_like(w)))
+    return jnp.where(low_half(NCOL), halves[0], halves[1])
+
+
+def slab_copies(slabs_ref, sbuf, sem, block):
+    return [
+        pltpu.make_async_copy(
+            slabs_ref.at[pl.ds(2 * k, 2), pl.ds(pl.multiple_of(block * NBQ, NBQ), NBQ), :],
+            sbuf.at[k],
+            sem.at[k],
+        )
+        for k in range(slabs_ref.shape[0] // 2)
+    ]
+
+
+def run_block(sbuf, lt_ref, r_ref, scratch, emit, prepare=None, beside=None):
+    even_ref, odd_ref, half_ref, diag = scratch
+    pairs = sbuf.shape[0]
     first = low_half(NBQ)
     first_s = low_half(BS)
     zero = jnp.zeros((BS, LANES), BF)
     wide, group = NBQ, 4
-
-    def wait(k):
-        slab_copy(slabs_ref, sbuf, sem, block, k).wait()
 
     def relayout(k, out):
         for j in range(sbuf.shape[3] // LANES):
@@ -96,12 +81,12 @@
                 half_ref[q + u, :, at] = half[:, u * LANES : (u + 1) * LANES]
 
     def two_pairs(i, carry):
-        wait(2 * i + 1)
-        wait(2 * i + 2)
         relayout(2 * i + 1, odd_ref)
         half_transform(2 * i, even_ref)
-        relayout(2 * i + 2, even_ref)
+        relayout(jnp.minimum(2 * i + 2, pairs - 1), even_ref)
         half_transform(2 * i + 1, odd_ref)
+        if beside is not None:
+            beside(i)
         return carry
 
     def second_transform(g):
@@ -130,7 +115,6 @@
                     jnp.where(eye, w[:NIN, :NIN], 0.0), axis=0, keepdims=True
                 )
 
-    wait(0)
     relayout(0, even_ref)
     if prepare is not None:
         prepare()
@@ -177,95 +161,115 @@
 
 
 def first_kernel(
-    where, rows_ref, cols_ref, live, slabs_ref, ot_ref, lt_out, r_out, msg, keep, dens,
-    rows, cols, ssem, windows, wsem, *scratch
+    where, rows_ref, cols_ref, live, slabs_ref, ot_ref, lt_out, r_out, msg, keep, dens, after,
+    rows, cols, ssem, windows, wsem, sbuf, bsem, sem, *scratch
 ):
     slabs = slabs_ref.shape[0]
+    pairs = slabs // 2
     core, x = where[0], where[1]
-    block = 2 * (1 - x) + (1 - core)
-    sbuf, sem, diag = scratch[0], scratch[5], scratch[4]
     small = [
         pltpu.make_async_copy(src, dst, ssem.at[n])
         for n, (src, dst) in enumerate(((rows_ref, rows), (cols_ref, cols)))
     ]
     for copy in small:
         copy.start()
-    start_slabs(slabs_ref, sbuf, sem, block)
+    now = slab_copies(slabs_ref, sbuf, bsem, 2 * (1 - x) + (1 - core))
+    for copy in now:
+        copy.start()
     for copy in small:
         copy.wait()
-    blocks = [rows[n] for n in range(slabs)] + [cols[n] for n in range(slabs)]
     copies = []
-    for n, blk in enumerate(blocks):
+    for n in range(2 * slabs):
+        blk = rows[n] if n < slabs else cols[n - slabs]
         base = pl.multiple_of((blk // 2) * PAIRED, PAIRED)
         copies.append(
             pltpu.make_async_copy(ot_ref.at[:, pl.ds(base, PAIRED)], windows.at[n], wsem.at[n])
         )
         copies[-1].start()
+    ahead = slab_copies(slabs_ref, after, sem, 2 * (1 - x) + core)
+    for copy in ahead:
+        copy.start()
+    now[0].wait()
+
+    def left(k):
+        lt_out[k] = orbital_pair(k, rows, 0, live[0], windows)
 
     def prepare():
-        for copy in copies:
+        for copy in copies + now[1:]:
             copy.wait()
-        orbital_blocks(blocks, live[0], slabs, windows, lt_out, r_out)
+        left(0)
+        left(1)
+
+    def beside(i):
+        for k in (2 * i, 2 * i + 1):
+            right = orbital_pair(k, cols, slabs, live[0], windows).astype(F32)
+            right = jnp.concatenate([right, right[NIN:]], axis=0)
+            r_out[pl.ds(pl.multiple_of(k * PAIRED, PAIRED), PAIRED), :] = right.T.astype(BF)
+            left(jnp.minimum(k + 2, pairs - 1))
 
     def emit(h, in0, in1, act):
         msg[pair_rows(h, 0), :] = in0.astype(BF)
         msg[pair_rows(h, 1), :] = in1.astype(BF)
         emit_active(h, act, core, x, msg, keep, INROWS)
 
-    run_block(slabs_ref, block, lt_out, r_out, scratch, emit, prepare)
-    dens[...] = density_of(diag[...])
+    run_block(sbuf, lt_out, r_out, scratch, emit, prepare, beside)
+    dens[...] = density_of(scratch[3][...])
     msg[pl.ds(INROWS + 2 * PER, NBQ), :] = split_wire(dens[...])
+    for copy in ahead:
+        copy.wait()
 
 
 def second_kernel(
-    where, slabs_ref, lt_ref, r_ref, keep_in, send, keep, dens, *scratch
+    where, slabs_ref, sbuf, lt_ref, r_ref, keep_in, send, keep, dens, after, sem, *scratch
 ):
     core, x = where[0], where[1]
-    block = 2 * (1 - x) + core
-    start_slabs(slabs_ref, scratch[0], scratch[5], block)
+    ahead = slab_copies(slabs_ref, after, sem, 2 * x + (1 - core))
+    for copy in ahead:
+        copy.start()
 
     def emit(h, in0, in1, act):
         keep_in[pair_rows(h, 0), :] = in0
         keep_in[pair_rows(h, 1), :] = in1
         emit_active(h, act, core, x, send, keep, 0)
 
-    run_block(slabs_ref, block, lt_ref, r_ref, scratch, emit)
-    dens[...] = density_of(scratch[4][...])
+    run_block(sbuf, lt_ref, r_ref, scratch, emit)
+    dens[...] = density_of(scratch[3][...])
+    for copy in ahead:
+        copy.wait()
 
 
 def third_kernel(
-    where, slabs_ref, lt_ref, r_ref, send2, dens2, msg, keep, dens, *scratch
+    where, slabs_ref, sbuf, lt_ref, r_ref, send2, dens2, msg, keep, dens, after, sem, *scratch
 ):
     core, x = where[0], where[1]
-    block = 2 * x + (1 - core)
-    start_slabs(slabs_ref, scratch[0], scratch[5], block)
+    ahead = slab_copies(slabs_ref, after, sem, 2 * x + core)
+    for copy in ahead:
+        copy.start()
 
     def emit(h, in0, in1, act):
         msg[pair_rows(h, 0), :] = in0.astype(BF)
         msg[pair_rows(h, 1), :] = in1.astype(BF)
         emit_active(h, act, core, x, msg, keep, INROWS)
 
-    run_block(slabs_ref, block, lt_ref, r_ref, scratch, emit)
+    run_block(sbuf, lt_ref, r_ref, scratch, emit)
     msg[pl.ds(INROWS + 2 * PER, 2 * PER), :] = send2[...]
-    dens[...] = density_of(scratch[4][...])
+    dens[...] = density_of(scratch[3][...])
     msg[pl.ds(INROWS + 4 * PER, NBQ), :] = split_wire(dens[...])
     msg[pl.ds(INROWS + 4 * PER + NBQ, NBQ), :] = split_wire(dens2[...])
-
-
-def fourth_kernel(
-    where, slabs_ref, lt_ref, r_ref, far1, msg, keep_in, keep, dens, *scratch
-):
+    for copy in ahead:
+        copy.wait()
+
+
+def fourth_kernel(where, sbuf, lt_ref, r_ref, far1, msg, keep_in, keep, dens, *scratch):
     core, x = where[0], where[1]
-    block = 2 * x + core
-    start_slabs(slabs_ref, scratch[0], scratch[5], block)
 
     def emit(h, in0, in1, act):
         for n, v in enumerate((in0, in1)):
             keep_in[pair_rows(h, n), :] = v + far1[pair_rows(h, n), :].astype(F32)
         emit_active(h, act, core, x, msg, keep, 0)
 
-    run_block(slabs_ref, block, lt_ref, r_ref, scratch, emit)
-    dens[...] = density_of(scratch[4][...])
+    run_block(sbuf, lt_ref, r_ref, scratch, emit)
+    dens[...] = density_of(scratch[3][...])
     msg[pl.ds(2 * PER, NBQ), :] = split_wire(dens[...])
 
 
@@ -275,13 +279,8 @@
         rows = pl.ds(q * NACT, NACT)
         parts.append(mine[rows, :] + near3[rows, :].astype(F32))
     v = jnp.concatenate(parts, axis=1)
-    hi = v.astype(BF)
-    lo = (v - hi.astype(F32)).astype(BF)
-    both = lax.dot_general(
-        jnp.concatenate([hi, lo], axis=0), hi, (((1,), (1,)), ((), ())),
-        preferred_element_type=F32,
-    )
-    total = both[:NACT] + both[NACT:] + both[NACT:].T
+    v = v.astype(BF)
+    total = lax.dot_general(v, v, (((1,), (1,)), ((), ())), preferred_element_type=F32)
     whole[...] = jnp.concatenate([total, total], axis=1)
     core, x = where[0], where[1]
     size = msg4.shape[0]
@@ -378,10 +377,10 @@
     n = lax.axis_size("aux")
     if n != 4:
         return lax.psum(part, "aux")
-    one, two, three = (
-        lax.ppermute(part, "aux", [(z, z ^ k) for z in range(n)]) for k in (1, 2, 3)
-    )
-    return (part + one) + (two + three)
+    three, two, one = (
+        lax.ppermute(part, "aux", [(z, z ^ k) for z in range(n)]) for k in (3, 2, 1)
+    )
+    return (three + two) + (one + part)
 
 
 def paired_body(slabs, block_row, block_col, live_count, orbitals, hcore):
@@ -391,32 +390,34 @@
     swap_core = [(0, 1), (1, 0), (2, 3), (3, 2)]
     swap_x = [(0, 2), (2, 0), (1, 3), (3, 1)]
     aos = nslab * BS
+    loaded = shape((nslab // 2, 2, NBQ, width), BF)
+    copies = pltpu.SemaphoreType.DMA((nslab // 2,))
     scratch = [
-        pltpu.VMEM((nslab // 2 + 1, 2, NBQ, width), BF),
         pltpu.VMEM((MSTEP * BS, LANES), F32),
         pltpu.VMEM((MSTEP * BS, LANES), F32),
         pltpu.VMEM((NBQ, NCOL, aos), BF),
         pltpu.VMEM((NBQ, LANES), F32),
-        pltpu.SemaphoreType.DMA((nslab // 2 + 1,)),
     ]
     cost = pl.CostEstimate(flops=6 * 10**9, bytes_accessed=10**7, transcendentals=0)
     keep, dens = shape((2 * PER, LANES), F32), shape((NBQ, LANES), F32)
-    lt, r, msg1, keep1, dens1 = pl.pallas_call(
+    lt, r, msg1, keep1, dens1, slabs2 = pl.pallas_call(
         first_kernel,
         name="slabs_first",
         in_specs=[SM, HB, HB, SM, HB, HB],
-        out_specs=[VM] * 5,
+        out_specs=[VM] * 6,
         out_shape=(
             shape((nslab // 2, NCOL, PAIRED), BF),
             shape((aos, 2 * LANES), BF),
             shape((INROWS + 2 * PER + NBQ, LANES), BF),
             keep,
             dens,
+            loaded,
         ),
         scratch_shapes=[
             pltpu.SMEM((nslab,), jnp.int32), pltpu.SMEM((nslab,), jnp.int32),
             pltpu.SemaphoreType.DMA((2,)),
             pltpu.VMEM((2 * nslab, NCOL, PAIRED), BF), pltpu.SemaphoreType.DMA((2 * nslab,)),
+            pltpu.VMEM(loaded.shape, BF), copies, copies,
         ] + scratch,
         compiler_params=PARAMS,
         cost_estimate=cost,
@@ -425,37 +426,37 @@
         in_hbm(orbitals.T),
     )
     near1 = lax.ppermute(msg1, "pair", swap_core)
-    keep_in2, send2, keep2, dens2 = pl.pallas_call(
+    keep_in2, send2, keep2, dens2, slabs3 = pl.pallas_call(
         second_kernel,
         name="slabs_second",
-        in_specs=[SM, HB, VM, VM],
-        out_specs=[VM] * 4,
+        in_specs=[SM, HB] + [VM] * 3,
+        out_specs=[VM] * 5,
         out_shape=(
-            shape((INROWS, LANES), F32), shape((2 * PER, LANES), BF), keep, dens,
+            shape((INROWS, LANES), F32), shape((2 * PER, LANES), BF), keep, dens, loaded,
         ),
-        scratch_shapes=scratch,
+        scratch_shapes=[copies] + scratch,
         compiler_params=PARAMS,
         cost_estimate=cost,
-    )(where, slabs, lt, r)
+    )(where, slabs, slabs2, lt, r)
     out2 = jnp.concatenate([keep_in2, keep2[:PER]], axis=0)
     out2 = (out2 + near1[: INROWS + PER].astype(F32)).astype(BF)
     out2, lt, r = lax.optimization_barrier((out2, lt, r))
     far1 = lax.ppermute(out2, "pair", swap_x)
-    msg3, keep3, dens3 = pl.pallas_call(
+    msg3, keep3, dens3, slabs4 = pl.pallas_call(
         third_kernel,
         name="slabs_third",
-        in_specs=[SM, HB] + [VM] * 4,
-        out_specs=[VM] * 3,
-        out_shape=(shape((INROWS + 4 * PER + 2 * NBQ, LANES), BF), keep, dens),
-        scratch_shapes=scratch,
+        in_specs=[SM, HB] + [VM] * 5,
+        out_specs=[VM] * 4,
+        out_shape=(shape((INROWS + 4 * PER + 2 * NBQ, LANES), BF), keep, dens, loaded),
+        scratch_shapes=[copies] + scratch,
         compiler_params=PARAMS,
         cost_estimate=cost,
-    )(where, slabs, lt, r, send2, dens2)
+    )(where, slabs, slabs3, lt, r, send2, dens2)
     near3 = lax.ppermute(msg3, "pair", swap_core)
     msg4, keep_in4, keep4, dens4 = pl.pallas_call(
         fourth_kernel,
         name="slabs_fourth",
-        in_specs=[SM, HB] + [VM] * 3,
+        in_specs=[SM] + [VM] * 4,
         out_specs=[VM] * 4,
         out_shape=(
             shape((2 * PER + NBQ, LANES), BF), shape((INROWS, LANES), F32), keep, dens,
@@ -463,7 +464,7 @@
         scratch_shapes=scratch,
         compiler_params=PARAMS,
         cost_estimate=cost,
-    )(where, slabs, lt, r, far1)
+    )(where, slabs4, lt, r, far1)
     msg4, exch = pl.pallas_call(
         exchange_kernel,
         name="exchange",
@@ -508,7 +509,7 @@
         compiler_params=PARAMS,
         cost_estimate=pl.CostEstimate(flops=10**6, bytes_accessed=10**6, transcendentals=0),
     )(where, act, far5)
-    return (active, hcore + sum_over_aux(partial))
+    return (active, sum_over_aux(partial) + hcore)
 
 
 def slab_terms(values, left, right):

time: 51.4 us -> 50.5 us (0.982)
  Pallas kernels: 31.1 us -> 27.9 us
  waiting for transfers between devices: 8.14 us -> 10.7 us
    pallas_call x2, Pallas kernels: 13 us -> 10.9 us  [the longest x1 5.49 us: paired_body(): pl.pallas_call(second_kernel, name='slabs_second', in_specs=[SM, HB] + [V...]
    ppermute x3, waiting for transfers between devices: 2.43 us -> 3.97 us  [sum_over_aux(): lax.ppermute(part, 'aux', [(z, z ^ k) for z in range(n)])]
    pallas_call x1, Pallas kernels: 6.5 us -> 5.51 us  [paired_body(): pl.pallas_call(third_kernel, name='slabs_third', in_specs=[SM, HB] + [VM]...]
    ppermute x1, waiting for transfers between devices: 0.89 us -> 1.87 us  [paired_body(): far1 = lax.ppermute(out2, 'pair', swap_x)]
  transfers between devices with their start and end apart: 8 -> 8, of which waited for: 4 -> 5; matrix products, arithmetic and copies ran while one was open for 0% -> 0% of each run, Pallas kernels for 41% -> 36%
where the time goes in v6:
time: 50.5 us; the launch traced here: 50.3 us
  Pallas kernels  27.9 us (55%)
  waiting for transfers between devices  10.7 us (21%)
  starting transfers between devices  9.66 us (19%)
  between operations  1.37 us (3%)
  other arithmetic  0.75 us (1%)
    pallas_call x1, Pallas kernels, paired_body(): pl.pallas_call(first_kernel, name='slabs_first', in_specs=[SM, HB, HB, SM...  8.84 us
    pallas_call x1, Pallas kernels, paired_body(): pl.pallas_call(third_kernel, name='slabs_third', in_specs=[SM, HB] + [VM]...  5.51 us
    pallas_call x1, Pallas kernels, paired_body(): pl.pallas_call(second_kernel, name='slabs_second', in_specs=[SM, HB] + [V...  5.49 us
    pallas_call x1, Pallas kernels, paired_body(): pl.pallas_call(fourth_kernel, name='slabs_fourth', in_specs=[SM] + [VM] *...  5.41 us
    ppermute x3, starting transfers between devices, sum_over_aux(): lax.ppermute(part, 'aux', [(z, z ^ k) for z in range(n)])  4.41 us
    ppermute x3, waiting for transfers between devices, sum_over_aux(): lax.ppermute(part, 'aux', [(z, z ^ k) for z in range(n)])  3.97 us
    ppermute x1, waiting for transfers between devices, paired_body(): far5 = lax.ppermute(msg5, 'pair', swap_x)  3.55 us
    ppermute x1, starting transfers between devices, paired_body(): far1 = lax.ppermute(out2, 'pair', swap_x)  2.58 us
  transfers between devices with their start and end apart: 8, of which 5 were waited for; matrix products, arithmetic and copies ran while one was open for 0% of the time, Pallas kernels for 36%

profile of v6, /device:TPU:0, one launch (start us, length us, event | category | flops | bytes accessed | tf_op | source)
XLA Modules:
  0.0 50.3 jit_solution(15783431726880797704)
XLA Ops:
  1.3 0.1 pad_add_fusion.where
  1.4 8.8 %slabs_first.1 = (bf16[8,192,128]{2,1,0:T(8,128)(2,1)S(1)}, bf16[1024,256]{1,0:T(8,128)(2,1)S(1)}, bf16[1296,128]{1,0:T(8,128)(2,1)S(1)}, f32[256,128]{1,0:T(8,1...) custom-call(s32[2]{0:T(128)S(1)} %pad_add_fusion.where, s32[16]{0:T(128)} %rows_ref.1, s32[16]{0:T(128)} %cols_ref.1, ...), custom_call_target="tpu_custom_call" | custom-call | flops 6000000000 | bytes 10000000 | tf_op jit(solution)/shard_map/slabs_first/pallas_call | solution.py:403
  10.2 0.5 collective-permute-start
  10.7 5.5 %slabs_second.1 = (f32[1024,128]{1,0:T(8,128)S(1)}, bf16[256,128]{1,0:T(8,128)(2,1)S(1)}, f32[256,128]{1,0:T(8,128)S(1)}, f32[16,128]{1,0:T(8,128)S(1)}, bf16[8,2,16,4096]{3,2,1,0:T(8,128)(2,1)S(1)}) custom-call(s32[2]{0:T(128)S(1)} %pad_add_fusion.where, bf16[16,64,4096]{2,1,0:T(8,128)(2,1)} %slabs_ref.5, ...), custom_call_target="tpu_custom_call" | custom-call | flops 6000000000 | bytes 10000000 | tf_op jit(solution)/shard_map/slabs_second/pallas_call | solution.py:429
  16.2 0.1 fusion
  16.3 2.6 %collective-permute-start.1 = (bf16[1152,128]{1,0:T(8,128)(2,1)S(1)}, bf16[1152,128]{1,0:T(8,128)(2,1)S(1)}, u32[]{:S(2)}, u32[]{:S(2)}) collective-permute-start(bf16[1152,128]{1,0:T(8,128)(2,1)S(1)} %fusion), channel_id=1, source_target_pairs={{0,8},{8,0},{4,12},{12,4},{1,9},{9,1},{5,13},{13,5},{2,10},{10,2},... | collective-permute-start | bytes 884744 | tf_op jit(solution)/shard_map/ppermute | solution.py:444
  18.9 5.5 %slabs_third.1 = (bf16[1568,128]{1,0:T(8,128)(2,1)S(1)}, f32[256,128]{1,0:T(8,128)S(1)}, f32[16,128]{1,0:T(8,128)S(1)}, bf16[8,2,16,4096]{3,2,1,0:T(8,128)(2,1)S(1)}) custom-call(s32[2]{0:T(128)S(1)} %pad_add_fusion.where, bf16[16,64,4096]{2,1,0:T(8,128)(2,1)} %slabs_ref.5, bf16[8,2,16,4096]{3,2,1,0:T(8,128)(2,1)S(1)} %get-tuple-element.35.sbuf, ...), custom_call_target="tpu_custom_call" | custom-call | flops 6000000000 | bytes 10000000 | tf_op jit(solution)/shard_map/slabs_third/pallas_call | solution.py:445
  24.4 0.3 collective-permute-start.2
  24.7 1.9 %collective-permute-done.1.far1 = bf16[1152,128]{1,0:T(8,128)(2,1)S(1)} collective-permute-done((bf16[1152,128]{1,0:T(8,128)(2,1)S(1)}, bf16[1152,128]{1,0:T(8,128)(2,1)S(1)}, u32[]{:S(2)}, u32[]{:S(2)}) %collective-permute-start.1) | collective-permute-done | bytes 294944 | tf_op jit(solution)/shard_map/ppermute | solution.py:444
  26.5 5.4 %slabs_fourth.1 = (bf16[272,128]{1,0:T(8,128)(2,1)S(1)}, f32[1024,128]{1,0:T(8,128)S(1)}, f32[256,128]{1,0:T(8,128)S(1)}, f32[16,128]{1,0:T(8,128)S(1)}) custom-call(s32[2]{0:T(128)S(1)} %pad_add_fusion.where, bf16[8,2,16,4096]{3,2,1,0:T(8,128)(2,1)S(1)} %get-tuple-element.43.sbuf, bf16[8,192,128]{2,1,0:T(8,128)(2,1)S(1)} %get-tuple-element.38.lt_ref, ...), custom_call_target="tpu_custom_call" | custom-call | flops 6000000000 | bytes 10000000 | tf_op jit(solution)/shard_map/slabs_fourth/pallas_call | solution.py:456
  32.0 0.0 copy-start
  32.0 0.8 %exchange.1 = (bf16[304,128]{1,0:T(8,128)(2,1)S(1)}, f32[32,128]{1,0:T(8,128)S(1)}) custom-call(s32[2]{0:T(128)S(1)} %pad_add_fusion.where, f32[1024,128]{1,0:T(8,128)S(1)} %get-tuple-element.49.mine, bf16[1568,128]{1,0:T(8,128)(2,1)S(1)} %collective-permute-done.2.near3, bf16[272,128]{1,0:T(8,128)(2,1)S(1)} %get-tuple-element.51.msg4), custom_call_target="tpu_custom_call" | custom-call | tf_op jit(solution)/shard_map/exchange/pallas_call | solution.py:468
  32.8 0.1 collective-permute-start.3
  32.9 1.3 %collective-permute-done.3.near4 = bf16[304,128]{1,0:T(8,128)(2,1)S(1)} collective-permute-done((bf16[304,128]{1,0:T(8,128)(2,1)S(1)}, bf16[304,128]{1,0:T(8,128)(2,1)S(1)}, u32[]{:S(2)}, u32[]{:S(2)}) %collective-permute-start.3) | collective-permute-done | bytes 77856 | tf_op jit(solution)/shard_map/ppermute | solution.py:480
  34.2 0.1 active_of_chip.1
  34.3 1.8 %collective-permute-start.4 = (bf16[464,128]{1,0:T(8,128)(2,1)S(1)}, bf16[464,128]{1,0:T(8,128)(2,1)S(1)}, u32[]{:S(2)}, u32[]{:S(2)}) collective-permute-start(bf16[464,128]{1,0:T(8,128)(2,1)S(1)} %get-tuple-element.55), channel_id=1, source_target_pairs={{0,8},{8,0},{4,12},{12,4},{1,9},{9,1},{5,13},{13,5},{2,10},{10,2},... | collective-permute-start | bytes 356360 | tf_op jit(solution)/shard_map/ppermute | solution.py:494
  36.1 3.6 %collective-permute-done.4.far = bf16[464,128]{1,0:T(8,128)(2,1)S(1)} collective-permute-done((bf16[464,128]{1,0:T(8,128)(2,1)S(1)}, bf16[464,128]{1,0:T(8,128)(2,1)S(1)}, u32[]{:S(2)}, u32[]{:S(2)}) %collective-permute-start.4) | collective-permute-done | bytes 118816 | tf_op jit(solution)/shard_map/ppermute | solution.py:494
  39.7 0.2 coulomb.1
  39.9 1.8 %collective-permute-start.7 = (f32[16,64]{1,0:T(8,128)S(1)}, f32[16,64]{1,0:T(8,128)S(1)}, u32[]{:S(2)}, u32[]{:S(2)}) collective-permute-start(f32[16,64]{1,0:T(8,128)S(1)} %coulomb.1), channel_id=1, source_target_pairs={{0,1},{1,0},{2,3},{3,2},{4,5},{5,4},{6,7},{7,6},{8,9},{9,8},{10,11... | collective-permute-start | bytes 12296 | tf_op jit(solution)/shard_map/ppermute | solution.py:381
  41.7 2.6 %collective-permute-start.6 = (f32[16,64]{1,0:T(8,128)S(1)}, f32[16,64]{1,0:T(8,128)S(1)}, u32[]{:S(2)}, u32[]{:S(2)}) collective-permute-start(f32[16,64]{1,0:T(8,128)S(1)} %coulomb.1), channel_id=1, source_target_pairs={{0,2},{1,3},{2,0},{3,1},{4,6},{5,7},{6,4},{7,5},{8,10},{9,11},{10,... | collective-permute-start | bytes 12296 | tf_op jit(solution)/shard_map/ppermute | solution.py:381
  44.3 1.5 %own_active.1 = f32[64,16,64]{2,1,0:T(8,128)} custom-call(s32[2]{0:T(128)S(1)} %pad_add_fusion.where, f32[512,128]{1,0:T(8,128)S(1)} %get-tuple-element.54.act, bf16[464,128]{1,0:T(8,128)(2,1)S(1)} %collective-permute-done.4.far), custom_call_target="tpu_custom_call" | custom-call | flops 1000000 | bytes 1000000 | tf_op jit(solution)/shard_map/own_active/pallas_call | solution.py:503
  45.8 0.5 collective-permute-done.6
  46.2 3.5 %collective-permute-done.5 = f32[16,64]{1,0:T(8,128)S(1)} collective-permute-done((f32[16,64]{1,0:T(8,128)S(1)}, f32[16,64]{1,0:T(8,128)S(1)}, u32[]{:S(2)}, u32[]{:S(2)}) %collective-permute-start.5) | collective-permute-done | bytes 4128 | tf_op jit(solution)/shard_map/ppermute | solution.py:381
  49.7 0.6 %add_add_fusion = f32[16,64]{1,0:T(8,128)} fusion(f32[16,64]{1,0:T(8,128)S(1)} %copy-done, f32[16,64]{1,0:T(8,128)S(1)} %collective-permute-done.7, f32[16,64]{1,0:T(8,128)S(1)} %coulomb.1, f32[16,64]{1,0:T(8,128)S(1)} %collective-permute-done.5, f32[16,64]{1,0:T(8,128)S(1)} %collective-permute-done.6), kind=kLoop, calls=%fused_computation.2 | loop fusion | flops 4096 | bytes 24576 | tf_op jit(solution)/shard_map/add | solution.py:512
  (6 shorter events, 0.0 us)
Async XLA Ops:
  10.2 6.0 %collective-permute-start = (bf16[1296,128]{1,0:T(8,128)(2,1)S(1)}, bf16[1296,128]{1,0:T(8,128)(2,1)S(1)}, u32[]{:S(2)}, u32[]{:S(2)}) collective-permute-start(bf16[1296,128]{1,0:T(8,128)(2,1)S(1)} %get-tuple-element.37), channel_id=1, source_target_pairs={{0,4},{4,0},{8,12},{12,8},{1,5},{5,1},{9,13},{13,9},{2,6},{6,2},{1... | collective-permute-start | bytes 995336 | tf_op jit(solution)/shard_map/ppermute | solution.py:428
  16.3 10.2 %collective-permute-start.1 = (bf16[1152,128]{1,0:T(8,128)(2,1)S(1)}, bf16[1152,128]{1,0:T(8,128)(2,1)S(1)}, u32[]{:S(2)}, u32[]{:S(2)}) collective-permute-start(bf16[1152,128]{1,0:T(8,128)(2,1)S(1)} %fusion), channel_id=1, source_target_pairs={{0,8},{8,0},{4,12},{12,4},{1,9},{9,1},{5,13},{13,5},{2,10},{10,2},... | collective-permute-start | bytes 884744 | tf_op jit(solution)/shard_map/ppermute | solution.py:444
  24.4 7.6 %collective-permute-start.2 = (bf16[1568,128]{1,0:T(8,128)(2,1)S(1)}, bf16[1568,128]{1,0:T(8,128)(2,1)S(1)}, u32[]{:S(2)}, u32[]{:S(2)}) collective-permute-start(bf16[1568,128]{1,0:T(8,128)(2,1)S(1)} %get-tuple-element.50), channel_id=1, source_target_pairs={{0,4},{4,0},{8,12},{12,8},{1,5},{5,1},{9,13},{13,9},{2,6},{6,2},{1... | collective-permute-start | bytes 1204232 | tf_op jit(solution)/shard_map/ppermute | solution.py:455
  32.0 17.8 %copy-start = (f32[16,64]{1,0:T(8,128)S(1)}, f32[16,64]{1,0:T(8,128)}, u32[]{:S(2)}) copy-start(f32[16,64]{1,0:T(8,128)} %param.11) | copy-start | bytes 12292
  32.8 1.3 %collective-permute-start.3 = (bf16[304,128]{1,0:T(8,128)(2,1)S(1)}, bf16[304,128]{1,0:T(8,128)(2,1)S(1)}, u32[]{:S(2)}, u32[]{:S(2)}) collective-permute-start(bf16[304,128]{1,0:T(8,128)(2,1)S(1)} %get-tuple-element.53), channel_id=1, source_target_pairs={{0,4},{4,0},{8,12},{12,8},{1,5},{5,1},{9,13},{13,9},{2,6},{6,2},{1... | collective-permute-start | bytes 233480 | tf_op jit(solution)/shard_map/ppermute | solution.py:480
  34.3 5.4 %collective-permute-start.4 = (bf16[464,128]{1,0:T(8,128)(2,1)S(1)}, bf16[464,128]{1,0:T(8,128)(2,1)S(1)}, u32[]{:S(2)}, u32[]{:S(2)}) collective-permute-start(bf16[464,128]{1,0:T(8,128)(2,1)S(1)} %get-tuple-element.55), channel_id=1, source_target_pairs={{0,8},{8,0},{4,12},{12,4},{1,9},{9,1},{5,13},{13,5},{2,10},{10,2},... | collective-permute-start | bytes 356360 | tf_op jit(solution)/shard_map/ppermute | solution.py:494
  39.9 5.9 %collective-permute-start.7 = (f32[16,64]{1,0:T(8,128)S(1)}, f32[16,64]{1,0:T(8,128)S(1)}, u32[]{:S(2)}, u32[]{:S(2)}) collective-permute-start(f32[16,64]{1,0:T(8,128)S(1)} %coulomb.1), channel_id=1, source_target_pairs={{0,1},{1,0},{2,3},{3,2},{4,5},{5,4},{6,7},{7,6},{8,9},{9,8},{10,11... | collective-permute-start | bytes 12296 | tf_op jit(solution)/shard_map/ppermute | solution.py:381
  41.7 4.5 %collective-permute-start.6 = (f32[16,64]{1,0:T(8,128)S(1)}, f32[16,64]{1,0:T(8,128)S(1)}, u32[]{:S(2)}, u32[]{:S(2)}) collective-permute-start(f32[16,64]{1,0:T(8,128)S(1)} %coulomb.1), channel_id=1, source_target_pairs={{0,2},{1,3},{2,0},{3,1},{4,6},{5,7},{6,4},{7,5},{8,10},{9,11},{10,... | collective-permute-start | bytes 12296 | tf_op jit(solution)/shard_map/ppermute | solution.py:381
  44.3 5.4 %collective-permute-start.5 = (f32[16,64]{1,0:T(8,128)S(1)}, f32[16,64]{1,0:T(8,128)S(1)}, u32[]{:S(2)}, u32[]{:S(2)}) collective-permute-start(f32[16,64]{1,0:T(8,128)S(1)} %coulomb.1), channel_id=1, source_target_pairs={{0,3},{1,2},{2,1},{3,0},{4,7},{5,6},{6,5},{7,4},{8,11},{9,10},{10,... | collective-permute-start | bytes 12296 | tf_op jit(solution)/shard_map/ppermute | solution.py:381

commit v7 on v6

--- a/solution.py
+++ b/solution.py
@@ -21,11 +21,12 @@
     return lax.broadcasted_iota(jnp.int32, (rows, LANES), 1) < BS
 
 
-def orbital_pair(k, blocks, first_window, live, windows):
+def orbital_pair(k, blocks, live, orbitals):
     halves = []
     for n in range(2):
         slot = 2 * k + n
-        w = windows[first_window + slot]
+        base = pl.multiple_of((blocks[slot] // 2) * PAIRED, PAIRED)
+        w = orbitals[:, pl.ds(base, PAIRED)]
         w = jnp.concatenate([w[NACT:], w[:NACT]], axis=0)
         w = jnp.where(lax.rem(blocks[slot], 2) != n, pltpu.roll(w, BS, 1), w)
         halves.append(jnp.where(slot < live, w, jnp.zeros_like(w)))
@@ -162,47 +163,36 @@
 
 def first_kernel(
     where, rows_ref, cols_ref, live, slabs_ref, ot_ref, lt_out, r_out, msg, keep, dens, after,
-    rows, cols, ssem, windows, wsem, sbuf, bsem, sem, *scratch
+    rows, cols, orbitals, ssem, sbuf, bsem, sem, *scratch
 ):
-    slabs = slabs_ref.shape[0]
-    pairs = slabs // 2
+    pairs = slabs_ref.shape[0] // 2
     core, x = where[0], where[1]
     small = [
         pltpu.make_async_copy(src, dst, ssem.at[n])
-        for n, (src, dst) in enumerate(((rows_ref, rows), (cols_ref, cols)))
+        for n, (src, dst) in enumerate(((rows_ref, rows), (cols_ref, cols), (ot_ref, orbitals)))
     ]
-    for copy in small:
+    now = slab_copies(slabs_ref, sbuf, bsem, 2 * (1 - x) + (1 - core))
+    for copy in [small[0], now[0], small[1], small[2]] + now[1:]:
         copy.start()
-    now = slab_copies(slabs_ref, sbuf, bsem, 2 * (1 - x) + (1 - core))
-    for copy in now:
-        copy.start()
-    for copy in small:
-        copy.wait()
-    copies = []
-    for n in range(2 * slabs):
-        blk = rows[n] if n < slabs else cols[n - slabs]
-        base = pl.multiple_of((blk // 2) * PAIRED, PAIRED)
-        copies.append(
-            pltpu.make_async_copy(ot_ref.at[:, pl.ds(base, PAIRED)], windows.at[n], wsem.at[n])
-        )
-        copies[-1].start()
     ahead = slab_copies(slabs_ref, after, sem, 2 * (1 - x) + core)
-    for copy in ahead:
-        copy.start()
     now[0].wait()
 
     def left(k):
-        lt_out[k] = orbital_pair(k, rows, 0, live[0], windows)
+        lt_out[k] = orbital_pair(k, rows, live[0], orbitals)
 
     def prepare():
-        for copy in copies + now[1:]:
+        for copy in small:
             copy.wait()
         left(0)
         left(1)
+        for copy in now[1:]:
+            copy.wait()
+        for copy in ahead:
+            copy.start()
 
     def beside(i):
         for k in (2 * i, 2 * i + 1):
-            right = orbital_pair(k, cols, slabs, live[0], windows).astype(F32)
+            right = orbital_pair(k, cols, live[0], orbitals).astype(F32)
             right = jnp.concatenate([right, right[NIN:]], axis=0)
             r_out[pl.ds(pl.multiple_of(k * PAIRED, PAIRED), PAIRED), :] = right.T.astype(BF)
             left(jnp.minimum(k + 2, pairs - 1))
@@ -260,12 +250,12 @@
         copy.wait()
 
 
-def fourth_kernel(where, sbuf, lt_ref, r_ref, far1, msg, keep_in, keep, dens, *scratch):
+def fourth_kernel(where, sbuf, lt_ref, r_ref, msg, keep_in, keep, dens, *scratch):
     core, x = where[0], where[1]
 
     def emit(h, in0, in1, act):
         for n, v in enumerate((in0, in1)):
-            keep_in[pair_rows(h, n), :] = v + far1[pair_rows(h, n), :].astype(F32)
+            keep_in[pair_rows(h, n), :] = v
         emit_active(h, act, core, x, msg, keep, 0)
 
     run_block(sbuf, lt_ref, r_ref, scratch, emit)
@@ -273,11 +263,13 @@
     msg[pl.ds(2 * PER, NBQ), :] = split_wire(dens[...])
 
 
-def exchange_kernel(where, mine, near3, msg4, msg, keep, whole):
+def exchange_kernel(where, mine, near3, far1a, far1b, msg4, msg, keep, whole):
     parts = []
     for q in range(NBQ):
         rows = pl.ds(q * NACT, NACT)
-        parts.append(mine[rows, :] + near3[rows, :].astype(F32))
+        at = q * NACT - far1a.shape[0]
+        far = far1a[rows, :] if at < 0 else far1b[pl.ds(at, NACT), :]
+        parts.append(mine[rows, :] + near3[rows, :].astype(F32) + far.astype(F32))
     v = jnp.concatenate(parts, axis=1)
     v = v.astype(BF)
     total = lax.dot_general(v, v, (((1,), (1,)), ((), ())), preferred_element_type=F32)
@@ -311,7 +303,7 @@
             sent += 1
         mine = keep[pl.ds(PER, PER), :] + near[pl.ds(at + PER, PER), :].astype(F32)
         if n == 3:
-            mine = mine + far1[pl.ds(INROWS, PER), :].astype(F32)
+            mine = mine + far1[pl.ds(far1.shape[0] - PER, PER), :].astype(F32)
         own[pl.ds(n * PER, PER), :] = mine
         total = d[...] + joined(near[pl.ds(dens_at, NBQ), :])
         dens[pl.ds(n * NBQ, NBQ), :] = total
@@ -373,14 +365,26 @@
     return jax.ShapeDtypeStruct(dims, dtype)
 
 
-def sum_over_aux(part):
+def sum_over_aux(part, active):
     n = lax.axis_size("aux")
     if n != 4:
-        return lax.psum(part, "aux")
-    three, two, one = (
-        lax.ppermute(part, "aux", [(z, z ^ k) for z in range(n)]) for k in (3, 2, 1)
-    )
-    return (three + two) + (one + part)
+        return lax.psum(part, "aux"), active
+    down, up = {}, {}
+    for k in range(1, n):
+        down[k] = lax.ppermute(part, "aux", [(z, z - k) for z in range(k, n)])
+    part, active = lax.optimization_barrier((part, active))
+    for k in range(1, n):
+        up[k] = lax.ppermute(part, "aux", [(z, z + k) for z in range(n - k)])
+    z = lax.axis_index("aux")
+
+    def from_device(s):
+        value = part
+        for other in range(n):
+            if other != s:
+                value = jnp.where(z == other, down[s - other] if s > other else up[other - s], value)
+        return value
+
+    return (from_device(0) + from_device(1)) + (from_device(2) + from_device(3)), active
 
 
 def paired_body(slabs, block_row, block_col, live_count, orbitals, hcore):
@@ -415,8 +419,7 @@
         ),
         scratch_shapes=[
             pltpu.SMEM((nslab,), jnp.int32), pltpu.SMEM((nslab,), jnp.int32),
-            pltpu.SemaphoreType.DMA((2,)),
-            pltpu.VMEM((2 * nslab, NCOL, PAIRED), BF), pltpu.SemaphoreType.DMA((2 * nslab,)),
+            pltpu.VMEM(orbitals.T.shape, BF), pltpu.SemaphoreType.DMA((3,)),
             pltpu.VMEM(loaded.shape, BF), copies, copies,
         ] + scratch,
         compiler_params=PARAMS,
@@ -441,7 +444,9 @@
     out2 = jnp.concatenate([keep_in2, keep2[:PER]], axis=0)
     out2 = (out2 + near1[: INROWS + PER].astype(F32)).astype(BF)
     out2, lt, r = lax.optimization_barrier((out2, lt, r))
-    far1 = lax.ppermute(out2, "pair", swap_x)
+    cut = INROWS // 2 + NACT
+    far1a = lax.ppermute(out2[:cut], "pair", swap_x)
+    far1b = lax.ppermute(out2[cut:], "pair", swap_x)
     msg3, keep3, dens3, slabs4 = pl.pallas_call(
         third_kernel,
         name="slabs_third",
@@ -453,10 +458,11 @@
         cost_estimate=cost,
     )(where, slabs, slabs3, lt, r, send2, dens2)
     near3 = lax.ppermute(msg3, "pair", swap_core)
+    far1a, lt, r = lax.optimization_barrier((far1a, lt, r))
     msg4, keep_in4, keep4, dens4 = pl.pallas_call(
         fourth_kernel,
         name="slabs_fourth",
-        in_specs=[SM] + [VM] * 4,
+        in_specs=[SM] + [VM] * 3,
         out_specs=[VM] * 4,
         out_shape=(
             shape((2 * PER + NBQ, LANES), BF), shape((INROWS, LANES), F32), keep, dens,
@@ -464,11 +470,11 @@
         scratch_shapes=scratch,
         compiler_params=PARAMS,
         cost_estimate=cost,
-    )(where, slabs4, lt, r, far1)
+    )(where, slabs4, lt, r)
     msg4, exch = pl.pallas_call(
         exchange_kernel,
         name="exchange",
-        in_specs=[SM] + [VM] * 3,
+        in_specs=[SM] + [VM] * 5,
         out_specs=[VM] * 2,
         out_shape=(
             shape((2 * PER + NBQ + 2 * QUARTER, LANES), BF),
@@ -476,7 +482,7 @@
         ),
         scratch_shapes=[pltpu.VMEM((NACT, LANES), F32)],
         compiler_params=PARAMS,
-    )(where, keep_in4, near3, msg4)
+    )(where, keep_in4, near3, far1a, far1b, msg4)
     near4 = lax.ppermute(msg4, "pair", swap_core)
     msg5, act, dens, exch = pl.pallas_call(
         gather_kernel,
@@ -490,7 +496,7 @@
             shape((QUARTER, LANES), F32),
         ),
         compiler_params=PARAMS,
-    )(keep1, keep2, keep3, keep4, dens1, dens2, dens3, dens4, exch, near1, near3, near4, far1)
+    )(keep1, keep2, keep3, keep4, dens1, dens2, dens3, dens4, exch, near1, near3, near4, far1b)
     far5 = lax.ppermute(msg5, "pair", swap_x)
     partial = pl.pallas_call(
         coulomb_kernel,
@@ -509,7 +515,8 @@
         compiler_params=PARAMS,
         cost_estimate=pl.CostEstimate(flops=10**6, bytes_accessed=10**6, transcendentals=0),
     )(where, act, far5)
-    return (active, sum_over_aux(partial) + hcore)
+    total, active = sum_over_aux(partial, active)
+    return (active, total + hcore)
 
 
 def slab_terms(values, left, right):

time: 50.5 us -> 56.4 us (1.12)
  starting transfers between devices: 9.66 us -> 20.3 us
  waiting for transfers between devices: 10.7 us -> 6.79 us
  Pallas kernels: 27.9 us -> 26.8 us
    ppermute x4 -> x8, starting transfers between devices: 6.99 us -> 18 us  [the longest x3 11.3 us: sum_over_aux(): up[k] = lax.ppermute(part, 'aux', [(z, z + k) for z in range(n - k)])]
    ppermute x4 -> x8, waiting for transfers between devices: 5.84 us -> 1.64 us  [the longest x3 1.3 us: sum_over_aux(): up[k] = lax.ppermute(part, 'aux', [(z, z + k) for z in range(n - k)])]
    pallas_call x1, Pallas kernels: 8.84 us -> 7.73 us  [paired_body(): pl.pallas_call(first_kernel, name='slabs_first', in_specs=[SM, HB, HB, SM...]
  transfers between devices with their start and end apart: 8 -> 12, of which waited for: 5 -> 4; matrix products, arithmetic and copies ran while one was open for 0% -> 0% of each run, Pallas kernels for 36% -> 32%
where the time goes in v7:
time: 56.4 us; the launch traced here: 56.2 us
  Pallas kernels  26.8 us (48%)
  starting transfers between devices  20.3 us (36%)
  waiting for transfers between devices  6.79 us (12%)
  between operations  1.46 us (3%)
  other arithmetic  0.75 us (1%)
    ppermute x3, starting transfers between devices, sum_over_aux(): up[k] = lax.ppermute(part, 'aux', [(z, z + k) for z in range(n - k)])  11.3 us
    pallas_call x1, Pallas kernels, paired_body(): pl.pallas_call(first_kernel, name='slabs_first', in_specs=[SM, HB, HB, SM...  7.73 us
    pallas_call x1, Pallas kernels, paired_body(): pl.pallas_call(third_kernel, name='slabs_third', in_specs=[SM, HB] + [VM]...  5.51 us
    pallas_call x1, Pallas kernels, paired_body(): pl.pallas_call(second_kernel, name='slabs_second', in_specs=[SM, HB] + [V...  5.48 us
    pallas_call x1, Pallas kernels, paired_body(): pl.pallas_call(fourth_kernel, name='slabs_fourth', in_specs=[SM] + [VM] *...  5.42 us
    ppermute x1, waiting for transfers between devices, paired_body(): far5 = lax.ppermute(msg5, 'pair', swap_x)  3.88 us
    ppermute x3, starting transfers between devices, sum_over_aux(): down[k] = lax.ppermute(part, 'aux', [(z, z - k) for z in range(k, n)])  3.87 us
    ppermute x1, starting transfers between devices, paired_body(): far1a = lax.ppermute(out2[:cut], 'pair', swap_x)  2.55 us
  transfers between devices with their start and end apart: 12, of which 4 were waited for; matrix products, arithmetic and copies ran while one was open for 0% of the time, Pallas kernels for 32%

profile of v7, /device:TPU:0, one launch (start us, length us, event | category | flops | bytes accessed | tf_op | source)
XLA Modules:
  0.0 56.2 jit_solution(8369577778558097361)
XLA Ops:
  1.4 7.7 %slabs_first.1 = (bf16[8,192,128]{2,1,0:T(8,128)(2,1)S(1)}, bf16[1024,256]{1,0:T(8,128)(2,1)S(1)}, bf16[1296,128]{1,0:T(8,128)(2,1)S(1)}, f32[256,128]{1,0:T(8,1...) custom-call(s32[2]{0:T(128)S(1)} %pad_add_fusion.where, s32[16]{0:T(128)} %rows_ref.1, s32[16]{0:T(128)} %cols_ref.1, ...), custom_call_target="tpu_custom_call" | custom-call | flops 6000000000 | bytes 10000000 | tf_op jit(solution)/shard_map/slabs_first/pallas_call | solution.py:407
  9.1 0.5 collective-permute-start
  9.6 5.5 %slabs_second.1 = (f32[1024,128]{1,0:T(8,128)S(1)}, bf16[256,128]{1,0:T(8,128)(2,1)S(1)}, f32[256,128]{1,0:T(8,128)S(1)}, f32[16,128]{1,0:T(8,128)S(1)}, bf16[8,2,16,4096]{3,2,1,0:T(8,128)(2,1)S(1)}) custom-call(s32[2]{0:T(128)S(1)} %pad_add_fusion.where, bf16[16,64,4096]{2,1,0:T(8,128)(2,1)} %slabs_ref.5, ...), custom_call_target="tpu_custom_call" | custom-call | flops 6000000000 | bytes 10000000 | tf_op jit(solution)/shard_map/slabs_second/pallas_call | solution.py:432
  15.2 2.5 %collective-permute-start.1 = (bf16[576,128]{1,0:T(8,128)(2,1)S(1)}, bf16[576,128]{1,0:T(8,128)(2,1)S(1)}, u32[]{:S(2)}, u32[]{:S(2)}) collective-permute-start(bf16[576,128]{1,0:T(8,128)(2,1)S(1)} %get-tuple-element.69), channel_id=1, source_target_pairs={{0,8},{8,0},{4,12},{12,4},{1,9},{9,1},{5,13},{13,5},{2,10},{10,2},... | collective-permute-start | bytes 442376 | tf_op jit(solution)/shard_map/ppermute | solution.py:448
  17.8 5.5 %slabs_third.1 = (bf16[1568,128]{1,0:T(8,128)(2,1)S(1)}, f32[256,128]{1,0:T(8,128)S(1)}, f32[16,128]{1,0:T(8,128)S(1)}, bf16[8,2,16,4096]{3,2,1,0:T(8,128)(2,1)S(1)}) custom-call(s32[2]{0:T(128)S(1)} %pad_add_fusion.where, bf16[16,64,4096]{2,1,0:T(8,128)(2,1)} %slabs_ref.5, bf16[8,2,16,4096]{3,2,1,0:T(8,128)(2,1)S(1)} %get-tuple-element.40.sbuf, ...), custom_call_target="tpu_custom_call" | custom-call | flops 6000000000 | bytes 10000000 | tf_op jit(solution)/shard_map/slabs_third/pallas_call | solution.py:450
  23.3 0.3 collective-permute-start.2
  23.6 0.3 collective-permute-start.3
  23.9 5.4 %slabs_fourth.1 = (bf16[272,128]{1,0:T(8,128)(2,1)S(1)}, f32[1024,128]{1,0:T(8,128)S(1)}, f32[256,128]{1,0:T(8,128)S(1)}, f32[16,128]{1,0:T(8,128)S(1)}) custom-call(s32[2]{0:T(128)S(1)} %pad_add_fusion.where, bf16[8,2,16,4096]{3,2,1,0:T(8,128)(2,1)S(1)} %get-tuple-element.48.sbuf, bf16[8,192,128]{2,1,0:T(8,128)(2,1)S(1)} %get-tuple-element.50.lt_ref, ...), custom_call_target="tpu_custom_call" | custom-call | flops 6000000000 | bytes 10000000 | tf_op jit(solution)/shard_map/slabs_fourth/pallas_call | solution.py:462
  29.3 0.3 collective-permute-done.3.far1b.far1
  29.6 0.9 %exchange.1 = (bf16[304,128]{1,0:T(8,128)(2,1)S(1)}, f32[32,128]{1,0:T(8,128)S(1)}) custom-call(s32[2]{0:T(128)S(1)} %pad_add_fusion.where, f32[1024,128]{1,0:T(8,128)S(1)} %get-tuple-element.56.mine, bf16[1568,128]{1,0:T(8,128)(2,1)S(1)} %collective-permute-done.2.near3, bf16[576,128]{1,0:T(8,128)(2,1)S(1)} %collective-permute-done.1.far1a, ...), custom_call_target="tpu_custom_call" | custom-call | tf_op jit(solution)/shard_map/exchange/pallas_call | solution.py:474
  30.6 1.3 %collective-permute-done.4.near4 = bf16[304,128]{1,0:T(8,128)(2,1)S(1)} collective-permute-done((bf16[304,128]{1,0:T(8,128)(2,1)S(1)}, bf16[304,128]{1,0:T(8,128)(2,1)S(1)}, u32[]{:S(2)}, u32[]{:S(2)}) %collective-permute-start.4) | collective-permute-done | bytes 77856 | tf_op jit(solution)/shard_map/ppermute | solution.py:486
  31.8 0.1 active_of_chip.1
  32.0 1.5 %collective-permute-start.5 = (bf16[464,128]{1,0:T(8,128)(2,1)S(1)}, bf16[464,128]{1,0:T(8,128)(2,1)S(1)}, u32[]{:S(2)}, u32[]{:S(2)}) collective-permute-start(bf16[464,128]{1,0:T(8,128)(2,1)S(1)} %get-tuple-element.63), channel_id=1, source_target_pairs={{0,8},{8,0},{4,12},{12,4},{1,9},{9,1},{5,13},{13,5},{2,10},{10,2},... | collective-permute-start | bytes 356360 | tf_op jit(solution)/shard_map/ppermute | solution.py:500
  33.5 3.9 %collective-permute-done.5.far = bf16[464,128]{1,0:T(8,128)(2,1)S(1)} collective-permute-done((bf16[464,128]{1,0:T(8,128)(2,1)S(1)}, bf16[464,128]{1,0:T(8,128)(2,1)S(1)}, u32[]{:S(2)}, u32[]{:S(2)}) %collective-permute-start.5) | collective-permute-done | bytes 118816 | tf_op jit(solution)/shard_map/ppermute | solution.py:500
  37.3 0.2 coulomb.1
  37.5 1.3 %collective-permute-start.9 = (f32[16,64]{1,0:T(8,128)S(1)}, f32[16,64]{1,0:T(8,128)S(1)}, u32[]{:S(2)}, u32[]{:S(2)}) collective-permute-start(f32[16,64]{1,0:T(8,128)S(1)} %coulomb.1), channel_id=1, source_target_pairs={{1,0},{2,1},{3,2},{5,4},{6,5},{7,6},{9,8},{10,9},{11,10},{13,12},{... | collective-permute-start | bytes 12296 | tf_op jit(solution)/shard_map/ppermute | solution.py:374
  38.8 1.3 %collective-permute-start.10 = (f32[16,64]{1,0:T(8,128)S(1)}, f32[16,64]{1,0:T(8,128)S(1)}, u32[]{:S(2)}, u32[]{:S(2)}) collective-permute-start(f32[16,64]{1,0:T(8,128)S(1)} %coulomb.1), channel_id=1, source_target_pairs={{2,0},{3,1},{6,4},{7,5},{10,8},{11,9},{14,12},{15,13},{18,16},{19,... | collective-permute-start | bytes 12296 | tf_op jit(solution)/shard_map/ppermute | solution.py:374
  40.1 1.3 %collective-permute-start.11 = (f32[16,64]{1,0:T(8,128)S(1)}, f32[16,64]{1,0:T(8,128)S(1)}, u32[]{:S(2)}, u32[]{:S(2)}) collective-permute-start(f32[16,64]{1,0:T(8,128)S(1)} %coulomb.1), channel_id=1, source_target_pairs={{3,0},{7,4},{11,8},{15,12},{19,16},{23,20},{27,24},{31,28}} | collective-permute-start | bytes 12296 | tf_op jit(solution)/shard_map/ppermute | solution.py:374
  41.4 1.5 %own_active.1 = f32[64,16,64]{2,1,0:T(8,128)} custom-call(s32[2]{0:T(128)S(1)} %pad_add_fusion.where, f32[512,128]{1,0:T(8,128)S(1)} %get-tuple-element.62.act, bf16[464,128]{1,0:T(8,128)(2,1)S(1)} %collective-permute-done.5.far), custom_call_target="tpu_custom_call" | custom-call | flops 1000000 | bytes 1000000 | tf_op jit(solution)/shard_map/own_active/pallas_call | solution.py:509
  42.9 3.9 %collective-permute-start.8 = (f32[16,64]{1,0:T(8,128)S(1)}, f32[16,64]{1,0:T(8,128)S(1)}, u32[]{:S(2)}, u32[]{:S(2)}) collective-permute-start(f32[16,64]{1,0:T(8,128)S(1)} %coulomb.1), channel_id=1, source_target_pairs={{0,1},{1,2},{2,3},{4,5},{5,6},{6,7},{8,9},{9,10},{10,11},{12,13},{... | collective-permute-start | bytes 12296 | tf_op jit(solution)/shard_map/ppermute | solution.py:377
  46.8 6.1 %collective-permute-start.7 = (f32[16,64]{1,0:T(8,128)S(1)}, f32[16,64]{1,0:T(8,128)S(1)}, u32[]{:S(2)}, u32[]{:S(2)}) collective-permute-start(f32[16,64]{1,0:T(8,128)S(1)} %coulomb.1), channel_id=1, source_target_pairs={{0,2},{1,3},{4,6},{5,7},{8,10},{9,11},{12,14},{13,15},{16,18},{17,... | collective-permute-start | bytes 12296 | tf_op jit(solution)/shard_map/ppermute | solution.py:377
  52.9 1.3 %collective-permute-start.6 = (f32[16,64]{1,0:T(8,128)S(1)}, f32[16,64]{1,0:T(8,128)S(1)}, u32[]{:S(2)}, u32[]{:S(2)}) collective-permute-start(f32[16,64]{1,0:T(8,128)S(1)} %coulomb.1), channel_id=1, source_target_pairs={{0,3},{4,7},{8,11},{12,15},{16,19},{20,23},{24,27},{28,31}} | collective-permute-start | bytes 12296 | tf_op jit(solution)/shard_map/ppermute | solution.py:377
  54.2 1.3 %collective-permute-done.6 = f32[16,64]{1,0:T(8,128)S(1)} collective-permute-done((f32[16,64]{1,0:T(8,128)S(1)}, f32[16,64]{1,0:T(8,128)S(1)}, u32[]{:S(2)}, u32[]{:S(2)}) %collective-permute-start.6) | collective-permute-done | bytes 4128 | tf_op jit(solution)/shard_map/ppermute | solution.py:377
  55.5 0.6 %add_add_fusion = f32[16,64]{1,0:T(8,128)} fusion(f32[16,64]{1,0:T(8,128)S(1)} %copy-done, f32[16,64]{1,0:T(8,128)S(1)} %collective-permute-done.9, f32[16,64]{1,0:T(8,128)S(1)} %collective-permute-done.10, f32[16,64]{1,0:T(8,128)S(1)} %collective-permute-done.11, f32[16,64]{1,0:T(8,128)S(1)} %coulomb.1, f32[16,64]{1,0:T(8,128)S(1)} %collective-permute-done.8, ...), kind=kLoop, calls=%fused_computation.2 | loop fusion | flops 16384 | bytes 36868 | tf_op jit(solution)/shard_map/add | solution.py:519
  (15 shorter events, 0.3 us)
Async XLA Ops:
  9.1 6.0 %collective-permute-start = (bf16[1296,128]{1,0:T(8,128)(2,1)S(1)}, bf16[1296,128]{1,0:T(8,128)(2,1)S(1)}, u32[]{:S(2)}, u32[]{:S(2)}) collective-permute-start(bf16[1296,128]{1,0:T(8,128)(2,1)S(1)} %get-tuple-element.42), channel_id=1, source_target_pairs={{0,4},{4,0},{8,12},{12,8},{1,5},{5,1},{9,13},{13,9},{2,6},{6,2},{1... | collective-permute-start | bytes 995336 | tf_op jit(solution)/shard_map/ppermute | solution.py:431
  15.2 8.6 %collective-permute-start.1 = (bf16[576,128]{1,0:T(8,128)(2,1)S(1)}, bf16[576,128]{1,0:T(8,128)(2,1)S(1)}, u32[]{:S(2)}, u32[]{:S(2)}) collective-permute-start(bf16[576,128]{1,0:T(8,128)(2,1)S(1)} %get-tuple-element.69), channel_id=1, source_target_pairs={{0,8},{8,0},{4,12},{12,4},{1,9},{9,1},{5,13},{13,5},{2,10},{10,2},... | collective-permute-start | bytes 442376 | tf_op jit(solution)/shard_map/ppermute | solution.py:448
  23.3 6.3 %collective-permute-start.2 = (bf16[1568,128]{1,0:T(8,128)(2,1)S(1)}, bf16[1568,128]{1,0:T(8,128)(2,1)S(1)}, u32[]{:S(2)}, u32[]{:S(2)}) collective-permute-start(bf16[1568,128]{1,0:T(8,128)(2,1)S(1)} %get-tuple-element.57), channel_id=1, source_target_pairs={{0,4},{4,0},{8,12},{12,8},{1,5},{5,1},{9,13},{13,9},{2,6},{6,2},{1... | collective-permute-start | bytes 1204232 | tf_op jit(solution)/shard_map/ppermute | solution.py:460
  23.6 6.1 %collective-permute-start.3 = (bf16[576,128]{1,0:T(8,128)(2,1)S(1)}, bf16[576,128]{1,0:T(8,128)(2,1)S(1)}, u32[]{:S(2)}, u32[]{:S(2)}) collective-permute-start(bf16[576,128]{1,0:T(8,128)(2,1)S(1)} %get-tuple-element.68), channel_id=1, source_target_pairs={{0,8},{8,0},{4,12},{12,4},{1,9},{9,1},{5,13},{13,5},{2,10},{10,2},... | collective-permute-start | bytes 442376 | tf_op jit(solution)/shard_map/ppermute | solution.py:449
  29.6 25.9 %copy-start = (f32[16,64]{1,0:T(8,128)S(1)}, f32[16,64]{1,0:T(8,128)}, u32[]{:S(2)}) copy-start(f32[16,64]{1,0:T(8,128)} %param.11) | copy-start | bytes 12292
  30.5 1.3 %collective-permute-start.4 = (bf16[304,128]{1,0:T(8,128)(2,1)S(1)}, bf16[304,128]{1,0:T(8,128)(2,1)S(1)}, u32[]{:S(2)}, u32[]{:S(2)}) collective-permute-start(bf16[304,128]{1,0:T(8,128)(2,1)S(1)} %get-tuple-element.61), channel_id=1, source_target_pairs={{0,4},{4,0},{8,12},{12,8},{1,5},{5,1},{9,13},{13,9},{2,6},{6,2},{1... | collective-permute-start | bytes 233480 | tf_op jit(solution)/shard_map/ppermute | solution.py:486
  32.0 5.4 %collective-permute-start.5 = (bf16[464,128]{1,0:T(8,128)(2,1)S(1)}, bf16[464,128]{1,0:T(8,128)(2,1)S(1)}, u32[]{:S(2)}, u32[]{:S(2)}) collective-permute-start(bf16[464,128]{1,0:T(8,128)(2,1)S(1)} %get-tuple-element.63), channel_id=1, source_target_pairs={{0,8},{8,0},{4,12},{12,4},{1,9},{9,1},{5,13},{13,5},{2,10},{10,2},... | collective-permute-start | bytes 356360 | tf_op jit(solution)/shard_map/ppermute | solution.py:500
  37.5 15.4 %collective-permute-start.9 = (f32[16,64]{1,0:T(8,128)S(1)}, f32[16,64]{1,0:T(8,128)S(1)}, u32[]{:S(2)}, u32[]{:S(2)}) collective-permute-start(f32[16,64]{1,0:T(8,128)S(1)} %coulomb.1), channel_id=1, source_target_pairs={{1,0},{2,1},{3,2},{5,4},{6,5},{7,6},{9,8},{10,9},{11,10},{13,12},{... | collective-permute-start | bytes 12296 | tf_op jit(solution)/shard_map/ppermute | solution.py:374
  38.8 15.4 %collective-permute-start.10 = (f32[16,64]{1,0:T(8,128)S(1)}, f32[16,64]{1,0:T(8,128)S(1)}, u32[]{:S(2)}, u32[]{:S(2)}) collective-permute-start(f32[16,64]{1,0:T(8,128)S(1)} %coulomb.1), channel_id=1, source_target_pairs={{2,0},{3,1},{6,4},{7,5},{10,8},{11,9},{14,12},{15,13},{18,16},{19,... | collective-permute-start | bytes 12296 | tf_op jit(solution)/shard_map/ppermute | solution.py:374
  40.1 14.1 %collective-permute-start.11 = (f32[16,64]{1,0:T(8,128)S(1)}, f32[16,64]{1,0:T(8,128)S(1)}, u32[]{:S(2)}, u32[]{:S(2)}) collective-permute-start(f32[16,64]{1,0:T(8,128)S(1)} %coulomb.1), channel_id=1, source_target_pairs={{3,0},{7,4},{11,8},{15,12},{19,16},{23,20},{27,24},{31,28}} | collective-permute-start | bytes 12296 | tf_op jit(solution)/shard_map/ppermute | solution.py:374
  42.9 11.3 %collective-permute-start.8 = (f32[16,64]{1,0:T(8,128)S(1)}, f32[16,64]{1,0:T(8,128)S(1)}, u32[]{:S(2)}, u32[]{:S(2)}) collective-permute-start(f32[16,64]{1,0:T(8,128)S(1)} %coulomb.1), channel_id=1, source_target_pairs={{0,1},{1,2},{2,3},{4,5},{5,6},{6,7},{8,9},{9,10},{10,11},{12,13},{... | collective-permute-start | bytes 12296 | tf_op jit(solution)/shard_map/ppermute | solution.py:377
  46.8 7.4 %collective-permute-start.7 = (f32[16,64]{1,0:T(8,128)S(1)}, f32[16,64]{1,0:T(8,128)S(1)}, u32[]{:S(2)}, u32[]{:S(2)}) collective-permute-start(f32[16,64]{1,0:T(8,128)S(1)} %coulomb.1), channel_id=1, source_target_pairs={{0,2},{1,3},{4,6},{5,7},{8,10},{9,11},{12,14},{13,15},{16,18},{17,... | collective-permute-start | bytes 12296 | tf_op jit(solution)/shard_map/ppermute | solution.py:377
  52.9 2.6 %collective-permute-start.6 = (f32[16,64]{1,0:T(8,128)S(1)}, f32[16,64]{1,0:T(8,128)S(1)}, u32[]{:S(2)}, u32[]{:S(2)}) collective-permute-start(f32[16,64]{1,0:T(8,128)S(1)} %coulomb.1), channel_id=1, source_target_pairs={{0,3},{4,7},{8,11},{12,15},{16,19},{20,23},{24,27},{28,31}} | collective-permute-start | bytes 12296 | tf_op jit(solution)/shard_map/ppermute | solution.py:377

commit v8 on v7

--- a/solution.py
+++ b/solution.py
@@ -66,7 +66,7 @@
 
     def half_transform(k, rows):
         left = lt_ref[k]
-        at = pl.ds(pl.multiple_of(k * LANES, LANES), LANES)
+        at = pl.ds(k * LANES, LANES)
         for q in range(0, NBQ, wide):
             cols = []
             for u in range(q, q + wide):
@@ -81,14 +81,14 @@
             for u in range(wide):
                 half_ref[q + u, :, at] = half[:, u * LANES : (u + 1) * LANES]
 
-    def two_pairs(i, carry):
+    def two_pairs(i):
         relayout(2 * i + 1, odd_ref)
         half_transform(2 * i, even_ref)
-        relayout(jnp.minimum(2 * i + 2, pairs - 1), even_ref)
+        if 2 * i + 2 < pairs:
+            relayout(2 * i + 2, even_ref)
         half_transform(2 * i + 1, odd_ref)
         if beside is not None:
             beside(i)
-        return carry
 
     def second_transform(g):
         lhs = half_ref[pl.ds(group * g, group)].reshape(group * NCOL, half_ref.shape[2])
@@ -119,7 +119,8 @@
     relayout(0, even_ref)
     if prepare is not None:
         prepare()
-    lax.fori_loop(0, pairs // 2, two_pairs, 0)
+    for i in range(pairs // 2):
+        two_pairs(i)
     whole = second_transform(0)
     for g in range(NBQ // group):
         following = second_transform(g + 1) if g + 1 < NBQ // group else None
@@ -194,8 +195,9 @@
         for k in (2 * i, 2 * i + 1):
             right = orbital_pair(k, cols, live[0], orbitals).astype(F32)
             right = jnp.concatenate([right, right[NIN:]], axis=0)
-            r_out[pl.ds(pl.multiple_of(k * PAIRED, PAIRED), PAIRED), :] = right.T.astype(BF)
-            left(jnp.minimum(k + 2, pairs - 1))
+            r_out[pl.ds(k * PAIRED, PAIRED), :] = right.T.astype(BF)
+            if k + 2 < pairs:
+                left(k + 2)
 
     def emit(h, in0, in1, act):
         msg[pair_rows(h, 0), :] = in0.astype(BF)
@@ -365,26 +367,13 @@
     return jax.ShapeDtypeStruct(dims, dtype)
 
 
-def sum_over_aux(part, active):
+def sum_over_aux(part):
     n = lax.axis_size("aux")
     if n != 4:
-        return lax.psum(part, "aux"), active
-    down, up = {}, {}
-    for k in range(1, n):
-        down[k] = lax.ppermute(part, "aux", [(z, z - k) for z in range(k, n)])
-    part, active = lax.optimization_barrier((part, active))
-    for k in range(1, n):
-        up[k] = lax.ppermute(part, "aux", [(z, z + k) for z in range(n - k)])
-    z = lax.axis_index("aux")
-
-    def from_device(s):
-        value = part
-        for other in range(n):
-            if other != s:
-                value = jnp.where(z == other, down[s - other] if s > other else up[other - s], value)
-        return value
-
-    return (from_device(0) + from_device(1)) + (from_device(2) + from_device(3)), active
+        return lax.psum(part, "aux")
+    for k in (1, 2):
+        part = part + lax.ppermute(part, "aux", [(z, z ^ k) for z in range(n)])
+    return part
 
 
 def paired_body(slabs, block_row, block_col, live_count, orbitals, hcore):
@@ -515,8 +504,7 @@
         compiler_params=PARAMS,
         cost_estimate=pl.CostEstimate(flops=10**6, bytes_accessed=10**6, transcendentals=0),
     )(where, act, far5)
-    total, active = sum_over_aux(partial, active)
-    return (active, total + hcore)
+    return (active, hcore + sum_over_aux(partial))
 
 
 def slab_terms(values, left, right):

time: 56.4 us -> 48.4 us (0.86)
  starting transfers between devices: 20.3 us -> 9.98 us
  Pallas kernels: 26.8 us -> 28.2 us
  waiting for transfers between devices: 6.79 us -> 7.84 us
    ppermute x6 -> x2, starting transfers between devices: 15.1 us -> 4.66 us  [sum_over_aux(): part = part + lax.ppermute(part, 'aux', [(z, z ^ k) for z in range(n)])]
    ppermute x1, starting transfers between devices: 2.55 us -> 0.08 us  [paired_body(): far1a = lax.ppermute(out2[:cut], 'pair', swap_x)]
    ppermute x1, starting transfers between devices: 0.3 us -> 2.57 us  [paired_body(): far1b = lax.ppermute(out2[cut:], 'pair', swap_x)]
    ppermute x1, waiting for transfers between devices: 0.01 us -> 0.95 us  [paired_body(): far1a = lax.ppermute(out2[:cut], 'pair', swap_x)]
    pallas_call x1, Pallas kernels: 5.48 us -> 6.34 us  [paired_body(): pl.pallas_call(second_kernel, name='slabs_second', in_specs=[SM, HB] + [V...]
    pallas_call x1, Pallas kernels: 5.51 us -> 6.35 us  [paired_body(): pl.pallas_call(third_kernel, name='slabs_third', in_specs=[SM, HB] + [VM]...]
    ppermute x6 -> x2, waiting for transfers between devices: 1.31 us -> 2.07 us  [sum_over_aux(): part = part + lax.ppermute(part, 'aux', [(z, z ^ k) for z in range(n)])]
  transfers between devices with their start and end apart: 12 -> 8, of which waited for: 4 -> 5; matrix products, arithmetic and copies ran while one was open for 0% -> 0% of each run, Pallas kernels for 32% -> 40%
where the time goes in v8:
time: 48.4 us; the launch traced here: 48.2 us
  Pallas kernels  28.2 us (58%)
  starting transfers between devices  9.98 us (21%)
  waiting for transfers between devices  7.84 us (16%)
  between operations  1.39 us (3%)
  other arithmetic  0.75 us (2%)
    pallas_call x1, Pallas kernels, paired_body(): pl.pallas_call(first_kernel, name='slabs_first', in_specs=[SM, HB, HB, SM...  7.84 us
    pallas_call x1, Pallas kernels, paired_body(): pl.pallas_call(third_kernel, name='slabs_third', in_specs=[SM, HB] + [VM]...  6.35 us
    pallas_call x1, Pallas kernels, paired_body(): pl.pallas_call(second_kernel, name='slabs_second', in_specs=[SM, HB] + [V...  6.34 us
    pallas_call x1, Pallas kernels, paired_body(): pl.pallas_call(fourth_kernel, name='slabs_fourth', in_specs=[SM] + [VM] *...  5.02 us
    ppermute x2, starting transfers between devices, sum_over_aux(): part = part + lax.ppermute(part, 'aux', [(z, z ^ k) for z in range(n)])  4.66 us
    ppermute x1, waiting for transfers between devices, paired_body(): far5 = lax.ppermute(msg5, 'pair', swap_x)  3.55 us
    ppermute x1, starting transfers between devices, paired_body(): far1b = lax.ppermute(out2[cut:], 'pair', swap_x)  2.57 us
    ppermute x2, waiting for transfers between devices, sum_over_aux(): part = part + lax.ppermute(part, 'aux', [(z, z ^ k) for z in range(n)])  2.07 us
  transfers between devices with their start and end apart: 8, of which 5 were waited for; matrix products, arithmetic and copies ran while one was open for 0% of the time, Pallas kernels for 40%

profile of v8, /device:TPU:0, one launch (start us, length us, event | category | flops | bytes accessed | tf_op | source)
XLA Modules:
  0.0 48.2 jit_solution(9675376339723185298)
XLA Ops:
  1.3 0.1 pad_add_fusion.where
  1.4 7.8 %slabs_first.1 = (bf16[8,192,128]{2,1,0:T(8,128)(2,1)S(1)}, bf16[1024,256]{1,0:T(8,128)(2,1)S(1)}, bf16[1296,128]{1,0:T(8,128)(2,1)S(1)}, f32[256,128]{1,0:T(8,1...) custom-call(s32[2]{0:T(128)S(1)} %pad_add_fusion.where, s32[16]{0:T(128)} %rows_ref.1, s32[16]{0:T(128)} %cols_ref.1, ...), custom_call_target="tpu_custom_call" | custom-call | flops 6000000000 | bytes 10000000 | tf_op jit(solution)/shard_map/slabs_first/pallas_call | solution.py:396
  9.2 0.5 %collective-permute-start = (bf16[1296,128]{1,0:T(8,128)(2,1)S(1)}, bf16[1296,128]{1,0:T(8,128)(2,1)S(1)}, u32[]{:S(2)}, u32[]{:S(2)}) collective-permute-start(bf16[1296,128]{1,0:T(8,128)(2,1)S(1)} %get-tuple-element.40), channel_id=1, source_target_pairs={{0,4},{4,0},{8,12},{12,8},{1,5},{5,1},{9,13},{13,9},{2,6},{6,2},{1... | collective-permute-start | bytes 995336 | tf_op jit(solution)/shard_map/ppermute | solution.py:420
  9.7 6.3 %slabs_second.1 = (f32[1024,128]{1,0:T(8,128)S(1)}, bf16[256,128]{1,0:T(8,128)(2,1)S(1)}, f32[256,128]{1,0:T(8,128)S(1)}, f32[16,128]{1,0:T(8,128)S(1)}, bf16[8,2,16,4096]{3,2,1,0:T(8,128)(2,1)S(1)}) custom-call(s32[2]{0:T(128)S(1)} %pad_add_fusion.where, bf16[16,64,4096]{2,1,0:T(8,128)(2,1)} %slabs_ref.5, ...), custom_call_target="tpu_custom_call" | custom-call | flops 6000000000 | bytes 10000000 | tf_op jit(solution)/shard_map/slabs_second/pallas_call | solution.py:421
  16.1 0.1 fusion
  16.2 2.6 %collective-permute-start.3 = (bf16[576,128]{1,0:T(8,128)(2,1)S(1)}, bf16[576,128]{1,0:T(8,128)(2,1)S(1)}, u32[]{:S(2)}, u32[]{:S(2)}) collective-permute-start(bf16[576,128]{1,0:T(8,128)(2,1)S(1)} %get-tuple-element.64), channel_id=1, source_target_pairs={{0,8},{8,0},{4,12},{12,4},{1,9},{9,1},{5,13},{13,5},{2,10},{10,2},... | collective-permute-start | bytes 442376 | tf_op jit(solution)/shard_map/ppermute | solution.py:438
  18.8 0.1 collective-permute-start.1
  18.9 6.3 %slabs_third.1 = (bf16[1568,128]{1,0:T(8,128)(2,1)S(1)}, f32[256,128]{1,0:T(8,128)S(1)}, f32[16,128]{1,0:T(8,128)S(1)}, bf16[8,2,16,4096]{3,2,1,0:T(8,128)(2,1)S(1)}) custom-call(s32[2]{0:T(128)S(1)} %pad_add_fusion.where, bf16[16,64,4096]{2,1,0:T(8,128)(2,1)} %slabs_ref.5, bf16[8,2,16,4096]{3,2,1,0:T(8,128)(2,1)S(1)} %get-tuple-element.38.sbuf, ...), custom_call_target="tpu_custom_call" | custom-call | flops 6000000000 | bytes 10000000 | tf_op jit(solution)/shard_map/slabs_third/pallas_call | solution.py:439
  25.2 0.3 collective-permute-start.2
  25.5 1.0 %collective-permute-done.1.far1a = bf16[576,128]{1,0:T(8,128)(2,1)S(1)} collective-permute-done((bf16[576,128]{1,0:T(8,128)(2,1)S(1)}, bf16[576,128]{1,0:T(8,128)(2,1)S(1)}, u32[]{:S(2)}, u32[]{:S(2)}) %collective-permute-start.1) | collective-permute-done | bytes 147488 | tf_op jit(solution)/shard_map/ppermute | solution.py:437
  26.4 5.0 %slabs_fourth.1 = (bf16[272,128]{1,0:T(8,128)(2,1)S(1)}, f32[1024,128]{1,0:T(8,128)S(1)}, f32[256,128]{1,0:T(8,128)S(1)}, f32[16,128]{1,0:T(8,128)S(1)}) custom-call(s32[2]{0:T(128)S(1)} %pad_add_fusion.where, bf16[8,2,16,4096]{3,2,1,0:T(8,128)(2,1)S(1)} %get-tuple-element.46.sbuf, bf16[8,192,128]{2,1,0:T(8,128)(2,1)S(1)} %get-tuple-element.48.lt_ref, ...), custom_call_target="tpu_custom_call" | custom-call | flops 6000000000 | bytes 10000000 | tf_op jit(solution)/shard_map/slabs_fourth/pallas_call | solution.py:451
  31.5 0.9 %exchange.1 = (bf16[304,128]{1,0:T(8,128)(2,1)S(1)}, f32[32,128]{1,0:T(8,128)S(1)}) custom-call(s32[2]{0:T(128)S(1)} %pad_add_fusion.where, f32[1024,128]{1,0:T(8,128)S(1)} %get-tuple-element.54.mine, bf16[1568,128]{1,0:T(8,128)(2,1)S(1)} %collective-permute-done.2.near3, bf16[576,128]{1,0:T(8,128)(2,1)S(1)} %collective-permute-done.1.far1a, ...), custom_call_target="tpu_custom_call" | custom-call | tf_op jit(solution)/shard_map/exchange/pallas_call | solution.py:463
  32.4 0.1 collective-permute-start.4
  32.4 1.3 %collective-permute-done.4.near4 = bf16[304,128]{1,0:T(8,128)(2,1)S(1)} collective-permute-done((bf16[304,128]{1,0:T(8,128)(2,1)S(1)}, bf16[304,128]{1,0:T(8,128)(2,1)S(1)}, u32[]{:S(2)}, u32[]{:S(2)}) %collective-permute-start.4) | collective-permute-done | bytes 77856 | tf_op jit(solution)/shard_map/ppermute | solution.py:475
  33.7 0.1 active_of_chip.1
  33.8 1.8 %collective-permute-start.5 = (bf16[464,128]{1,0:T(8,128)(2,1)S(1)}, bf16[464,128]{1,0:T(8,128)(2,1)S(1)}, u32[]{:S(2)}, u32[]{:S(2)}) collective-permute-start(bf16[464,128]{1,0:T(8,128)(2,1)S(1)} %get-tuple-element.61), channel_id=1, source_target_pairs={{0,8},{8,0},{4,12},{12,4},{1,9},{9,1},{5,13},{13,5},{2,10},{10,2},... | collective-permute-start | bytes 356360 | tf_op jit(solution)/shard_map/ppermute | solution.py:489
  35.6 3.6 %collective-permute-done.5.far = bf16[464,128]{1,0:T(8,128)(2,1)S(1)} collective-permute-done((bf16[464,128]{1,0:T(8,128)(2,1)S(1)}, bf16[464,128]{1,0:T(8,128)(2,1)S(1)}, u32[]{:S(2)}, u32[]{:S(2)}) %collective-permute-start.5) | collective-permute-done | bytes 118816 | tf_op jit(solution)/shard_map/ppermute | solution.py:489
  39.2 0.2 coulomb.1
  39.4 1.8 %collective-permute-start.6 = (f32[16,64]{1,0:T(8,128)S(1)}, f32[16,64]{1,0:T(8,128)S(1)}, u32[]{:S(2)}, u32[]{:S(2)}) collective-permute-start(f32[16,64]{1,0:T(8,128)S(1)} %coulomb.1), channel_id=1, source_target_pairs={{0,1},{1,0},{2,3},{3,2},{4,5},{5,4},{6,7},{7,6},{8,9},{9,8},{10,11... | collective-permute-start | bytes 12296 | tf_op jit(solution)/shard_map/ppermute | solution.py:375
  41.2 1.8 %collective-permute-done.6 = f32[16,64]{1,0:T(8,128)S(1)} collective-permute-done((f32[16,64]{1,0:T(8,128)S(1)}, f32[16,64]{1,0:T(8,128)S(1)}, u32[]{:S(2)}, u32[]{:S(2)}) %collective-permute-start.6) | collective-permute-done | bytes 4128 | tf_op jit(solution)/shard_map/ppermute | solution.py:375
  43.0 2.8 %collective-permute-start.7 = (f32[16,64]{1,0:T(8,128)S(1)}, f32[16,64]{1,0:T(8,128)S(1)}, u32[]{:S(2)}, u32[]{:S(2)}) collective-permute-start(f32[16,64]{1,0:T(8,128)S(1)} %add.14), channel_id=1, source_target_pairs={{0,2},{1,3},{2,0},{3,1},{4,6},{5,7},{6,4},{7,5},{8,10},{9,11},{10,... | collective-permute-start | bytes 12296 | tf_op jit(solution)/shard_map/ppermute | solution.py:375
  45.9 1.5 %own_active.1 = f32[64,16,64]{2,1,0:T(8,128)} custom-call(s32[2]{0:T(128)S(1)} %pad_add_fusion.where, f32[512,128]{1,0:T(8,128)S(1)} %get-tuple-element.60.act, bf16[464,128]{1,0:T(8,128)(2,1)S(1)} %collective-permute-done.5.far), custom_call_target="tpu_custom_call" | custom-call | flops 1000000 | bytes 1000000 | tf_op jit(solution)/shard_map/own_active/pallas_call | solution.py:498
  47.4 0.2 collective-permute-done.7
  47.6 0.6 %add_add_fusion = f32[16,64]{1,0:T(8,128)} fusion(f32[16,64]{1,0:T(8,128)S(1)} %copy-done, f32[16,64]{1,0:T(8,128)S(1)} %add.14, f32[16,64]{1,0:T(8,128)S(1)} %collective-permute-done.7), kind=kLoop, calls=%fused_computation.2 | loop fusion | flops 2048 | bytes 16384 | tf_op jit(solution)/shard_map/add | solution.py:507
  (8 shorter events, 0.0 us)
Async XLA Ops:
  9.2 6.9 %collective-permute-start = (bf16[1296,128]{1,0:T(8,128)(2,1)S(1)}, bf16[1296,128]{1,0:T(8,128)(2,1)S(1)}, u32[]{:S(2)}, u32[]{:S(2)}) collective-permute-start(bf16[1296,128]{1,0:T(8,128)(2,1)S(1)} %get-tuple-element.40), channel_id=1, source_target_pairs={{0,4},{4,0},{8,12},{12,8},{1,5},{5,1},{9,13},{13,9},{2,6},{6,2},{1... | collective-permute-start | bytes 995336 | tf_op jit(solution)/shard_map/ppermute | solution.py:420
  16.2 15.3 %collective-permute-start.3 = (bf16[576,128]{1,0:T(8,128)(2,1)S(1)}, bf16[576,128]{1,0:T(8,128)(2,1)S(1)}, u32[]{:S(2)}, u32[]{:S(2)}) collective-permute-start(bf16[576,128]{1,0:T(8,128)(2,1)S(1)} %get-tuple-element.64), channel_id=1, source_target_pairs={{0,8},{8,0},{4,12},{12,4},{1,9},{9,1},{5,13},{13,5},{2,10},{10,2},... | collective-permute-start | bytes 442376 | tf_op jit(solution)/shard_map/ppermute | solution.py:438
  18.8 7.7 %collective-permute-start.1 = (bf16[576,128]{1,0:T(8,128)(2,1)S(1)}, bf16[576,128]{1,0:T(8,128)(2,1)S(1)}, u32[]{:S(2)}, u32[]{:S(2)}) collective-permute-start(bf16[576,128]{1,0:T(8,128)(2,1)S(1)} %get-tuple-element.65), channel_id=1, source_target_pairs={{0,8},{8,0},{4,12},{12,4},{1,9},{9,1},{5,13},{13,5},{2,10},{10,2},... | collective-permute-start | bytes 442376 | tf_op jit(solution)/shard_map/ppermute | solution.py:437
  25.2 6.3 %collective-permute-start.2 = (bf16[1568,128]{1,0:T(8,128)(2,1)S(1)}, bf16[1568,128]{1,0:T(8,128)(2,1)S(1)}, u32[]{:S(2)}, u32[]{:S(2)}) collective-permute-start(bf16[1568,128]{1,0:T(8,128)(2,1)S(1)} %get-tuple-element.55), channel_id=1, source_target_pairs={{0,4},{4,0},{8,12},{12,8},{1,5},{5,1},{9,13},{13,9},{2,6},{6,2},{1... | collective-permute-start | bytes 1204232 | tf_op jit(solution)/shard_map/ppermute | solution.py:449
  31.5 16.1 %copy-start = (f32[16,64]{1,0:T(8,128)S(1)}, f32[16,64]{1,0:T(8,128)}, u32[]{:S(2)}) copy-start(f32[16,64]{1,0:T(8,128)} %param.11) | copy-start | bytes 12292
  32.4 1.3 %collective-permute-start.4 = (bf16[304,128]{1,0:T(8,128)(2,1)S(1)}, bf16[304,128]{1,0:T(8,128)(2,1)S(1)}, u32[]{:S(2)}, u32[]{:S(2)}) collective-permute-start(bf16[304,128]{1,0:T(8,128)(2,1)S(1)} %get-tuple-element.59), channel_id=1, source_target_pairs={{0,4},{4,0},{8,12},{12,8},{1,5},{5,1},{9,13},{13,9},{2,6},{6,2},{1... | collective-permute-start | bytes 233480 | tf_op jit(solution)/shard_map/ppermute | solution.py:475
  33.8 5.4 %collective-permute-start.5 = (bf16[464,128]{1,0:T(8,128)(2,1)S(1)}, bf16[464,128]{1,0:T(8,128)(2,1)S(1)}, u32[]{:S(2)}, u32[]{:S(2)}) collective-permute-start(bf16[464,128]{1,0:T(8,128)(2,1)S(1)} %get-tuple-element.61), channel_id=1, source_target_pairs={{0,8},{8,0},{4,12},{12,4},{1,9},{9,1},{5,13},{13,5},{2,10},{10,2},... | collective-permute-start | bytes 356360 | tf_op jit(solution)/shard_map/ppermute | solution.py:489
  39.4 3.7 %collective-permute-start.6 = (f32[16,64]{1,0:T(8,128)S(1)}, f32[16,64]{1,0:T(8,128)S(1)}, u32[]{:S(2)}, u32[]{:S(2)}) collective-permute-start(f32[16,64]{1,0:T(8,128)S(1)} %coulomb.1), channel_id=1, source_target_pairs={{0,1},{1,0},{2,3},{3,2},{4,5},{5,4},{6,7},{7,6},{8,9},{9,8},{10,11... | collective-permute-start | bytes 12296 | tf_op jit(solution)/shard_map/ppermute | solution.py:375
  43.0 4.5 %collective-permute-start.7 = (f32[16,64]{1,0:T(8,128)S(1)}, f32[16,64]{1,0:T(8,128)S(1)}, u32[]{:S(2)}, u32[]{:S(2)}) collective-permute-start(f32[16,64]{1,0:T(8,128)S(1)} %add.14), channel_id=1, source_target_pairs={{0,2},{1,3},{2,0},{3,1},{4,6},{5,7},{6,4},{7,5},{8,10},{9,11},{10,... | collective-permute-start | bytes 12296 | tf_op jit(solution)/shard_map/ppermute | solution.py:375

commit v9 on v8

--- a/solution.py
+++ b/solution.py
@@ -44,13 +44,14 @@
     ]
 
 
-def run_block(sbuf, lt_ref, r_ref, scratch, emit, prepare=None, beside=None):
-    even_ref, odd_ref, half_ref, diag = scratch
-    pairs = sbuf.shape[0]
+def run_block(sbuf, weights, scratch, emit, ready=None, midway=None):
+    lt_ref, r_ref, bd_ref, d_ref = weights
+    pt_ref, q_ref, diag = scratch[4:]
+    quads = sbuf.shape[0] // 2
     first = low_half(NBQ)
     first_s = low_half(BS)
     zero = jnp.zeros((BS, LANES), BF)
-    wide, group = NBQ, 4
+    group = 8
 
     def relayout(k, out):
         for j in range(sbuf.shape[3] // LANES):
@@ -64,66 +65,90 @@
                 first, pltpu.roll(a, BS, 1), b
             ).astype(F32)
 
-    def half_transform(k, rows):
-        left = lt_ref[k]
-        at = pl.ds(k * LANES, LANES)
-        for q in range(0, NBQ, wide):
-            cols = []
-            for u in range(q, q + wide):
-                s = rows[pl.ds(u * QSTEP, BS, stride=MSTEP), :].astype(BF)
-                cols.append(
+    def transform(g, bufs):
+        dens = [d_ref[2 * g + n] for n in range(2)]
+        for q in range(0, NBQ, group):
+            slabs = [[], []]
+            for u in range(q, q + group):
+                total = None
+                for n in range(2):
+                    s = bufs[n][pl.ds(u * QSTEP, BS, stride=MSTEP), :]
+                    part = jnp.sum((s * dens[n]).reshape(BS // 8, 8, LANES), axis=0)
+                    total = part if total is None else total + part
+                    slabs[n].append(s.astype(BF))
+                diag[u] = total if g == 0 else diag[u] + total
+            for n in range(2):
+                k = 2 * g + n
+                cols = [
                     jnp.concatenate(
                         [jnp.where(first_s, s, zero), jnp.where(first_s, zero, s)], axis=0
                     )
-                )
-            half = jnp.dot(left, jnp.concatenate(cols, axis=1), preferred_element_type=F32)
-            half = half.astype(BF)
-            for u in range(wide):
-                half_ref[q + u, :, at] = half[:, u * LANES : (u + 1) * LANES]
-
-    def two_pairs(i):
-        relayout(2 * i + 1, odd_ref)
-        half_transform(2 * i, even_ref)
-        if 2 * i + 2 < pairs:
-            relayout(2 * i + 2, even_ref)
-        half_transform(2 * i + 1, odd_ref)
-        if beside is not None:
-            beside(i)
+                    for s in slabs[n]
+                ]
+                p = jnp.dot(
+                    lt_ref[NIN:, k * LANES : (k + 1) * LANES],
+                    jnp.concatenate(cols, axis=1),
+                    preferred_element_type=F32,
+                ).astype(BF)
+                for u in range(group):
+                    pt_ref[q + u, :, k * LANES : (k + 1) * LANES] = p[
+                        :, u * LANES : (u + 1) * LANES
+                    ]
+            rows = jnp.concatenate(
+                [jnp.concatenate([s0, s1], axis=1) for s0, s1 in zip(*slabs)], axis=0
+            )
+            out = jnp.dot(rows, bd_ref[g], preferred_element_type=F32).astype(BF)
+            for u in range(0, group, 2):
+                for n in range(2):
+                    lanes = slice(n * LANES, (n + 1) * LANES)
+                    q0 = out[u * BS : (u + 1) * BS, lanes]
+                    q1 = out[(u + 1) * BS : (u + 2) * BS, lanes]
+                    at = slice((q + u) * BS, (q + u + 2) * BS)
+                    row = (4 * g + 2 * n) * BS
+                    q_ref[row : row + BS, at] = jnp.where(first_s, q0, pltpu.roll(q1, BS, 1))
+                    q_ref[row + BS : row + 2 * BS, at] = jnp.where(
+                        first_s, pltpu.roll(q0, BS, 1), q1
+                    )
 
     def second_transform(g):
-        lhs = half_ref[pl.ds(group * g, group)].reshape(group * NCOL, half_ref.shape[2])
-        return jnp.dot(lhs, r_ref[...], preferred_element_type=F32)
-
-    def assemble(g, whole):
-        eye = lax.broadcasted_iota(jnp.int32, (NIN, NIN), 0) == lax.broadcasted_iota(
-            jnp.int32, (NIN, NIN), 1
+        rows = pt_ref[4 * g : 4 * g + 4].reshape(4 * NACT, pt_ref.shape[2])
+        one = jnp.dot(rows, r_ref[...], preferred_element_type=F32)
+        two = jnp.dot(
+            lt_ref[...], q_ref[:, 4 * g * BS : (4 * g + 4) * BS], preferred_element_type=F32
         )
-        for p in range(group // 2):
-            w0 = whole[2 * p * NCOL : (2 * p + 1) * NCOL]
-            w1 = whole[(2 * p + 1) * NCOL : (2 * p + 2) * NCOL]
-            side = jnp.where(low_half(NCOL), w0[:, LANES:], w1[:, LANES:])
-            across = side[:NIN].T
-            square = jnp.concatenate([w0[NIN:, LANES:], w1[NIN:, LANES:]], axis=0).T
-            h = group // 2 * g + p
+        return one, two
+
+    def assemble(g, both):
+        one, two = both
+        for p in range(2):
+            w0 = one[2 * p * NACT : (2 * p + 1) * NACT]
+            w1 = one[(2 * p + 1) * NACT : (2 * p + 2) * NACT]
+            turned = two[:, p * LANES : (p + 1) * LANES]
+            across = turned[:NIN].T
+            square = jnp.concatenate([turned[NIN:], turned[NIN:]], axis=0).T
             emit(
-                h,
-                w0[NIN:, :NIN] + across[:NACT],
-                w1[NIN:, :NIN] + across[NACT:],
-                side[NIN:] + square[:NACT],
+                2 * g + p,
+                w0[:, :NIN] + across[:NACT],
+                w1[:, :NIN] + across[NACT:],
+                jnp.where(first_s, w0[:, NIN:] + square[:NACT], w1[:, NIN:] + square[NACT:]),
             )
-            for n, w in enumerate((w0, w1)):
-                diag[pl.ds(2 * h + n, 1), :] = jnp.sum(
-                    jnp.where(eye, w[:NIN, :NIN], 0.0), axis=0, keepdims=True
-                )
-
-    relayout(0, even_ref)
-    if prepare is not None:
-        prepare()
-    for i in range(pairs // 2):
-        two_pairs(i)
+
+    def load(g):
+        for n in range(2):
+            if ready is not None:
+                ready(2 * g + n)
+            relayout(2 * g + n, scratch[2 * (g % 2) + n])
+
+    load(0)
+    for g in range(quads):
+        if g + 1 < quads:
+            load(g + 1)
+        transform(g, scratch[2 * (g % 2) : 2 * (g % 2) + 2])
+    if midway is not None:
+        midway()
     whole = second_transform(0)
-    for g in range(NBQ // group):
-        following = second_transform(g + 1) if g + 1 < NBQ // group else None
+    for g in range(NBQ // 4):
+        following = second_transform(g + 1) if g + 1 < NBQ // 4 else None
         assemble(g, whole)
         whole = following
 
@@ -139,8 +164,8 @@
 
 
 def density_of(diag):
-    d = 2.0 * jnp.sum(diag, axis=1, keepdims=True)
-    return jnp.broadcast_to(d, diag.shape)
+    d = 2.0 * jnp.sum(jnp.sum(diag, axis=1), axis=1, keepdims=True)
+    return jnp.broadcast_to(d, (NBQ, LANES))
 
 
 QUARTER = NACT // 4
@@ -163,105 +188,129 @@
 
 
 def first_kernel(
-    where, rows_ref, cols_ref, live, slabs_ref, ot_ref, lt_out, r_out, msg, keep, dens, after,
+    where, rows_ref, cols_ref, live, slabs_ref, ot_ref,
+    lt_out, r_out, bd_out, d_out, msg, keep, dens, after,
     rows, cols, orbitals, ssem, sbuf, bsem, sem, *scratch
 ):
     pairs = slabs_ref.shape[0] // 2
     core, x = where[0], where[1]
+    part = NACT // 2
     small = [
         pltpu.make_async_copy(src, dst, ssem.at[n])
-        for n, (src, dst) in enumerate(((rows_ref, rows), (cols_ref, cols), (ot_ref, orbitals)))
+        for n, (src, dst) in enumerate(((rows_ref, rows), (cols_ref, cols)))
+    ] + [
+        pltpu.make_async_copy(
+            ot_ref.at[pl.ds(n * part, part)], orbitals.at[pl.ds(n * part, part)], ssem.at[2 + n]
+        )
+        for n in range(NCOL // part)
     ]
     now = slab_copies(slabs_ref, sbuf, bsem, 2 * (1 - x) + (1 - core))
-    for copy in [small[0], now[0], small[1], small[2]] + now[1:]:
+    for copy in now[:2] + small + now[2:]:
         copy.start()
     ahead = slab_copies(slabs_ref, after, sem, 2 * (1 - x) + core)
-    now[0].wait()
-
-    def left(k):
-        lt_out[k] = orbital_pair(k, rows, live[0], orbitals)
-
-    def prepare():
-        for copy in small:
-            copy.wait()
-        left(0)
-        left(1)
-        for copy in now[1:]:
-            copy.wait()
+    bd_out[...] = jnp.zeros_like(bd_out)
+
+    def prepare(k):
+        left = orbital_pair(k, rows, live[0], orbitals)
+        right = orbital_pair(k, cols, live[0], orbitals)
+        at = slice(k * PAIRED, (k + 1) * PAIRED)
+        lt_out[:, at] = left
+        turned = jnp.concatenate([right, right[NIN:]], axis=0).astype(F32).T.astype(BF)
+        r_out[at, :] = turned
+        inner = (lax.broadcasted_iota(jnp.int32, (PAIRED, LANES), 0) < BS) == low_half(PAIRED)
+        place = slice((k % 2) * PAIRED, (k % 2 + 1) * PAIRED)
+        bd_out[k // 2, place, place] = jnp.where(
+            inner, turned[:, NIN:], jnp.zeros((PAIRED, LANES), BF)
+        )
+        both = jnp.dot(
+            left[:NIN].astype(F32).T.astype(BF), right[:NIN], preferred_element_type=F32
+        )
+        d_out[k] = jnp.where(low_half(BS), both[:BS], both[BS:])
+
+    def ready(k):
+        now[k].wait()
+        if k == 1:
+            for copy in small:
+                copy.wait()
+        if k % 2 == 1:
+            prepare(k - 1)
+            prepare(k)
+
+    def midway():
         for copy in ahead:
             copy.start()
-
-    def beside(i):
-        for k in (2 * i, 2 * i + 1):
-            right = orbital_pair(k, cols, live[0], orbitals).astype(F32)
-            right = jnp.concatenate([right, right[NIN:]], axis=0)
-            r_out[pl.ds(k * PAIRED, PAIRED), :] = right.T.astype(BF)
-            if k + 2 < pairs:
-                left(k + 2)
 
     def emit(h, in0, in1, act):
         msg[pair_rows(h, 0), :] = in0.astype(BF)
         msg[pair_rows(h, 1), :] = in1.astype(BF)
         emit_active(h, act, core, x, msg, keep, INROWS)
 
-    run_block(sbuf, lt_out, r_out, scratch, emit, prepare, beside)
-    dens[...] = density_of(scratch[3][...])
+    run_block(sbuf, (lt_out, r_out, bd_out, d_out), scratch, emit, ready, midway)
+    dens[...] = density_of(scratch[6][...])
     msg[pl.ds(INROWS + 2 * PER, NBQ), :] = split_wire(dens[...])
     for copy in ahead:
         copy.wait()
 
 
 def second_kernel(
-    where, slabs_ref, sbuf, lt_ref, r_ref, keep_in, send, keep, dens, after, sem, *scratch
+    where, slabs_ref, sbuf, lt_ref, r_ref, bd_ref, d_ref, keep_in, send, keep, dens, after,
+    sem, *scratch
 ):
     core, x = where[0], where[1]
     ahead = slab_copies(slabs_ref, after, sem, 2 * x + (1 - core))
-    for copy in ahead:
-        copy.start()
+
+    def midway():
+        for copy in ahead:
+            copy.start()
 
     def emit(h, in0, in1, act):
         keep_in[pair_rows(h, 0), :] = in0
         keep_in[pair_rows(h, 1), :] = in1
         emit_active(h, act, core, x, send, keep, 0)
 
-    run_block(sbuf, lt_ref, r_ref, scratch, emit)
-    dens[...] = density_of(scratch[3][...])
+    run_block(sbuf, (lt_ref, r_ref, bd_ref, d_ref), scratch, emit, None, midway)
+    dens[...] = density_of(scratch[6][...])
     for copy in ahead:
         copy.wait()
 
 
 def third_kernel(
-    where, slabs_ref, sbuf, lt_ref, r_ref, send2, dens2, msg, keep, dens, after, sem, *scratch
+    where, slabs_ref, sbuf, lt_ref, r_ref, bd_ref, d_ref, send2, dens2, msg, keep, dens, after,
+    sem, *scratch
 ):
     core, x = where[0], where[1]
     ahead = slab_copies(slabs_ref, after, sem, 2 * x + core)
-    for copy in ahead:
-        copy.start()
+
+    def midway():
+        for copy in ahead:
+            copy.start()
 
     def emit(h, in0, in1, act):
         msg[pair_rows(h, 0), :] = in0.astype(BF)
         msg[pair_rows(h, 1), :] = in1.astype(BF)
         emit_active(h, act, core, x, msg, keep, INROWS)
 
-    run_block(sbuf, lt_ref, r_ref, scratch, emit)
+    run_block(sbuf, (lt_ref, r_ref, bd_ref, d_ref), scratch, emit, None, midway)
     msg[pl.ds(INROWS + 2 * PER, 2 * PER), :] = send2[...]
-    dens[...] = density_of(scratch[3][...])
+    dens[...] = density_of(scratch[6][...])
     msg[pl.ds(INROWS + 4 * PER, NBQ), :] = split_wire(dens[...])
     msg[pl.ds(INROWS + 4 * PER + NBQ, NBQ), :] = split_wire(dens2[...])
     for copy in ahead:
         copy.wait()
 
 
-def fourth_kernel(where, sbuf, lt_ref, r_ref, msg, keep_in, keep, dens, *scratch):
+def fourth_kernel(
+    where, sbuf, lt_ref, r_ref, bd_ref, d_ref, msg, keep_in, keep, dens, *scratch
+):
     core, x = where[0], where[1]
 
     def emit(h, in0, in1, act):
-        for n, v in enumerate((in0, in1)):
-            keep_in[pair_rows(h, n), :] = v
+        keep_in[pair_rows(h, 0), :] = in0
+        keep_in[pair_rows(h, 1), :] = in1
         emit_active(h, act, core, x, msg, keep, 0)
 
-    run_block(sbuf, lt_ref, r_ref, scratch, emit)
-    dens[...] = density_of(scratch[3][...])
+    run_block(sbuf, (lt_ref, r_ref, bd_ref, d_ref), scratch, emit)
+    dens[...] = density_of(scratch[6][...])
     msg[pl.ds(2 * PER, NBQ), :] = split_wire(dens[...])
 
 
@@ -356,7 +405,7 @@
 VM = pl.BlockSpec(memory_space=pltpu.VMEM)
 SM = pl.BlockSpec(memory_space=pltpu.SMEM)
 HB = pl.BlockSpec(memory_space=pltpu.HBM)
-PARAMS = pltpu.CompilerParams(vmem_limit_bytes=48 * 1024 * 1024)
+PARAMS = pltpu.CompilerParams(vmem_limit_bytes=32 * 1024 * 1024)
 
 
 def in_hbm(array):
@@ -385,30 +434,30 @@
     aos = nslab * BS
     loaded = shape((nslab // 2, 2, NBQ, width), BF)
     copies = pltpu.SemaphoreType.DMA((nslab // 2,))
-    scratch = [
-        pltpu.VMEM((MSTEP * BS, LANES), F32),
-        pltpu.VMEM((MSTEP * BS, LANES), F32),
-        pltpu.VMEM((NBQ, NCOL, aos), BF),
-        pltpu.VMEM((NBQ, LANES), F32),
+    scratch = [pltpu.VMEM((MSTEP * BS, LANES), F32)] * 4 + [
+        pltpu.VMEM((NBQ, NACT, aos), BF),
+        pltpu.VMEM((aos, NBQ * BS), BF),
+        pltpu.VMEM((NBQ, 8, LANES), F32),
     ]
+    weights = (
+        shape((NCOL, aos), BF),
+        shape((aos, 2 * LANES), BF),
+        shape((nslab // 4, 2 * PAIRED, 2 * PAIRED), BF),
+        shape((nslab // 2, BS, PAIRED), F32),
+    )
     cost = pl.CostEstimate(flops=6 * 10**9, bytes_accessed=10**7, transcendentals=0)
     keep, dens = shape((2 * PER, LANES), F32), shape((NBQ, LANES), F32)
-    lt, r, msg1, keep1, dens1, slabs2 = pl.pallas_call(
+    lt, r, bd, d, msg1, keep1, dens1, slabs2 = pl.pallas_call(
         first_kernel,
         name="slabs_first",
         in_specs=[SM, HB, HB, SM, HB, HB],
-        out_specs=[VM] * 6,
-        out_shape=(
-            shape((nslab // 2, NCOL, PAIRED), BF),
-            shape((aos, 2 * LANES), BF),
-            shape((INROWS + 2 * PER + NBQ, LANES), BF),
-            keep,
-            dens,
-            loaded,
+        out_specs=[VM] * 8,
+        out_shape=weights + (
+            shape((INROWS + 2 * PER + NBQ, LANES), BF), keep, dens, loaded,
         ),
         scratch_shapes=[
             pltpu.SMEM((nslab,), jnp.int32), pltpu.SMEM((nslab,), jnp.int32),
-            pltpu.VMEM(orbitals.T.shape, BF), pltpu.SemaphoreType.DMA((3,)),
+            pltpu.VMEM(orbitals.T.shape, BF), pltpu.SemaphoreType.DMA((8,)),
             pltpu.VMEM(loaded.shape, BF), copies, copies,
         ] + scratch,
         compiler_params=PARAMS,
@@ -421,7 +470,7 @@
     keep_in2, send2, keep2, dens2, slabs3 = pl.pallas_call(
         second_kernel,
         name="slabs_second",
-        in_specs=[SM, HB] + [VM] * 3,
+        in_specs=[SM, HB] + [VM] * 5,
         out_specs=[VM] * 5,
         out_shape=(
             shape((INROWS, LANES), F32), shape((2 * PER, LANES), BF), keep, dens, loaded,
@@ -429,29 +478,30 @@
         scratch_shapes=[copies] + scratch,
         compiler_params=PARAMS,
         cost_estimate=cost,
-    )(where, slabs, slabs2, lt, r)
+    )(where, slabs, slabs2, lt, r, bd, d)
     out2 = jnp.concatenate([keep_in2, keep2[:PER]], axis=0)
     out2 = (out2 + near1[: INROWS + PER].astype(F32)).astype(BF)
-    out2, lt, r = lax.optimization_barrier((out2, lt, r))
+    out2, lt = lax.optimization_barrier((out2, lt))
     cut = INROWS // 2 + NACT
     far1a = lax.ppermute(out2[:cut], "pair", swap_x)
-    far1b = lax.ppermute(out2[cut:], "pair", swap_x)
     msg3, keep3, dens3, slabs4 = pl.pallas_call(
         third_kernel,
         name="slabs_third",
-        in_specs=[SM, HB] + [VM] * 5,
+        in_specs=[SM, HB] + [VM] * 7,
         out_specs=[VM] * 4,
         out_shape=(shape((INROWS + 4 * PER + 2 * NBQ, LANES), BF), keep, dens, loaded),
         scratch_shapes=[copies] + scratch,
         compiler_params=PARAMS,
         cost_estimate=cost,
-    )(where, slabs, slabs3, lt, r, send2, dens2)
+    )(where, slabs, slabs3, lt, r, bd, d, send2, dens2)
     near3 = lax.ppermute(msg3, "pair", swap_core)
-    far1a, lt, r = lax.optimization_barrier((far1a, lt, r))
+    rest, msg3 = lax.optimization_barrier((out2[cut:], msg3))
+    far1b = lax.ppermute(rest, "pair", swap_x)
+    far1a, lt = lax.optimization_barrier((far1a, lt))
     msg4, keep_in4, keep4, dens4 = pl.pallas_call(
         fourth_kernel,
         name="slabs_fourth",
-        in_specs=[SM] + [VM] * 3,
+        in_specs=[SM] + [VM] * 5,
         out_specs=[VM] * 4,
         out_shape=(
             shape((2 * PER + NBQ, LANES), BF), shape((INROWS, LANES), F32), keep, dens,
@@ -459,7 +509,7 @@
         scratch_shapes=scratch,
         compiler_params=PARAMS,
         cost_estimate=cost,
-    )(where, slabs4, lt, r)
+    )(where, slabs4, lt, r, bd, d)
     msg4, exch = pl.pallas_call(
         exchange_kernel,
         name="exchange",

time: 48.4 us -> 47.4 us (0.979)
  Pallas kernels: 28.2 us -> 22.8 us
  local copies, waits for them, and re-layouts: 0.03 us -> 3.41 us
  waiting for transfers between devices: 7.84 us -> 10.6 us
  starting transfers between devices: 9.98 us -> 8.25 us
    unnamed x2 -> x4, local copies, waits for them, and re-layouts: 0.01 us -> 3.39 us
    ppermute x1, starting transfers between devices: 0.08 us -> 2.56 us  [paired_body(): far1a = lax.ppermute(out2[:cut], 'pair', swap_x)]
    ppermute x1, starting transfers between devices: 2.57 us -> 0.3 us  [paired_body(): far1b = lax.ppermute(rest, 'pair', swap_x)]
    pallas_call x1, Pallas kernels: 6.34 us -> 4.45 us  [paired_body(): pl.pallas_call(second_kernel, name='slabs_second', in_specs=[SM, HB] + [V...]
    ppermute x1, waiting for transfers between devices: 0.01 us -> 1.79 us  [paired_body(): far1b = lax.ppermute(rest, 'pair', swap_x)]
    pallas_call x1, Pallas kernels: 6.35 us -> 4.62 us  [paired_body(): pl.pallas_call(third_kernel, name='slabs_third', in_specs=[SM, HB] + [VM]...]
    ppermute x1, starting transfers between devices: 1.81 us -> 0.35 us  [paired_body(): far5 = lax.ppermute(msg5, 'pair', swap_x)]
    ppermute x1, waiting for transfers between devices: 3.55 us -> 5.01 us  [paired_body(): far5 = lax.ppermute(msg5, 'pair', swap_x)]
  transfers between devices with their start and end apart: 8 -> 8, of which waited for: 5 -> 5; matrix products, arithmetic and copies ran while one was open for 0% -> 0% of each run, Pallas kernels for 40% -> 31%
where the time goes in v9:
time: 47.4 us; the launch traced here: 47.2 us
  Pallas kernels  22.8 us (48%)
  waiting for transfers between devices  10.6 us (22%)
  starting transfers between devices  8.25 us (17%)
  local copies, waits for them, and re-layouts  3.41 us (7%)
  between operations  1.37 us (3%)
  other arithmetic  0.75 us (2%)
    pallas_call x1, Pallas kernels, paired_body(): pl.pallas_call(first_kernel, name='slabs_first', in_specs=[SM, HB, HB, SM...  7.15 us
    ppermute x1, waiting for transfers between devices, paired_body(): far5 = lax.ppermute(msg5, 'pair', swap_x)  5.01 us
    pallas_call x1, Pallas kernels, paired_body(): pl.pallas_call(third_kernel, name='slabs_third', in_specs=[SM, HB] + [VM]...  4.62 us
    pallas_call x1, Pallas kernels, paired_body(): pl.pallas_call(second_kernel, name='slabs_second', in_specs=[SM, HB] + [V...  4.45 us
    ppermute x2, starting transfers between devices, sum_over_aux(): part = part + lax.ppermute(part, 'aux', [(z, z ^ k) for z in range(n)])  4.18 us
    pallas_call x1, Pallas kernels, paired_body(): pl.pallas_call(fourth_kernel, name='slabs_fourth', in_specs=[SM] + [VM] *...  3.96 us
    unnamed x4, local copies, waits for them, and re-layouts  3.39 us
    ppermute x1, starting transfers between devices, paired_body(): far1a = lax.ppermute(out2[:cut], 'pair', swap_x)  2.56 us
  transfers between devices with their start and end apart: 8, of which 5 were waited for; matrix products, arithmetic and copies ran while one was open for 0% of the time, Pallas kernels for 31%

profile of v9, /device:TPU:0, one launch (start us, length us, event | category | flops | bytes accessed | tf_op | source)
XLA Modules:
  0.0 47.2 jit_solution(14133129913161999955)
XLA Ops:
  1.3 0.1 pad_add_fusion.where
  1.4 3.4 %copy-done = bf16[16,64,4096]{2,1,0:T(8,128)(2,1)S(1)} copy-done((bf16[16,64,4096]{2,1,0:T(8,128)(2,1)S(1)}, bf16[16,64,4096]{2,1,0:T(8,128)(2,1)}, u32[]{:S(2)}) %copy-start) | copy-done | bytes 8388632
  4.7 7.1 %slabs_first.1 = (bf16[192,1024]{1,0:T(8,128)(2,1)S(1)}, bf16[1024,256]{1,0:T(8,128)(2,1)S(1)}, bf16[4,256,256]{2,1,0:T(8,128)(2,1)S(1)}, f32[8,64,128]{2,1,0:T(...) custom-call(s32[2]{0:T(128)S(1)} %pad_add_fusion.where, ...), custom_call_target="tpu_custom_call" | custom-call | flops 6000000000 | bytes 10000000 | tf_op jit(solution)/shard_map/slabs_first/pallas_call | solution.py:450
  11.9 0.5 %collective-permute-start = (bf16[1296,128]{1,0:T(8,128)(2,1)S(1)}, bf16[1296,128]{1,0:T(8,128)(2,1)S(1)}, u32[]{:S(2)}, u32[]{:S(2)}) collective-permute-start(bf16[1296,128]{1,0:T(8,128)(2,1)S(1)} %get-tuple-element.43), channel_id=1, source_target_pairs={{0,4},{4,0},{8,12},{12,8},{1,5},{5,1},{9,13},{13,9},{2,6},{6,2},{1... | collective-permute-start | bytes 995336 | tf_op jit(solution)/shard_map/ppermute | solution.py:469
  12.4 4.4 %slabs_second.1 = (f32[1024,128]{1,0:T(8,128)S(1)}, bf16[256,128]{1,0:T(8,128)(2,1)S(1)}, f32[256,128]{1,0:T(8,128)S(1)}, f32[16,128]{1,0:T(8,128)S(1)}, bf16[8,2,16,4096]{3,2,1,0:T(8,128)(2,1)S(1)}) custom-call(s32[2]{0:T(128)S(1)} %pad_add_fusion.where, bf16[16,64,4096]{2,1,0:T(8,128)(2,1)S(1)} %copy-done, ...), custom_call_target="tpu_custom_call" | custom-call | flops 6000000000 | bytes 10000000 | tf_op jit(solution)/shard_map/slabs_second/pallas_call | solution.py:470
  17.0 2.6 %collective-permute-start.1 = (bf16[576,128]{1,0:T(8,128)(2,1)S(1)}, bf16[576,128]{1,0:T(8,128)(2,1)S(1)}, u32[]{:S(2)}, u32[]{:S(2)}) collective-permute-start(bf16[576,128]{1,0:T(8,128)(2,1)S(1)} %get-tuple-element.67), channel_id=1, source_target_pairs={{0,8},{8,0},{4,12},{12,4},{1,9},{9,1},{5,13},{13,5},{2,10},{10,2},... | collective-permute-start | bytes 442376 | tf_op jit(solution)/shard_map/ppermute | solution.py:486
  19.6 4.6 %slabs_third.1 = (bf16[1568,128]{1,0:T(8,128)(2,1)S(1)}, f32[256,128]{1,0:T(8,128)S(1)}, f32[16,128]{1,0:T(8,128)S(1)}, bf16[8,2,16,4096]{3,2,1,0:T(8,128)(2,1)S(1)}) custom-call(s32[2]{0:T(128)S(1)} %pad_add_fusion.where, bf16[16,64,4096]{2,1,0:T(8,128)(2,1)S(1)} %copy-done, bf16[8,2,16,4096]{3,2,1,0:T(8,128)(2,1)S(1)} %get-tuple-element.41.sbuf, ...), custom_call_target="tpu_custom_call" | custom-call | flops 6000000000 | bytes 10000000 | tf_op jit(solution)/shard_map/slabs_third/pallas_call | solution.py:487
  24.2 0.3 collective-permute-start.2
  24.5 0.3 collective-permute-start.3
  24.8 4.0 %slabs_fourth.1 = (bf16[272,128]{1,0:T(8,128)(2,1)S(1)}, f32[1024,128]{1,0:T(8,128)S(1)}, f32[256,128]{1,0:T(8,128)S(1)}, f32[16,128]{1,0:T(8,128)S(1)}) custom-call(s32[2]{0:T(128)S(1)} %pad_add_fusion.where, bf16[8,2,16,4096]{3,2,1,0:T(8,128)(2,1)S(1)} %get-tuple-element.48.sbuf, bf16[192,1024]{1,0:T(8,128)(2,1)S(1)} %get-tuple-element.50.lt_ref, ...), custom_call_target="tpu_custom_call" | custom-call | flops 6000000000 | bytes 10000000 | tf_op jit(solution)/shard_map/slabs_fourth/pallas_call | solution.py:501
  28.7 1.8 %collective-permute-done.3.far1b.far1 = bf16[576,128]{1,0:T(8,128)(2,1)S(1)} collective-permute-done((bf16[576,128]{1,0:T(8,128)(2,1)S(1)}, bf16[576,128]{1,0:T(8,128)(2,1)S(1)}, u32[]{:S(2)}, u32[]{:S(2)}) %collective-permute-start.3) | collective-permute-done | bytes 147488 | tf_op jit(solution)/shard_map/ppermute | solution.py:499
  30.5 0.9 %exchange.1 = (bf16[304,128]{1,0:T(8,128)(2,1)S(1)}, f32[32,128]{1,0:T(8,128)S(1)}) custom-call(s32[2]{0:T(128)S(1)} %pad_add_fusion.where, f32[1024,128]{1,0:T(8,128)S(1)} %get-tuple-element.55.mine, bf16[1568,128]{1,0:T(8,128)(2,1)S(1)} %collective-permute-done.2.near3, bf16[576,128]{1,0:T(8,128)(2,1)S(1)} %collective-permute-done.1.far1a, ...), custom_call_target="tpu_custom_call" | custom-call | tf_op jit(solution)/shard_map/exchange/pallas_call | solution.py:513
  31.4 0.1 collective-permute-start.4
  31.5 1.3 %collective-permute-done.4.near4 = bf16[304,128]{1,0:T(8,128)(2,1)S(1)} collective-permute-done((bf16[304,128]{1,0:T(8,128)(2,1)S(1)}, bf16[304,128]{1,0:T(8,128)(2,1)S(1)}, u32[]{:S(2)}, u32[]{:S(2)}) %collective-permute-start.4) | collective-permute-done | bytes 77856 | tf_op jit(solution)/shard_map/ppermute | solution.py:525
  32.7 0.1 active_of_chip.1
  32.9 0.3 collective-permute-start.5
  33.2 5.0 %collective-permute-done.5.far = bf16[464,128]{1,0:T(8,128)(2,1)S(1)} collective-permute-done((bf16[464,128]{1,0:T(8,128)(2,1)S(1)}, bf16[464,128]{1,0:T(8,128)(2,1)S(1)}, u32[]{:S(2)}, u32[]{:S(2)}) %collective-permute-start.5) | collective-permute-done | bytes 118816 | tf_op jit(solution)/shard_map/ppermute | solution.py:539
  38.2 0.2 coulomb.1
  38.4 1.6 %collective-permute-start.6 = (f32[16,64]{1,0:T(8,128)S(1)}, f32[16,64]{1,0:T(8,128)S(1)}, u32[]{:S(2)}, u32[]{:S(2)}) collective-permute-start(f32[16,64]{1,0:T(8,128)S(1)} %coulomb.1), channel_id=1, source_target_pairs={{0,1},{1,0},{2,3},{3,2},{4,5},{5,4},{6,7},{7,6},{8,9},{9,8},{10,11... | collective-permute-start | bytes 12296 | tf_op jit(solution)/shard_map/ppermute | solution.py:424
  40.0 2.1 %collective-permute-done.6 = f32[16,64]{1,0:T(8,128)S(1)} collective-permute-done((f32[16,64]{1,0:T(8,128)S(1)}, f32[16,64]{1,0:T(8,128)S(1)}, u32[]{:S(2)}, u32[]{:S(2)}) %collective-permute-start.6) | collective-permute-done | bytes 4128 | tf_op jit(solution)/shard_map/ppermute | solution.py:424
  42.1 2.6 %collective-permute-start.7 = (f32[16,64]{1,0:T(8,128)S(1)}, f32[16,64]{1,0:T(8,128)S(1)}, u32[]{:S(2)}, u32[]{:S(2)}) collective-permute-start(f32[16,64]{1,0:T(8,128)S(1)} %add.14), channel_id=1, source_target_pairs={{0,2},{1,3},{2,0},{3,1},{4,6},{5,7},{6,4},{7,5},{8,10},{9,11},{10,... | collective-permute-start | bytes 12296 | tf_op jit(solution)/shard_map/ppermute | solution.py:424
  44.7 1.5 %own_active.1 = f32[64,16,64]{2,1,0:T(8,128)} custom-call(s32[2]{0:T(128)S(1)} %pad_add_fusion.where, f32[512,128]{1,0:T(8,128)S(1)} %get-tuple-element.62.act, bf16[464,128]{1,0:T(8,128)(2,1)S(1)} %collective-permute-done.5.far), custom_call_target="tpu_custom_call" | custom-call | flops 1000000 | bytes 1000000 | tf_op jit(solution)/shard_map/own_active/pallas_call | solution.py:548
  46.1 0.5 %collective-permute-done.7 = f32[16,64]{1,0:T(8,128)S(1)} collective-permute-done((f32[16,64]{1,0:T(8,128)S(1)}, f32[16,64]{1,0:T(8,128)S(1)}, u32[]{:S(2)}, u32[]{:S(2)}) %collective-permute-start.7) | collective-permute-done | bytes 4128 | tf_op jit(solution)/shard_map/ppermute | solution.py:424
  46.6 0.6 %add_add_fusion = f32[16,64]{1,0:T(8,128)} fusion(f32[16,64]{1,0:T(8,128)S(1)} %copy-done.1, f32[16,64]{1,0:T(8,128)S(1)} %add.14, f32[16,64]{1,0:T(8,128)S(1)} %collective-permute-done.7), kind=kLoop, calls=%fused_computation.2 | loop fusion | flops 2048 | bytes 16384 | tf_op jit(solution)/shard_map/add | solution.py:557
  (10 shorter events, 0.1 us)
Async XLA Ops:
  1.4 3.4 %copy-start = (bf16[16,64,4096]{2,1,0:T(8,128)(2,1)S(1)}, bf16[16,64,4096]{2,1,0:T(8,128)(2,1)}, u32[]{:S(2)}) copy-start(bf16[16,64,4096]{2,1,0:T(8,128)(2,1)} %slabs_ref.5) | copy-start | bytes 25165828
  11.9 5.0 %collective-permute-start = (bf16[1296,128]{1,0:T(8,128)(2,1)S(1)}, bf16[1296,128]{1,0:T(8,128)(2,1)S(1)}, u32[]{:S(2)}, u32[]{:S(2)}) collective-permute-start(bf16[1296,128]{1,0:T(8,128)(2,1)S(1)} %get-tuple-element.43), channel_id=1, source_target_pairs={{0,4},{4,0},{8,12},{12,8},{1,5},{5,1},{9,13},{13,9},{2,6},{6,2},{1... | collective-permute-start | bytes 995336 | tf_op jit(solution)/shard_map/ppermute | solution.py:469
  17.0 7.8 %collective-permute-start.1 = (bf16[576,128]{1,0:T(8,128)(2,1)S(1)}, bf16[576,128]{1,0:T(8,128)(2,1)S(1)}, u32[]{:S(2)}, u32[]{:S(2)}) collective-permute-start(bf16[576,128]{1,0:T(8,128)(2,1)S(1)} %get-tuple-element.67), channel_id=1, source_target_pairs={{0,8},{8,0},{4,12},{12,4},{1,9},{9,1},{5,13},{13,5},{2,10},{10,2},... | collective-permute-start | bytes 442376 | tf_op jit(solution)/shard_map/ppermute | solution.py:486
  24.2 6.3 %collective-permute-start.2 = (bf16[1568,128]{1,0:T(8,128)(2,1)S(1)}, bf16[1568,128]{1,0:T(8,128)(2,1)S(1)}, u32[]{:S(2)}, u32[]{:S(2)}) collective-permute-start(bf16[1568,128]{1,0:T(8,128)(2,1)S(1)} %get-tuple-element.56), channel_id=1, source_target_pairs={{0,4},{4,0},{8,12},{12,8},{1,5},{5,1},{9,13},{13,9},{2,6},{6,2},{1... | collective-permute-start | bytes 1204232 | tf_op jit(solution)/shard_map/ppermute | solution.py:497
  24.5 6.1 %collective-permute-start.3 = (bf16[576,128]{1,0:T(8,128)(2,1)S(1)}, bf16[576,128]{1,0:T(8,128)(2,1)S(1)}, u32[]{:S(2)}, u32[]{:S(2)}) collective-permute-start(bf16[576,128]{1,0:T(8,128)(2,1)S(1)} %get-tuple-element.58), channel_id=1, source_target_pairs={{0,8},{8,0},{4,12},{12,4},{1,9},{9,1},{5,13},{13,5},{2,10},{10,2},... | collective-permute-start | bytes 442376 | tf_op jit(solution)/shard_map/ppermute | solution.py:499
  30.5 16.1 %copy-start.1 = (f32[16,64]{1,0:T(8,128)S(1)}, f32[16,64]{1,0:T(8,128)}, u32[]{:S(2)}) copy-start(f32[16,64]{1,0:T(8,128)} %param.11) | copy-start | bytes 12292
  31.4 1.3 %collective-permute-start.4 = (bf16[304,128]{1,0:T(8,128)(2,1)S(1)}, bf16[304,128]{1,0:T(8,128)(2,1)S(1)}, u32[]{:S(2)}, u32[]{:S(2)}) collective-permute-start(bf16[304,128]{1,0:T(8,128)(2,1)S(1)} %get-tuple-element.61), channel_id=1, source_target_pairs={{0,4},{4,0},{8,12},{12,8},{1,5},{5,1},{9,13},{13,9},{2,6},{6,2},{1... | collective-permute-start | bytes 233480 | tf_op jit(solution)/shard_map/ppermute | solution.py:525
  32.9 5.4 %collective-permute-start.5 = (bf16[464,128]{1,0:T(8,128)(2,1)S(1)}, bf16[464,128]{1,0:T(8,128)(2,1)S(1)}, u32[]{:S(2)}, u32[]{:S(2)}) collective-permute-start(bf16[464,128]{1,0:T(8,128)(2,1)S(1)} %get-tuple-element.63), channel_id=1, source_target_pairs={{0,8},{8,0},{4,12},{12,4},{1,9},{9,1},{5,13},{13,5},{2,10},{10,2},... | collective-permute-start | bytes 356360 | tf_op jit(solution)/shard_map/ppermute | solution.py:539
  38.4 3.7 %collective-permute-start.6 = (f32[16,64]{1,0:T(8,128)S(1)}, f32[16,64]{1,0:T(8,128)S(1)}, u32[]{:S(2)}, u32[]{:S(2)}) collective-permute-start(f32[16,64]{1,0:T(8,128)S(1)} %coulomb.1), channel_id=1, source_target_pairs={{0,1},{1,0},{2,3},{3,2},{4,5},{5,4},{6,7},{7,6},{8,9},{9,8},{10,11... | collective-permute-start | bytes 12296 | tf_op jit(solution)/shard_map/ppermute | solution.py:424
  42.1 4.5 %collective-permute-start.7 = (f32[16,64]{1,0:T(8,128)S(1)}, f32[16,64]{1,0:T(8,128)S(1)}, u32[]{:S(2)}, u32[]{:S(2)}) collective-permute-start(f32[16,64]{1,0:T(8,128)S(1)} %add.14), channel_id=1, source_target_pairs={{0,2},{1,3},{2,0},{3,1},{4,6},{5,7},{6,4},{7,5},{8,10},{9,11},{10,... | collective-permute-start | bytes 12296 | tf_op jit(solution)/shard_map/ppermute | solution.py:424

commit v10 on v9

--- a/solution.py
+++ b/solution.py
@@ -173,14 +173,14 @@
 INROWS = NBQ * NACT
 
 
-def emit_active(h, act, core, x, send, keep, send_at):
+def emit_active(h, act, core, x, keep, sends):
     upper, lower = act[: 2 * QUARTER], act[2 * QUARTER :]
-    parts = (jnp.where(x == 0, lower, upper), jnp.where(x == 0, upper, lower))
-    for place, part in enumerate(parts):
+    near, far = jnp.where(x == 0, upper, lower), jnp.where(x == 0, lower, upper)
+    at = pl.ds(h * QUARTER, QUARTER)
+    for part, own, other in ((near, keep, sends.at[0]), (far, sends.at[1], sends.at[2])):
         one, two = part[:QUARTER], part[QUARTER:]
-        off = place * PER + h * QUARTER
-        keep[pl.ds(off, QUARTER), :] = jnp.where(core == 0, one, two)
-        send[pl.ds(send_at + off, QUARTER), :] = jnp.where(core == 0, two, one).astype(BF)
+        own[at, :] = jnp.where(core == 0, one, two).astype(own.dtype)
+        other[at, :] = jnp.where(core == 0, two, one).astype(BF)
 
 
 def pair_rows(h, n):
@@ -189,7 +189,7 @@
 
 def first_kernel(
     where, rows_ref, cols_ref, live, slabs_ref, ot_ref,
-    lt_out, r_out, bd_out, d_out, msg, keep, dens, after,
+    lt_out, r_out, bd_out, d_out, msg, keep, sends, dens, after,
     rows, cols, orbitals, ssem, sbuf, bsem, sem, *scratch
 ):
     pairs = slabs_ref.shape[0] // 2
@@ -228,9 +228,10 @@
         d_out[k] = jnp.where(low_half(BS), both[:BS], both[BS:])
 
     def ready(k):
-        now[k].wait()
+        if k < 2:
+            now[k].wait()
         if k == 1:
-            for copy in small:
+            for copy in small + now[2:]:
                 copy.wait()
         if k % 2 == 1:
             prepare(k - 1)
@@ -243,17 +244,16 @@
     def emit(h, in0, in1, act):
         msg[pair_rows(h, 0), :] = in0.astype(BF)
         msg[pair_rows(h, 1), :] = in1.astype(BF)
-        emit_active(h, act, core, x, msg, keep, INROWS)
+        emit_active(h, act, core, x, keep, sends)
 
     run_block(sbuf, (lt_out, r_out, bd_out, d_out), scratch, emit, ready, midway)
     dens[...] = density_of(scratch[6][...])
-    msg[pl.ds(INROWS + 2 * PER, NBQ), :] = split_wire(dens[...])
     for copy in ahead:
         copy.wait()
 
 
 def second_kernel(
-    where, slabs_ref, sbuf, lt_ref, r_ref, bd_ref, d_ref, keep_in, send, keep, dens, after,
+    where, slabs_ref, sbuf, lt_ref, r_ref, bd_ref, d_ref, keep_in, keep, sends, dens, after,
     sem, *scratch
 ):
     core, x = where[0], where[1]
@@ -266,7 +266,7 @@
     def emit(h, in0, in1, act):
         keep_in[pair_rows(h, 0), :] = in0
         keep_in[pair_rows(h, 1), :] = in1
-        emit_active(h, act, core, x, send, keep, 0)
+        emit_active(h, act, core, x, keep, sends)
 
     run_block(sbuf, (lt_ref, r_ref, bd_ref, d_ref), scratch, emit, None, midway)
     dens[...] = density_of(scratch[6][...])
@@ -275,8 +275,8 @@
 
 
 def third_kernel(
-    where, slabs_ref, sbuf, lt_ref, r_ref, bd_ref, d_ref, send2, dens2, msg, keep, dens, after,
-    sem, *scratch
+    where, slabs_ref, sbuf, lt_ref, r_ref, bd_ref, d_ref, sends1, sends2, dens1, dens2,
+    near, far, cross, keep, dens, after, sem, sends, *scratch
 ):
     core, x = where[0], where[1]
     ahead = slab_copies(slabs_ref, after, sem, 2 * x + core)
@@ -286,107 +286,88 @@
             copy.start()
 
     def emit(h, in0, in1, act):
-        msg[pair_rows(h, 0), :] = in0.astype(BF)
-        msg[pair_rows(h, 1), :] = in1.astype(BF)
-        emit_active(h, act, core, x, msg, keep, INROWS)
+        near[pair_rows(h, 0), :] = in0.astype(BF)
+        near[pair_rows(h, 1), :] = in1.astype(BF)
+        emit_active(h, act, core, x, keep, sends)
 
     run_block(sbuf, (lt_ref, r_ref, bd_ref, d_ref), scratch, emit, None, midway)
-    msg[pl.ds(INROWS + 2 * PER, 2 * PER), :] = send2[...]
     dens[...] = density_of(scratch[6][...])
-    msg[pl.ds(INROWS + 4 * PER, NBQ), :] = split_wire(dens[...])
-    msg[pl.ds(INROWS + 4 * PER + NBQ, NBQ), :] = split_wire(dens2[...])
+    wires = [split_wire(d[...]) for d in (dens1, dens2, dens)]
+    for k, (msg, base) in enumerate(((near, INROWS), (far, 0), (cross, 0))):
+        for n, source in enumerate((sends1, sends2, sends)):
+            msg[pl.ds(base + n * PER, PER), :] = source[k]
+            msg[pl.ds(base + 3 * PER + n * NBQ, NBQ), :] = wires[n]
     for copy in ahead:
         copy.wait()
 
 
 def fourth_kernel(
-    where, sbuf, lt_ref, r_ref, bd_ref, d_ref, msg, keep_in, keep, dens, *scratch
+    where, sbuf, lt_ref, r_ref, bd_ref, d_ref, keep_in, keep, sends, dens, *scratch
 ):
     core, x = where[0], where[1]
 
     def emit(h, in0, in1, act):
         keep_in[pair_rows(h, 0), :] = in0
         keep_in[pair_rows(h, 1), :] = in1
-        emit_active(h, act, core, x, msg, keep, 0)
+        emit_active(h, act, core, x, keep, sends)
 
     run_block(sbuf, (lt_ref, r_ref, bd_ref, d_ref), scratch, emit)
     dens[...] = density_of(scratch[6][...])
-    msg[pl.ds(2 * PER, NBQ), :] = split_wire(dens[...])
-
-
-def exchange_kernel(where, mine, near3, far1a, far1b, msg4, msg, keep, whole):
+
+
+def exchange_kernel(
+    where, mine, near3, far1a, far1b, sends, dens, near, far, cross, keep, whole
+):
     parts = []
     for q in range(NBQ):
         rows = pl.ds(q * NACT, NACT)
         at = q * NACT - far1a.shape[0]
-        far = far1a[rows, :] if at < 0 else far1b[pl.ds(at, NACT), :]
-        parts.append(mine[rows, :] + near3[rows, :].astype(F32) + far.astype(F32))
+        other = far1a[rows, :] if at < 0 else far1b[pl.ds(at, NACT), :]
+        parts.append(mine[rows, :] + near3[rows, :].astype(F32) + other.astype(F32))
     v = jnp.concatenate(parts, axis=1)
     v = v.astype(BF)
     total = lax.dot_general(v, v, (((1,), (1,)), ((), ())), preferred_element_type=F32)
     whole[...] = jnp.concatenate([total, total], axis=1)
-    core, x = where[0], where[1]
-    size = msg4.shape[0]
-    msg[pl.ds(0, size), :] = msg4[...]
-    for place, xx in enumerate((1 - x, x)):
-        there = pl.multiple_of((2 * xx + 1 - core) * QUARTER, QUARTER)
-        here = pl.multiple_of((2 * xx + core) * QUARTER, QUARTER)
-        msg[pl.ds(size + place * QUARTER, QUARTER), :] = split_wire(whole[pl.ds(there, QUARTER), :])
-        keep[pl.ds(place * QUARTER, QUARTER), :] = whole[pl.ds(here, QUARTER), :]
-
-
-def gather_kernel(
-    keep1, keep2, keep3, keep4, dens1, dens2, dens3, dens4, exch, near1, near3, near4, far1,
-    msg, own, dens, exch_own,
+    index = 2 * where[1] + where[0]
+    keep[...] = whole[pl.ds(pl.multiple_of(index * QUARTER, QUARTER), QUARTER), :]
+    wire = split_wire(dens[...])
+    for k, msg in enumerate((near, far, cross)):
+        msg[pl.ds(0, PER), :] = sends[k]
+        msg[pl.ds(PER, NBQ), :] = wire
+        at = pl.multiple_of((index ^ (k + 1)) * QUARTER, QUARTER)
+        msg[pl.ds(PER + NBQ, QUARTER), :] = split_wire(whole[pl.ds(at, QUARTER), :])
+
+
+def coulomb_kernel(
+    keep1, keep2, keep3, keep4, dens1, dens2, dens3, dens4, exch,
+    near3, far3, cross3, near4, far4, cross4, act, partial,
 ):
-    base = INROWS + 2 * PER
-    here = (
-        (keep1, near3, base, dens1, base + 2 * PER + NBQ),
-        (keep2, near1, INROWS, dens2, base),
-        (keep3, near4, 0, dens3, 2 * PER),
-        (keep4, near3, INROWS, dens4, base + 2 * PER),
-    )
-    sent = 0
-    for n, (keep, near, at, d, dens_at) in enumerate(here):
-        if n != 1:
-            other = keep[pl.ds(0, PER), :] + near[pl.ds(at, PER), :].astype(F32)
-            msg[pl.ds(sent * PER, PER), :] = other.astype(BF)
-            sent += 1
-        mine = keep[pl.ds(PER, PER), :] + near[pl.ds(at + PER, PER), :].astype(F32)
-        if n == 3:
-            mine = mine + far1[pl.ds(far1.shape[0] - PER, PER), :].astype(F32)
-        own[pl.ds(n * PER, PER), :] = mine
-        total = d[...] + joined(near[pl.ds(dens_at, NBQ), :])
-        dens[pl.ds(n * NBQ, NBQ), :] = total
-        msg[pl.ds(3 * PER + n * NBQ, NBQ), :] = split_wire(total)
-    rows = exch[...] + joined(near4[pl.ds(2 * PER + NBQ, 2 * QUARTER), :])
-    msg[pl.ds(3 * PER + 4 * NBQ, QUARTER), :] = split_wire(rows[:QUARTER])
-    exch_own[...] = rows[QUARTER:]
-
-
-FAR_ACTIVE = (1, 2, 0)
-
-
-def coulomb_kernel(act, far, dens, exch, partial):
     first = low_half(QUARTER)
+    early, late = (near3, far3, cross3), (near4, far4, cross4)
     total = jnp.zeros((QUARTER, LANES), F32)
-    for n in range(4):
-        d = dens[pl.ds(n * NBQ, NBQ), :] + joined(
-            far[pl.ds(3 * PER + (n ^ 2) * NBQ, NBQ), :]
-        )
+    for m, (keep, dens) in enumerate(
+        ((keep1, dens1), (keep2, dens2), (keep3, dens3), (keep4, dens4))
+    ):
+        rows, d = keep[...], dens[...]
+        for k in (1, 2, 3):
+            n = m ^ k
+            msg = late[k - 1] if n == 3 else early[k - 1]
+            base = INROWS if n < 3 and k == 1 else 0
+            at, dens_at = (0, PER) if n == 3 else (base + n * PER, base + 3 * PER + n * NBQ)
+            rows = rows + msg[pl.ds(at, PER), :].astype(F32)
+            d = d + joined(msg[pl.ds(dens_at, NBQ), :])
+        act[pl.ds(m * PER, PER), :] = rows
         for h in range(NBQ // 2):
-            a = act[pl.ds(n * PER + h * QUARTER, QUARTER), :]
-            if n < 3:
-                a = a + far[
-                    pl.ds(FAR_ACTIVE[n] * PER + h * QUARTER, QUARTER), :
-                ].astype(F32)
-            total = total + a * jnp.where(first, d[2 * h : 2 * h + 1], d[2 * h + 1 : 2 * h + 2])
-    total = 2.0 * (total + pltpu.roll(total, BS, 1))
-    total = total - exch[...] - joined(far[pl.ds(3 * PER + 4 * NBQ, QUARTER), :])
+            total = total + rows[h * QUARTER : (h + 1) * QUARTER] * jnp.where(
+                first, d[2 * h : 2 * h + 1], d[2 * h + 1 : 2 * h + 2]
+            )
+    total = 2.0 * (total + pltpu.roll(total, BS, 1)) - exch[...]
+    for msg in late:
+        total = total - joined(msg[pl.ds(PER + NBQ, QUARTER), :])
     partial[...] = total[:, :BS]
 
 
-def active_kernel(where, act, far, out):
+def active_kernel(where, act, out):
     core, x = where[0], where[1]
     for n in range(4):
         xx = (1 - x) if n < 2 else x
@@ -394,10 +375,6 @@
         base = NBQ * (2 * xx + cc)
         for h in range(NBQ // 2):
             a = act[pl.ds(n * PER + h * QUARTER, QUARTER), :]
-            if n < 3:
-                a = a + far[
-                    pl.ds(FAR_ACTIVE[n] * PER + h * QUARTER, QUARTER), :
-                ].astype(F32)
             out[base + 2 * h] = a[:, :BS]
             out[base + 2 * h + 1] = a[:, BS:]
 
@@ -405,6 +382,7 @@
 VM = pl.BlockSpec(memory_space=pltpu.VMEM)
 SM = pl.BlockSpec(memory_space=pltpu.SMEM)
 HB = pl.BlockSpec(memory_space=pltpu.HBM)
+
 PARAMS = pltpu.CompilerParams(vmem_limit_bytes=32 * 1024 * 1024)
 
 
@@ -425,13 +403,29 @@
     return part
 
 
+def call(kernel, name, inputs, out_shape, scratch, args, work=0):
+    return pl.pallas_call(
+        kernel,
+        name=name,
+        in_specs=inputs,
+        out_specs=[VM] * len(out_shape),
+        out_shape=out_shape,
+        scratch_shapes=scratch,
+        compiler_params=PARAMS,
+        cost_estimate=pl.CostEstimate(flops=work, bytes_accessed=10**5, transcendentals=0),
+    )(*args)
+
+
 def paired_body(slabs, block_row, block_col, live_count, orbitals, hcore):
     nslab, batch, width = slabs.shape
     index = lax.axis_index("pair")
     where = jnp.stack([lax.rem(index, 2), index // 2])
-    swap_core = [(0, 1), (1, 0), (2, 3), (3, 2)]
-    swap_x = [(0, 2), (2, 0), (1, 3), (3, 1)]
     aos = nslab * BS
+    slabs = in_hbm(slabs)
+
+    def to_peer(k, array):
+        return lax.ppermute(array, "pair", [(p, p ^ k) for p in range(4)])
+
     loaded = shape((nslab // 2, 2, NBQ, width), BF)
     copies = pltpu.SemaphoreType.DMA((nslab // 2,))
     scratch = [pltpu.VMEM((MSTEP * BS, LANES), F32)] * 4 + [
@@ -445,115 +439,96 @@
         shape((nslab // 4, 2 * PAIRED, 2 * PAIRED), BF),
         shape((nslab // 2, BS, PAIRED), F32),
     )
-    cost = pl.CostEstimate(flops=6 * 10**9, bytes_accessed=10**7, transcendentals=0)
-    keep, dens = shape((2 * PER, LANES), F32), shape((NBQ, LANES), F32)
-    lt, r, bd, d, msg1, keep1, dens1, slabs2 = pl.pallas_call(
+    kept = (
+        shape((PER, LANES), F32), shape((3, PER, LANES), BF), shape((NBQ, LANES), F32),
+    )
+    work = 5 * 10**9
+    lt, r, bd, d, msg1, keep1, sends1, dens1, slabs2 = call(
         first_kernel,
-        name="slabs_first",
-        in_specs=[SM, HB, HB, SM, HB, HB],
-        out_specs=[VM] * 8,
-        out_shape=weights + (
-            shape((INROWS + 2 * PER + NBQ, LANES), BF), keep, dens, loaded,
-        ),
-        scratch_shapes=[
+        "slabs_first",
+        [SM, HB, HB, SM, HB, HB],
+        weights + (shape((INROWS, LANES), BF),) + kept + (loaded,),
+        [
             pltpu.SMEM((nslab,), jnp.int32), pltpu.SMEM((nslab,), jnp.int32),
             pltpu.VMEM(orbitals.T.shape, BF), pltpu.SemaphoreType.DMA((8,)),
             pltpu.VMEM(loaded.shape, BF), copies, copies,
         ] + scratch,
-        compiler_params=PARAMS,
-        cost_estimate=cost,
-    )(
-        where, in_hbm(block_row), in_hbm(block_col), live_count, slabs,
-        in_hbm(orbitals.T),
-    )
-    near1 = lax.ppermute(msg1, "pair", swap_core)
-    keep_in2, send2, keep2, dens2, slabs3 = pl.pallas_call(
+        (
+            where, in_hbm(block_row), in_hbm(block_col), live_count, slabs,
+            in_hbm(orbitals.T),
+        ),
+        work,
+    )
+    near1 = to_peer(1, msg1)
+    keep_in2, keep2, sends2, dens2, slabs3 = call(
         second_kernel,
-        name="slabs_second",
-        in_specs=[SM, HB] + [VM] * 5,
-        out_specs=[VM] * 5,
-        out_shape=(
-            shape((INROWS, LANES), F32), shape((2 * PER, LANES), BF), keep, dens, loaded,
+        "slabs_second",
+        [SM, HB] + [VM] * 5,
+        (shape((INROWS, LANES), F32),) + kept + (loaded,),
+        [copies] + scratch,
+        (where, slabs, slabs2, lt, r, bd, d),
+        work,
+    )
+    out2 = (keep_in2 + near1.astype(F32)).astype(BF)
+    out2, lt = lax.optimization_barrier((out2, lt))
+    cut = INROWS // 4
+    far1a = to_peer(2, out2[:cut])
+    news = 3 * PER + 3 * NBQ
+    msg3, msg3x, msg3c, keep3, dens3, slabs4 = call(
+        third_kernel,
+        "slabs_third",
+        [SM, HB] + [VM] * 9,
+        (
+            shape((INROWS + news, LANES), BF), shape((news, LANES), BF),
+            shape((news, LANES), BF), kept[0], kept[2], loaded,
         ),
-        scratch_shapes=[copies] + scratch,
-        compiler_params=PARAMS,
-        cost_estimate=cost,
-    )(where, slabs, slabs2, lt, r, bd, d)
-    out2 = jnp.concatenate([keep_in2, keep2[:PER]], axis=0)
-    out2 = (out2 + near1[: INROWS + PER].astype(F32)).astype(BF)
-    out2, lt = lax.optimization_barrier((out2, lt))
-    cut = INROWS // 2 + NACT
-    far1a = lax.ppermute(out2[:cut], "pair", swap_x)
-    msg3, keep3, dens3, slabs4 = pl.pallas_call(
-        third_kernel,
-        name="slabs_third",
-        in_specs=[SM, HB] + [VM] * 7,
-        out_specs=[VM] * 4,
-        out_shape=(shape((INROWS + 4 * PER + 2 * NBQ, LANES), BF), keep, dens, loaded),
-        scratch_shapes=[copies] + scratch,
-        compiler_params=PARAMS,
-        cost_estimate=cost,
-    )(where, slabs, slabs3, lt, r, bd, d, send2, dens2)
-    near3 = lax.ppermute(msg3, "pair", swap_core)
-    rest, msg3 = lax.optimization_barrier((out2[cut:], msg3))
-    far1b = lax.ppermute(rest, "pair", swap_x)
+        [copies, pltpu.VMEM((3, PER, LANES), BF)] + scratch,
+        (where, slabs, slabs3, lt, r, bd, d, sends1, sends2, dens1, dens2),
+        work,
+    )
+    near3 = to_peer(1, msg3)
+    far1b = to_peer(2, out2[cut:])
+    far3, cross3 = to_peer(2, msg3x), to_peer(3, msg3c)
     far1a, lt = lax.optimization_barrier((far1a, lt))
-    msg4, keep_in4, keep4, dens4 = pl.pallas_call(
+    keep_in4, keep4, sends4, dens4 = call(
         fourth_kernel,
-        name="slabs_fourth",
-        in_specs=[SM] + [VM] * 5,
-        out_specs=[VM] * 4,
-        out_shape=(
-            shape((2 * PER + NBQ, LANES), BF), shape((INROWS, LANES), F32), keep, dens,
+        "slabs_fourth",
+        [SM] + [VM] * 5,
+        (shape((INROWS, LANES), F32),) + kept,
+        scratch,
+        (where, slabs4, lt, r, bd, d),
+        work,
+    )
+    last = shape((PER + NBQ + QUARTER, LANES), BF)
+    near4, far4, cross4, exch = call(
+        exchange_kernel,
+        "exchange",
+        [SM] + [VM] * 6,
+        (last,) * 3 + (shape((QUARTER, LANES), F32),),
+        [pltpu.VMEM((NACT, LANES), F32)],
+        (where, keep_in4, near3, far1a, far1b, sends4, dens4),
+    )
+    far4, cross4, near4 = to_peer(2, far4), to_peer(3, cross4), to_peer(1, near4)
+    act, partial = call(
+        coulomb_kernel,
+        "coulomb",
+        [VM] * 15,
+        (shape((4 * PER, LANES), F32), shape((QUARTER, NACT), F32)),
+        [],
+        (
+            keep1, keep2, keep3, keep4, dens1, dens2, dens3, dens4, exch,
+            near3, far3, cross3, near4, far4, cross4,
         ),
-        scratch_shapes=scratch,
-        compiler_params=PARAMS,
-        cost_estimate=cost,
-    )(where, slabs4, lt, r, bd, d)
-    msg4, exch = pl.pallas_call(
-        exchange_kernel,
-        name="exchange",
-        in_specs=[SM] + [VM] * 5,
-        out_specs=[VM] * 2,
-        out_shape=(
-            shape((2 * PER + NBQ + 2 * QUARTER, LANES), BF),
-            shape((2 * QUARTER, LANES), F32),
-        ),
-        scratch_shapes=[pltpu.VMEM((NACT, LANES), F32)],
-        compiler_params=PARAMS,
-    )(where, keep_in4, near3, far1a, far1b, msg4)
-    near4 = lax.ppermute(msg4, "pair", swap_core)
-    msg5, act, dens, exch = pl.pallas_call(
-        gather_kernel,
-        name="active_of_chip",
-        in_specs=[VM] * 13,
-        out_specs=[VM] * 4,
-        out_shape=(
-            shape((3 * PER + 4 * NBQ + QUARTER, LANES), BF),
-            shape((4 * PER, LANES), F32),
-            shape((4 * NBQ, LANES), F32),
-            shape((QUARTER, LANES), F32),
-        ),
-        compiler_params=PARAMS,
-    )(keep1, keep2, keep3, keep4, dens1, dens2, dens3, dens4, exch, near1, near3, near4, far1b)
-    far5 = lax.ppermute(msg5, "pair", swap_x)
-    partial = pl.pallas_call(
-        coulomb_kernel,
-        name="coulomb",
-        in_specs=[VM] * 4,
-        out_specs=VM,
-        out_shape=shape((QUARTER, NACT), F32),
-        compiler_params=PARAMS,
-    )(act, far5, dens, exch)
-    active = pl.pallas_call(
+    )
+    (active,) = call(
         active_kernel,
-        name="own_active",
-        in_specs=[SM, VM, VM],
-        out_specs=VM,
-        out_shape=shape((batch, QUARTER, NACT), F32),
-        compiler_params=PARAMS,
-        cost_estimate=pl.CostEstimate(flops=10**6, bytes_accessed=10**6, transcendentals=0),
-    )(where, act, far5)
+        "own_active",
+        [SM, VM],
+        (shape((batch, QUARTER, NACT), F32),),
+        [],
+        (where, act),
+        10**6,
+    )
     return (active, hcore + sum_over_aux(partial))
 
 

time: 47.4 us -> 44.9 us (0.947)
  waiting for transfers between devices: 10.6 us -> 6.02 us
  starting transfers between devices: 8.25 us -> 11.7 us
  local copies, waits for them, and re-layouts: 3.41 us -> 0.03 us
  Pallas kernels: 22.8 us -> 24.8 us
    ppermute x6 -> x9, waiting for transfers between devices: 8.06 us -> 3.46 us  [to_peer(): return lax.ppermute(array, 'pair', [(p, p ^ k) for p in range(4)])]
    ppermute x6 -> x9, starting transfers between devices: 4.08 us -> 7.53 us  [to_peer(): return lax.ppermute(array, 'pair', [(p, p ^ k) for p in range(4)])]
    unnamed x4 -> x2, local copies, waits for them, and re-layouts: 3.39 us -> 0.01 us
    pallas_call x8 -> x7, Pallas kernels: 22.8 us -> 24.8 us  [call(): pl.pallas_call(kernel, name=name, in_specs=inputs, out_specs=[VM] * len(o...]
  transfers between devices with their start and end apart: 8 -> 11, of which waited for: 5 -> 4; matrix products, arithmetic and copies ran while one was open for 0% -> 0% of each run, Pallas kernels for 31% -> 38%
where the time goes in v10:
time: 44.9 us; the launch traced here: 44.7 us
  Pallas kernels  24.8 us (55%)
  starting transfers between devices  11.7 us (26%)
  waiting for transfers between devices  6.02 us (13%)
  between operations  1.39 us (3%)
  other arithmetic  0.74 us (2%)
    pallas_call x7, Pallas kernels, call(): pl.pallas_call(kernel, name=name, in_specs=inputs, out_specs=[VM] * len(o...  24.8 us
    ppermute x9, starting transfers between devices, to_peer(): return lax.ppermute(array, 'pair', [(p, p ^ k) for p in range(4)])  7.53 us
    ppermute x2, starting transfers between devices, sum_over_aux(): part = part + lax.ppermute(part, 'aux', [(z, z ^ k) for z in range(n)])  4.18 us
    ppermute x9, waiting for transfers between devices, to_peer(): return lax.ppermute(array, 'pair', [(p, p ^ k) for p in range(4)])  3.46 us
    ppermute x2, waiting for transfers between devices, sum_over_aux(): part = part + lax.ppermute(part, 'aux', [(z, z ^ k) for z in range(n)])  2.57 us
  transfers between devices with their start and end apart: 11, of which 4 were waited for; matrix products, arithmetic and copies ran while one was open for 0% of the time, Pallas kernels for 38%

profile of v10, /device:TPU:0, one launch (start us, length us, event | category | flops | bytes accessed | tf_op | source)
XLA Modules:
  0.0 44.7 jit_solution(4611615052264156023)
XLA Ops:
  1.3 0.1 pad_add_fusion.where
  1.4 7.7 %slabs_first.1 = (bf16[192,1024]{1,0:T(8,128)(2,1)S(1)}, bf16[1024,256]{1,0:T(8,128)(2,1)S(1)}, bf16[4,256,256]{2,1,0:T(8,128)(2,1)S(1)}, f32[8,64,128]{2,1,0:T(...) custom-call(s32[2]{0:T(128)S(1)} %pad_add_fusion.where, ...), custom_call_target="tpu_custom_call" | custom-call | flops 5000000000 | bytes 100000 | tf_op jit(solution)/shard_map/slabs_first/pallas_call | solution.py:407
  9.1 0.5 %collective-permute-start = (bf16[1024,128]{1,0:T(8,128)(2,1)S(1)}, bf16[1024,128]{1,0:T(8,128)(2,1)S(1)}, u32[]{:S(2)}, u32[]{:S(2)}) collective-permute-start(bf16[1024,128]{1,0:T(8,128)(2,1)S(1)} %get-tuple-element.45), channel_id=1, source_target_pairs={{0,4},{4,0},{8,12},{12,8},{1,5},{5,1},{9,13},{13,9},{2,6},{6,2},{1... | collective-permute-start | bytes 786440 | tf_op jit(solution)/shard_map/ppermute | solution.py:427
  9.6 5.3 %slabs_second.1 = (f32[1024,128]{1,0:T(8,128)S(1)}, f32[128,128]{1,0:T(8,128)S(1)}, bf16[3,128,128]{2,1,0:T(8,128)(2,1)S(1)}, f32[16,128]{1,0:T(8,128)S(1)}, bf16[8,2,16,4096]{3,2,1,0:T(8,128)(2,1)S(1)}) custom-call(s32[2]{0:T(128)S(1)} %pad_add_fusion.where, bf16[16,64,4096]{2,1,0:T(8,128)(2,1)} %slabs_ref.5, ...), custom_call_target="tpu_custom_call" | custom-call | flops 5000000000 | bytes 100000 | tf_op jit(solution)/shard_map/slabs_second/pallas_call | solution.py:407
  14.9 0.1 add_convert_fusion
  15.0 2.6 %collective-permute-start.1 = (bf16[256,128]{1,0:T(8,128)(2,1)S(1)}, bf16[256,128]{1,0:T(8,128)(2,1)S(1)}, u32[]{:S(2)}, u32[]{:S(2)}) collective-permute-start(bf16[256,128]{1,0:T(8,128)(2,1)S(1)} %slice.6), channel_id=1, source_target_pairs={{0,8},{4,12},{8,0},{12,4},{1,9},{5,13},{9,1},{13,5},{2,10},{6,14},... | collective-permute-start | bytes 196616 | tf_op jit(solution)/shard_map/ppermute | solution.py:427
  17.6 0.1 collective-permute-start.3
  17.6 5.4 %slabs_third.1 = (bf16[1456,128]{1,0:T(8,128)(2,1)S(1)}, bf16[432,128]{1,0:T(8,128)(2,1)S(1)}, bf16[432,128]{1,0:T(8,128)(2,1)S(1)}, f32[128,128]{1,0:T(8,128)S(...) custom-call(s32[2]{0:T(128)S(1)} %pad_add_fusion.where, bf16[16,64,4096]{2,1,0:T(8,128)(2,1)} %slabs_ref.5, ...), custom_call_target="tpu_custom_call" | custom-call | flops 5000000000 | bytes 100000 | tf_op jit(solution)/shard_map/slabs_third/pallas_call | solution.py:407
  23.0 2.0 %collective-permute-start.4 = (bf16[432,128]{1,0:T(8,128)(2,1)S(1)}, bf16[432,128]{1,0:T(8,128)(2,1)S(1)}, u32[]{:S(2)}, u32[]{:S(2)}) collective-permute-start(bf16[432,128]{1,0:T(8,128)(2,1)S(1)} %get-tuple-element.63), channel_id=1, source_target_pairs={{0,8},{4,12},{8,0},{12,4},{1,9},{5,13},{9,1},{13,5},{2,10},{6,14},... | collective-permute-start | bytes 331784 | tf_op jit(solution)/shard_map/ppermute | solution.py:427
  25.0 0.2 collective-permute-start.2
  25.2 3.9 %slabs_fourth.1 = (f32[1024,128]{1,0:T(8,128)S(1)}, f32[128,128]{1,0:T(8,128)S(1)}, bf16[3,128,128]{2,1,0:T(8,128)(2,1)S(1)}, f32[16,128]{1,0:T(8,128)S(1)}) custom-call(s32[2]{0:T(128)S(1)} %pad_add_fusion.where, bf16[8,2,16,4096]{3,2,1,0:T(8,128)(2,1)S(1)} %get-tuple-element.52.sbuf, bf16[192,1024]{1,0:T(8,128)(2,1)S(1)} %get-tuple-element.54.lt_ref, ...), custom_call_target="tpu_custom_call" | custom-call | flops 5000000000 | bytes 100000 | tf_op jit(solution)/shard_map/slabs_fourth/pallas_call | solution.py:407
  29.2 0.9 %exchange.1 = (bf16[160,128]{1,0:T(8,128)(2,1)S(1)}, bf16[160,128]{1,0:T(8,128)(2,1)S(1)}, bf16[160,128]{1,0:T(8,128)(2,1)S(1)}, f32[16,128]{1,0:T(8,128)S(1)}) custom-call(s32[2]{0:T(128)S(1)} %pad_add_fusion.where, f32[1024,128]{1,0:T(8,128)S(1)} %get-tuple-element.58.mine, bf16[1456,128]{1,0:T(8,128)(2,1)S(1)} %collective-permute-done.2.near3, ...), custom_call_target="tpu_custom_call" | custom-call | bytes 100000 | tf_op jit(solution)/shard_map/exchange/pallas_call | solution.py:407
  30.0 0.4 collective-permute-start.6
  30.4 1.7 %collective-permute-start.7 = (bf16[160,128]{1,0:T(8,128)(2,1)S(1)}, bf16[160,128]{1,0:T(8,128)(2,1)S(1)}, u32[]{:S(2)}, u32[]{:S(2)}) collective-permute-start(bf16[160,128]{1,0:T(8,128)(2,1)S(1)} %get-tuple-element.66), channel_id=1, source_target_pairs={{0,8},{4,12},{8,0},{12,4},{1,9},{5,13},{9,1},{13,5},{2,10},{6,14},... | collective-permute-start | bytes 122888 | tf_op jit(solution)/shard_map/ppermute | solution.py:427
  32.1 0.1 collective-permute-start.8
  32.2 2.2 %collective-permute-done.7.far4 = bf16[160,128]{1,0:T(8,128)(2,1)S(1)} collective-permute-done((bf16[160,128]{1,0:T(8,128)(2,1)S(1)}, bf16[160,128]{1,0:T(8,128)(2,1)S(1)}, u32[]{:S(2)}, u32[]{:S(2)}) %collective-permute-start.7) | collective-permute-done | bytes 40992 | tf_op jit(solution)/shard_map/ppermute | solution.py:427
  34.4 1.2 %collective-permute-done.8.cross4 = bf16[160,128]{1,0:T(8,128)(2,1)S(1)} collective-permute-done((bf16[160,128]{1,0:T(8,128)(2,1)S(1)}, bf16[160,128]{1,0:T(8,128)(2,1)S(1)}, u32[]{:S(2)}, u32[]{:S(2)}) %collective-permute-start.8) | collective-permute-done | bytes 40992 | tf_op jit(solution)/shard_map/ppermute | solution.py:427
  35.6 0.2 coulomb.1
  35.9 1.6 %collective-permute-start.9 = (f32[16,64]{1,0:T(8,128)S(1)}, f32[16,64]{1,0:T(8,128)S(1)}, u32[]{:S(2)}, u32[]{:S(2)}) collective-permute-start(f32[16,64]{1,0:T(8,128)S(1)} %get-tuple-element.69), channel_id=1, source_target_pairs={{0,1},{1,0},{2,3},{3,2},{4,5},{5,4},{6,7},{7,6},{8,9},{9,8},{10,11... | collective-permute-start | bytes 12296 | tf_op jit(solution)/shard_map/ppermute | solution.py:402
  37.4 2.1 %collective-permute-done.9 = f32[16,64]{1,0:T(8,128)S(1)} collective-permute-done((f32[16,64]{1,0:T(8,128)S(1)}, f32[16,64]{1,0:T(8,128)S(1)}, u32[]{:S(2)}, u32[]{:S(2)}) %collective-permute-start.9) | collective-permute-done | bytes 4128 | tf_op jit(solution)/shard_map/ppermute | solution.py:402
  39.5 2.6 %collective-permute-start.10 = (f32[16,64]{1,0:T(8,128)S(1)}, f32[16,64]{1,0:T(8,128)S(1)}, u32[]{:S(2)}, u32[]{:S(2)}) collective-permute-start(f32[16,64]{1,0:T(8,128)S(1)} %add.14), channel_id=1, source_target_pairs={{0,2},{1,3},{2,0},{3,1},{4,6},{5,7},{6,4},{7,5},{8,10},{9,11},{10,... | collective-permute-start | bytes 12296 | tf_op jit(solution)/shard_map/ppermute | solution.py:402
  42.1 1.5 %own_active.1 = f32[64,16,64]{2,1,0:T(8,128)} custom-call(s32[2]{0:T(128)S(1)} %pad_add_fusion.where, f32[512,128]{1,0:T(8,128)S(1)} %get-tuple-element.68.act), custom_call_target="tpu_custom_call" | custom-call | flops 1000000 | bytes 100000 | tf_op jit(solution)/shard_map/own_active/pallas_call | solution.py:407
  43.6 0.5 %collective-permute-done.10 = f32[16,64]{1,0:T(8,128)S(1)} collective-permute-done((f32[16,64]{1,0:T(8,128)S(1)}, f32[16,64]{1,0:T(8,128)S(1)}, u32[]{:S(2)}, u32[]{:S(2)}) %collective-permute-start.10) | collective-permute-done | bytes 4128 | tf_op jit(solution)/shard_map/ppermute | solution.py:402
  44.1 0.6 %add_add_fusion = f32[16,64]{1,0:T(8,128)} fusion(f32[16,64]{1,0:T(8,128)S(1)} %copy-done, f32[16,64]{1,0:T(8,128)S(1)} %add.14, f32[16,64]{1,0:T(8,128)S(1)} %collective-permute-done.10), kind=kLoop, calls=%fused_computation.1 | loop fusion | flops 2048 | bytes 16384 | tf_op jit(solution)/shard_map/add | solution.py:532
  (13 shorter events, 0.1 us)
Async XLA Ops:
  9.1 5.8 %collective-permute-start = (bf16[1024,128]{1,0:T(8,128)(2,1)S(1)}, bf16[1024,128]{1,0:T(8,128)(2,1)S(1)}, u32[]{:S(2)}, u32[]{:S(2)}) collective-permute-start(bf16[1024,128]{1,0:T(8,128)(2,1)S(1)} %get-tuple-element.45), channel_id=1, source_target_pairs={{0,4},{4,0},{8,12},{12,8},{1,5},{5,1},{9,13},{13,9},{2,6},{6,2},{1... | collective-permute-start | bytes 786440 | tf_op jit(solution)/shard_map/ppermute | solution.py:427
  15.0 10.2 %collective-permute-start.1 = (bf16[256,128]{1,0:T(8,128)(2,1)S(1)}, bf16[256,128]{1,0:T(8,128)(2,1)S(1)}, u32[]{:S(2)}, u32[]{:S(2)}) collective-permute-start(bf16[256,128]{1,0:T(8,128)(2,1)S(1)} %slice.6), channel_id=1, source_target_pairs={{0,8},{4,12},{8,0},{12,4},{1,9},{5,13},{9,1},{13,5},{2,10},{6,14},... | collective-permute-start | bytes 196616 | tf_op jit(solution)/shard_map/ppermute | solution.py:427
  17.6 11.6 %collective-permute-start.3 = (bf16[768,128]{1,0:T(8,128)(2,1)S(1)}, bf16[768,128]{1,0:T(8,128)(2,1)S(1)}, u32[]{:S(2)}, u32[]{:S(2)}) collective-permute-start(bf16[768,128]{1,0:T(8,128)(2,1)S(1)} %slice.7), channel_id=1, source_target_pairs={{0,8},{4,12},{8,0},{12,4},{1,9},{5,13},{9,1},{13,5},{2,10},{6,14},... | collective-permute-start | bytes 589832 | tf_op jit(solution)/shard_map/ppermute | solution.py:427
  23.0 9.2 %collective-permute-start.4 = (bf16[432,128]{1,0:T(8,128)(2,1)S(1)}, bf16[432,128]{1,0:T(8,128)(2,1)S(1)}, u32[]{:S(2)}, u32[]{:S(2)}) collective-permute-start(bf16[432,128]{1,0:T(8,128)(2,1)S(1)} %get-tuple-element.63), channel_id=1, source_target_pairs={{0,8},{4,12},{8,0},{12,4},{1,9},{5,13},{9,1},{13,5},{2,10},{6,14},... | collective-permute-start | bytes 331784 | tf_op jit(solution)/shard_map/ppermute | solution.py:427
  25.0 7.2 %collective-permute-start.5 = (bf16[432,128]{1,0:T(8,128)(2,1)S(1)}, bf16[432,128]{1,0:T(8,128)(2,1)S(1)}, u32[]{:S(2)}, u32[]{:S(2)}) collective-permute-start(bf16[432,128]{1,0:T(8,128)(2,1)S(1)} %get-tuple-element.64), channel_id=1, source_target_pairs={{0,12},{4,8},{8,4},{12,0},{1,13},{5,9},{9,5},{13,1},{2,14},{6,10},... | collective-permute-start | bytes 331784 | tf_op jit(solution)/shard_map/ppermute | solution.py:427
  25.0 4.1 %collective-permute-start.2 = (bf16[1456,128]{1,0:T(8,128)(2,1)S(1)}, bf16[1456,128]{1,0:T(8,128)(2,1)S(1)}, u32[]{:S(2)}, u32[]{:S(2)}) collective-permute-start(bf16[1456,128]{1,0:T(8,128)(2,1)S(1)} %get-tuple-element.59), channel_id=1, source_target_pairs={{0,4},{4,0},{8,12},{12,8},{1,5},{5,1},{9,13},{13,9},{2,6},{6,2},{1... | collective-permute-start | bytes 1118216 | tf_op jit(solution)/shard_map/ppermute | solution.py:427
  29.1 14.9 %copy-start = (f32[16,64]{1,0:T(8,128)S(1)}, f32[16,64]{1,0:T(8,128)}, u32[]{:S(2)}) copy-start(f32[16,64]{1,0:T(8,128)} %param.11) | copy-start | bytes 12292
  30.0 2.2 %collective-permute-start.6 = (bf16[160,128]{1,0:T(8,128)(2,1)S(1)}, bf16[160,128]{1,0:T(8,128)(2,1)S(1)}, u32[]{:S(2)}, u32[]{:S(2)}) collective-permute-start(bf16[160,128]{1,0:T(8,128)(2,1)S(1)} %get-tuple-element.65), channel_id=1, source_target_pairs={{0,4},{4,0},{8,12},{12,8},{1,5},{5,1},{9,13},{13,9},{2,6},{6,2},{1... | collective-permute-start | bytes 122888 | tf_op jit(solution)/shard_map/ppermute | solution.py:427
  30.4 4.0 %collective-permute-start.7 = (bf16[160,128]{1,0:T(8,128)(2,1)S(1)}, bf16[160,128]{1,0:T(8,128)(2,1)S(1)}, u32[]{:S(2)}, u32[]{:S(2)}) collective-permute-start(bf16[160,128]{1,0:T(8,128)(2,1)S(1)} %get-tuple-element.66), channel_id=1, source_target_pairs={{0,8},{4,12},{8,0},{12,4},{1,9},{5,13},{9,1},{13,5},{2,10},{6,14},... | collective-permute-start | bytes 122888 | tf_op jit(solution)/shard_map/ppermute | solution.py:427
  32.1 3.5 %collective-permute-start.8 = (bf16[160,128]{1,0:T(8,128)(2,1)S(1)}, bf16[160,128]{1,0:T(8,128)(2,1)S(1)}, u32[]{:S(2)}, u32[]{:S(2)}) collective-permute-start(bf16[160,128]{1,0:T(8,128)(2,1)S(1)} %get-tuple-element.67), channel_id=1, source_target_pairs={{0,12},{4,8},{8,4},{12,0},{1,13},{5,9},{9,5},{13,1},{2,14},{6,10},... | collective-permute-start | bytes 122888 | tf_op jit(solution)/shard_map/ppermute | solution.py:427
  35.9 3.7 %collective-permute-start.9 = (f32[16,64]{1,0:T(8,128)S(1)}, f32[16,64]{1,0:T(8,128)S(1)}, u32[]{:S(2)}, u32[]{:S(2)}) collective-permute-start(f32[16,64]{1,0:T(8,128)S(1)} %get-tuple-element.69), channel_id=1, source_target_pairs={{0,1},{1,0},{2,3},{3,2},{4,5},{5,4},{6,7},{7,6},{8,9},{9,8},{10,11... | collective-permute-start | bytes 12296 | tf_op jit(solution)/shard_map/ppermute | solution.py:402
  39.5 4.5 %collective-permute-start.10 = (f32[16,64]{1,0:T(8,128)S(1)}, f32[16,64]{1,0:T(8,128)S(1)}, u32[]{:S(2)}, u32[]{:S(2)}) collective-permute-start(f32[16,64]{1,0:T(8,128)S(1)} %add.14), channel_id=1, source_target_pairs={{0,2},{1,3},{2,0},{3,1},{4,6},{5,7},{6,4},{7,5},{8,10},{9,11},{10,... | collective-permute-start | bytes 12296 | tf_op jit(solution)/shard_map/ppermute | solution.py:402

commit v11 on v10

--- a/solution.py
+++ b/solution.py
@@ -44,7 +44,7 @@
     ]
 
 
-def run_block(sbuf, weights, scratch, emit, ready=None, midway=None):
+def run_block(sbuf, weights, scratch, emit, ready=None, ahead=()):
     lt_ref, r_ref, bd_ref, d_ref = weights
     pt_ref, q_ref, diag = scratch[4:]
     quads = sbuf.shape[0] // 2
@@ -144,8 +144,8 @@
         if g + 1 < quads:
             load(g + 1)
         transform(g, scratch[2 * (g % 2) : 2 * (g % 2) + 2])
-    if midway is not None:
-        midway()
+        for copy in ahead[2 * g : 2 * g + 2]:
+            copy.start()
     whole = second_transform(0)
     for g in range(NBQ // 4):
         following = second_transform(g + 1) if g + 1 < NBQ // 4 else None
@@ -205,7 +205,7 @@
         for n in range(NCOL // part)
     ]
     now = slab_copies(slabs_ref, sbuf, bsem, 2 * (1 - x) + (1 - core))
-    for copy in now[:2] + small + now[2:]:
+    for copy in small[:2] + now[:2] + small[2:]:
         copy.start()
     ahead = slab_copies(slabs_ref, after, sem, 2 * (1 - x) + core)
     bd_out[...] = jnp.zeros_like(bd_out)
@@ -215,7 +215,7 @@
         right = orbital_pair(k, cols, live[0], orbitals)
         at = slice(k * PAIRED, (k + 1) * PAIRED)
         lt_out[:, at] = left
-        turned = jnp.concatenate([right, right[NIN:]], axis=0).astype(F32).T.astype(BF)
+        turned = jnp.concatenate([right, right[NIN:]], axis=0).T
         r_out[at, :] = turned
         inner = (lax.broadcasted_iota(jnp.int32, (PAIRED, LANES), 0) < BS) == low_half(PAIRED)
         place = slice((k % 2) * PAIRED, (k % 2 + 1) * PAIRED)
@@ -223,30 +223,29 @@
             inner, turned[:, NIN:], jnp.zeros((PAIRED, LANES), BF)
         )
         both = jnp.dot(
-            left[:NIN].astype(F32).T.astype(BF), right[:NIN], preferred_element_type=F32
+            left[:NIN].T, right[:NIN], preferred_element_type=F32
         )
         d_out[k] = jnp.where(low_half(BS), both[:BS], both[BS:])
 
     def ready(k):
-        if k < 2:
+        if k % 2 == 0:
             now[k].wait()
+            now[k + 1].wait()
+            for copy in now[k + 2 : k + 4]:
+                copy.start()
         if k == 1:
-            for copy in small + now[2:]:
+            for copy in small:
                 copy.wait()
         if k % 2 == 1:
             prepare(k - 1)
             prepare(k)
 
-    def midway():
-        for copy in ahead:
-            copy.start()
-
     def emit(h, in0, in1, act):
         msg[pair_rows(h, 0), :] = in0.astype(BF)
         msg[pair_rows(h, 1), :] = in1.astype(BF)
         emit_active(h, act, core, x, keep, sends)
 
-    run_block(sbuf, (lt_out, r_out, bd_out, d_out), scratch, emit, ready, midway)
+    run_block(sbuf, (lt_out, r_out, bd_out, d_out), scratch, emit, ready, ahead)
     dens[...] = density_of(scratch[6][...])
     for copy in ahead:
         copy.wait()
@@ -259,16 +258,12 @@
     core, x = where[0], where[1]
     ahead = slab_copies(slabs_ref, after, sem, 2 * x + (1 - core))
 
-    def midway():
-        for copy in ahead:
-            copy.start()
-
     def emit(h, in0, in1, act):
         keep_in[pair_rows(h, 0), :] = in0
         keep_in[pair_rows(h, 1), :] = in1
         emit_active(h, act, core, x, keep, sends)
 
-    run_block(sbuf, (lt_ref, r_ref, bd_ref, d_ref), scratch, emit, None, midway)
+    run_block(sbuf, (lt_ref, r_ref, bd_ref, d_ref), scratch, emit, None, ahead)
     dens[...] = density_of(scratch[6][...])
     for copy in ahead:
         copy.wait()
@@ -281,16 +276,12 @@
     core, x = where[0], where[1]
     ahead = slab_copies(slabs_ref, after, sem, 2 * x + core)
 
-    def midway():
-        for copy in ahead:
-            copy.start()
-
     def emit(h, in0, in1, act):
         near[pair_rows(h, 0), :] = in0.astype(BF)
         near[pair_rows(h, 1), :] = in1.astype(BF)
         emit_active(h, act, core, x, keep, sends)
 
-    run_block(sbuf, (lt_ref, r_ref, bd_ref, d_ref), scratch, emit, None, midway)
+    run_block(sbuf, (lt_ref, r_ref, bd_ref, d_ref), scratch, emit, None, ahead)
     dens[...] = density_of(scratch[6][...])
     wires = [split_wire(d[...]) for d in (dens1, dens2, dens)]
     for k, (msg, base) in enumerate(((near, INROWS), (far, 0), (cross, 0))):

time: 44.9 us -> 46.3 us (1.031)
  Pallas kernels: 24.8 us -> 26.1 us
    pallas_call x7, Pallas kernels: 24.8 us -> 26.1 us  [call(): pl.pallas_call(kernel, name=name, in_specs=inputs, out_specs=[VM] * len(o...]
  transfers between devices with their start and end apart: 11 -> 11, of which waited for: 4 -> 4; matrix products, arithmetic and copies ran while one was open for 0% -> 0% of each run, Pallas kernels for 38% -> 37%
where the time goes in v11:
time: 46.3 us; the launch traced here: 46 us
  Pallas kernels  26.1 us (56%)
  starting transfers between devices  11.7 us (25%)
  waiting for transfers between devices  6.02 us (13%)
  between operations  1.39 us (3%)
  other arithmetic  0.74 us (2%)
    pallas_call x7, Pallas kernels, call(): pl.pallas_call(kernel, name=name, in_specs=inputs, out_specs=[VM] * len(o...  26.1 us
    ppermute x9, starting transfers between devices, to_peer(): return lax.ppermute(array, 'pair', [(p, p ^ k) for p in range(4)])  7.53 us
    ppermute x2, starting transfers between devices, sum_over_aux(): part = part + lax.ppermute(part, 'aux', [(z, z ^ k) for z in range(n)])  4.18 us
    ppermute x9, waiting for transfers between devices, to_peer(): return lax.ppermute(array, 'pair', [(p, p ^ k) for p in range(4)])  3.46 us
    ppermute x2, waiting for transfers between devices, sum_over_aux(): part = part + lax.ppermute(part, 'aux', [(z, z ^ k) for z in range(n)])  2.57 us
  transfers between devices with their start and end apart: 11, of which 4 were waited for; matrix products, arithmetic and copies ran while one was open for 0% of the time, Pallas kernels for 37%

profile of v11, /device:TPU:0, one launch (start us, length us, event | category | flops | bytes accessed | tf_op | source)
XLA Modules:
  0.0 46.0 jit_solution(2381975841256364878)
XLA Ops:
  1.3 0.1 pad_add_fusion.where
  1.4 8.8 %slabs_first.1 = (bf16[192,1024]{1,0:T(8,128)(2,1)S(1)}, bf16[1024,256]{1,0:T(8,128)(2,1)S(1)}, bf16[4,256,256]{2,1,0:T(8,128)(2,1)S(1)}, f32[8,64,128]{2,1,0:T(...) custom-call(s32[2]{0:T(128)S(1)} %pad_add_fusion.where, ...), custom_call_target="tpu_custom_call" | custom-call | flops 5000000000 | bytes 100000 | tf_op jit(solution)/shard_map/slabs_first/pallas_call | solution.py:398
  10.2 0.5 %collective-permute-start = (bf16[1024,128]{1,0:T(8,128)(2,1)S(1)}, bf16[1024,128]{1,0:T(8,128)(2,1)S(1)}, u32[]{:S(2)}, u32[]{:S(2)}) collective-permute-start(bf16[1024,128]{1,0:T(8,128)(2,1)S(1)} %get-tuple-element.45), channel_id=1, source_target_pairs={{0,4},{4,0},{8,12},{12,8},{1,5},{5,1},{9,13},{13,9},{2,6},{6,2},{1... | collective-permute-start | bytes 786440 | tf_op jit(solution)/shard_map/ppermute | solution.py:418
  10.7 5.3 %slabs_second.1 = (f32[1024,128]{1,0:T(8,128)S(1)}, f32[128,128]{1,0:T(8,128)S(1)}, bf16[3,128,128]{2,1,0:T(8,128)(2,1)S(1)}, f32[16,128]{1,0:T(8,128)S(1)}, bf16[8,2,16,4096]{3,2,1,0:T(8,128)(2,1)S(1)}) custom-call(s32[2]{0:T(128)S(1)} %pad_add_fusion.where, bf16[16,64,4096]{2,1,0:T(8,128)(2,1)} %slabs_ref.5, ...), custom_call_target="tpu_custom_call" | custom-call | flops 5000000000 | bytes 100000 | tf_op jit(solution)/shard_map/slabs_second/pallas_call | solution.py:398
  16.0 0.1 add_convert_fusion
  16.1 2.6 %collective-permute-start.1 = (bf16[256,128]{1,0:T(8,128)(2,1)S(1)}, bf16[256,128]{1,0:T(8,128)(2,1)S(1)}, u32[]{:S(2)}, u32[]{:S(2)}) collective-permute-start(bf16[256,128]{1,0:T(8,128)(2,1)S(1)} %slice.6), channel_id=1, source_target_pairs={{0,8},{4,12},{8,0},{12,4},{1,9},{5,13},{9,1},{13,5},{2,10},{6,14},... | collective-permute-start | bytes 196616 | tf_op jit(solution)/shard_map/ppermute | solution.py:418
  18.7 0.1 collective-permute-start.3
  18.8 5.4 %slabs_third.1 = (bf16[1456,128]{1,0:T(8,128)(2,1)S(1)}, bf16[432,128]{1,0:T(8,128)(2,1)S(1)}, bf16[432,128]{1,0:T(8,128)(2,1)S(1)}, f32[128,128]{1,0:T(8,128)S(...) custom-call(s32[2]{0:T(128)S(1)} %pad_add_fusion.where, bf16[16,64,4096]{2,1,0:T(8,128)(2,1)} %slabs_ref.5, ...), custom_call_target="tpu_custom_call" | custom-call | flops 5000000000 | bytes 100000 | tf_op jit(solution)/shard_map/slabs_third/pallas_call | solution.py:398
  24.1 2.0 %collective-permute-start.4 = (bf16[432,128]{1,0:T(8,128)(2,1)S(1)}, bf16[432,128]{1,0:T(8,128)(2,1)S(1)}, u32[]{:S(2)}, u32[]{:S(2)}) collective-permute-start(bf16[432,128]{1,0:T(8,128)(2,1)S(1)} %get-tuple-element.63), channel_id=1, source_target_pairs={{0,8},{4,12},{8,0},{12,4},{1,9},{5,13},{9,1},{13,5},{2,10},{6,14},... | collective-permute-start | bytes 331784 | tf_op jit(solution)/shard_map/ppermute | solution.py:418
  26.1 0.2 collective-permute-start.2
  26.3 4.1 %slabs_fourth.1 = (f32[1024,128]{1,0:T(8,128)S(1)}, f32[128,128]{1,0:T(8,128)S(1)}, bf16[3,128,128]{2,1,0:T(8,128)(2,1)S(1)}, f32[16,128]{1,0:T(8,128)S(1)}) custom-call(s32[2]{0:T(128)S(1)} %pad_add_fusion.where, bf16[8,2,16,4096]{3,2,1,0:T(8,128)(2,1)S(1)} %get-tuple-element.52.sbuf, bf16[192,1024]{1,0:T(8,128)(2,1)S(1)} %get-tuple-element.54.lt_ref, ...), custom_call_target="tpu_custom_call" | custom-call | flops 5000000000 | bytes 100000 | tf_op jit(solution)/shard_map/slabs_fourth/pallas_call | solution.py:398
  30.5 0.9 %exchange.1 = (bf16[160,128]{1,0:T(8,128)(2,1)S(1)}, bf16[160,128]{1,0:T(8,128)(2,1)S(1)}, bf16[160,128]{1,0:T(8,128)(2,1)S(1)}, f32[16,128]{1,0:T(8,128)S(1)}) custom-call(s32[2]{0:T(128)S(1)} %pad_add_fusion.where, f32[1024,128]{1,0:T(8,128)S(1)} %get-tuple-element.58.mine, bf16[1456,128]{1,0:T(8,128)(2,1)S(1)} %collective-permute-done.2.near3, ...), custom_call_target="tpu_custom_call" | custom-call | bytes 100000 | tf_op jit(solution)/shard_map/exchange/pallas_call | solution.py:398
  31.3 0.4 collective-permute-start.6
  31.7 1.7 %collective-permute-start.7 = (bf16[160,128]{1,0:T(8,128)(2,1)S(1)}, bf16[160,128]{1,0:T(8,128)(2,1)S(1)}, u32[]{:S(2)}, u32[]{:S(2)}) collective-permute-start(bf16[160,128]{1,0:T(8,128)(2,1)S(1)} %get-tuple-element.66), channel_id=1, source_target_pairs={{0,8},{4,12},{8,0},{12,4},{1,9},{5,13},{9,1},{13,5},{2,10},{6,14},... | collective-permute-start | bytes 122888 | tf_op jit(solution)/shard_map/ppermute | solution.py:418
  33.4 0.1 collective-permute-start.8
  33.5 2.2 %collective-permute-done.7.far4 = bf16[160,128]{1,0:T(8,128)(2,1)S(1)} collective-permute-done((bf16[160,128]{1,0:T(8,128)(2,1)S(1)}, bf16[160,128]{1,0:T(8,128)(2,1)S(1)}, u32[]{:S(2)}, u32[]{:S(2)}) %collective-permute-start.7) | collective-permute-done | bytes 40992 | tf_op jit(solution)/shard_map/ppermute | solution.py:418
  35.7 1.2 %collective-permute-done.8.cross4 = bf16[160,128]{1,0:T(8,128)(2,1)S(1)} collective-permute-done((bf16[160,128]{1,0:T(8,128)(2,1)S(1)}, bf16[160,128]{1,0:T(8,128)(2,1)S(1)}, u32[]{:S(2)}, u32[]{:S(2)}) %collective-permute-start.8) | collective-permute-done | bytes 40992 | tf_op jit(solution)/shard_map/ppermute | solution.py:418
  37.0 0.2 coulomb.1
  37.2 1.6 %collective-permute-start.9 = (f32[16,64]{1,0:T(8,128)S(1)}, f32[16,64]{1,0:T(8,128)S(1)}, u32[]{:S(2)}, u32[]{:S(2)}) collective-permute-start(f32[16,64]{1,0:T(8,128)S(1)} %get-tuple-element.69), channel_id=1, source_target_pairs={{0,1},{1,0},{2,3},{3,2},{4,5},{5,4},{6,7},{7,6},{8,9},{9,8},{10,11... | collective-permute-start | bytes 12296 | tf_op jit(solution)/shard_map/ppermute | solution.py:393
  38.8 2.1 %collective-permute-done.9 = f32[16,64]{1,0:T(8,128)S(1)} collective-permute-done((f32[16,64]{1,0:T(8,128)S(1)}, f32[16,64]{1,0:T(8,128)S(1)}, u32[]{:S(2)}, u32[]{:S(2)}) %collective-permute-start.9) | collective-permute-done | bytes 4128 | tf_op jit(solution)/shard_map/ppermute | solution.py:393
  40.8 2.6 %collective-permute-start.10 = (f32[16,64]{1,0:T(8,128)S(1)}, f32[16,64]{1,0:T(8,128)S(1)}, u32[]{:S(2)}, u32[]{:S(2)}) collective-permute-start(f32[16,64]{1,0:T(8,128)S(1)} %add.14), channel_id=1, source_target_pairs={{0,2},{1,3},{2,0},{3,1},{4,6},{5,7},{6,4},{7,5},{8,10},{9,11},{10,... | collective-permute-start | bytes 12296 | tf_op jit(solution)/shard_map/ppermute | solution.py:393
  43.4 1.5 %own_active.1 = f32[64,16,64]{2,1,0:T(8,128)} custom-call(s32[2]{0:T(128)S(1)} %pad_add_fusion.where, f32[512,128]{1,0:T(8,128)S(1)} %get-tuple-element.68.act), custom_call_target="tpu_custom_call" | custom-call | flops 1000000 | bytes 100000 | tf_op jit(solution)/shard_map/own_active/pallas_call | solution.py:398
  44.9 0.5 %collective-permute-done.10 = f32[16,64]{1,0:T(8,128)S(1)} collective-permute-done((f32[16,64]{1,0:T(8,128)S(1)}, f32[16,64]{1,0:T(8,128)S(1)}, u32[]{:S(2)}, u32[]{:S(2)}) %collective-permute-start.10) | collective-permute-done | bytes 4128 | tf_op jit(solution)/shard_map/ppermute | solution.py:393
  45.4 0.6 %add_add_fusion = f32[16,64]{1,0:T(8,128)} fusion(f32[16,64]{1,0:T(8,128)S(1)} %copy-done, f32[16,64]{1,0:T(8,128)S(1)} %add.14, f32[16,64]{1,0:T(8,128)S(1)} %collective-permute-done.10), kind=kLoop, calls=%fused_computation.1 | loop fusion | flops 2048 | bytes 16384 | tf_op jit(solution)/shard_map/add | solution.py:523
  (13 shorter events, 0.1 us)
Async XLA Ops:
  10.2 5.8 %collective-permute-start = (bf16[1024,128]{1,0:T(8,128)(2,1)S(1)}, bf16[1024,128]{1,0:T(8,128)(2,1)S(1)}, u32[]{:S(2)}, u32[]{:S(2)}) collective-permute-start(bf16[1024,128]{1,0:T(8,128)(2,1)S(1)} %get-tuple-element.45), channel_id=1, source_target_pairs={{0,4},{4,0},{8,12},{12,8},{1,5},{5,1},{9,13},{13,9},{2,6},{6,2},{1... | collective-permute-start | bytes 786440 | tf_op jit(solution)/shard_map/ppermute | solution.py:418
  16.1 10.2 %collective-permute-start.1 = (bf16[256,128]{1,0:T(8,128)(2,1)S(1)}, bf16[256,128]{1,0:T(8,128)(2,1)S(1)}, u32[]{:S(2)}, u32[]{:S(2)}) collective-permute-start(bf16[256,128]{1,0:T(8,128)(2,1)S(1)} %slice.6), channel_id=1, source_target_pairs={{0,8},{4,12},{8,0},{12,4},{1,9},{5,13},{9,1},{13,5},{2,10},{6,14},... | collective-permute-start | bytes 196616 | tf_op jit(solution)/shard_map/ppermute | solution.py:418
  18.7 11.8 %collective-permute-start.3 = (bf16[768,128]{1,0:T(8,128)(2,1)S(1)}, bf16[768,128]{1,0:T(8,128)(2,1)S(1)}, u32[]{:S(2)}, u32[]{:S(2)}) collective-permute-start(bf16[768,128]{1,0:T(8,128)(2,1)S(1)} %slice.7), channel_id=1, source_target_pairs={{0,8},{4,12},{8,0},{12,4},{1,9},{5,13},{9,1},{13,5},{2,10},{6,14},... | collective-permute-start | bytes 589832 | tf_op jit(solution)/shard_map/ppermute | solution.py:418
  24.1 9.4 %collective-permute-start.4 = (bf16[432,128]{1,0:T(8,128)(2,1)S(1)}, bf16[432,128]{1,0:T(8,128)(2,1)S(1)}, u32[]{:S(2)}, u32[]{:S(2)}) collective-permute-start(bf16[432,128]{1,0:T(8,128)(2,1)S(1)} %get-tuple-element.63), channel_id=1, source_target_pairs={{0,8},{4,12},{8,0},{12,4},{1,9},{5,13},{9,1},{13,5},{2,10},{6,14},... | collective-permute-start | bytes 331784 | tf_op jit(solution)/shard_map/ppermute | solution.py:418
  26.1 7.4 %collective-permute-start.5 = (bf16[432,128]{1,0:T(8,128)(2,1)S(1)}, bf16[432,128]{1,0:T(8,128)(2,1)S(1)}, u32[]{:S(2)}, u32[]{:S(2)}) collective-permute-start(bf16[432,128]{1,0:T(8,128)(2,1)S(1)} %get-tuple-element.64), channel_id=1, source_target_pairs={{0,12},{4,8},{8,4},{12,0},{1,13},{5,9},{9,5},{13,1},{2,14},{6,10},... | collective-permute-start | bytes 331784 | tf_op jit(solution)/shard_map/ppermute | solution.py:418
  26.1 4.3 %collective-permute-start.2 = (bf16[1456,128]{1,0:T(8,128)(2,1)S(1)}, bf16[1456,128]{1,0:T(8,128)(2,1)S(1)}, u32[]{:S(2)}, u32[]{:S(2)}) collective-permute-start(bf16[1456,128]{1,0:T(8,128)(2,1)S(1)} %get-tuple-element.59), channel_id=1, source_target_pairs={{0,4},{4,0},{8,12},{12,8},{1,5},{5,1},{9,13},{13,9},{2,6},{6,2},{1... | collective-permute-start | bytes 1118216 | tf_op jit(solution)/shard_map/ppermute | solution.py:418
  30.4 14.9 %copy-start = (f32[16,64]{1,0:T(8,128)S(1)}, f32[16,64]{1,0:T(8,128)}, u32[]{:S(2)}) copy-start(f32[16,64]{1,0:T(8,128)} %param.11) | copy-start | bytes 12292
  31.3 2.2 %collective-permute-start.6 = (bf16[160,128]{1,0:T(8,128)(2,1)S(1)}, bf16[160,128]{1,0:T(8,128)(2,1)S(1)}, u32[]{:S(2)}, u32[]{:S(2)}) collective-permute-start(bf16[160,128]{1,0:T(8,128)(2,1)S(1)} %get-tuple-element.65), channel_id=1, source_target_pairs={{0,4},{4,0},{8,12},{12,8},{1,5},{5,1},{9,13},{13,9},{2,6},{6,2},{1... | collective-permute-start | bytes 122888 | tf_op jit(solution)/shard_map/ppermute | solution.py:418
  31.7 4.0 %collective-permute-start.7 = (bf16[160,128]{1,0:T(8,128)(2,1)S(1)}, bf16[160,128]{1,0:T(8,128)(2,1)S(1)}, u32[]{:S(2)}, u32[]{:S(2)}) collective-permute-start(bf16[160,128]{1,0:T(8,128)(2,1)S(1)} %get-tuple-element.66), channel_id=1, source_target_pairs={{0,8},{4,12},{8,0},{12,4},{1,9},{5,13},{9,1},{13,5},{2,10},{6,14},... | collective-permute-start | bytes 122888 | tf_op jit(solution)/shard_map/ppermute | solution.py:418
  33.4 3.5 %collective-permute-start.8 = (bf16[160,128]{1,0:T(8,128)(2,1)S(1)}, bf16[160,128]{1,0:T(8,128)(2,1)S(1)}, u32[]{:S(2)}, u32[]{:S(2)}) collective-permute-start(bf16[160,128]{1,0:T(8,128)(2,1)S(1)} %get-tuple-element.67), channel_id=1, source_target_pairs={{0,12},{4,8},{8,4},{12,0},{1,13},{5,9},{9,5},{13,1},{2,14},{6,10},... | collective-permute-start | bytes 122888 | tf_op jit(solution)/shard_map/ppermute | solution.py:418
  37.2 3.7 %collective-permute-start.9 = (f32[16,64]{1,0:T(8,128)S(1)}, f32[16,64]{1,0:T(8,128)S(1)}, u32[]{:S(2)}, u32[]{:S(2)}) collective-permute-start(f32[16,64]{1,0:T(8,128)S(1)} %get-tuple-element.69), channel_id=1, source_target_pairs={{0,1},{1,0},{2,3},{3,2},{4,5},{5,4},{6,7},{7,6},{8,9},{9,8},{10,11... | collective-permute-start | bytes 12296 | tf_op jit(solution)/shard_map/ppermute | solution.py:393
  40.8 4.5 %collective-permute-start.10 = (f32[16,64]{1,0:T(8,128)S(1)}, f32[16,64]{1,0:T(8,128)S(1)}, u32[]{:S(2)}, u32[]{:S(2)}) collective-permute-start(f32[16,64]{1,0:T(8,128)S(1)} %add.14), channel_id=1, source_target_pairs={{0,2},{1,3},{2,0},{3,1},{4,6},{5,7},{6,4},{7,5},{8,10},{9,11},{10,... | collective-permute-start | bytes 12296 | tf_op jit(solution)/shard_map/ppermute | solution.py:393

commit v12 on v11

--- a/solution.py
+++ b/solution.py
@@ -44,7 +44,7 @@
     ]
 
 
-def run_block(sbuf, weights, scratch, emit, ready=None, ahead=()):
+def run_block(sbuf, weights, scratch, emit, prepare=None):
     lt_ref, r_ref, bd_ref, d_ref = weights
     pt_ref, q_ref, diag = scratch[4:]
     quads = sbuf.shape[0] // 2
@@ -67,18 +67,21 @@
 
     def transform(g, bufs):
         dens = [d_ref[2 * g + n] for n in range(2)]
+        left = [
+            lt_ref[NIN:, pl.ds(pl.multiple_of((2 * g + n) * LANES, LANES), LANES)]
+            for n in range(2)
+        ]
         for q in range(0, NBQ, group):
             slabs = [[], []]
             for u in range(q, q + group):
-                total = None
+                total = diag[u]
                 for n in range(2):
                     s = bufs[n][pl.ds(u * QSTEP, BS, stride=MSTEP), :]
-                    part = jnp.sum((s * dens[n]).reshape(BS // 8, 8, LANES), axis=0)
-                    total = part if total is None else total + part
+                    total = total + jnp.sum((s * dens[n]).reshape(BS // 8, 8, LANES), axis=0)
                     slabs[n].append(s.astype(BF))
-                diag[u] = total if g == 0 else diag[u] + total
+                diag[u] = total
             for n in range(2):
-                k = 2 * g + n
+                at = pl.ds(pl.multiple_of((2 * g + n) * LANES, LANES), LANES)
                 cols = [
                     jnp.concatenate(
                         [jnp.where(first_s, s, zero), jnp.where(first_s, zero, s)], axis=0
@@ -86,14 +89,10 @@
                     for s in slabs[n]
                 ]
                 p = jnp.dot(
-                    lt_ref[NIN:, k * LANES : (k + 1) * LANES],
-                    jnp.concatenate(cols, axis=1),
-                    preferred_element_type=F32,
+                    left[n], jnp.concatenate(cols, axis=1), preferred_element_type=F32
                 ).astype(BF)
                 for u in range(group):
-                    pt_ref[q + u, :, k * LANES : (k + 1) * LANES] = p[
-                        :, u * LANES : (u + 1) * LANES
-                    ]
+                    pt_ref[q + u, :, at] = p[:, u * LANES : (u + 1) * LANES]
             rows = jnp.concatenate(
                 [jnp.concatenate([s0, s1], axis=1) for s0, s1 in zip(*slabs)], axis=0
             )
@@ -104,9 +103,9 @@
                     q0 = out[u * BS : (u + 1) * BS, lanes]
                     q1 = out[(u + 1) * BS : (u + 2) * BS, lanes]
                     at = slice((q + u) * BS, (q + u + 2) * BS)
-                    row = (4 * g + 2 * n) * BS
-                    q_ref[row : row + BS, at] = jnp.where(first_s, q0, pltpu.roll(q1, BS, 1))
-                    q_ref[row + BS : row + 2 * BS, at] = jnp.where(
+                    row = pl.multiple_of((4 * g + 2 * n) * BS, 2 * BS)
+                    q_ref[pl.ds(row, BS), at] = jnp.where(first_s, q0, pltpu.roll(q1, BS, 1))
+                    q_ref[pl.ds(row + BS, BS), at] = jnp.where(
                         first_s, pltpu.roll(q0, BS, 1), q1
                     )
 
@@ -133,19 +132,28 @@
                 jnp.where(first_s, w0[:, NIN:] + square[:NACT], w1[:, NIN:] + square[NACT:]),
             )
 
-    def load(g):
+    def load(g, bufs):
         for n in range(2):
-            if ready is not None:
-                ready(2 * g + n)
-            relayout(2 * g + n, scratch[2 * (g % 2) + n])
-
-    load(0)
-    for g in range(quads):
-        if g + 1 < quads:
-            load(g + 1)
-        transform(g, scratch[2 * (g % 2) : 2 * (g % 2) + 2])
-        for copy in ahead[2 * g : 2 * g + 2]:
-            copy.start()
+            relayout(2 * g + n, bufs[n])
+
+    def two_quads(i, carry):
+        one, two = scratch[:2], scratch[2:4]
+        after = jnp.minimum(2 * i + 2, quads - 1)
+        if prepare is not None:
+            prepare(2 * i + 1)
+        load(2 * i + 1, two)
+        transform(2 * i, one)
+        if prepare is not None:
+            prepare(after)
+        load(after, one)
+        transform(2 * i + 1, two)
+        return carry
+
+    diag[...] = jnp.zeros_like(diag)
+    load(0, scratch[:2])
+    if prepare is not None:
+        prepare(0)
+    lax.fori_loop(0, quads // 2, two_quads, 0)
     whole = second_transform(0)
     for g in range(NBQ // 4):
         following = second_transform(g + 1) if g + 1 < NBQ // 4 else None
@@ -205,47 +213,41 @@
         for n in range(NCOL // part)
     ]
     now = slab_copies(slabs_ref, sbuf, bsem, 2 * (1 - x) + (1 - core))
-    for copy in small[:2] + now[:2] + small[2:]:
+    for copy in now[:2] + small + now[2:]:
         copy.start()
     ahead = slab_copies(slabs_ref, after, sem, 2 * (1 - x) + core)
     bd_out[...] = jnp.zeros_like(bd_out)
 
-    def prepare(k):
-        left = orbital_pair(k, rows, live[0], orbitals)
-        right = orbital_pair(k, cols, live[0], orbitals)
-        at = slice(k * PAIRED, (k + 1) * PAIRED)
-        lt_out[:, at] = left
-        turned = jnp.concatenate([right, right[NIN:]], axis=0).T
-        r_out[at, :] = turned
-        inner = (lax.broadcasted_iota(jnp.int32, (PAIRED, LANES), 0) < BS) == low_half(PAIRED)
-        place = slice((k % 2) * PAIRED, (k % 2 + 1) * PAIRED)
-        bd_out[k // 2, place, place] = jnp.where(
-            inner, turned[:, NIN:], jnp.zeros((PAIRED, LANES), BF)
-        )
-        both = jnp.dot(
-            left[:NIN].T, right[:NIN], preferred_element_type=F32
-        )
-        d_out[k] = jnp.where(low_half(BS), both[:BS], both[BS:])
-
-    def ready(k):
-        if k % 2 == 0:
-            now[k].wait()
-            now[k + 1].wait()
-            for copy in now[k + 2 : k + 4]:
-                copy.start()
-        if k == 1:
-            for copy in small:
-                copy.wait()
-        if k % 2 == 1:
-            prepare(k - 1)
-            prepare(k)
+    for copy in now + small:
+        copy.wait()
+    for copy in ahead:
+        copy.start()
+
+    def prepare(g):
+        for n in range(2):
+            k = 2 * g + n
+            left = orbital_pair(k, rows, live[0], orbitals)
+            right = orbital_pair(k, cols, live[0], orbitals)
+            at = pl.ds(pl.multiple_of(k * PAIRED, PAIRED), PAIRED)
+            lt_out[:, at] = left
+            turned = jnp.concatenate([right, right[NIN:]], axis=0).astype(F32).T.astype(BF)
+            r_out[at, :] = turned
+            inner = (lax.broadcasted_iota(jnp.int32, (PAIRED, LANES), 0) < BS) == low_half(PAIRED)
+            place = slice(n * PAIRED, (n + 1) * PAIRED)
+            bd_out[g, place, place] = jnp.where(
+                inner, turned[:, NIN:], jnp.zeros((PAIRED, LANES), BF)
+            )
+            both = jnp.dot(
+                left[:NIN].astype(F32).T.astype(BF), right[:NIN], preferred_element_type=F32
+            )
+            d_out[k] = jnp.where(low_half(BS), both[:BS], both[BS:])
 
     def emit(h, in0, in1, act):
         msg[pair_rows(h, 0), :] = in0.astype(BF)
         msg[pair_rows(h, 1), :] = in1.astype(BF)
         emit_active(h, act, core, x, keep, sends)
 
-    run_block(sbuf, (lt_out, r_out, bd_out, d_out), scratch, emit, ready, ahead)
+    run_block(sbuf, (lt_out, r_out, bd_out, d_out), scratch, emit, prepare)
     dens[...] = density_of(scratch[6][...])
     for copy in ahead:
         copy.wait()
@@ -258,12 +260,15 @@
     core, x = where[0], where[1]
     ahead = slab_copies(slabs_ref, after, sem, 2 * x + (1 - core))
 
+    for copy in ahead:
+        copy.start()
+
     def emit(h, in0, in1, act):
         keep_in[pair_rows(h, 0), :] = in0
         keep_in[pair_rows(h, 1), :] = in1
         emit_active(h, act, core, x, keep, sends)
 
-    run_block(sbuf, (lt_ref, r_ref, bd_ref, d_ref), scratch, emit, None, ahead)
+    run_block(sbuf, (lt_ref, r_ref, bd_ref, d_ref), scratch, emit)
     dens[...] = density_of(scratch[6][...])
     for copy in ahead:
         copy.wait()
@@ -276,12 +281,15 @@
     core, x = where[0], where[1]
     ahead = slab_copies(slabs_ref, after, sem, 2 * x + core)
 
+    for copy in ahead:
+        copy.start()
+
     def emit(h, in0, in1, act):
         near[pair_rows(h, 0), :] = in0.astype(BF)
         near[pair_rows(h, 1), :] = in1.astype(BF)
         emit_active(h, act, core, x, keep, sends)
 
-    run_block(sbuf, (lt_ref, r_ref, bd_ref, d_ref), scratch, emit, None, ahead)
+    run_block(sbuf, (lt_ref, r_ref, bd_ref, d_ref), scratch, emit)
     dens[...] = density_of(scratch[6][...])
     wires = [split_wire(d[...]) for d in (dens1, dens2, dens)]
     for k, (msg, base) in enumerate(((near, INROWS), (far, 0), (cross, 0))):

time: 46.3 us -> 44.5 us (0.961)
  Pallas kernels: 26.1 us -> 24.5 us
    pallas_call x7, Pallas kernels: 26.1 us -> 24.5 us  [call(): pl.pallas_call(kernel, name=name, in_specs=inputs, out_specs=[VM] * len(o...]
where the time goes in v12:
time: 44.5 us; the launch traced here: 44.4 us
  Pallas kernels  24.5 us (55%)
  starting transfers between devices  11.7 us (26%)
  waiting for transfers between devices  6.05 us (14%)
  between operations  1.39 us (3%)
  other arithmetic  0.74 us (2%)
    pallas_call x7, Pallas kernels, call(): pl.pallas_call(kernel, name=name, in_specs=inputs, out_specs=[VM] * len(o...  24.5 us
    ppermute x9, starting transfers between devices, to_peer(): return lax.ppermute(array, 'pair', [(p, p ^ k) for p in range(4)])  7.54 us
    ppermute x2, starting transfers between devices, sum_over_aux(): part = part + lax.ppermute(part, 'aux', [(z, z ^ k) for z in range(n)])  4.16 us
    ppermute x9, waiting for transfers between devices, to_peer(): return lax.ppermute(array, 'pair', [(p, p ^ k) for p in range(4)])  3.46 us
    ppermute x2, waiting for transfers between devices, sum_over_aux(): part = part + lax.ppermute(part, 'aux', [(z, z ^ k) for z in range(n)])  2.59 us
  transfers between devices with their start and end apart: 11, of which 4 were waited for; matrix products, arithmetic and copies ran while one was open for 0% of the time, Pallas kernels for 37%

profile of v12, /device:TPU:0, one launch (start us, length us, event | category | flops | bytes accessed | tf_op | source)
XLA Modules:
  0.0 44.4 jit_solution(9245752211247221344)
XLA Ops:
  1.3 0.1 pad_add_fusion.where
  1.4 7.7 %slabs_first.1 = (bf16[192,1024]{1,0:T(8,128)(2,1)S(1)}, bf16[1024,256]{1,0:T(8,128)(2,1)S(1)}, bf16[4,256,256]{2,1,0:T(8,128)(2,1)S(1)}, f32[8,64,128]{2,1,0:T(...) custom-call(s32[2]{0:T(128)S(1)} %pad_add_fusion.where, ...), custom_call_target="tpu_custom_call" | custom-call | flops 5000000000 | bytes 100000 | tf_op jit(solution)/shard_map/slabs_first/pallas_call | solution.py:406
  9.1 0.5 %collective-permute-start = (bf16[1024,128]{1,0:T(8,128)(2,1)S(1)}, bf16[1024,128]{1,0:T(8,128)(2,1)S(1)}, u32[]{:S(2)}, u32[]{:S(2)}) collective-permute-start(bf16[1024,128]{1,0:T(8,128)(2,1)S(1)} %get-tuple-element.45), channel_id=1, source_target_pairs={{0,4},{4,0},{8,12},{12,8},{1,5},{5,1},{9,13},{13,9},{2,6},{6,2},{1... | collective-permute-start | bytes 786440 | tf_op jit(solution)/shard_map/ppermute | solution.py:426
  9.6 4.9 %slabs_second.1 = (f32[1024,128]{1,0:T(8,128)S(1)}, f32[128,128]{1,0:T(8,128)S(1)}, bf16[3,128,128]{2,1,0:T(8,128)(2,1)S(1)}, f32[16,128]{1,0:T(8,128)S(1)}, bf16[8,2,16,4096]{3,2,1,0:T(8,128)(2,1)S(1)}) custom-call(s32[2]{0:T(128)S(1)} %pad_add_fusion.where, bf16[16,64,4096]{2,1,0:T(8,128)(2,1)} %slabs_ref.5, ...), custom_call_target="tpu_custom_call" | custom-call | flops 5000000000 | bytes 100000 | tf_op jit(solution)/shard_map/slabs_second/pallas_call | solution.py:406
  14.5 0.1 add_convert_fusion
  14.6 2.6 %collective-permute-start.1 = (bf16[256,128]{1,0:T(8,128)(2,1)S(1)}, bf16[256,128]{1,0:T(8,128)(2,1)S(1)}, u32[]{:S(2)}, u32[]{:S(2)}) collective-permute-start(bf16[256,128]{1,0:T(8,128)(2,1)S(1)} %slice.6), channel_id=1, source_target_pairs={{0,8},{4,12},{8,0},{12,4},{1,9},{5,13},{9,1},{13,5},{2,10},{6,14},... | collective-permute-start | bytes 196616 | tf_op jit(solution)/shard_map/ppermute | solution.py:426
  17.1 0.1 collective-permute-start.3
  17.2 4.8 %slabs_third.1 = (bf16[1456,128]{1,0:T(8,128)(2,1)S(1)}, bf16[432,128]{1,0:T(8,128)(2,1)S(1)}, bf16[432,128]{1,0:T(8,128)(2,1)S(1)}, f32[128,128]{1,0:T(8,128)S(...) custom-call(s32[2]{0:T(128)S(1)} %pad_add_fusion.where, bf16[16,64,4096]{2,1,0:T(8,128)(2,1)} %slabs_ref.5, ...), custom_call_target="tpu_custom_call" | custom-call | flops 5000000000 | bytes 100000 | tf_op jit(solution)/shard_map/slabs_third/pallas_call | solution.py:406
  22.0 2.0 %collective-permute-start.4 = (bf16[432,128]{1,0:T(8,128)(2,1)S(1)}, bf16[432,128]{1,0:T(8,128)(2,1)S(1)}, u32[]{:S(2)}, u32[]{:S(2)}) collective-permute-start(bf16[432,128]{1,0:T(8,128)(2,1)S(1)} %get-tuple-element.63), channel_id=1, source_target_pairs={{0,8},{4,12},{8,0},{12,4},{1,9},{5,13},{9,1},{13,5},{2,10},{6,14},... | collective-permute-start | bytes 331784 | tf_op jit(solution)/shard_map/ppermute | solution.py:426
  24.1 0.2 collective-permute-start.2
  24.3 4.6 %slabs_fourth.1 = (f32[1024,128]{1,0:T(8,128)S(1)}, f32[128,128]{1,0:T(8,128)S(1)}, bf16[3,128,128]{2,1,0:T(8,128)(2,1)S(1)}, f32[16,128]{1,0:T(8,128)S(1)}) custom-call(s32[2]{0:T(128)S(1)} %pad_add_fusion.where, bf16[8,2,16,4096]{3,2,1,0:T(8,128)(2,1)S(1)} %get-tuple-element.52.sbuf, bf16[192,1024]{1,0:T(8,128)(2,1)S(1)} %get-tuple-element.54.lt_ref, ...), custom_call_target="tpu_custom_call" | custom-call | flops 5000000000 | bytes 100000 | tf_op jit(solution)/shard_map/slabs_fourth/pallas_call | solution.py:406
  28.9 0.9 %exchange.1 = (bf16[160,128]{1,0:T(8,128)(2,1)S(1)}, bf16[160,128]{1,0:T(8,128)(2,1)S(1)}, bf16[160,128]{1,0:T(8,128)(2,1)S(1)}, f32[16,128]{1,0:T(8,128)S(1)}) custom-call(s32[2]{0:T(128)S(1)} %pad_add_fusion.where, f32[1024,128]{1,0:T(8,128)S(1)} %get-tuple-element.58.mine, bf16[1456,128]{1,0:T(8,128)(2,1)S(1)} %collective-permute-done.2.near3, ...), custom_call_target="tpu_custom_call" | custom-call | bytes 100000 | tf_op jit(solution)/shard_map/exchange/pallas_call | solution.py:406
  29.7 0.4 collective-permute-start.6
  30.1 1.7 %collective-permute-start.7 = (bf16[160,128]{1,0:T(8,128)(2,1)S(1)}, bf16[160,128]{1,0:T(8,128)(2,1)S(1)}, u32[]{:S(2)}, u32[]{:S(2)}) collective-permute-start(bf16[160,128]{1,0:T(8,128)(2,1)S(1)} %get-tuple-element.66), channel_id=1, source_target_pairs={{0,8},{4,12},{8,0},{12,4},{1,9},{5,13},{9,1},{13,5},{2,10},{6,14},... | collective-permute-start | bytes 122888 | tf_op jit(solution)/shard_map/ppermute | solution.py:426
  31.8 0.1 collective-permute-start.8
  31.9 2.2 %collective-permute-done.7.far4 = bf16[160,128]{1,0:T(8,128)(2,1)S(1)} collective-permute-done((bf16[160,128]{1,0:T(8,128)(2,1)S(1)}, bf16[160,128]{1,0:T(8,128)(2,1)S(1)}, u32[]{:S(2)}, u32[]{:S(2)}) %collective-permute-start.7) | collective-permute-done | bytes 40992 | tf_op jit(solution)/shard_map/ppermute | solution.py:426
  34.1 1.2 %collective-permute-done.8.cross4 = bf16[160,128]{1,0:T(8,128)(2,1)S(1)} collective-permute-done((bf16[160,128]{1,0:T(8,128)(2,1)S(1)}, bf16[160,128]{1,0:T(8,128)(2,1)S(1)}, u32[]{:S(2)}, u32[]{:S(2)}) %collective-permute-start.8) | collective-permute-done | bytes 40992 | tf_op jit(solution)/shard_map/ppermute | solution.py:426
  35.4 0.2 coulomb.1
  35.6 1.6 %collective-permute-start.9 = (f32[16,64]{1,0:T(8,128)S(1)}, f32[16,64]{1,0:T(8,128)S(1)}, u32[]{:S(2)}, u32[]{:S(2)}) collective-permute-start(f32[16,64]{1,0:T(8,128)S(1)} %get-tuple-element.69), channel_id=1, source_target_pairs={{0,1},{1,0},{2,3},{3,2},{4,5},{5,4},{6,7},{7,6},{8,9},{9,8},{10,11... | collective-permute-start | bytes 12296 | tf_op jit(solution)/shard_map/ppermute | solution.py:401
  37.1 2.1 %collective-permute-done.9 = f32[16,64]{1,0:T(8,128)S(1)} collective-permute-done((f32[16,64]{1,0:T(8,128)S(1)}, f32[16,64]{1,0:T(8,128)S(1)}, u32[]{:S(2)}, u32[]{:S(2)}) %collective-permute-start.9) | collective-permute-done | bytes 4128 | tf_op jit(solution)/shard_map/ppermute | solution.py:401
  39.2 2.6 %collective-permute-start.10 = (f32[16,64]{1,0:T(8,128)S(1)}, f32[16,64]{1,0:T(8,128)S(1)}, u32[]{:S(2)}, u32[]{:S(2)}) collective-permute-start(f32[16,64]{1,0:T(8,128)S(1)} %add.14), channel_id=1, source_target_pairs={{0,2},{1,3},{2,0},{3,1},{4,6},{5,7},{6,4},{7,5},{8,10},{9,11},{10,... | collective-permute-start | bytes 12296 | tf_op jit(solution)/shard_map/ppermute | solution.py:401
  41.8 1.5 %own_active.1 = f32[64,16,64]{2,1,0:T(8,128)} custom-call(s32[2]{0:T(128)S(1)} %pad_add_fusion.where, f32[512,128]{1,0:T(8,128)S(1)} %get-tuple-element.68.act), custom_call_target="tpu_custom_call" | custom-call | flops 1000000 | bytes 100000 | tf_op jit(solution)/shard_map/own_active/pallas_call | solution.py:406
  43.3 0.5 %collective-permute-done.10 = f32[16,64]{1,0:T(8,128)S(1)} collective-permute-done((f32[16,64]{1,0:T(8,128)S(1)}, f32[16,64]{1,0:T(8,128)S(1)}, u32[]{:S(2)}, u32[]{:S(2)}) %collective-permute-start.10) | collective-permute-done | bytes 4128 | tf_op jit(solution)/shard_map/ppermute | solution.py:401
  43.8 0.6 %add_add_fusion = f32[16,64]{1,0:T(8,128)} fusion(f32[16,64]{1,0:T(8,128)S(1)} %copy-done, f32[16,64]{1,0:T(8,128)S(1)} %add.14, f32[16,64]{1,0:T(8,128)S(1)} %collective-permute-done.10), kind=kLoop, calls=%fused_computation.1 | loop fusion | flops 2048 | bytes 16384 | tf_op jit(solution)/shard_map/add | solution.py:531
  (13 shorter events, 0.1 us)
Async XLA Ops:
  9.1 5.4 %collective-permute-start = (bf16[1024,128]{1,0:T(8,128)(2,1)S(1)}, bf16[1024,128]{1,0:T(8,128)(2,1)S(1)}, u32[]{:S(2)}, u32[]{:S(2)}) collective-permute-start(bf16[1024,128]{1,0:T(8,128)(2,1)S(1)} %get-tuple-element.45), channel_id=1, source_target_pairs={{0,4},{4,0},{8,12},{12,8},{1,5},{5,1},{9,13},{13,9},{2,6},{6,2},{1... | collective-permute-start | bytes 786440 | tf_op jit(solution)/shard_map/ppermute | solution.py:426
  14.6 9.7 %collective-permute-start.1 = (bf16[256,128]{1,0:T(8,128)(2,1)S(1)}, bf16[256,128]{1,0:T(8,128)(2,1)S(1)}, u32[]{:S(2)}, u32[]{:S(2)}) collective-permute-start(bf16[256,128]{1,0:T(8,128)(2,1)S(1)} %slice.6), channel_id=1, source_target_pairs={{0,8},{4,12},{8,0},{12,4},{1,9},{5,13},{9,1},{13,5},{2,10},{6,14},... | collective-permute-start | bytes 196616 | tf_op jit(solution)/shard_map/ppermute | solution.py:426
  17.1 11.7 %collective-permute-start.3 = (bf16[768,128]{1,0:T(8,128)(2,1)S(1)}, bf16[768,128]{1,0:T(8,128)(2,1)S(1)}, u32[]{:S(2)}, u32[]{:S(2)}) collective-permute-start(bf16[768,128]{1,0:T(8,128)(2,1)S(1)} %slice.7), channel_id=1, source_target_pairs={{0,8},{4,12},{8,0},{12,4},{1,9},{5,13},{9,1},{13,5},{2,10},{6,14},... | collective-permute-start | bytes 589832 | tf_op jit(solution)/shard_map/ppermute | solution.py:426
  22.0 9.9 %collective-permute-start.4 = (bf16[432,128]{1,0:T(8,128)(2,1)S(1)}, bf16[432,128]{1,0:T(8,128)(2,1)S(1)}, u32[]{:S(2)}, u32[]{:S(2)}) collective-permute-start(bf16[432,128]{1,0:T(8,128)(2,1)S(1)} %get-tuple-element.63), channel_id=1, source_target_pairs={{0,8},{4,12},{8,0},{12,4},{1,9},{5,13},{9,1},{13,5},{2,10},{6,14},... | collective-permute-start | bytes 331784 | tf_op jit(solution)/shard_map/ppermute | solution.py:426
  24.1 7.9 %collective-permute-start.5 = (bf16[432,128]{1,0:T(8,128)(2,1)S(1)}, bf16[432,128]{1,0:T(8,128)(2,1)S(1)}, u32[]{:S(2)}, u32[]{:S(2)}) collective-permute-start(bf16[432,128]{1,0:T(8,128)(2,1)S(1)} %get-tuple-element.64), channel_id=1, source_target_pairs={{0,12},{4,8},{8,4},{12,0},{1,13},{5,9},{9,5},{13,1},{2,14},{6,10},... | collective-permute-start | bytes 331784 | tf_op jit(solution)/shard_map/ppermute | solution.py:426
  24.1 4.8 %collective-permute-start.2 = (bf16[1456,128]{1,0:T(8,128)(2,1)S(1)}, bf16[1456,128]{1,0:T(8,128)(2,1)S(1)}, u32[]{:S(2)}, u32[]{:S(2)}) collective-permute-start(bf16[1456,128]{1,0:T(8,128)(2,1)S(1)} %get-tuple-element.59), channel_id=1, source_target_pairs={{0,4},{4,0},{8,12},{12,8},{1,5},{5,1},{9,13},{13,9},{2,6},{6,2},{1... | collective-permute-start | bytes 1118216 | tf_op jit(solution)/shard_map/ppermute | solution.py:426
  28.8 14.9 %copy-start = (f32[16,64]{1,0:T(8,128)S(1)}, f32[16,64]{1,0:T(8,128)}, u32[]{:S(2)}) copy-start(f32[16,64]{1,0:T(8,128)} %param.11) | copy-start | bytes 12292
  29.7 2.2 %collective-permute-start.6 = (bf16[160,128]{1,0:T(8,128)(2,1)S(1)}, bf16[160,128]{1,0:T(8,128)(2,1)S(1)}, u32[]{:S(2)}, u32[]{:S(2)}) collective-permute-start(bf16[160,128]{1,0:T(8,128)(2,1)S(1)} %get-tuple-element.65), channel_id=1, source_target_pairs={{0,4},{4,0},{8,12},{12,8},{1,5},{5,1},{9,13},{13,9},{2,6},{6,2},{1... | collective-permute-start | bytes 122888 | tf_op jit(solution)/shard_map/ppermute | solution.py:426
  30.1 4.0 %collective-permute-start.7 = (bf16[160,128]{1,0:T(8,128)(2,1)S(1)}, bf16[160,128]{1,0:T(8,128)(2,1)S(1)}, u32[]{:S(2)}, u32[]{:S(2)}) collective-permute-start(bf16[160,128]{1,0:T(8,128)(2,1)S(1)} %get-tuple-element.66), channel_id=1, source_target_pairs={{0,8},{4,12},{8,0},{12,4},{1,9},{5,13},{9,1},{13,5},{2,10},{6,14},... | collective-permute-start | bytes 122888 | tf_op jit(solution)/shard_map/ppermute | solution.py:426
  31.8 3.5 %collective-permute-start.8 = (bf16[160,128]{1,0:T(8,128)(2,1)S(1)}, bf16[160,128]{1,0:T(8,128)(2,1)S(1)}, u32[]{:S(2)}, u32[]{:S(2)}) collective-permute-start(bf16[160,128]{1,0:T(8,128)(2,1)S(1)} %get-tuple-element.67), channel_id=1, source_target_pairs={{0,12},{4,8},{8,4},{12,0},{1,13},{5,9},{9,5},{13,1},{2,14},{6,10},... | collective-permute-start | bytes 122888 | tf_op jit(solution)/shard_map/ppermute | solution.py:426
  35.6 3.7 %collective-permute-start.9 = (f32[16,64]{1,0:T(8,128)S(1)}, f32[16,64]{1,0:T(8,128)S(1)}, u32[]{:S(2)}, u32[]{:S(2)}) collective-permute-start(f32[16,64]{1,0:T(8,128)S(1)} %get-tuple-element.69), channel_id=1, source_target_pairs={{0,1},{1,0},{2,3},{3,2},{4,5},{5,4},{6,7},{7,6},{8,9},{9,8},{10,11... | collective-permute-start | bytes 12296 | tf_op jit(solution)/shard_map/ppermute | solution.py:401
  39.2 4.5 %collective-permute-start.10 = (f32[16,64]{1,0:T(8,128)S(1)}, f32[16,64]{1,0:T(8,128)S(1)}, u32[]{:S(2)}, u32[]{:S(2)}) collective-permute-start(f32[16,64]{1,0:T(8,128)S(1)} %add.14), channel_id=1, source_target_pairs={{0,2},{1,3},{2,0},{3,1},{4,6},{5,7},{6,4},{7,5},{8,10},{9,11},{10,... | collective-permute-start | bytes 12296 | tf_op jit(solution)/shard_map/ppermute | solution.py:401

commit v13 on v12

--- a/solution.py
+++ b/solution.py
@@ -42,6 +42,10 @@
         )
         for k in range(slabs_ref.shape[0] // 2)
     ]
+
+
+def lanes_of(k):
+    return pl.ds(k * PAIRED if isinstance(k, int) else pl.multiple_of(k * PAIRED, PAIRED), PAIRED)
 
 
 def run_block(sbuf, weights, scratch, emit, prepare=None):
@@ -67,10 +71,7 @@
 
     def transform(g, bufs):
         dens = [d_ref[2 * g + n] for n in range(2)]
-        left = [
-            lt_ref[NIN:, pl.ds(pl.multiple_of((2 * g + n) * LANES, LANES), LANES)]
-            for n in range(2)
-        ]
+        left = [lt_ref[NIN:, lanes_of(2 * g + n)] for n in range(2)]
         for q in range(0, NBQ, group):
             slabs = [[], []]
             for u in range(q, q + group):
@@ -81,7 +82,7 @@
                     slabs[n].append(s.astype(BF))
                 diag[u] = total
             for n in range(2):
-                at = pl.ds(pl.multiple_of((2 * g + n) * LANES, LANES), LANES)
+                at = lanes_of(2 * g + n)
                 cols = [
                     jnp.concatenate(
                         [jnp.where(first_s, s, zero), jnp.where(first_s, zero, s)], axis=0
@@ -103,7 +104,7 @@
                     q0 = out[u * BS : (u + 1) * BS, lanes]
                     q1 = out[(u + 1) * BS : (u + 2) * BS, lanes]
                     at = slice((q + u) * BS, (q + u + 2) * BS)
-                    row = pl.multiple_of((4 * g + 2 * n) * BS, 2 * BS)
+                    row = lanes_of(2 * g + n).start
                     q_ref[pl.ds(row, BS), at] = jnp.where(first_s, q0, pltpu.roll(q1, BS, 1))
                     q_ref[pl.ds(row + BS, BS), at] = jnp.where(
                         first_s, pltpu.roll(q0, BS, 1), q1
@@ -139,12 +140,10 @@
     def two_quads(i, carry):
         one, two = scratch[:2], scratch[2:4]
         after = jnp.minimum(2 * i + 2, quads - 1)
-        if prepare is not None:
-            prepare(2 * i + 1)
+        prepare(2 * i + 1)
         load(2 * i + 1, two)
         transform(2 * i, one)
-        if prepare is not None:
-            prepare(after)
+        prepare(after)
         load(after, one)
         transform(2 * i + 1, two)
         return carry
@@ -153,7 +152,12 @@
     load(0, scratch[:2])
     if prepare is not None:
         prepare(0)
-    lax.fori_loop(0, quads // 2, two_quads, 0)
+        lax.fori_loop(0, quads // 2, two_quads, 0)
+    else:
+        for g in range(quads):
+            if g + 1 < quads:
+                load(g + 1, scratch[2 * ((g + 1) % 2) : 2 * ((g + 1) % 2) + 2])
+            transform(g, scratch[2 * (g % 2) : 2 * (g % 2) + 2])
     whole = second_transform(0)
     for g in range(NBQ // 4):
         following = second_transform(g + 1) if g + 1 < NBQ // 4 else None
@@ -197,10 +201,9 @@
 
 def first_kernel(
     where, rows_ref, cols_ref, live, slabs_ref, ot_ref,
-    lt_out, r_out, bd_out, d_out, msg, keep, sends, dens, after,
-    rows, cols, orbitals, ssem, sbuf, bsem, sem, *scratch
+    lt_out, r_out, bd_out, d_out, msg, keep, sends, dens, after2, after3, after4,
+    rows, cols, orbitals, ssem, sbuf, sem, *scratch
 ):
-    pairs = slabs_ref.shape[0] // 2
     core, x = where[0], where[1]
     part = NACT // 2
     small = [
@@ -212,23 +215,29 @@
         )
         for n in range(NCOL // part)
     ]
-    now = slab_copies(slabs_ref, sbuf, bsem, 2 * (1 - x) + (1 - core))
+    blocks = (2 * (1 - x) + (1 - core), 2 * (1 - x) + core, 2 * x + (1 - core), 2 * x + core)
+    now, *later = [
+        slab_copies(slabs_ref, ref, sem.at[n], block)
+        for n, (ref, block) in enumerate(zip((sbuf, after2, after3, after4), blocks))
+    ]
+    ahead = [copy for copies in later for copy in copies]
     for copy in now[:2] + small + now[2:]:
         copy.start()
-    ahead = slab_copies(slabs_ref, after, sem, 2 * (1 - x) + core)
     bd_out[...] = jnp.zeros_like(bd_out)
-
-    for copy in now + small:
+    for copy in now[:2]:
         copy.wait()
-    for copy in ahead:
-        copy.start()
 
     def prepare(g):
+        if isinstance(g, int):
+            for copy in small + now[2:]:
+                copy.wait()
+            for copy in ahead:
+                copy.start()
         for n in range(2):
             k = 2 * g + n
             left = orbital_pair(k, rows, live[0], orbitals)
             right = orbital_pair(k, cols, live[0], orbitals)
-            at = pl.ds(pl.multiple_of(k * PAIRED, PAIRED), PAIRED)
+            at = lanes_of(k)
             lt_out[:, at] = left
             turned = jnp.concatenate([right, right[NIN:]], axis=0).astype(F32).T.astype(BF)
             r_out[at, :] = turned
@@ -254,15 +263,9 @@
 
 
 def second_kernel(
-    where, slabs_ref, sbuf, lt_ref, r_ref, bd_ref, d_ref, keep_in, keep, sends, dens, after,
-    sem, *scratch
+    where, sbuf, lt_ref, r_ref, bd_ref, d_ref, keep_in, keep, sends, dens, *scratch
 ):
     core, x = where[0], where[1]
-    ahead = slab_copies(slabs_ref, after, sem, 2 * x + (1 - core))
-
-    for copy in ahead:
-        copy.start()
-
     def emit(h, in0, in1, act):
         keep_in[pair_rows(h, 0), :] = in0
         keep_in[pair_rows(h, 1), :] = in1
@@ -270,20 +273,13 @@
 
     run_block(sbuf, (lt_ref, r_ref, bd_ref, d_ref), scratch, emit)
     dens[...] = density_of(scratch[6][...])
-    for copy in ahead:
-        copy.wait()
 
 
 def third_kernel(
-    where, slabs_ref, sbuf, lt_ref, r_ref, bd_ref, d_ref, sends1, sends2, dens1, dens2,
-    near, far, cross, keep, dens, after, sem, sends, *scratch
+    where, sbuf, lt_ref, r_ref, bd_ref, d_ref, sends1, sends2, dens1, dens2,
+    near, far, cross, keep, dens, sends, *scratch
 ):
     core, x = where[0], where[1]
-    ahead = slab_copies(slabs_ref, after, sem, 2 * x + core)
-
-    for copy in ahead:
-        copy.start()
-
     def emit(h, in0, in1, act):
         near[pair_rows(h, 0), :] = in0.astype(BF)
         near[pair_rows(h, 1), :] = in1.astype(BF)
@@ -296,8 +292,6 @@
         for n, source in enumerate((sends1, sends2, sends)):
             msg[pl.ds(base + n * PER, PER), :] = source[k]
             msg[pl.ds(base + 3 * PER + n * NBQ, NBQ), :] = wires[n]
-    for copy in ahead:
-        copy.wait()
 
 
 def fourth_kernel(
@@ -426,7 +420,6 @@
         return lax.ppermute(array, "pair", [(p, p ^ k) for p in range(4)])
 
     loaded = shape((nslab // 2, 2, NBQ, width), BF)
-    copies = pltpu.SemaphoreType.DMA((nslab // 2,))
     scratch = [pltpu.VMEM((MSTEP * BS, LANES), F32)] * 4 + [
         pltpu.VMEM((NBQ, NACT, aos), BF),
         pltpu.VMEM((aos, NBQ * BS), BF),
@@ -442,15 +435,15 @@
         shape((PER, LANES), F32), shape((3, PER, LANES), BF), shape((NBQ, LANES), F32),
     )
     work = 5 * 10**9
-    lt, r, bd, d, msg1, keep1, sends1, dens1, slabs2 = call(
+    lt, r, bd, d, msg1, keep1, sends1, dens1, slabs2, slabs3, slabs4 = call(
         first_kernel,
         "slabs_first",
         [SM, HB, HB, SM, HB, HB],
-        weights + (shape((INROWS, LANES), BF),) + kept + (loaded,),
+        weights + (shape((INROWS, LANES), BF),) + kept + (loaded,) * 3,
         [
             pltpu.SMEM((nslab,), jnp.int32), pltpu.SMEM((nslab,), jnp.int32),
             pltpu.VMEM(orbitals.T.shape, BF), pltpu.SemaphoreType.DMA((8,)),
-            pltpu.VMEM(loaded.shape, BF), copies, copies,
+            pltpu.VMEM(loaded.shape, BF), pltpu.SemaphoreType.DMA((4, nslab // 2)),
         ] + scratch,
         (
             where, in_hbm(block_row), in_hbm(block_col), live_count, slabs,
@@ -459,13 +452,13 @@
         work,
     )
     near1 = to_peer(1, msg1)
-    keep_in2, keep2, sends2, dens2, slabs3 = call(
+    keep_in2, keep2, sends2, dens2 = call(
         second_kernel,
         "slabs_second",
-        [SM, HB] + [VM] * 5,
-        (shape((INROWS, LANES), F32),) + kept + (loaded,),
-        [copies] + scratch,
-        (where, slabs, slabs2, lt, r, bd, d),
+        [SM] + [VM] * 5,
+        (shape((INROWS, LANES), F32),) + kept,
+        scratch,
+        (where, slabs2, lt, r, bd, d),
         work,
     )
     out2 = (keep_in2 + near1.astype(F32)).astype(BF)
@@ -473,16 +466,16 @@
     cut = INROWS // 4
     far1a = to_peer(2, out2[:cut])
     news = 3 * PER + 3 * NBQ
-    msg3, msg3x, msg3c, keep3, dens3, slabs4 = call(
+    msg3, msg3x, msg3c, keep3, dens3 = call(
         third_kernel,
         "slabs_third",
-        [SM, HB] + [VM] * 9,
+        [SM] + [VM] * 9,
         (
             shape((INROWS + news, LANES), BF), shape((news, LANES), BF),
-            shape((news, LANES), BF), kept[0], kept[2], loaded,
+            shape((news, LANES), BF), kept[0], kept[2],
         ),
-        [copies, pltpu.VMEM((3, PER, LANES), BF)] + scratch,
-        (where, slabs, slabs3, lt, r, bd, d, sends1, sends2, dens1, dens2),
+        [pltpu.VMEM((3, PER, LANES), BF)] + scratch,
+        (where, slabs3, lt, r, bd, d, sends1, sends2, dens1, dens2),
         work,
     )
     near3 = to_peer(1, msg3)

time: 44.5 us -> 46.6 us (1.047)
  waiting for transfers between devices: 6.05 us -> 10.6 us
  Pallas kernels: 24.5 us -> 22.2 us
    ppermute x9, waiting for transfers between devices: 3.46 us -> 8.15 us  [to_peer(): return lax.ppermute(array, 'pair', [(p, p ^ k) for p in range(4)])]
    pallas_call x7, Pallas kernels: 24.5 us -> 22.2 us  [call(): pl.pallas_call(kernel, name=name, in_specs=inputs, out_specs=[VM] * len(o...]
  transfers between devices with their start and end apart: 11 -> 11, of which waited for: 4 -> 4; matrix products, arithmetic and copies ran while one was open for 0% -> 0% of each run, Pallas kernels for 37% -> 31%
where the time goes in v13:
time: 46.6 us; the launch traced here: 46.4 us
  Pallas kernels  22.2 us (48%)
  starting transfers between devices  11.5 us (25%)
  waiting for transfers between devices  10.6 us (23%)
  between operations  1.37 us (3%)
  other arithmetic  0.75 us (2%)
    pallas_call x7, Pallas kernels, call(): pl.pallas_call(kernel, name=name, in_specs=inputs, out_specs=[VM] * len(o...  22.2 us
    ppermute x9, waiting for transfers between devices, to_peer(): return lax.ppermute(array, 'pair', [(p, p ^ k) for p in range(4)])  8.15 us
    ppermute x9, starting transfers between devices, to_peer(): return lax.ppermute(array, 'pair', [(p, p ^ k) for p in range(4)])  7.23 us
    ppermute x2, starting transfers between devices, sum_over_aux(): part = part + lax.ppermute(part, 'aux', [(z, z ^ k) for z in range(n)])  4.3 us
    ppermute x2, waiting for transfers between devices, sum_over_aux(): part = part + lax.ppermute(part, 'aux', [(z, z ^ k) for z in range(n)])  2.45 us
  transfers between devices with their start and end apart: 11, of which 4 were waited for; matrix products, arithmetic and copies ran while one was open for 0% of the time, Pallas kernels for 31%

profile of v13, /device:TPU:0, one launch (start us, length us, event | category | flops | bytes accessed | tf_op | source)
XLA Modules:
  0.0 46.4 jit_solution(12512362015480005494)
XLA Ops:
  1.3 0.1 pad_add_fusion.where
  1.4 7.7 %slabs_first.1 = (bf16[192,1024]{1,0:T(8,128)(2,1)S(1)}, bf16[1024,256]{1,0:T(8,128)(2,1)S(1)}, bf16[4,256,256]{2,1,0:T(8,128)(2,1)S(1)}, f32[8,64,128]{2,1,0:T(...) custom-call(s32[2]{0:T(128)S(1)} %pad_add_fusion.where, ...), custom_call_target="tpu_custom_call" | custom-call | flops 5000000000 | bytes 100000 | tf_op jit(solution)/shard_map/slabs_first/pallas_call | solution.py:400
  9.1 0.5 %collective-permute-start = (bf16[1024,128]{1,0:T(8,128)(2,1)S(1)}, bf16[1024,128]{1,0:T(8,128)(2,1)S(1)}, u32[]{:S(2)}, u32[]{:S(2)}) collective-permute-start(bf16[1024,128]{1,0:T(8,128)(2,1)S(1)} %get-tuple-element.45), channel_id=1, source_target_pairs={{0,4},{4,0},{8,12},{12,8},{1,5},{5,1},{9,13},{13,9},{2,6},{6,2},{1... | collective-permute-start | bytes 786440 | tf_op jit(solution)/shard_map/ppermute | solution.py:420
  9.6 4.0 %slabs_second.1 = (f32[1024,128]{1,0:T(8,128)S(1)}, f32[128,128]{1,0:T(8,128)S(1)}, bf16[3,128,128]{2,1,0:T(8,128)(2,1)S(1)}, f32[16,128]{1,0:T(8,128)S(1)}) custom-call(s32[2]{0:T(128)S(1)} %pad_add_fusion.where, bf16[8,2,16,4096]{3,2,1,0:T(8,128)(2,1)S(1)} %get-tuple-element.37.sbuf, bf16[192,1024]{1,0:T(8,128)(2,1)S(1)} %get-tuple-element.54.lt_ref, ...), custom_call_target="tpu_custom_call" | custom-call | flops 5000000000 | bytes 100000 | tf_op jit(solution)/shard_map/slabs_second/pallas_call | solution.py:400
  13.7 2.6 %collective-permute-start.1 = (bf16[256,128]{1,0:T(8,128)(2,1)S(1)}, bf16[256,128]{1,0:T(8,128)(2,1)S(1)}, u32[]{:S(2)}, u32[]{:S(2)}) collective-permute-start(bf16[256,128]{1,0:T(8,128)(2,1)S(1)} %slice.6), channel_id=1, source_target_pairs={{0,8},{4,12},{8,0},{12,4},{1,9},{5,13},{9,1},{13,5},{2,10},{6,14},... | collective-permute-start | bytes 196616 | tf_op jit(solution)/shard_map/ppermute | solution.py:420
  16.2 3.9 %slabs_third.1 = (bf16[1456,128]{1,0:T(8,128)(2,1)S(1)}, bf16[432,128]{1,0:T(8,128)(2,1)S(1)}, bf16[432,128]{1,0:T(8,128)(2,1)S(1)}, f32[128,128]{1,0:T(8,128)S(1)}, f32[16,128]{1,0:T(8,128)S(1)}) custom-call(s32[2]{0:T(128)S(1)} %pad_add_fusion.where, bf16[8,2,16,4096]{3,2,1,0:T(8,128)(2,1)S(1)} %get-tuple-element.43.sbuf, ...), custom_call_target="tpu_custom_call" | custom-call | flops 5000000000 | bytes 100000 | tf_op jit(solution)/shard_map/slabs_third/pallas_call | solution.py:400
  20.2 0.1 collective-permute-start.4
  20.3 1.6 %collective-permute-start.5 = (bf16[432,128]{1,0:T(8,128)(2,1)S(1)}, bf16[432,128]{1,0:T(8,128)(2,1)S(1)}, u32[]{:S(2)}, u32[]{:S(2)}) collective-permute-start(bf16[432,128]{1,0:T(8,128)(2,1)S(1)} %get-tuple-element.64), channel_id=1, source_target_pairs={{0,12},{4,8},{8,4},{12,0},{1,13},{5,9},{9,5},{13,1},{2,14},{6,10},... | collective-permute-start | bytes 331784 | tf_op jit(solution)/shard_map/ppermute | solution.py:420
  21.8 0.5 %collective-permute-start.3 = (bf16[768,128]{1,0:T(8,128)(2,1)S(1)}, bf16[768,128]{1,0:T(8,128)(2,1)S(1)}, u32[]{:S(2)}, u32[]{:S(2)}) collective-permute-start(bf16[768,128]{1,0:T(8,128)(2,1)S(1)} %slice.7), channel_id=1, source_target_pairs={{0,8},{4,12},{8,0},{12,4},{1,9},{5,13},{9,1},{13,5},{2,10},{6,14},... | collective-permute-start | bytes 589832 | tf_op jit(solution)/shard_map/ppermute | solution.py:420
  22.3 0.1 collective-permute-start.2
  22.4 4.0 %slabs_fourth.1 = (f32[1024,128]{1,0:T(8,128)S(1)}, f32[128,128]{1,0:T(8,128)S(1)}, bf16[3,128,128]{2,1,0:T(8,128)(2,1)S(1)}, f32[16,128]{1,0:T(8,128)S(1)}) custom-call(s32[2]{0:T(128)S(1)} %pad_add_fusion.where, bf16[8,2,16,4096]{3,2,1,0:T(8,128)(2,1)S(1)} %get-tuple-element.52.sbuf, bf16[192,1024]{1,0:T(8,128)(2,1)S(1)} %get-tuple-element.54.lt_ref, ...), custom_call_target="tpu_custom_call" | custom-call | flops 5000000000 | bytes 100000 | tf_op jit(solution)/shard_map/slabs_fourth/pallas_call | solution.py:400
  26.4 5.6 %collective-permute-done.3.far1b = bf16[768,128]{1,0:T(8,128)(2,1)S(1)} collective-permute-done((bf16[768,128]{1,0:T(8,128)(2,1)S(1)}, bf16[768,128]{1,0:T(8,128)(2,1)S(1)}, u32[]{:S(2)}, u32[]{:S(2)}) %collective-permute-start.3) | collective-permute-done | bytes 196640 | tf_op jit(solution)/shard_map/ppermute | solution.py:420
  32.0 0.9 %exchange.1 = (bf16[160,128]{1,0:T(8,128)(2,1)S(1)}, bf16[160,128]{1,0:T(8,128)(2,1)S(1)}, bf16[160,128]{1,0:T(8,128)(2,1)S(1)}, f32[16,128]{1,0:T(8,128)S(1)}) custom-call(s32[2]{0:T(128)S(1)} %pad_add_fusion.where, f32[1024,128]{1,0:T(8,128)S(1)} %get-tuple-element.58.mine, bf16[1456,128]{1,0:T(8,128)(2,1)S(1)} %collective-permute-done.2.near3, ...), custom_call_target="tpu_custom_call" | custom-call | bytes 100000 | tf_op jit(solution)/shard_map/exchange/pallas_call | solution.py:400
  32.9 0.1 collective-permute-start.6
  33.0 0.4 collective-permute-start.7
  33.3 1.5 %collective-permute-start.8 = (bf16[160,128]{1,0:T(8,128)(2,1)S(1)}, bf16[160,128]{1,0:T(8,128)(2,1)S(1)}, u32[]{:S(2)}, u32[]{:S(2)}) collective-permute-start(bf16[160,128]{1,0:T(8,128)(2,1)S(1)} %get-tuple-element.67), channel_id=1, source_target_pairs={{0,12},{4,8},{8,4},{12,0},{1,13},{5,9},{9,5},{13,1},{2,14},{6,10},... | collective-permute-start | bytes 122888 | tf_op jit(solution)/shard_map/ppermute | solution.py:420
  34.9 2.5 %collective-permute-done.7.far4 = bf16[160,128]{1,0:T(8,128)(2,1)S(1)} collective-permute-done((bf16[160,128]{1,0:T(8,128)(2,1)S(1)}, bf16[160,128]{1,0:T(8,128)(2,1)S(1)}, u32[]{:S(2)}, u32[]{:S(2)}) %collective-permute-start.7) | collective-permute-done | bytes 40992 | tf_op jit(solution)/shard_map/ppermute | solution.py:420
  37.4 0.2 coulomb.1
  37.6 1.7 %collective-permute-start.9 = (f32[16,64]{1,0:T(8,128)S(1)}, f32[16,64]{1,0:T(8,128)S(1)}, u32[]{:S(2)}, u32[]{:S(2)}) collective-permute-start(f32[16,64]{1,0:T(8,128)S(1)} %get-tuple-element.69), channel_id=1, source_target_pairs={{0,1},{1,0},{2,3},{3,2},{4,5},{5,4},{6,7},{7,6},{8,9},{9,8},{10,11... | collective-permute-start | bytes 12296 | tf_op jit(solution)/shard_map/ppermute | solution.py:395
  39.3 2.0 %collective-permute-done.9 = f32[16,64]{1,0:T(8,128)S(1)} collective-permute-done((f32[16,64]{1,0:T(8,128)S(1)}, f32[16,64]{1,0:T(8,128)S(1)}, u32[]{:S(2)}, u32[]{:S(2)}) %collective-permute-start.9) | collective-permute-done | bytes 4128 | tf_op jit(solution)/shard_map/ppermute | solution.py:395
  41.3 2.6 %collective-permute-start.10 = (f32[16,64]{1,0:T(8,128)S(1)}, f32[16,64]{1,0:T(8,128)S(1)}, u32[]{:S(2)}, u32[]{:S(2)}) collective-permute-start(f32[16,64]{1,0:T(8,128)S(1)} %add.14), channel_id=1, source_target_pairs={{0,2},{1,3},{2,0},{3,1},{4,6},{5,7},{6,4},{7,5},{8,10},{9,11},{10,... | collective-permute-start | bytes 12296 | tf_op jit(solution)/shard_map/ppermute | solution.py:395
  43.9 1.5 %own_active.1 = f32[64,16,64]{2,1,0:T(8,128)} custom-call(s32[2]{0:T(128)S(1)} %pad_add_fusion.where, f32[512,128]{1,0:T(8,128)S(1)} %get-tuple-element.68.act), custom_call_target="tpu_custom_call" | custom-call | flops 1000000 | bytes 100000 | tf_op jit(solution)/shard_map/own_active/pallas_call | solution.py:400
  45.4 0.4 collective-permute-done.10
  45.8 0.6 %add_add_fusion = f32[16,64]{1,0:T(8,128)} fusion(f32[16,64]{1,0:T(8,128)S(1)} %copy-done, f32[16,64]{1,0:T(8,128)S(1)} %add.14, f32[16,64]{1,0:T(8,128)S(1)} %collective-permute-done.10), kind=kLoop, calls=%fused_computation.1 | loop fusion | flops 2048 | bytes 16384 | tf_op jit(solution)/shard_map/add | solution.py:524
  (13 shorter events, 0.1 us)
Async XLA Ops:
  9.1 4.5 %collective-permute-start = (bf16[1024,128]{1,0:T(8,128)(2,1)S(1)}, bf16[1024,128]{1,0:T(8,128)(2,1)S(1)}, u32[]{:S(2)}, u32[]{:S(2)}) collective-permute-start(bf16[1024,128]{1,0:T(8,128)(2,1)S(1)} %get-tuple-element.45), channel_id=1, source_target_pairs={{0,4},{4,0},{8,12},{12,8},{1,5},{5,1},{9,13},{13,9},{2,6},{6,2},{1... | collective-permute-start | bytes 786440 | tf_op jit(solution)/shard_map/ppermute | solution.py:420
  13.7 8.7 %collective-permute-start.1 = (bf16[256,128]{1,0:T(8,128)(2,1)S(1)}, bf16[256,128]{1,0:T(8,128)(2,1)S(1)}, u32[]{:S(2)}, u32[]{:S(2)}) collective-permute-start(bf16[256,128]{1,0:T(8,128)(2,1)S(1)} %slice.6), channel_id=1, source_target_pairs={{0,8},{4,12},{8,0},{12,4},{1,9},{5,13},{9,1},{13,5},{2,10},{6,14},... | collective-permute-start | bytes 196616 | tf_op jit(solution)/shard_map/ppermute | solution.py:420
  20.2 14.6 %collective-permute-start.4 = (bf16[432,128]{1,0:T(8,128)(2,1)S(1)}, bf16[432,128]{1,0:T(8,128)(2,1)S(1)}, u32[]{:S(2)}, u32[]{:S(2)}) collective-permute-start(bf16[432,128]{1,0:T(8,128)(2,1)S(1)} %get-tuple-element.63), channel_id=1, source_target_pairs={{0,8},{4,12},{8,0},{12,4},{1,9},{5,13},{9,1},{13,5},{2,10},{6,14},... | collective-permute-start | bytes 331784 | tf_op jit(solution)/shard_map/ppermute | solution.py:420
  20.3 14.6 %collective-permute-start.5 = (bf16[432,128]{1,0:T(8,128)(2,1)S(1)}, bf16[432,128]{1,0:T(8,128)(2,1)S(1)}, u32[]{:S(2)}, u32[]{:S(2)}) collective-permute-start(bf16[432,128]{1,0:T(8,128)(2,1)S(1)} %get-tuple-element.64), channel_id=1, source_target_pairs={{0,12},{4,8},{8,4},{12,0},{1,13},{5,9},{9,5},{13,1},{2,14},{6,10},... | collective-permute-start | bytes 331784 | tf_op jit(solution)/shard_map/ppermute | solution.py:420
  21.8 10.2 %collective-permute-start.3 = (bf16[768,128]{1,0:T(8,128)(2,1)S(1)}, bf16[768,128]{1,0:T(8,128)(2,1)S(1)}, u32[]{:S(2)}, u32[]{:S(2)}) collective-permute-start(bf16[768,128]{1,0:T(8,128)(2,1)S(1)} %slice.7), channel_id=1, source_target_pairs={{0,8},{4,12},{8,0},{12,4},{1,9},{5,13},{9,1},{13,5},{2,10},{6,14},... | collective-permute-start | bytes 589832 | tf_op jit(solution)/shard_map/ppermute | solution.py:420
  22.3 9.7 %collective-permute-start.2 = (bf16[1456,128]{1,0:T(8,128)(2,1)S(1)}, bf16[1456,128]{1,0:T(8,128)(2,1)S(1)}, u32[]{:S(2)}, u32[]{:S(2)}) collective-permute-start(bf16[1456,128]{1,0:T(8,128)(2,1)S(1)} %get-tuple-element.59), channel_id=1, source_target_pairs={{0,4},{4,0},{8,12},{12,8},{1,5},{5,1},{9,13},{13,9},{2,6},{6,2},{1... | collective-permute-start | bytes 1118216 | tf_op jit(solution)/shard_map/ppermute | solution.py:420
  26.4 19.4 %copy-start = (f32[16,64]{1,0:T(8,128)S(1)}, f32[16,64]{1,0:T(8,128)}, u32[]{:S(2)}) copy-start(f32[16,64]{1,0:T(8,128)} %param.11) | copy-start | bytes 12292
  32.9 2.0 %collective-permute-start.6 = (bf16[160,128]{1,0:T(8,128)(2,1)S(1)}, bf16[160,128]{1,0:T(8,128)(2,1)S(1)}, u32[]{:S(2)}, u32[]{:S(2)}) collective-permute-start(bf16[160,128]{1,0:T(8,128)(2,1)S(1)} %get-tuple-element.65), channel_id=1, source_target_pairs={{0,4},{4,0},{8,12},{12,8},{1,5},{5,1},{9,13},{13,9},{2,6},{6,2},{1... | collective-permute-start | bytes 122888 | tf_op jit(solution)/shard_map/ppermute | solution.py:420
  33.0 4.4 %collective-permute-start.7 = (bf16[160,128]{1,0:T(8,128)(2,1)S(1)}, bf16[160,128]{1,0:T(8,128)(2,1)S(1)}, u32[]{:S(2)}, u32[]{:S(2)}) collective-permute-start(bf16[160,128]{1,0:T(8,128)(2,1)S(1)} %get-tuple-element.66), channel_id=1, source_target_pairs={{0,8},{4,12},{8,0},{12,4},{1,9},{5,13},{9,1},{13,5},{2,10},{6,14},... | collective-permute-start | bytes 122888 | tf_op jit(solution)/shard_map/ppermute | solution.py:420
  33.3 4.1 %collective-permute-start.8 = (bf16[160,128]{1,0:T(8,128)(2,1)S(1)}, bf16[160,128]{1,0:T(8,128)(2,1)S(1)}, u32[]{:S(2)}, u32[]{:S(2)}) collective-permute-start(bf16[160,128]{1,0:T(8,128)(2,1)S(1)} %get-tuple-element.67), channel_id=1, source_target_pairs={{0,12},{4,8},{8,4},{12,0},{1,13},{5,9},{9,5},{13,1},{2,14},{6,10},... | collective-permute-start | bytes 122888 | tf_op jit(solution)/shard_map/ppermute | solution.py:420
  37.6 3.7 %collective-permute-start.9 = (f32[16,64]{1,0:T(8,128)S(1)}, f32[16,64]{1,0:T(8,128)S(1)}, u32[]{:S(2)}, u32[]{:S(2)}) collective-permute-start(f32[16,64]{1,0:T(8,128)S(1)} %get-tuple-element.69), channel_id=1, source_target_pairs={{0,1},{1,0},{2,3},{3,2},{4,5},{5,4},{6,7},{7,6},{8,9},{9,8},{10,11... | collective-permute-start | bytes 12296 | tf_op jit(solution)/shard_map/ppermute | solution.py:395
  41.3 4.5 %collective-permute-start.10 = (f32[16,64]{1,0:T(8,128)S(1)}, f32[16,64]{1,0:T(8,128)S(1)}, u32[]{:S(2)}, u32[]{:S(2)}) collective-permute-start(f32[16,64]{1,0:T(8,128)S(1)} %add.14), channel_id=1, source_target_pairs={{0,2},{1,3},{2,0},{3,1},{4,6},{5,7},{6,4},{7,5},{8,10},{9,11},{10,... | collective-permute-start | bytes 12296 | tf_op jit(solution)/shard_map/ppermute | solution.py:395

commit v14 on v13

--- a/solution.py
+++ b/solution.py
@@ -277,18 +277,19 @@
 
 def third_kernel(
     where, sbuf, lt_ref, r_ref, bd_ref, d_ref, sends1, sends2, dens1, dens2,
-    near, far, cross, keep, dens, sends, *scratch
+    near, near_more, far, cross, keep, dens, sends, *scratch
 ):
     core, x = where[0], where[1]
     def emit(h, in0, in1, act):
-        near[pair_rows(h, 0), :] = in0.astype(BF)
-        near[pair_rows(h, 1), :] = in1.astype(BF)
+        place, at = (near, h) if h < NBQ // 4 else (near_more, h - NBQ // 4)
+        place[pair_rows(at, 0), :] = in0.astype(BF)
+        place[pair_rows(at, 1), :] = in1.astype(BF)
         emit_active(h, act, core, x, keep, sends)
 
     run_block(sbuf, (lt_ref, r_ref, bd_ref, d_ref), scratch, emit)
     dens[...] = density_of(scratch[6][...])
     wires = [split_wire(d[...]) for d in (dens1, dens2, dens)]
-    for k, (msg, base) in enumerate(((near, INROWS), (far, 0), (cross, 0))):
+    for k, (msg, base) in enumerate(((near, INROWS // 2), (far, 0), (cross, 0))):
         for n, source in enumerate((sends1, sends2, sends)):
             msg[pl.ds(base + n * PER, PER), :] = source[k]
             msg[pl.ds(base + 3 * PER + n * NBQ, NBQ), :] = wires[n]
@@ -309,14 +310,13 @@
 
 
 def exchange_kernel(
-    where, mine, near3, far1a, far1b, sends, dens, near, far, cross, keep, whole
+    where, mine, near3, near3b, far1, sends, dens, near, far, cross, keep, whole
 ):
     parts = []
     for q in range(NBQ):
         rows = pl.ds(q * NACT, NACT)
-        at = q * NACT - far1a.shape[0]
-        other = far1a[rows, :] if at < 0 else far1b[pl.ds(at, NACT), :]
-        parts.append(mine[rows, :] + near3[rows, :].astype(F32) + other.astype(F32))
+        other = (near3 if q < NBQ // 2 else near3b)[pl.ds(q % (NBQ // 2) * NACT, NACT), :]
+        parts.append(mine[rows, :] + other.astype(F32) + far1[rows, :].astype(F32))
     v = jnp.concatenate(parts, axis=1)
     v = v.astype(BF)
     total = lax.dot_general(v, v, (((1,), (1,)), ((), ())), preferred_element_type=F32)
@@ -345,7 +345,7 @@
         for k in (1, 2, 3):
             n = m ^ k
             msg = late[k - 1] if n == 3 else early[k - 1]
-            base = INROWS if n < 3 and k == 1 else 0
+            base = INROWS // 2 if n < 3 and k == 1 else 0
             at, dens_at = (0, PER) if n == 3 else (base + n * PER, base + 3 * PER + n * NBQ)
             rows = rows + msg[pl.ds(at, PER), :].astype(F32)
             d = d + joined(msg[pl.ds(dens_at, NBQ), :])
@@ -376,6 +376,7 @@
 SM = pl.BlockSpec(memory_space=pltpu.SMEM)
 HB = pl.BlockSpec(memory_space=pltpu.HBM)
 
+LAST_WORK = 10**9
 PARAMS = pltpu.CompilerParams(vmem_limit_bytes=32 * 1024 * 1024)
 
 
@@ -463,25 +464,22 @@
     )
     out2 = (keep_in2 + near1.astype(F32)).astype(BF)
     out2, lt = lax.optimization_barrier((out2, lt))
-    cut = INROWS // 4
-    far1a = to_peer(2, out2[:cut])
+    far1 = to_peer(2, out2)
     news = 3 * PER + 3 * NBQ
-    msg3, msg3x, msg3c, keep3, dens3 = call(
+    msg3, msg3b, msg3x, msg3c, keep3, dens3 = call(
         third_kernel,
         "slabs_third",
         [SM] + [VM] * 9,
         (
-            shape((INROWS + news, LANES), BF), shape((news, LANES), BF),
-            shape((news, LANES), BF), kept[0], kept[2],
+            shape((INROWS // 2 + news, LANES), BF), shape((INROWS // 2, LANES), BF),
+            shape((news, LANES), BF), shape((news, LANES), BF), kept[0], kept[2],
         ),
         [pltpu.VMEM((3, PER, LANES), BF)] + scratch,
         (where, slabs3, lt, r, bd, d, sends1, sends2, dens1, dens2),
         work,
     )
-    near3 = to_peer(1, msg3)
-    far1b = to_peer(2, out2[cut:])
+    near3, near3b = to_peer(1, msg3), to_peer(1, msg3b)
     far3, cross3 = to_peer(2, msg3x), to_peer(3, msg3c)
-    far1a, lt = lax.optimization_barrier((far1a, lt))
     keep_in4, keep4, sends4, dens4 = call(
         fourth_kernel,
         "slabs_fourth",
@@ -489,7 +487,7 @@
         (shape((INROWS, LANES), F32),) + kept,
         scratch,
         (where, slabs4, lt, r, bd, d),
-        work,
+        LAST_WORK,
     )
     last = shape((PER + NBQ + QUARTER, LANES), BF)
     near4, far4, cross4, exch = call(
@@ -498,7 +496,7 @@
         [SM] + [VM] * 6,
         (last,) * 3 + (shape((QUARTER, LANES), F32),),
         [pltpu.VMEM((NACT, LANES), F32)],
-        (where, keep_in4, near3, far1a, far1b, sends4, dens4),
+        (where, keep_in4, near3, near3b, far1, sends4, dens4),
     )
     far4, cross4, near4 = to_peer(2, far4), to_peer(3, cross4), to_peer(1, near4)
     act, partial = call(

time: 46.6 us -> 41.5 us (0.89)
  waiting for transfers between devices: 10.6 us -> 4.41 us
  starting transfers between devices: 11.5 us -> 12.3 us
    ppermute x9, waiting for transfers between devices: 8.15 us -> 2.58 us  [to_peer(): return lax.ppermute(array, 'pair', [(p, p ^ k) for p in range(4)])]
    ppermute x2, starting transfers between devices: 4.3 us -> 5 us  [sum_over_aux(): part = part + lax.ppermute(part, 'aux', [(z, z ^ k) for z in range(n)])]
    ppermute x2, waiting for transfers between devices: 2.45 us -> 1.83 us  [sum_over_aux(): part = part + lax.ppermute(part, 'aux', [(z, z ^ k) for z in range(n)])]
  transfers between devices with their start and end apart: 11 -> 11, of which waited for: 4 -> 3; matrix products, arithmetic and copies ran while one was open for 0% -> 0% of each run, Pallas kernels for 31% -> 35%
where the time goes in v14:
time: 41.5 us; the launch traced here: 41.3 us
  Pallas kernels  22.5 us (54%)
  starting transfers between devices  12.3 us (30%)
  waiting for transfers between devices  4.41 us (11%)
  between operations  1.37 us (3%)
  other arithmetic  0.76 us (2%)
    pallas_call x7, Pallas kernels, call(): pl.pallas_call(kernel, name=name, in_specs=inputs, out_specs=[VM] * len(o...  22.5 us
    ppermute x9, starting transfers between devices, to_peer(): return lax.ppermute(array, 'pair', [(p, p ^ k) for p in range(4)])  7.29 us
    ppermute x2, starting transfers between devices, sum_over_aux(): part = part + lax.ppermute(part, 'aux', [(z, z ^ k) for z in range(n)])  5 us
    ppermute x9, waiting for transfers between devices, to_peer(): return lax.ppermute(array, 'pair', [(p, p ^ k) for p in range(4)])  2.58 us
    ppermute x2, waiting for transfers between devices, sum_over_aux(): part = part + lax.ppermute(part, 'aux', [(z, z ^ k) for z in range(n)])  1.83 us
  transfers between devices with their start and end apart: 11, of which 3 were waited for; matrix products, arithmetic and copies ran while one was open for 0% of the time, Pallas kernels for 35%

profile of v14, /device:TPU:0, one launch (start us, length us, event | category | flops | bytes accessed | tf_op | source)
XLA Modules:
  0.0 41.3 jit_solution(15982774493200165441)
XLA Ops:
  1.3 0.1 pad_add_fusion.where
  1.4 7.8 %slabs_first.1 = (bf16[192,1024]{1,0:T(8,128)(2,1)S(1)}, bf16[1024,256]{1,0:T(8,128)(2,1)S(1)}, bf16[4,256,256]{2,1,0:T(8,128)(2,1)S(1)}, f32[8,64,128]{2,1,0:T(...) custom-call(s32[2]{0:T(128)S(1)} %pad_add_fusion.where, ...), custom_call_target="tpu_custom_call" | custom-call | flops 5000000000 | bytes 100000 | tf_op jit(solution)/shard_map/slabs_first/pallas_call | solution.py:401
  9.1 0.5 %collective-permute-start = (bf16[1024,128]{1,0:T(8,128)(2,1)S(1)}, bf16[1024,128]{1,0:T(8,128)(2,1)S(1)}, u32[]{:S(2)}, u32[]{:S(2)}) collective-permute-start(bf16[1024,128]{1,0:T(8,128)(2,1)S(1)} %get-tuple-element.44), channel_id=1, source_target_pairs={{0,4},{4,0},{8,12},{12,8},{1,5},{5,1},{9,13},{13,9},{2,6},{6,2},{1... | collective-permute-start | bytes 786440 | tf_op jit(solution)/shard_map/ppermute | solution.py:421
  9.6 4.1 %slabs_second.1 = (f32[1024,128]{1,0:T(8,128)S(1)}, f32[128,128]{1,0:T(8,128)S(1)}, bf16[3,128,128]{2,1,0:T(8,128)(2,1)S(1)}, f32[16,128]{1,0:T(8,128)S(1)}) custom-call(s32[2]{0:T(128)S(1)} %pad_add_fusion.where, bf16[8,2,16,4096]{3,2,1,0:T(8,128)(2,1)S(1)} %get-tuple-element.36.sbuf, bf16[192,1024]{1,0:T(8,128)(2,1)S(1)} %get-tuple-element.45.lt_ref, ...), custom_call_target="tpu_custom_call" | custom-call | flops 5000000000 | bytes 100000 | tf_op jit(solution)/shard_map/slabs_second/pallas_call | solution.py:401
  13.7 0.1 add_convert_fusion
  13.8 2.6 %collective-permute-start.3 = (bf16[1024,128]{1,0:T(8,128)(2,1)S(1)}, bf16[1024,128]{1,0:T(8,128)(2,1)S(1)}, u32[]{:S(2)}, u32[]{:S(2)}) collective-permute-start(bf16[1024,128]{1,0:T(8,128)(2,1)S(1)} %add_convert_fusion), channel_id=1, source_target_pairs={{0,8},{4,12},{8,0},{12,4},{1,9},{5,13},{9,1},{13,5},{2,10},{6,14},... | collective-permute-start | bytes 786440 | tf_op jit(solution)/shard_map/ppermute | solution.py:421
  16.4 4.0 %slabs_third.1 = (bf16[944,128]{1,0:T(8,128)(2,1)S(1)}, bf16[512,128]{1,0:T(8,128)(2,1)S(1)}, bf16[432,128]{1,0:T(8,128)(2,1)S(1)}, bf16[432,128]{1,0:T(8,128)(2...) custom-call(s32[2]{0:T(128)S(1)} %pad_add_fusion.where, bf16[8,2,16,4096]{3,2,1,0:T(8,128)(2,1)S(1)} %get-tuple-element.42.sbuf, ...), custom_call_target="tpu_custom_call" | custom-call | flops 5000000000 | bytes 100000 | tf_op jit(solution)/shard_map/slabs_third/pallas_call | solution.py:401
  20.4 0.3 collective-permute-start.1
  20.7 0.3 collective-permute-start.2
  21.0 0.1 collective-permute-start.4
  21.1 1.5 %collective-permute-start.5 = (bf16[432,128]{1,0:T(8,128)(2,1)S(1)}, bf16[432,128]{1,0:T(8,128)(2,1)S(1)}, u32[]{:S(2)}, u32[]{:S(2)}) collective-permute-start(bf16[432,128]{1,0:T(8,128)(2,1)S(1)} %get-tuple-element.62), channel_id=1, source_target_pairs={{0,12},{4,8},{8,4},{12,0},{1,13},{5,9},{9,5},{13,1},{2,14},{6,10},... | collective-permute-start | bytes 331784 | tf_op jit(solution)/shard_map/ppermute | solution.py:421
  22.6 4.1 %slabs_fourth.1 = (f32[1024,128]{1,0:T(8,128)S(1)}, f32[128,128]{1,0:T(8,128)S(1)}, bf16[3,128,128]{2,1,0:T(8,128)(2,1)S(1)}, f32[16,128]{1,0:T(8,128)S(1)}) custom-call(s32[2]{0:T(128)S(1)} %pad_add_fusion.where, bf16[8,2,16,4096]{3,2,1,0:T(8,128)(2,1)S(1)} %get-tuple-element.51.sbuf, bf16[192,1024]{1,0:T(8,128)(2,1)S(1)} %get-tuple-element.45.lt_ref, ...), custom_call_target="tpu_custom_call" | custom-call | flops 1000000000 | bytes 100000 | tf_op jit(solution)/shard_map/slabs_fourth/pallas_call | solution.py:401
  26.7 0.9 %exchange.1 = (bf16[160,128]{1,0:T(8,128)(2,1)S(1)}, bf16[160,128]{1,0:T(8,128)(2,1)S(1)}, bf16[160,128]{1,0:T(8,128)(2,1)S(1)}, f32[16,128]{1,0:T(8,128)S(1)}) custom-call(s32[2]{0:T(128)S(1)} %pad_add_fusion.where, f32[1024,128]{1,0:T(8,128)S(1)} %get-tuple-element.55.mine, bf16[944,128]{1,0:T(8,128)(2,1)S(1)} %collective-permute-done.1.near3, ...), custom_call_target="tpu_custom_call" | custom-call | bytes 100000 | tf_op jit(solution)/shard_map/exchange/pallas_call | solution.py:401
  27.5 0.6 %collective-permute-start.6 = (bf16[160,128]{1,0:T(8,128)(2,1)S(1)}, bf16[160,128]{1,0:T(8,128)(2,1)S(1)}, u32[]{:S(2)}, u32[]{:S(2)}) collective-permute-start(bf16[160,128]{1,0:T(8,128)(2,1)S(1)} %get-tuple-element.63), channel_id=1, source_target_pairs={{0,4},{4,0},{8,12},{12,8},{1,5},{5,1},{9,13},{13,9},{2,6},{6,2},{1... | collective-permute-start | bytes 122888 | tf_op jit(solution)/shard_map/ppermute | solution.py:421
  28.2 0.1 collective-permute-start.7
  28.3 1.3 %collective-permute-start.8 = (bf16[160,128]{1,0:T(8,128)(2,1)S(1)}, bf16[160,128]{1,0:T(8,128)(2,1)S(1)}, u32[]{:S(2)}, u32[]{:S(2)}) collective-permute-start(bf16[160,128]{1,0:T(8,128)(2,1)S(1)} %get-tuple-element.65), channel_id=1, source_target_pairs={{0,12},{4,8},{8,4},{12,0},{1,13},{5,9},{9,5},{13,1},{2,14},{6,10},... | collective-permute-start | bytes 122888 | tf_op jit(solution)/shard_map/ppermute | solution.py:421
  29.6 2.6 %collective-permute-done.7.far4 = bf16[160,128]{1,0:T(8,128)(2,1)S(1)} collective-permute-done((bf16[160,128]{1,0:T(8,128)(2,1)S(1)}, bf16[160,128]{1,0:T(8,128)(2,1)S(1)}, u32[]{:S(2)}, u32[]{:S(2)}) %collective-permute-start.7) | collective-permute-done | bytes 40992 | tf_op jit(solution)/shard_map/ppermute | solution.py:421
  32.2 0.2 coulomb.1
  32.4 2.0 %collective-permute-start.9 = (f32[16,64]{1,0:T(8,128)S(1)}, f32[16,64]{1,0:T(8,128)S(1)}, u32[]{:S(2)}, u32[]{:S(2)}) collective-permute-start(f32[16,64]{1,0:T(8,128)S(1)} %get-tuple-element.67), channel_id=1, source_target_pairs={{0,1},{1,0},{2,3},{3,2},{4,5},{5,4},{6,7},{7,6},{8,9},{9,8},{10,11... | collective-permute-start | bytes 12296 | tf_op jit(solution)/shard_map/ppermute | solution.py:396
  34.4 1.7 %collective-permute-done.9 = f32[16,64]{1,0:T(8,128)S(1)} collective-permute-done((f32[16,64]{1,0:T(8,128)S(1)}, f32[16,64]{1,0:T(8,128)S(1)}, u32[]{:S(2)}, u32[]{:S(2)}) %collective-permute-start.9) | collective-permute-done | bytes 4128 | tf_op jit(solution)/shard_map/ppermute | solution.py:396
  36.1 3.0 %collective-permute-start.10 = (f32[16,64]{1,0:T(8,128)S(1)}, f32[16,64]{1,0:T(8,128)S(1)}, u32[]{:S(2)}, u32[]{:S(2)}) collective-permute-start(f32[16,64]{1,0:T(8,128)S(1)} %add.14), channel_id=1, source_target_pairs={{0,2},{1,3},{2,0},{3,1},{4,6},{5,7},{6,4},{7,5},{8,10},{9,11},{10,... | collective-permute-start | bytes 12296 | tf_op jit(solution)/shard_map/ppermute | solution.py:396
  39.1 1.5 %own_active.1 = f32[64,16,64]{2,1,0:T(8,128)} custom-call(s32[2]{0:T(128)S(1)} %pad_add_fusion.where, f32[512,128]{1,0:T(8,128)S(1)} %get-tuple-element.66.act), custom_call_target="tpu_custom_call" | custom-call | flops 1000000 | bytes 100000 | tf_op jit(solution)/shard_map/own_active/pallas_call | solution.py:401
  40.5 0.2 collective-permute-done.10
  40.7 0.6 %add_add_fusion = f32[16,64]{1,0:T(8,128)} fusion(f32[16,64]{1,0:T(8,128)S(1)} %copy-done, f32[16,64]{1,0:T(8,128)S(1)} %add.14, f32[16,64]{1,0:T(8,128)S(1)} %collective-permute-done.10), kind=kLoop, calls=%fused_computation.1 | loop fusion | flops 2048 | bytes 16384 | tf_op jit(solution)/shard_map/add | solution.py:522
  (11 shorter events, 0.0 us)
Async XLA Ops:
  9.1 4.6 %collective-permute-start = (bf16[1024,128]{1,0:T(8,128)(2,1)S(1)}, bf16[1024,128]{1,0:T(8,128)(2,1)S(1)}, u32[]{:S(2)}, u32[]{:S(2)}) collective-permute-start(bf16[1024,128]{1,0:T(8,128)(2,1)S(1)} %get-tuple-element.44), channel_id=1, source_target_pairs={{0,4},{4,0},{8,12},{12,8},{1,5},{5,1},{9,13},{13,9},{2,6},{6,2},{1... | collective-permute-start | bytes 786440 | tf_op jit(solution)/shard_map/ppermute | solution.py:421
  13.8 12.9 %collective-permute-start.3 = (bf16[1024,128]{1,0:T(8,128)(2,1)S(1)}, bf16[1024,128]{1,0:T(8,128)(2,1)S(1)}, u32[]{:S(2)}, u32[]{:S(2)}) collective-permute-start(bf16[1024,128]{1,0:T(8,128)(2,1)S(1)} %add_convert_fusion), channel_id=1, source_target_pairs={{0,8},{4,12},{8,0},{12,4},{1,9},{5,13},{9,1},{13,5},{2,10},{6,14},... | collective-permute-start | bytes 786440 | tf_op jit(solution)/shard_map/ppermute | solution.py:421
  20.4 6.2 %collective-permute-start.1 = (bf16[944,128]{1,0:T(8,128)(2,1)S(1)}, bf16[944,128]{1,0:T(8,128)(2,1)S(1)}, u32[]{:S(2)}, u32[]{:S(2)}) collective-permute-start(bf16[944,128]{1,0:T(8,128)(2,1)S(1)} %get-tuple-element.56), channel_id=1, source_target_pairs={{0,4},{4,0},{8,12},{12,8},{1,5},{5,1},{9,13},{13,9},{2,6},{6,2},{1... | collective-permute-start | bytes 725000 | tf_op jit(solution)/shard_map/ppermute | solution.py:421
  20.7 5.9 %collective-permute-start.2 = (bf16[512,128]{1,0:T(8,128)(2,1)S(1)}, bf16[512,128]{1,0:T(8,128)(2,1)S(1)}, u32[]{:S(2)}, u32[]{:S(2)}) collective-permute-start(bf16[512,128]{1,0:T(8,128)(2,1)S(1)} %get-tuple-element.57), channel_id=1, source_target_pairs={{0,4},{4,0},{8,12},{12,8},{1,5},{5,1},{9,13},{13,9},{2,6},{6,2},{1... | collective-permute-start | bytes 393224 | tf_op jit(solution)/shard_map/ppermute | solution.py:421
  21.0 8.6 %collective-permute-start.4 = (bf16[432,128]{1,0:T(8,128)(2,1)S(1)}, bf16[432,128]{1,0:T(8,128)(2,1)S(1)}, u32[]{:S(2)}, u32[]{:S(2)}) collective-permute-start(bf16[432,128]{1,0:T(8,128)(2,1)S(1)} %get-tuple-element.61), channel_id=1, source_target_pairs={{0,8},{4,12},{8,0},{12,4},{1,9},{5,13},{9,1},{13,5},{2,10},{6,14},... | collective-permute-start | bytes 331784 | tf_op jit(solution)/shard_map/ppermute | solution.py:421
  21.1 8.5 %collective-permute-start.5 = (bf16[432,128]{1,0:T(8,128)(2,1)S(1)}, bf16[432,128]{1,0:T(8,128)(2,1)S(1)}, u32[]{:S(2)}, u32[]{:S(2)}) collective-permute-start(bf16[432,128]{1,0:T(8,128)(2,1)S(1)} %get-tuple-element.62), channel_id=1, source_target_pairs={{0,12},{4,8},{8,4},{12,0},{1,13},{5,9},{9,5},{13,1},{2,14},{6,10},... | collective-permute-start | bytes 331784 | tf_op jit(solution)/shard_map/ppermute | solution.py:421
  26.6 14.1 %copy-start = (f32[16,64]{1,0:T(8,128)S(1)}, f32[16,64]{1,0:T(8,128)}, u32[]{:S(2)}) copy-start(f32[16,64]{1,0:T(8,128)} %param.11) | copy-start | bytes 12292
  27.5 2.1 %collective-permute-start.6 = (bf16[160,128]{1,0:T(8,128)(2,1)S(1)}, bf16[160,128]{1,0:T(8,128)(2,1)S(1)}, u32[]{:S(2)}, u32[]{:S(2)}) collective-permute-start(bf16[160,128]{1,0:T(8,128)(2,1)S(1)} %get-tuple-element.63), channel_id=1, source_target_pairs={{0,4},{4,0},{8,12},{12,8},{1,5},{5,1},{9,13},{13,9},{2,6},{6,2},{1... | collective-permute-start | bytes 122888 | tf_op jit(solution)/shard_map/ppermute | solution.py:421
  28.2 4.0 %collective-permute-start.7 = (bf16[160,128]{1,0:T(8,128)(2,1)S(1)}, bf16[160,128]{1,0:T(8,128)(2,1)S(1)}, u32[]{:S(2)}, u32[]{:S(2)}) collective-permute-start(bf16[160,128]{1,0:T(8,128)(2,1)S(1)} %get-tuple-element.64), channel_id=1, source_target_pairs={{0,8},{4,12},{8,0},{12,4},{1,9},{5,13},{9,1},{13,5},{2,10},{6,14},... | collective-permute-start | bytes 122888 | tf_op jit(solution)/shard_map/ppermute | solution.py:421
  28.3 3.9 %collective-permute-start.8 = (bf16[160,128]{1,0:T(8,128)(2,1)S(1)}, bf16[160,128]{1,0:T(8,128)(2,1)S(1)}, u32[]{:S(2)}, u32[]{:S(2)}) collective-permute-start(bf16[160,128]{1,0:T(8,128)(2,1)S(1)} %get-tuple-element.65), channel_id=1, source_target_pairs={{0,12},{4,8},{8,4},{12,0},{1,13},{5,9},{9,5},{13,1},{2,14},{6,10},... | collective-permute-start | bytes 122888 | tf_op jit(solution)/shard_map/ppermute | solution.py:421
  32.4 3.7 %collective-permute-start.9 = (f32[16,64]{1,0:T(8,128)S(1)}, f32[16,64]{1,0:T(8,128)S(1)}, u32[]{:S(2)}, u32[]{:S(2)}) collective-permute-start(f32[16,64]{1,0:T(8,128)S(1)} %get-tuple-element.67), channel_id=1, source_target_pairs={{0,1},{1,0},{2,3},{3,2},{4,5},{5,4},{6,7},{7,6},{8,9},{9,8},{10,11... | collective-permute-start | bytes 12296 | tf_op jit(solution)/shard_map/ppermute | solution.py:396
  36.1 4.6 %collective-permute-start.10 = (f32[16,64]{1,0:T(8,128)S(1)}, f32[16,64]{1,0:T(8,128)S(1)}, u32[]{:S(2)}, u32[]{:S(2)}) collective-permute-start(f32[16,64]{1,0:T(8,128)S(1)} %add.14), channel_id=1, source_target_pairs={{0,2},{1,3},{2,0},{3,1},{4,6},{5,7},{6,4},{7,5},{8,10},{9,11},{10,... | collective-permute-start | bytes 12296 | tf_op jit(solution)/shard_map/ppermute | solution.py:396

commit v15 on v14

--- a/solution.py
+++ b/solution.py
@@ -139,21 +139,19 @@
 
     def two_quads(i, carry):
         one, two = scratch[:2], scratch[2:4]
-        after = jnp.minimum(2 * i + 2, quads - 1)
+        load(2 * i, one)
+        prepare(2 * i)
+        load(2 * i + 1, two)
         prepare(2 * i + 1)
-        load(2 * i + 1, two)
         transform(2 * i, one)
-        prepare(after)
-        load(after, one)
         transform(2 * i + 1, two)
         return carry
 
     diag[...] = jnp.zeros_like(diag)
-    load(0, scratch[:2])
     if prepare is not None:
-        prepare(0)
         lax.fori_loop(0, quads // 2, two_quads, 0)
     else:
+        load(0, scratch[:2])
         for g in range(quads):
             if g + 1 < quads:
                 load(g + 1, scratch[2 * ((g + 1) % 2) : 2 * ((g + 1) % 2) + 2])
@@ -221,18 +219,15 @@
         for n, (ref, block) in enumerate(zip((sbuf, after2, after3, after4), blocks))
     ]
     ahead = [copy for copies in later for copy in copies]
-    for copy in now[:2] + small + now[2:]:
+    for copy in small + now:
         copy.start()
     bd_out[...] = jnp.zeros_like(bd_out)
-    for copy in now[:2]:
+    for copy in small + now:
         copy.wait()
+    for copy in ahead:
+        copy.start()
 
     def prepare(g):
-        if isinstance(g, int):
-            for copy in small + now[2:]:
-                copy.wait()
-            for copy in ahead:
-                copy.start()
         for n in range(2):
             k = 2 * g + n
             left = orbital_pair(k, rows, live[0], orbitals)

time: 41.5 us -> 41.2 us (level)
  no operation moved by 1% of the time
where the time goes in v15:
time: 41.2 us; the launch traced here: 41 us
  Pallas kernels  22.2 us (54%)
  starting transfers between devices  12.3 us (30%)
  waiting for transfers between devices  4.42 us (11%)
  between operations  1.37 us (3%)
  other arithmetic  0.76 us (2%)
    pallas_call x7, Pallas kernels, call(): pl.pallas_call(kernel, name=name, in_specs=inputs, out_specs=[VM] * len(o...  22.2 us
    ppermute x9, starting transfers between devices, to_peer(): return lax.ppermute(array, 'pair', [(p, p ^ k) for p in range(4)])  7.3 us
    ppermute x2, starting transfers between devices, sum_over_aux(): part = part + lax.ppermute(part, 'aux', [(z, z ^ k) for z in range(n)])  4.97 us
    ppermute x9, waiting for transfers between devices, to_peer(): return lax.ppermute(array, 'pair', [(p, p ^ k) for p in range(4)])  2.58 us
    ppermute x2, waiting for transfers between devices, sum_over_aux(): part = part + lax.ppermute(part, 'aux', [(z, z ^ k) for z in range(n)])  1.84 us
  transfers between devices with their start and end apart: 11, of which 3 were waited for; matrix products, arithmetic and copies ran while one was open for 0% of the time, Pallas kernels for 35%

profile of v15, /device:TPU:0, one launch (start us, length us, event | category | flops | bytes accessed | tf_op | source)
XLA Modules:
  0.0 41.0 jit_solution(531900073813978888)
XLA Ops:
  1.3 0.1 pad_add_fusion.where
  1.4 7.5 %slabs_first.1 = (bf16[192,1024]{1,0:T(8,128)(2,1)S(1)}, bf16[1024,256]{1,0:T(8,128)(2,1)S(1)}, bf16[4,256,256]{2,1,0:T(8,128)(2,1)S(1)}, f32[8,64,128]{2,1,0:T(...) custom-call(s32[2]{0:T(128)S(1)} %pad_add_fusion.where, ...), custom_call_target="tpu_custom_call" | custom-call | flops 5000000000 | bytes 100000 | tf_op jit(solution)/shard_map/slabs_first/pallas_call | solution.py:396
  8.8 0.5 %collective-permute-start = (bf16[1024,128]{1,0:T(8,128)(2,1)S(1)}, bf16[1024,128]{1,0:T(8,128)(2,1)S(1)}, u32[]{:S(2)}, u32[]{:S(2)}) collective-permute-start(bf16[1024,128]{1,0:T(8,128)(2,1)S(1)} %get-tuple-element.44), channel_id=1, source_target_pairs={{0,4},{4,0},{8,12},{12,8},{1,5},{5,1},{9,13},{13,9},{2,6},{6,2},{1... | collective-permute-start | bytes 786440 | tf_op jit(solution)/shard_map/ppermute | solution.py:416
  9.4 4.1 %slabs_second.1 = (f32[1024,128]{1,0:T(8,128)S(1)}, f32[128,128]{1,0:T(8,128)S(1)}, bf16[3,128,128]{2,1,0:T(8,128)(2,1)S(1)}, f32[16,128]{1,0:T(8,128)S(1)}) custom-call(s32[2]{0:T(128)S(1)} %pad_add_fusion.where, bf16[8,2,16,4096]{3,2,1,0:T(8,128)(2,1)S(1)} %get-tuple-element.36.sbuf, bf16[192,1024]{1,0:T(8,128)(2,1)S(1)} %get-tuple-element.45.lt_ref, ...), custom_call_target="tpu_custom_call" | custom-call | flops 5000000000 | bytes 100000 | tf_op jit(solution)/shard_map/slabs_second/pallas_call | solution.py:396
  13.4 0.1 add_convert_fusion
  13.5 2.6 %collective-permute-start.3 = (bf16[1024,128]{1,0:T(8,128)(2,1)S(1)}, bf16[1024,128]{1,0:T(8,128)(2,1)S(1)}, u32[]{:S(2)}, u32[]{:S(2)}) collective-permute-start(bf16[1024,128]{1,0:T(8,128)(2,1)S(1)} %add_convert_fusion), channel_id=1, source_target_pairs={{0,8},{4,12},{8,0},{12,4},{1,9},{5,13},{9,1},{13,5},{2,10},{6,14},... | collective-permute-start | bytes 786440 | tf_op jit(solution)/shard_map/ppermute | solution.py:416
  16.1 4.0 %slabs_third.1 = (bf16[944,128]{1,0:T(8,128)(2,1)S(1)}, bf16[512,128]{1,0:T(8,128)(2,1)S(1)}, bf16[432,128]{1,0:T(8,128)(2,1)S(1)}, bf16[432,128]{1,0:T(8,128)(2...) custom-call(s32[2]{0:T(128)S(1)} %pad_add_fusion.where, bf16[8,2,16,4096]{3,2,1,0:T(8,128)(2,1)S(1)} %get-tuple-element.42.sbuf, ...), custom_call_target="tpu_custom_call" | custom-call | flops 5000000000 | bytes 100000 | tf_op jit(solution)/shard_map/slabs_third/pallas_call | solution.py:396
  20.1 0.3 collective-permute-start.1
  20.4 0.3 collective-permute-start.2
  20.7 0.1 collective-permute-start.4
  20.8 1.5 %collective-permute-start.5 = (bf16[432,128]{1,0:T(8,128)(2,1)S(1)}, bf16[432,128]{1,0:T(8,128)(2,1)S(1)}, u32[]{:S(2)}, u32[]{:S(2)}) collective-permute-start(bf16[432,128]{1,0:T(8,128)(2,1)S(1)} %get-tuple-element.62), channel_id=1, source_target_pairs={{0,12},{4,8},{8,4},{12,0},{1,13},{5,9},{9,5},{13,1},{2,14},{6,10},... | collective-permute-start | bytes 331784 | tf_op jit(solution)/shard_map/ppermute | solution.py:416
  22.3 4.1 %slabs_fourth.1 = (f32[1024,128]{1,0:T(8,128)S(1)}, f32[128,128]{1,0:T(8,128)S(1)}, bf16[3,128,128]{2,1,0:T(8,128)(2,1)S(1)}, f32[16,128]{1,0:T(8,128)S(1)}) custom-call(s32[2]{0:T(128)S(1)} %pad_add_fusion.where, bf16[8,2,16,4096]{3,2,1,0:T(8,128)(2,1)S(1)} %get-tuple-element.51.sbuf, bf16[192,1024]{1,0:T(8,128)(2,1)S(1)} %get-tuple-element.45.lt_ref, ...), custom_call_target="tpu_custom_call" | custom-call | flops 1000000000 | bytes 100000 | tf_op jit(solution)/shard_map/slabs_fourth/pallas_call | solution.py:396
  26.4 0.9 %exchange.1 = (bf16[160,128]{1,0:T(8,128)(2,1)S(1)}, bf16[160,128]{1,0:T(8,128)(2,1)S(1)}, bf16[160,128]{1,0:T(8,128)(2,1)S(1)}, f32[16,128]{1,0:T(8,128)S(1)}) custom-call(s32[2]{0:T(128)S(1)} %pad_add_fusion.where, f32[1024,128]{1,0:T(8,128)S(1)} %get-tuple-element.55.mine, bf16[944,128]{1,0:T(8,128)(2,1)S(1)} %collective-permute-done.1.near3, ...), custom_call_target="tpu_custom_call" | custom-call | bytes 100000 | tf_op jit(solution)/shard_map/exchange/pallas_call | solution.py:396
  27.3 0.6 %collective-permute-start.6 = (bf16[160,128]{1,0:T(8,128)(2,1)S(1)}, bf16[160,128]{1,0:T(8,128)(2,1)S(1)}, u32[]{:S(2)}, u32[]{:S(2)}) collective-permute-start(bf16[160,128]{1,0:T(8,128)(2,1)S(1)} %get-tuple-element.63), channel_id=1, source_target_pairs={{0,4},{4,0},{8,12},{12,8},{1,5},{5,1},{9,13},{13,9},{2,6},{6,2},{1... | collective-permute-start | bytes 122888 | tf_op jit(solution)/shard_map/ppermute | solution.py:416
  27.9 0.1 collective-permute-start.7
  28.0 1.3 %collective-permute-start.8 = (bf16[160,128]{1,0:T(8,128)(2,1)S(1)}, bf16[160,128]{1,0:T(8,128)(2,1)S(1)}, u32[]{:S(2)}, u32[]{:S(2)}) collective-permute-start(bf16[160,128]{1,0:T(8,128)(2,1)S(1)} %get-tuple-element.65), channel_id=1, source_target_pairs={{0,12},{4,8},{8,4},{12,0},{1,13},{5,9},{9,5},{13,1},{2,14},{6,10},... | collective-permute-start | bytes 122888 | tf_op jit(solution)/shard_map/ppermute | solution.py:416
  29.4 2.6 %collective-permute-done.7.far4 = bf16[160,128]{1,0:T(8,128)(2,1)S(1)} collective-permute-done((bf16[160,128]{1,0:T(8,128)(2,1)S(1)}, bf16[160,128]{1,0:T(8,128)(2,1)S(1)}, u32[]{:S(2)}, u32[]{:S(2)}) %collective-permute-start.7) | collective-permute-done | bytes 40992 | tf_op jit(solution)/shard_map/ppermute | solution.py:416
  31.9 0.2 coulomb.1
  32.1 2.0 %collective-permute-start.9 = (f32[16,64]{1,0:T(8,128)S(1)}, f32[16,64]{1,0:T(8,128)S(1)}, u32[]{:S(2)}, u32[]{:S(2)}) collective-permute-start(f32[16,64]{1,0:T(8,128)S(1)} %get-tuple-element.67), channel_id=1, source_target_pairs={{0,1},{1,0},{2,3},{3,2},{4,5},{5,4},{6,7},{7,6},{8,9},{9,8},{10,11... | collective-permute-start | bytes 12296 | tf_op jit(solution)/shard_map/ppermute | solution.py:391
  34.1 1.7 %collective-permute-done.9 = f32[16,64]{1,0:T(8,128)S(1)} collective-permute-done((f32[16,64]{1,0:T(8,128)S(1)}, f32[16,64]{1,0:T(8,128)S(1)}, u32[]{:S(2)}, u32[]{:S(2)}) %collective-permute-start.9) | collective-permute-done | bytes 4128 | tf_op jit(solution)/shard_map/ppermute | solution.py:391
  35.8 3.0 %collective-permute-start.10 = (f32[16,64]{1,0:T(8,128)S(1)}, f32[16,64]{1,0:T(8,128)S(1)}, u32[]{:S(2)}, u32[]{:S(2)}) collective-permute-start(f32[16,64]{1,0:T(8,128)S(1)} %add.14), channel_id=1, source_target_pairs={{0,2},{1,3},{2,0},{3,1},{4,6},{5,7},{6,4},{7,5},{8,10},{9,11},{10,... | collective-permute-start | bytes 12296 | tf_op jit(solution)/shard_map/ppermute | solution.py:391
  38.8 1.5 %own_active.1 = f32[64,16,64]{2,1,0:T(8,128)} custom-call(s32[2]{0:T(128)S(1)} %pad_add_fusion.where, f32[512,128]{1,0:T(8,128)S(1)} %get-tuple-element.66.act), custom_call_target="tpu_custom_call" | custom-call | flops 1000000 | bytes 100000 | tf_op jit(solution)/shard_map/own_active/pallas_call | solution.py:396
  40.2 0.2 collective-permute-done.10
  40.4 0.6 %add_add_fusion = f32[16,64]{1,0:T(8,128)} fusion(f32[16,64]{1,0:T(8,128)S(1)} %copy-done, f32[16,64]{1,0:T(8,128)S(1)} %add.14, f32[16,64]{1,0:T(8,128)S(1)} %collective-permute-done.10), kind=kLoop, calls=%fused_computation.1 | loop fusion | flops 2048 | bytes 16384 | tf_op jit(solution)/shard_map/add | solution.py:517
  (11 shorter events, 0.0 us)
Async XLA Ops:
  8.8 4.6 %collective-permute-start = (bf16[1024,128]{1,0:T(8,128)(2,1)S(1)}, bf16[1024,128]{1,0:T(8,128)(2,1)S(1)}, u32[]{:S(2)}, u32[]{:S(2)}) collective-permute-start(bf16[1024,128]{1,0:T(8,128)(2,1)S(1)} %get-tuple-element.44), channel_id=1, source_target_pairs={{0,4},{4,0},{8,12},{12,8},{1,5},{5,1},{9,13},{13,9},{2,6},{6,2},{1... | collective-permute-start | bytes 786440 | tf_op jit(solution)/shard_map/ppermute | solution.py:416
  13.5 12.9 %collective-permute-start.3 = (bf16[1024,128]{1,0:T(8,128)(2,1)S(1)}, bf16[1024,128]{1,0:T(8,128)(2,1)S(1)}, u32[]{:S(2)}, u32[]{:S(2)}) collective-permute-start(bf16[1024,128]{1,0:T(8,128)(2,1)S(1)} %add_convert_fusion), channel_id=1, source_target_pairs={{0,8},{4,12},{8,0},{12,4},{1,9},{5,13},{9,1},{13,5},{2,10},{6,14},... | collective-permute-start | bytes 786440 | tf_op jit(solution)/shard_map/ppermute | solution.py:416
  20.1 6.2 %collective-permute-start.1 = (bf16[944,128]{1,0:T(8,128)(2,1)S(1)}, bf16[944,128]{1,0:T(8,128)(2,1)S(1)}, u32[]{:S(2)}, u32[]{:S(2)}) collective-permute-start(bf16[944,128]{1,0:T(8,128)(2,1)S(1)} %get-tuple-element.56), channel_id=1, source_target_pairs={{0,4},{4,0},{8,12},{12,8},{1,5},{5,1},{9,13},{13,9},{2,6},{6,2},{1... | collective-permute-start | bytes 725000 | tf_op jit(solution)/shard_map/ppermute | solution.py:416
  20.4 6.0 %collective-permute-start.2 = (bf16[512,128]{1,0:T(8,128)(2,1)S(1)}, bf16[512,128]{1,0:T(8,128)(2,1)S(1)}, u32[]{:S(2)}, u32[]{:S(2)}) collective-permute-start(bf16[512,128]{1,0:T(8,128)(2,1)S(1)} %get-tuple-element.57), channel_id=1, source_target_pairs={{0,4},{4,0},{8,12},{12,8},{1,5},{5,1},{9,13},{13,9},{2,6},{6,2},{1... | collective-permute-start | bytes 393224 | tf_op jit(solution)/shard_map/ppermute | solution.py:416
  20.7 8.6 %collective-permute-start.4 = (bf16[432,128]{1,0:T(8,128)(2,1)S(1)}, bf16[432,128]{1,0:T(8,128)(2,1)S(1)}, u32[]{:S(2)}, u32[]{:S(2)}) collective-permute-start(bf16[432,128]{1,0:T(8,128)(2,1)S(1)} %get-tuple-element.61), channel_id=1, source_target_pairs={{0,8},{4,12},{8,0},{12,4},{1,9},{5,13},{9,1},{13,5},{2,10},{6,14},... | collective-permute-start | bytes 331784 | tf_op jit(solution)/shard_map/ppermute | solution.py:416
  20.8 8.6 %collective-permute-start.5 = (bf16[432,128]{1,0:T(8,128)(2,1)S(1)}, bf16[432,128]{1,0:T(8,128)(2,1)S(1)}, u32[]{:S(2)}, u32[]{:S(2)}) collective-permute-start(bf16[432,128]{1,0:T(8,128)(2,1)S(1)} %get-tuple-element.62), channel_id=1, source_target_pairs={{0,12},{4,8},{8,4},{12,0},{1,13},{5,9},{9,5},{13,1},{2,14},{6,10},... | collective-permute-start | bytes 331784 | tf_op jit(solution)/shard_map/ppermute | solution.py:416
  26.4 14.0 %copy-start = (f32[16,64]{1,0:T(8,128)S(1)}, f32[16,64]{1,0:T(8,128)}, u32[]{:S(2)}) copy-start(f32[16,64]{1,0:T(8,128)} %param.11) | copy-start | bytes 12292
  27.3 2.1 %collective-permute-start.6 = (bf16[160,128]{1,0:T(8,128)(2,1)S(1)}, bf16[160,128]{1,0:T(8,128)(2,1)S(1)}, u32[]{:S(2)}, u32[]{:S(2)}) collective-permute-start(bf16[160,128]{1,0:T(8,128)(2,1)S(1)} %get-tuple-element.63), channel_id=1, source_target_pairs={{0,4},{4,0},{8,12},{12,8},{1,5},{5,1},{9,13},{13,9},{2,6},{6,2},{1... | collective-permute-start | bytes 122888 | tf_op jit(solution)/shard_map/ppermute | solution.py:416
  27.9 4.0 %collective-permute-start.7 = (bf16[160,128]{1,0:T(8,128)(2,1)S(1)}, bf16[160,128]{1,0:T(8,128)(2,1)S(1)}, u32[]{:S(2)}, u32[]{:S(2)}) collective-permute-start(bf16[160,128]{1,0:T(8,128)(2,1)S(1)} %get-tuple-element.64), channel_id=1, source_target_pairs={{0,8},{4,12},{8,0},{12,4},{1,9},{5,13},{9,1},{13,5},{2,10},{6,14},... | collective-permute-start | bytes 122888 | tf_op jit(solution)/shard_map/ppermute | solution.py:416
  28.0 3.9 %collective-permute-start.8 = (bf16[160,128]{1,0:T(8,128)(2,1)S(1)}, bf16[160,128]{1,0:T(8,128)(2,1)S(1)}, u32[]{:S(2)}, u32[]{:S(2)}) collective-permute-start(bf16[160,128]{1,0:T(8,128)(2,1)S(1)} %get-tuple-element.65), channel_id=1, source_target_pairs={{0,12},{4,8},{8,4},{12,0},{1,13},{5,9},{9,5},{13,1},{2,14},{6,10},... | collective-permute-start | bytes 122888 | tf_op jit(solution)/shard_map/ppermute | solution.py:416
  32.1 3.7 %collective-permute-start.9 = (f32[16,64]{1,0:T(8,128)S(1)}, f32[16,64]{1,0:T(8,128)S(1)}, u32[]{:S(2)}, u32[]{:S(2)}) collective-permute-start(f32[16,64]{1,0:T(8,128)S(1)} %get-tuple-element.67), channel_id=1, source_target_pairs={{0,1},{1,0},{2,3},{3,2},{4,5},{5,4},{6,7},{7,6},{8,9},{9,8},{10,11... | collective-permute-start | bytes 12296 | tf_op jit(solution)/shard_map/ppermute | solution.py:391
  35.8 4.6 %collective-permute-start.10 = (f32[16,64]{1,0:T(8,128)S(1)}, f32[16,64]{1,0:T(8,128)S(1)}, u32[]{:S(2)}, u32[]{:S(2)}) collective-permute-start(f32[16,64]{1,0:T(8,128)S(1)} %add.14), channel_id=1, source_target_pairs={{0,2},{1,3},{2,0},{3,1},{4,6},{5,7},{6,4},{7,5},{8,10},{9,11},{10,... | collective-permute-start | bytes 12296 | tf_op jit(solution)/shard_map/ppermute | solution.py:391

commit v16 on v15

--- a/solution.py
+++ b/solution.py
@@ -48,7 +48,7 @@
     return pl.ds(k * PAIRED if isinstance(k, int) else pl.multiple_of(k * PAIRED, PAIRED), PAIRED)
 
 
-def run_block(sbuf, weights, scratch, emit, prepare=None):
+def run_block(sbuf, weights, scratch, emit, prepare=None, arrive=None):
     lt_ref, r_ref, bd_ref, d_ref = weights
     pt_ref, q_ref, diag = scratch[4:]
     quads = sbuf.shape[0] // 2
@@ -139,6 +139,7 @@
 
     def two_quads(i, carry):
         one, two = scratch[:2], scratch[2:4]
+        pl.when(i > 0)(arrive)
         load(2 * i, one)
         prepare(2 * i)
         load(2 * i + 1, two)
@@ -181,6 +182,7 @@
 QUARTER = NACT // 4
 PER = NBQ // 2 * QUARTER
 INROWS = NBQ * NACT
+LAST = PER + NBQ + QUARTER
 
 
 def emit_active(h, act, core, x, keep, sends):
@@ -222,10 +224,14 @@
     for copy in small + now:
         copy.start()
     bd_out[...] = jnp.zeros_like(bd_out)
-    for copy in small + now:
+    for copy in small + now[: len(now) // 2]:
         copy.wait()
     for copy in ahead:
         copy.start()
+
+    def arrive():
+        for copy in now[len(now) // 2 :]:
+            copy.wait()
 
     def prepare(g):
         for n in range(2):
@@ -251,7 +257,7 @@
         msg[pair_rows(h, 1), :] = in1.astype(BF)
         emit_active(h, act, core, x, keep, sends)
 
-    run_block(sbuf, (lt_out, r_out, bd_out, d_out), scratch, emit, prepare)
+    run_block(sbuf, (lt_out, r_out, bd_out, d_out), scratch, emit, prepare, arrive)
     dens[...] = density_of(scratch[6][...])
     for copy in ahead:
         copy.wait()
@@ -272,7 +278,7 @@
 
 def third_kernel(
     where, sbuf, lt_ref, r_ref, bd_ref, d_ref, sends1, sends2, dens1, dens2,
-    near, near_more, far, cross, keep, dens, sends, *scratch
+    near, near_more, far, keep, dens, sends, *scratch
 ):
     core, x = where[0], where[1]
     def emit(h, in0, in1, act):
@@ -284,7 +290,9 @@
     run_block(sbuf, (lt_ref, r_ref, bd_ref, d_ref), scratch, emit)
     dens[...] = density_of(scratch[6][...])
     wires = [split_wire(d[...]) for d in (dens1, dens2, dens)]
-    for k, (msg, base) in enumerate(((near, INROWS // 2), (far, 0), (cross, 0))):
+    for n, source in enumerate((sends1, sends2, sends)):
+        near_more[pl.ds(INROWS // 2 + n * PER, PER), :] = source[2]
+    for k, (msg, base) in enumerate(((near, INROWS // 2), (far, 0))):
         for n, source in enumerate((sends1, sends2, sends)):
             msg[pl.ds(base + n * PER, PER), :] = source[k]
             msg[pl.ds(base + 3 * PER + n * NBQ, NBQ), :] = wires[n]
@@ -320,18 +328,24 @@
     keep[...] = whole[pl.ds(pl.multiple_of(index * QUARTER, QUARTER), QUARTER), :]
     wire = split_wire(dens[...])
     for k, msg in enumerate((near, far, cross)):
-        msg[pl.ds(0, PER), :] = sends[k]
+        rows = sends[k]
+        if k == 1:
+            passed = near3b[pl.ds(INROWS // 2 + 2 * PER, PER), :]
+            rows = (rows.astype(F32) + passed.astype(F32)).astype(BF)
+        msg[pl.ds(0, PER), :] = rows
         msg[pl.ds(PER, NBQ), :] = wire
         at = pl.multiple_of((index ^ (k + 1)) * QUARTER, QUARTER)
         msg[pl.ds(PER + NBQ, QUARTER), :] = split_wire(whole[pl.ds(at, QUARTER), :])
+    far[pl.ds(LAST, 2 * PER), :] = near3b[pl.ds(INROWS // 2, 2 * PER), :]
+    far[pl.ds(LAST + 2 * PER, 3 * NBQ), :] = near3[pl.ds(INROWS // 2 + 3 * PER, 3 * NBQ), :]
 
 
 def coulomb_kernel(
     keep1, keep2, keep3, keep4, dens1, dens2, dens3, dens4, exch,
-    near3, far3, cross3, near4, far4, cross4, act, partial,
+    near3, far3, near4, far4, cross4, act, partial,
 ):
     first = low_half(QUARTER)
-    early, late = (near3, far3, cross3), (near4, far4, cross4)
+    early, late = (near3, far3, far4), (near4, far4, cross4)
     total = jnp.zeros((QUARTER, LANES), F32)
     for m, (keep, dens) in enumerate(
         ((keep1, dens1), (keep2, dens2), (keep3, dens3), (keep4, dens4))
@@ -340,9 +354,15 @@
         for k in (1, 2, 3):
             n = m ^ k
             msg = late[k - 1] if n == 3 else early[k - 1]
-            base = INROWS // 2 if n < 3 and k == 1 else 0
-            at, dens_at = (0, PER) if n == 3 else (base + n * PER, base + 3 * PER + n * NBQ)
-            rows = rows + msg[pl.ds(at, PER), :].astype(F32)
+            if n == 3:
+                at, dens_at = 0, PER
+            elif k == 3:
+                at, dens_at = LAST + n * PER, LAST + 2 * PER + n * NBQ
+            else:
+                base = INROWS // 2 if k == 1 else 0
+                at, dens_at = base + n * PER, base + 3 * PER + n * NBQ
+            if not (k == 3 and n == 2):
+                rows = rows + msg[pl.ds(at, PER), :].astype(F32)
             d = d + joined(msg[pl.ds(dens_at, NBQ), :])
         act[pl.ds(m * PER, PER), :] = rows
         for h in range(NBQ // 2):
@@ -461,20 +481,20 @@
     out2, lt = lax.optimization_barrier((out2, lt))
     far1 = to_peer(2, out2)
     news = 3 * PER + 3 * NBQ
-    msg3, msg3b, msg3x, msg3c, keep3, dens3 = call(
+    msg3, msg3b, msg3x, keep3, dens3 = call(
         third_kernel,
         "slabs_third",
         [SM] + [VM] * 9,
         (
-            shape((INROWS // 2 + news, LANES), BF), shape((INROWS // 2, LANES), BF),
-            shape((news, LANES), BF), shape((news, LANES), BF), kept[0], kept[2],
+            shape((INROWS // 2 + news, LANES), BF), shape((INROWS // 2 + 3 * PER, LANES), BF),
+            shape((news, LANES), BF), kept[0], kept[2],
         ),
         [pltpu.VMEM((3, PER, LANES), BF)] + scratch,
         (where, slabs3, lt, r, bd, d, sends1, sends2, dens1, dens2),
         work,
     )
     near3, near3b = to_peer(1, msg3), to_peer(1, msg3b)
-    far3, cross3 = to_peer(2, msg3x), to_peer(3, msg3c)
+    far3 = to_peer(2, msg3x)
     keep_in4, keep4, sends4, dens4 = call(
         fourth_kernel,
         "slabs_fourth",
@@ -484,12 +504,14 @@
         (where, slabs4, lt, r, bd, d),
         LAST_WORK,
     )
-    last = shape((PER + NBQ + QUARTER, LANES), BF)
+    last = shape((LAST, LANES), BF)
+    last_far = shape((LAST + 2 * PER + 3 * NBQ, LANES), BF)
+    far3, keep_in4 = lax.optimization_barrier((far3, keep_in4))
     near4, far4, cross4, exch = call(
         exchange_kernel,
         "exchange",
         [SM] + [VM] * 6,
-        (last,) * 3 + (shape((QUARTER, LANES), F32),),
+        (last, last_far, last, shape((QUARTER, LANES), F32)),
         [pltpu.VMEM((NACT, LANES), F32)],
         (where, keep_in4, near3, near3b, far1, sends4, dens4),
     )
@@ -497,12 +519,12 @@
     act, partial = call(
         coulomb_kernel,
         "coulomb",
-        [VM] * 15,
+        [VM] * 14,
         (shape((4 * PER, LANES), F32), shape((QUARTER, NACT), F32)),
         [],
         (
             keep1, keep2, keep3, keep4, dens1, dens2, dens3, dens4, exch,
-            near3, far3, cross3, near4, far4, cross4,
+            near3, far3, near4, far4, cross4,
         ),
     )
     (active,) = call(
@@ -561,7 +583,7 @@
     )
 
     def body(slabs, *rest):
-        fits = mesh.shape["pair"] == 4 and slabs.shape[1] == 4 * NBQ and slabs.shape[0] % 4 == 0
+        fits = mesh.shape["pair"] == 4 and slabs.shape[1] == 4 * NBQ and slabs.shape[0] % 8 == 0
         return (paired_body if fits else general_body)(slabs, *rest)
 
     return jax.shard_map(

time: 41.2 us -> 41.2 us (level)
  waiting for transfers between devices: 4.42 us -> 6.71 us
  starting transfers between devices: 12.3 us -> 10.1 us
    ppermute x9 -> x8, waiting for transfers between devices: 2.58 us -> 4.15 us  [to_peer(): return lax.ppermute(array, 'pair', [(p, p ^ k) for p in range(4)])]
    ppermute x9 -> x8, starting transfers between devices: 7.3 us -> 5.95 us  [to_peer(): return lax.ppermute(array, 'pair', [(p, p ^ k) for p in range(4)])]
    ppermute x2, starting transfers between devices: 4.97 us -> 4.19 us  [sum_over_aux(): part = part + lax.ppermute(part, 'aux', [(z, z ^ k) for z in range(n)])]
    ppermute x2, waiting for transfers between devices: 1.84 us -> 2.57 us  [sum_over_aux(): part = part + lax.ppermute(part, 'aux', [(z, z ^ k) for z in range(n)])]
  transfers between devices with their start and end apart: 11 -> 10, of which waited for: 3 -> 6; matrix products, arithmetic and copies ran while one was open for 0% -> 0% of each run, Pallas kernels for 35% -> 33%
where the time goes in v16:
time: 41.2 us; the launch traced here: 41.1 us
  Pallas kernels  22.1 us (54%)
  starting transfers between devices  10.1 us (25%)
  waiting for transfers between devices  6.71 us (16%)
  between operations  1.35 us (3%)
  other arithmetic  0.75 us (2%)
    pallas_call x7, Pallas kernels, call(): pl.pallas_call(kernel, name=name, in_specs=inputs, out_specs=[VM] * len(o...  22.1 us
    ppermute x8, starting transfers between devices, to_peer(): return lax.ppermute(array, 'pair', [(p, p ^ k) for p in range(4)])  5.95 us
    ppermute x2, starting transfers between devices, sum_over_aux(): part = part + lax.ppermute(part, 'aux', [(z, z ^ k) for z in range(n)])  4.19 us
    ppermute x8, waiting for transfers between devices, to_peer(): return lax.ppermute(array, 'pair', [(p, p ^ k) for p in range(4)])  4.15 us
    ppermute x2, waiting for transfers between devices, sum_over_aux(): part = part + lax.ppermute(part, 'aux', [(z, z ^ k) for z in range(n)])  2.57 us
  transfers between devices with their start and end apart: 10, of which 6 were waited for; matrix products, arithmetic and copies ran while one was open for 0% of the time, Pallas kernels for 33%

profile of v16, /device:TPU:0, one launch (start us, length us, event | category | flops | bytes accessed | tf_op | source)
XLA Modules:
  0.0 41.1 jit_solution(2581329536763343310)
XLA Ops:
  1.3 0.1 pad_add_fusion.where
  1.4 7.4 %slabs_first.1 = (bf16[192,1024]{1,0:T(8,128)(2,1)S(1)}, bf16[1024,256]{1,0:T(8,128)(2,1)S(1)}, bf16[4,256,256]{2,1,0:T(8,128)(2,1)S(1)}, f32[8,64,128]{2,1,0:T(...) custom-call(s32[2]{0:T(128)S(1)} %pad_add_fusion.where, ...), custom_call_target="tpu_custom_call" | custom-call | flops 5000000000 | bytes 100000 | tf_op jit(solution)/shard_map/slabs_first/pallas_call | solution.py:416
  8.8 0.5 %collective-permute-start = (bf16[1024,128]{1,0:T(8,128)(2,1)S(1)}, bf16[1024,128]{1,0:T(8,128)(2,1)S(1)}, u32[]{:S(2)}, u32[]{:S(2)}) collective-permute-start(bf16[1024,128]{1,0:T(8,128)(2,1)S(1)} %get-tuple-element.45), channel_id=1, source_target_pairs={{0,4},{4,0},{8,12},{12,8},{1,5},{5,1},{9,13},{13,9},{2,6},{6,2},{1... | collective-permute-start | bytes 786440 | tf_op jit(solution)/shard_map/ppermute | solution.py:436
  9.3 4.1 %slabs_second.1 = (f32[1024,128]{1,0:T(8,128)S(1)}, f32[128,128]{1,0:T(8,128)S(1)}, bf16[3,128,128]{2,1,0:T(8,128)(2,1)S(1)}, f32[16,128]{1,0:T(8,128)S(1)}) custom-call(s32[2]{0:T(128)S(1)} %pad_add_fusion.where, bf16[8,2,16,4096]{3,2,1,0:T(8,128)(2,1)S(1)} %get-tuple-element.37.sbuf, bf16[192,1024]{1,0:T(8,128)(2,1)S(1)} %get-tuple-element.46.lt_ref, ...), custom_call_target="tpu_custom_call" | custom-call | flops 5000000000 | bytes 100000 | tf_op jit(solution)/shard_map/slabs_second/pallas_call | solution.py:416
  13.5 2.6 %collective-permute-start.4 = (bf16[1024,128]{1,0:T(8,128)(2,1)S(1)}, bf16[1024,128]{1,0:T(8,128)(2,1)S(1)}, u32[]{:S(2)}, u32[]{:S(2)}) collective-permute-start(bf16[1024,128]{1,0:T(8,128)(2,1)S(1)} %add_convert_fusion), channel_id=1, source_target_pairs={{0,8},{4,12},{8,0},{12,4},{1,9},{5,13},{9,1},{13,5},{2,10},{6,14},... | collective-permute-start | bytes 786440 | tf_op jit(solution)/shard_map/ppermute | solution.py:436
  16.0 4.0 %slabs_third.1 = (bf16[944,128]{1,0:T(8,128)(2,1)S(1)}, bf16[896,128]{1,0:T(8,128)(2,1)S(1)}, bf16[432,128]{1,0:T(8,128)(2,1)S(1)}, f32[128,128]{1,0:T(8,128)S(1)}, f32[16,128]{1,0:T(8,128)S(1)}) custom-call(s32[2]{0:T(128)S(1)} %pad_add_fusion.where, bf16[8,2,16,4096]{3,2,1,0:T(8,128)(2,1)S(1)} %get-tuple-element.43.sbuf, ...), custom_call_target="tpu_custom_call" | custom-call | flops 5000000000 | bytes 100000 | tf_op jit(solution)/shard_map/slabs_third/pallas_call | solution.py:416
  20.1 0.3 collective-permute-start.2
  20.4 0.3 collective-permute-start.3
  20.6 0.1 collective-permute-start.1
  20.7 4.1 %slabs_fourth.1 = (f32[1024,128]{1,0:T(8,128)S(1)}, f32[128,128]{1,0:T(8,128)S(1)}, bf16[3,128,128]{2,1,0:T(8,128)(2,1)S(1)}, f32[16,128]{1,0:T(8,128)S(1)}) custom-call(s32[2]{0:T(128)S(1)} %pad_add_fusion.where, bf16[8,2,16,4096]{3,2,1,0:T(8,128)(2,1)S(1)} %get-tuple-element.52.sbuf, bf16[192,1024]{1,0:T(8,128)(2,1)S(1)} %get-tuple-element.46.lt_ref, ...), custom_call_target="tpu_custom_call" | custom-call | flops 1000000000 | bytes 100000 | tf_op jit(solution)/shard_map/slabs_fourth/pallas_call | solution.py:416
  24.8 1.0 %collective-permute-done.1.far3 = bf16[432,128]{1,0:T(8,128)(2,1)S(1)} collective-permute-done((bf16[432,128]{1,0:T(8,128)(2,1)S(1)}, bf16[432,128]{1,0:T(8,128)(2,1)S(1)}, u32[]{:S(2)}, u32[]{:S(2)}) %collective-permute-start.1) | collective-permute-done | bytes 110624 | tf_op jit(solution)/shard_map/ppermute | solution.py:436
  25.8 0.9 %exchange.1 = (bf16[160,128]{1,0:T(8,128)(2,1)S(1)}, bf16[464,128]{1,0:T(8,128)(2,1)S(1)}, bf16[160,128]{1,0:T(8,128)(2,1)S(1)}, f32[16,128]{1,0:T(8,128)S(1)}) custom-call(s32[2]{0:T(128)S(1)} %pad_add_fusion.where, f32[1024,128]{1,0:T(8,128)S(1)} %get-tuple-element.58.mine, bf16[944,128]{1,0:T(8,128)(2,1)S(1)} %collective-permute-done.2.near3, ...), custom_call_target="tpu_custom_call" | custom-call | bytes 100000 | tf_op jit(solution)/shard_map/exchange/pallas_call | solution.py:416
  26.7 1.3 %collective-permute-start.6 = (bf16[464,128]{1,0:T(8,128)(2,1)S(1)}, bf16[464,128]{1,0:T(8,128)(2,1)S(1)}, u32[]{:S(2)}, u32[]{:S(2)}) collective-permute-start(bf16[464,128]{1,0:T(8,128)(2,1)S(1)} %get-tuple-element.66), channel_id=1, source_target_pairs={{0,8},{4,12},{8,0},{12,4},{1,9},{5,13},{9,1},{13,5},{2,10},{6,14},... | collective-permute-start | bytes 356360 | tf_op jit(solution)/shard_map/ppermute | solution.py:436
  28.0 0.9 %collective-permute-start.7 = (bf16[160,128]{1,0:T(8,128)(2,1)S(1)}, bf16[160,128]{1,0:T(8,128)(2,1)S(1)}, u32[]{:S(2)}, u32[]{:S(2)}) collective-permute-start(bf16[160,128]{1,0:T(8,128)(2,1)S(1)} %get-tuple-element.67), channel_id=1, source_target_pairs={{0,12},{4,8},{8,4},{12,0},{1,13},{5,9},{9,5},{13,1},{2,14},{6,10},... | collective-permute-start | bytes 122888 | tf_op jit(solution)/shard_map/ppermute | solution.py:436
  28.9 0.3 collective-permute-done.5.near4
  29.3 2.6 %collective-permute-done.7.cross4 = bf16[160,128]{1,0:T(8,128)(2,1)S(1)} collective-permute-done((bf16[160,128]{1,0:T(8,128)(2,1)S(1)}, bf16[160,128]{1,0:T(8,128)(2,1)S(1)}, u32[]{:S(2)}, u32[]{:S(2)}) %collective-permute-start.7) | collective-permute-done | bytes 40992 | tf_op jit(solution)/shard_map/ppermute | solution.py:436
  31.9 0.2 collective-permute-done.6.far4
  32.0 0.2 coulomb.1
  32.2 1.6 %collective-permute-start.8 = (f32[16,64]{1,0:T(8,128)S(1)}, f32[16,64]{1,0:T(8,128)S(1)}, u32[]{:S(2)}, u32[]{:S(2)}) collective-permute-start(f32[16,64]{1,0:T(8,128)S(1)} %get-tuple-element.69), channel_id=1, source_target_pairs={{0,1},{1,0},{2,3},{3,2},{4,5},{5,4},{6,7},{7,6},{8,9},{9,8},{10,11... | collective-permute-start | bytes 12296 | tf_op jit(solution)/shard_map/ppermute | solution.py:411
  33.8 2.1 %collective-permute-done.8 = f32[16,64]{1,0:T(8,128)S(1)} collective-permute-done((f32[16,64]{1,0:T(8,128)S(1)}, f32[16,64]{1,0:T(8,128)S(1)}, u32[]{:S(2)}, u32[]{:S(2)}) %collective-permute-start.8) | collective-permute-done | bytes 4128 | tf_op jit(solution)/shard_map/ppermute | solution.py:411
  35.9 2.6 %collective-permute-start.9 = (f32[16,64]{1,0:T(8,128)S(1)}, f32[16,64]{1,0:T(8,128)S(1)}, u32[]{:S(2)}, u32[]{:S(2)}) collective-permute-start(f32[16,64]{1,0:T(8,128)S(1)} %add.14), channel_id=1, source_target_pairs={{0,2},{1,3},{2,0},{3,1},{4,6},{5,7},{6,4},{7,5},{8,10},{9,11},{10,... | collective-permute-start | bytes 12296 | tf_op jit(solution)/shard_map/ppermute | solution.py:411
  38.5 1.5 %own_active.1 = f32[64,16,64]{2,1,0:T(8,128)} custom-call(s32[2]{0:T(128)S(1)} %pad_add_fusion.where, f32[512,128]{1,0:T(8,128)S(1)} %get-tuple-element.68.act), custom_call_target="tpu_custom_call" | custom-call | flops 1000000 | bytes 100000 | tf_op jit(solution)/shard_map/own_active/pallas_call | solution.py:416
  40.0 0.5 %collective-permute-done.9 = f32[16,64]{1,0:T(8,128)S(1)} collective-permute-done((f32[16,64]{1,0:T(8,128)S(1)}, f32[16,64]{1,0:T(8,128)S(1)}, u32[]{:S(2)}, u32[]{:S(2)}) %collective-permute-start.9) | collective-permute-done | bytes 4128 | tf_op jit(solution)/shard_map/ppermute | solution.py:411
  40.5 0.6 %add_add_fusion = f32[16,64]{1,0:T(8,128)} fusion(f32[16,64]{1,0:T(8,128)S(1)} %copy-done, f32[16,64]{1,0:T(8,128)S(1)} %add.14, f32[16,64]{1,0:T(8,128)S(1)} %collective-permute-done.9), kind=kLoop, calls=%fused_computation.1 | loop fusion | flops 2048 | bytes 16384 | tf_op jit(solution)/shard_map/add | solution.py:539
  (9 shorter events, 0.1 us)
Async XLA Ops:
  8.8 4.6 %collective-permute-start = (bf16[1024,128]{1,0:T(8,128)(2,1)S(1)}, bf16[1024,128]{1,0:T(8,128)(2,1)S(1)}, u32[]{:S(2)}, u32[]{:S(2)}) collective-permute-start(bf16[1024,128]{1,0:T(8,128)(2,1)S(1)} %get-tuple-element.45), channel_id=1, source_target_pairs={{0,4},{4,0},{8,12},{12,8},{1,5},{5,1},{9,13},{13,9},{2,6},{6,2},{1... | collective-permute-start | bytes 786440 | tf_op jit(solution)/shard_map/ppermute | solution.py:436
  13.5 12.4 %collective-permute-start.4 = (bf16[1024,128]{1,0:T(8,128)(2,1)S(1)}, bf16[1024,128]{1,0:T(8,128)(2,1)S(1)}, u32[]{:S(2)}, u32[]{:S(2)}) collective-permute-start(bf16[1024,128]{1,0:T(8,128)(2,1)S(1)} %add_convert_fusion), channel_id=1, source_target_pairs={{0,8},{4,12},{8,0},{12,4},{1,9},{5,13},{9,1},{13,5},{2,10},{6,14},... | collective-permute-start | bytes 786440 | tf_op jit(solution)/shard_map/ppermute | solution.py:436
  20.1 5.8 %collective-permute-start.2 = (bf16[944,128]{1,0:T(8,128)(2,1)S(1)}, bf16[944,128]{1,0:T(8,128)(2,1)S(1)}, u32[]{:S(2)}, u32[]{:S(2)}) collective-permute-start(bf16[944,128]{1,0:T(8,128)(2,1)S(1)} %get-tuple-element.59), channel_id=1, source_target_pairs={{0,4},{4,0},{8,12},{12,8},{1,5},{5,1},{9,13},{13,9},{2,6},{6,2},{1... | collective-permute-start | bytes 725000 | tf_op jit(solution)/shard_map/ppermute | solution.py:436
  20.4 5.5 %collective-permute-start.3 = (bf16[896,128]{1,0:T(8,128)(2,1)S(1)}, bf16[896,128]{1,0:T(8,128)(2,1)S(1)}, u32[]{:S(2)}, u32[]{:S(2)}) collective-permute-start(bf16[896,128]{1,0:T(8,128)(2,1)S(1)} %get-tuple-element.60), channel_id=1, source_target_pairs={{0,4},{4,0},{8,12},{12,8},{1,5},{5,1},{9,13},{13,9},{2,6},{6,2},{1... | collective-permute-start | bytes 688136 | tf_op jit(solution)/shard_map/ppermute | solution.py:436
  20.6 5.2 %collective-permute-start.1 = (bf16[432,128]{1,0:T(8,128)(2,1)S(1)}, bf16[432,128]{1,0:T(8,128)(2,1)S(1)}, u32[]{:S(2)}, u32[]{:S(2)}) collective-permute-start(bf16[432,128]{1,0:T(8,128)(2,1)S(1)} %get-tuple-element.56), channel_id=1, source_target_pairs={{0,8},{4,12},{8,0},{12,4},{1,9},{5,13},{9,1},{13,5},{2,10},{6,14},... | collective-permute-start | bytes 331784 | tf_op jit(solution)/shard_map/ppermute | solution.py:436
  24.8 15.7 %copy-start = (f32[16,64]{1,0:T(8,128)S(1)}, f32[16,64]{1,0:T(8,128)}, u32[]{:S(2)}) copy-start(f32[16,64]{1,0:T(8,128)} %param.11) | copy-start | bytes 12292
  26.7 5.3 %collective-permute-start.6 = (bf16[464,128]{1,0:T(8,128)(2,1)S(1)}, bf16[464,128]{1,0:T(8,128)(2,1)S(1)}, u32[]{:S(2)}, u32[]{:S(2)}) collective-permute-start(bf16[464,128]{1,0:T(8,128)(2,1)S(1)} %get-tuple-element.66), channel_id=1, source_target_pairs={{0,8},{4,12},{8,0},{12,4},{1,9},{5,13},{9,1},{13,5},{2,10},{6,14},... | collective-permute-start | bytes 356360 | tf_op jit(solution)/shard_map/ppermute | solution.py:436
  28.0 1.2 %collective-permute-start.5 = (bf16[160,128]{1,0:T(8,128)(2,1)S(1)}, bf16[160,128]{1,0:T(8,128)(2,1)S(1)}, u32[]{:S(2)}, u32[]{:S(2)}) collective-permute-start(bf16[160,128]{1,0:T(8,128)(2,1)S(1)} %get-tuple-element.65), channel_id=1, source_target_pairs={{0,4},{4,0},{8,12},{12,8},{1,5},{5,1},{9,13},{13,9},{2,6},{6,2},{1... | collective-permute-start | bytes 122888 | tf_op jit(solution)/shard_map/ppermute | solution.py:436
  28.0 3.8 %collective-permute-start.7 = (bf16[160,128]{1,0:T(8,128)(2,1)S(1)}, bf16[160,128]{1,0:T(8,128)(2,1)S(1)}, u32[]{:S(2)}, u32[]{:S(2)}) collective-permute-start(bf16[160,128]{1,0:T(8,128)(2,1)S(1)} %get-tuple-element.67), channel_id=1, source_target_pairs={{0,12},{4,8},{8,4},{12,0},{1,13},{5,9},{9,5},{13,1},{2,14},{6,10},... | collective-permute-start | bytes 122888 | tf_op jit(solution)/shard_map/ppermute | solution.py:436
  32.2 3.7 %collective-permute-start.8 = (f32[16,64]{1,0:T(8,128)S(1)}, f32[16,64]{1,0:T(8,128)S(1)}, u32[]{:S(2)}, u32[]{:S(2)}) collective-permute-start(f32[16,64]{1,0:T(8,128)S(1)} %get-tuple-element.69), channel_id=1, source_target_pairs={{0,1},{1,0},{2,3},{3,2},{4,5},{5,4},{6,7},{7,6},{8,9},{9,8},{10,11... | collective-permute-start | bytes 12296 | tf_op jit(solution)/shard_map/ppermute | solution.py:411
  35.9 4.5 %collective-permute-start.9 = (f32[16,64]{1,0:T(8,128)S(1)}, f32[16,64]{1,0:T(8,128)S(1)}, u32[]{:S(2)}, u32[]{:S(2)}) collective-permute-start(f32[16,64]{1,0:T(8,128)S(1)} %add.14), channel_id=1, source_target_pairs={{0,2},{1,3},{2,0},{3,1},{4,6},{5,7},{6,4},{7,5},{8,10},{9,11},{10,... | collective-permute-start | bytes 12296 | tf_op jit(solution)/shard_map/ppermute | solution.py:411

commit v17 on v16

--- a/solution.py
+++ b/solution.py
@@ -506,7 +506,6 @@
     )
     last = shape((LAST, LANES), BF)
     last_far = shape((LAST + 2 * PER + 3 * NBQ, LANES), BF)
-    far3, keep_in4 = lax.optimization_barrier((far3, keep_in4))
     near4, far4, cross4, exch = call(
         exchange_kernel,
         "exchange",
@@ -515,6 +514,7 @@
         [pltpu.VMEM((NACT, LANES), F32)],
         (where, keep_in4, near3, near3b, far1, sends4, dens4),
     )
+    far3, far4 = lax.optimization_barrier((far3, far4))
     far4, cross4, near4 = to_peer(2, far4), to_peer(3, cross4), to_peer(1, near4)
     act, partial = call(
         coulomb_kernel,

time: 41.2 us -> 40.8 us (level)
  waiting for transfers between devices: 6.71 us -> 6.15 us
  transfers between devices with their start and end apart: 10 -> 10, of which waited for: 6 -> 5; matrix products, arithmetic and copies ran while one was open for 0% -> 0% of each run, Pallas kernels for 33% -> 36%
where the time goes in v17:
time: 40.8 us; the launch traced here: 40.7 us
  Pallas kernels  22.1 us (54%)
  starting transfers between devices  10.3 us (25%)
  waiting for transfers between devices  6.15 us (15%)
  between operations  1.37 us (3%)
  other arithmetic  0.75 us (2%)
    pallas_call x7, Pallas kernels, call(): pl.pallas_call(kernel, name=name, in_specs=inputs, out_specs=[VM] * len(o...  22.1 us
    ppermute x8, starting transfers between devices, to_peer(): return lax.ppermute(array, 'pair', [(p, p ^ k) for p in range(4)])  5.88 us
    ppermute x2, starting transfers between devices, sum_over_aux(): part = part + lax.ppermute(part, 'aux', [(z, z ^ k) for z in range(n)])  4.39 us
    ppermute x8, waiting for transfers between devices, to_peer(): return lax.ppermute(array, 'pair', [(p, p ^ k) for p in range(4)])  3.79 us
    ppermute x2, waiting for transfers between devices, sum_over_aux(): part = part + lax.ppermute(part, 'aux', [(z, z ^ k) for z in range(n)])  2.36 us
  transfers between devices with their start and end apart: 10, of which 5 were waited for; matrix products, arithmetic and copies ran while one was open for 0% of the time, Pallas kernels for 36%

profile of v17, /device:TPU:0, one launch (start us, length us, event | category | flops | bytes accessed | tf_op | source)
XLA Modules:
  0.0 40.7 jit_solution(880090627558340117)
XLA Ops:
  1.3 0.1 pad_add_fusion.where
  1.4 7.4 %slabs_first.1 = (bf16[192,1024]{1,0:T(8,128)(2,1)S(1)}, bf16[1024,256]{1,0:T(8,128)(2,1)S(1)}, bf16[4,256,256]{2,1,0:T(8,128)(2,1)S(1)}, f32[8,64,128]{2,1,0:T(...) custom-call(s32[2]{0:T(128)S(1)} %pad_add_fusion.where, ...), custom_call_target="tpu_custom_call" | custom-call | flops 5000000000 | bytes 100000 | tf_op jit(solution)/shard_map/slabs_first/pallas_call | solution.py:416
  8.8 0.5 %collective-permute-start = (bf16[1024,128]{1,0:T(8,128)(2,1)S(1)}, bf16[1024,128]{1,0:T(8,128)(2,1)S(1)}, u32[]{:S(2)}, u32[]{:S(2)}) collective-permute-start(bf16[1024,128]{1,0:T(8,128)(2,1)S(1)} %get-tuple-element.45), channel_id=1, source_target_pairs={{0,4},{4,0},{8,12},{12,8},{1,5},{5,1},{9,13},{13,9},{2,6},{6,2},{1... | collective-permute-start | bytes 786440 | tf_op jit(solution)/shard_map/ppermute | solution.py:436
  9.3 4.1 %slabs_second.1 = (f32[1024,128]{1,0:T(8,128)S(1)}, f32[128,128]{1,0:T(8,128)S(1)}, bf16[3,128,128]{2,1,0:T(8,128)(2,1)S(1)}, f32[16,128]{1,0:T(8,128)S(1)}) custom-call(s32[2]{0:T(128)S(1)} %pad_add_fusion.where, bf16[8,2,16,4096]{3,2,1,0:T(8,128)(2,1)S(1)} %get-tuple-element.37.sbuf, bf16[192,1024]{1,0:T(8,128)(2,1)S(1)} %get-tuple-element.46.lt_ref, ...), custom_call_target="tpu_custom_call" | custom-call | flops 5000000000 | bytes 100000 | tf_op jit(solution)/shard_map/slabs_second/pallas_call | solution.py:416
  13.4 0.1 add_convert_fusion
  13.5 2.6 %collective-permute-start.3 = (bf16[1024,128]{1,0:T(8,128)(2,1)S(1)}, bf16[1024,128]{1,0:T(8,128)(2,1)S(1)}, u32[]{:S(2)}, u32[]{:S(2)}) collective-permute-start(bf16[1024,128]{1,0:T(8,128)(2,1)S(1)} %add_convert_fusion), channel_id=1, source_target_pairs={{0,8},{4,12},{8,0},{12,4},{1,9},{5,13},{9,1},{13,5},{2,10},{6,14},... | collective-permute-start | bytes 786440 | tf_op jit(solution)/shard_map/ppermute | solution.py:436
  16.0 4.0 %slabs_third.1 = (bf16[944,128]{1,0:T(8,128)(2,1)S(1)}, bf16[896,128]{1,0:T(8,128)(2,1)S(1)}, bf16[432,128]{1,0:T(8,128)(2,1)S(1)}, f32[128,128]{1,0:T(8,128)S(1)}, f32[16,128]{1,0:T(8,128)S(1)}) custom-call(s32[2]{0:T(128)S(1)} %pad_add_fusion.where, bf16[8,2,16,4096]{3,2,1,0:T(8,128)(2,1)S(1)} %get-tuple-element.43.sbuf, ...), custom_call_target="tpu_custom_call" | custom-call | flops 5000000000 | bytes 100000 | tf_op jit(solution)/shard_map/slabs_third/pallas_call | solution.py:416
  20.1 0.3 collective-permute-start.1
  20.4 0.3 collective-permute-start.2
  20.6 0.1 collective-permute-start.4
  20.7 4.1 %slabs_fourth.1 = (f32[1024,128]{1,0:T(8,128)S(1)}, f32[128,128]{1,0:T(8,128)S(1)}, bf16[3,128,128]{2,1,0:T(8,128)(2,1)S(1)}, f32[16,128]{1,0:T(8,128)S(1)}) custom-call(s32[2]{0:T(128)S(1)} %pad_add_fusion.where, bf16[8,2,16,4096]{3,2,1,0:T(8,128)(2,1)S(1)} %get-tuple-element.52.sbuf, bf16[192,1024]{1,0:T(8,128)(2,1)S(1)} %get-tuple-element.46.lt_ref, ...), custom_call_target="tpu_custom_call" | custom-call | flops 1000000000 | bytes 100000 | tf_op jit(solution)/shard_map/slabs_fourth/pallas_call | solution.py:416
  24.8 0.9 %exchange.1 = (bf16[160,128]{1,0:T(8,128)(2,1)S(1)}, bf16[464,128]{1,0:T(8,128)(2,1)S(1)}, bf16[160,128]{1,0:T(8,128)(2,1)S(1)}, f32[16,128]{1,0:T(8,128)S(1)}) custom-call(s32[2]{0:T(128)S(1)} %pad_add_fusion.where, f32[1024,128]{1,0:T(8,128)S(1)} %get-tuple-element.56.mine, bf16[944,128]{1,0:T(8,128)(2,1)S(1)} %collective-permute-done.1.near3, ...), custom_call_target="tpu_custom_call" | custom-call | bytes 100000 | tf_op jit(solution)/shard_map/exchange/pallas_call | solution.py:416
  25.7 0.1 collective-permute-done.4.far3
  25.8 1.9 %collective-permute-start.6 = (bf16[464,128]{1,0:T(8,128)(2,1)S(1)}, bf16[464,128]{1,0:T(8,128)(2,1)S(1)}, u32[]{:S(2)}, u32[]{:S(2)}) collective-permute-start(bf16[464,128]{1,0:T(8,128)(2,1)S(1)} %get-tuple-element.66), channel_id=1, source_target_pairs={{0,8},{4,12},{8,0},{12,4},{1,9},{5,13},{9,1},{13,5},{2,10},{6,14},... | collective-permute-start | bytes 356360 | tf_op jit(solution)/shard_map/ppermute | solution.py:436
  27.7 0.2 collective-permute-start.7
  28.0 1.0 %collective-permute-done.5.near4 = bf16[160,128]{1,0:T(8,128)(2,1)S(1)} collective-permute-done((bf16[160,128]{1,0:T(8,128)(2,1)S(1)}, bf16[160,128]{1,0:T(8,128)(2,1)S(1)}, u32[]{:S(2)}, u32[]{:S(2)}) %collective-permute-start.5) | collective-permute-done | bytes 40992 | tf_op jit(solution)/shard_map/ppermute | solution.py:436
  28.9 2.7 %collective-permute-done.7.cross4 = bf16[160,128]{1,0:T(8,128)(2,1)S(1)} collective-permute-done((bf16[160,128]{1,0:T(8,128)(2,1)S(1)}, bf16[160,128]{1,0:T(8,128)(2,1)S(1)}, u32[]{:S(2)}, u32[]{:S(2)}) %collective-permute-start.7) | collective-permute-done | bytes 40992 | tf_op jit(solution)/shard_map/ppermute | solution.py:436
  31.6 0.2 coulomb.1
  31.8 1.7 %collective-permute-start.8 = (f32[16,64]{1,0:T(8,128)S(1)}, f32[16,64]{1,0:T(8,128)S(1)}, u32[]{:S(2)}, u32[]{:S(2)}) collective-permute-start(f32[16,64]{1,0:T(8,128)S(1)} %get-tuple-element.69), channel_id=1, source_target_pairs={{0,1},{1,0},{2,3},{3,2},{4,5},{5,4},{6,7},{7,6},{8,9},{9,8},{10,11... | collective-permute-start | bytes 12296 | tf_op jit(solution)/shard_map/ppermute | solution.py:411
  33.5 2.0 %collective-permute-done.8 = f32[16,64]{1,0:T(8,128)S(1)} collective-permute-done((f32[16,64]{1,0:T(8,128)S(1)}, f32[16,64]{1,0:T(8,128)S(1)}, u32[]{:S(2)}, u32[]{:S(2)}) %collective-permute-start.8) | collective-permute-done | bytes 4128 | tf_op jit(solution)/shard_map/ppermute | solution.py:411
  35.5 2.7 %collective-permute-start.9 = (f32[16,64]{1,0:T(8,128)S(1)}, f32[16,64]{1,0:T(8,128)S(1)}, u32[]{:S(2)}, u32[]{:S(2)}) collective-permute-start(f32[16,64]{1,0:T(8,128)S(1)} %add.14), channel_id=1, source_target_pairs={{0,2},{1,3},{2,0},{3,1},{4,6},{5,7},{6,4},{7,5},{8,10},{9,11},{10,... | collective-permute-start | bytes 12296 | tf_op jit(solution)/shard_map/ppermute | solution.py:411
  38.2 1.5 %own_active.1 = f32[64,16,64]{2,1,0:T(8,128)} custom-call(s32[2]{0:T(128)S(1)} %pad_add_fusion.where, f32[512,128]{1,0:T(8,128)S(1)} %get-tuple-element.68.act), custom_call_target="tpu_custom_call" | custom-call | flops 1000000 | bytes 100000 | tf_op jit(solution)/shard_map/own_active/pallas_call | solution.py:416
  39.7 0.4 collective-permute-done.9
  40.1 0.6 %add_add_fusion = f32[16,64]{1,0:T(8,128)} fusion(f32[16,64]{1,0:T(8,128)S(1)} %copy-done, f32[16,64]{1,0:T(8,128)S(1)} %add.14, f32[16,64]{1,0:T(8,128)S(1)} %collective-permute-done.9), kind=kLoop, calls=%fused_computation.1 | loop fusion | flops 2048 | bytes 16384 | tf_op jit(solution)/shard_map/add | solution.py:539
  (9 shorter events, 0.0 us)
Async XLA Ops:
  8.8 4.6 %collective-permute-start = (bf16[1024,128]{1,0:T(8,128)(2,1)S(1)}, bf16[1024,128]{1,0:T(8,128)(2,1)S(1)}, u32[]{:S(2)}, u32[]{:S(2)}) collective-permute-start(bf16[1024,128]{1,0:T(8,128)(2,1)S(1)} %get-tuple-element.45), channel_id=1, source_target_pairs={{0,4},{4,0},{8,12},{12,8},{1,5},{5,1},{9,13},{13,9},{2,6},{6,2},{1... | collective-permute-start | bytes 786440 | tf_op jit(solution)/shard_map/ppermute | solution.py:436
  13.5 11.4 %collective-permute-start.3 = (bf16[1024,128]{1,0:T(8,128)(2,1)S(1)}, bf16[1024,128]{1,0:T(8,128)(2,1)S(1)}, u32[]{:S(2)}, u32[]{:S(2)}) collective-permute-start(bf16[1024,128]{1,0:T(8,128)(2,1)S(1)} %add_convert_fusion), channel_id=1, source_target_pairs={{0,8},{4,12},{8,0},{12,4},{1,9},{5,13},{9,1},{13,5},{2,10},{6,14},... | collective-permute-start | bytes 786440 | tf_op jit(solution)/shard_map/ppermute | solution.py:436
  20.1 4.8 %collective-permute-start.1 = (bf16[944,128]{1,0:T(8,128)(2,1)S(1)}, bf16[944,128]{1,0:T(8,128)(2,1)S(1)}, u32[]{:S(2)}, u32[]{:S(2)}) collective-permute-start(bf16[944,128]{1,0:T(8,128)(2,1)S(1)} %get-tuple-element.57), channel_id=1, source_target_pairs={{0,4},{4,0},{8,12},{12,8},{1,5},{5,1},{9,13},{13,9},{2,6},{6,2},{1... | collective-permute-start | bytes 725000 | tf_op jit(solution)/shard_map/ppermute | solution.py:436
  20.4 4.5 %collective-permute-start.2 = (bf16[896,128]{1,0:T(8,128)(2,1)S(1)}, bf16[896,128]{1,0:T(8,128)(2,1)S(1)}, u32[]{:S(2)}, u32[]{:S(2)}) collective-permute-start(bf16[896,128]{1,0:T(8,128)(2,1)S(1)} %get-tuple-element.58), channel_id=1, source_target_pairs={{0,4},{4,0},{8,12},{12,8},{1,5},{5,1},{9,13},{13,9},{2,6},{6,2},{1... | collective-permute-start | bytes 688136 | tf_op jit(solution)/shard_map/ppermute | solution.py:436
  20.6 5.2 %collective-permute-start.4 = (bf16[432,128]{1,0:T(8,128)(2,1)S(1)}, bf16[432,128]{1,0:T(8,128)(2,1)S(1)}, u32[]{:S(2)}, u32[]{:S(2)}) collective-permute-start(bf16[432,128]{1,0:T(8,128)(2,1)S(1)} %get-tuple-element.62), channel_id=1, source_target_pairs={{0,8},{4,12},{8,0},{12,4},{1,9},{5,13},{9,1},{13,5},{2,10},{6,14},... | collective-permute-start | bytes 331784 | tf_op jit(solution)/shard_map/ppermute | solution.py:436
  24.8 15.3 %copy-start = (f32[16,64]{1,0:T(8,128)S(1)}, f32[16,64]{1,0:T(8,128)}, u32[]{:S(2)}) copy-start(f32[16,64]{1,0:T(8,128)} %param.11) | copy-start | bytes 12292
  25.8 5.8 %collective-permute-start.6 = (bf16[464,128]{1,0:T(8,128)(2,1)S(1)}, bf16[464,128]{1,0:T(8,128)(2,1)S(1)}, u32[]{:S(2)}, u32[]{:S(2)}) collective-permute-start(bf16[464,128]{1,0:T(8,128)(2,1)S(1)} %get-tuple-element.66), channel_id=1, source_target_pairs={{0,8},{4,12},{8,0},{12,4},{1,9},{5,13},{9,1},{13,5},{2,10},{6,14},... | collective-permute-start | bytes 356360 | tf_op jit(solution)/shard_map/ppermute | solution.py:436
  27.7 1.2 %collective-permute-start.5 = (bf16[160,128]{1,0:T(8,128)(2,1)S(1)}, bf16[160,128]{1,0:T(8,128)(2,1)S(1)}, u32[]{:S(2)}, u32[]{:S(2)}) collective-permute-start(bf16[160,128]{1,0:T(8,128)(2,1)S(1)} %get-tuple-element.65), channel_id=1, source_target_pairs={{0,4},{4,0},{8,12},{12,8},{1,5},{5,1},{9,13},{13,9},{2,6},{6,2},{1... | collective-permute-start | bytes 122888 | tf_op jit(solution)/shard_map/ppermute | solution.py:436
  27.7 3.9 %collective-permute-start.7 = (bf16[160,128]{1,0:T(8,128)(2,1)S(1)}, bf16[160,128]{1,0:T(8,128)(2,1)S(1)}, u32[]{:S(2)}, u32[]{:S(2)}) collective-permute-start(bf16[160,128]{1,0:T(8,128)(2,1)S(1)} %get-tuple-element.67), channel_id=1, source_target_pairs={{0,12},{4,8},{8,4},{12,0},{1,13},{5,9},{9,5},{13,1},{2,14},{6,10},... | collective-permute-start | bytes 122888 | tf_op jit(solution)/shard_map/ppermute | solution.py:436
  31.8 3.7 %collective-permute-start.8 = (f32[16,64]{1,0:T(8,128)S(1)}, f32[16,64]{1,0:T(8,128)S(1)}, u32[]{:S(2)}, u32[]{:S(2)}) collective-permute-start(f32[16,64]{1,0:T(8,128)S(1)} %get-tuple-element.69), channel_id=1, source_target_pairs={{0,1},{1,0},{2,3},{3,2},{4,5},{5,4},{6,7},{7,6},{8,9},{9,8},{10,11... | collective-permute-start | bytes 12296 | tf_op jit(solution)/shard_map/ppermute | solution.py:411
  35.5 4.5 %collective-permute-start.9 = (f32[16,64]{1,0:T(8,128)S(1)}, f32[16,64]{1,0:T(8,128)S(1)}, u32[]{:S(2)}, u32[]{:S(2)}) collective-permute-start(f32[16,64]{1,0:T(8,128)S(1)} %add.14), channel_id=1, source_target_pairs={{0,2},{1,3},{2,0},{3,1},{4,6},{5,7},{6,4},{7,5},{8,10},{9,11},{10,... | collective-permute-start | bytes 12296 | tf_op jit(solution)/shard_map/ppermute | solution.py:411

commit v18 on v17

--- a/solution.py
+++ b/solution.py
@@ -258,6 +258,7 @@
         emit_active(h, act, core, x, keep, sends)
 
     run_block(sbuf, (lt_out, r_out, bd_out, d_out), scratch, emit, prepare, arrive)
+    msg[pl.ds(INROWS, PER), :] = sends[2]
     dens[...] = density_of(scratch[6][...])
     for copy in ahead:
         copy.wait()
@@ -277,7 +278,7 @@
 
 
 def third_kernel(
-    where, sbuf, lt_ref, r_ref, bd_ref, d_ref, sends1, sends2, dens1, dens2,
+    where, sbuf, lt_ref, r_ref, bd_ref, d_ref, sends1, sends2, dens1, dens2, near1,
     near, near_more, far, keep, dens, sends, *scratch
 ):
     core, x = where[0], where[1]
@@ -290,11 +291,15 @@
     run_block(sbuf, (lt_ref, r_ref, bd_ref, d_ref), scratch, emit)
     dens[...] = density_of(scratch[6][...])
     wires = [split_wire(d[...]) for d in (dens1, dens2, dens)]
-    for n, source in enumerate((sends1, sends2, sends)):
+    for n, source in enumerate((sends2, sends)):
         near_more[pl.ds(INROWS // 2 + n * PER, PER), :] = source[2]
+    passed = near1[pl.ds(INROWS, PER), :]
     for k, (msg, base) in enumerate(((near, INROWS // 2), (far, 0))):
         for n, source in enumerate((sends1, sends2, sends)):
-            msg[pl.ds(base + n * PER, PER), :] = source[k]
+            rows = source[k]
+            if (k, n) == (1, 1):
+                rows = (rows.astype(F32) + passed.astype(F32)).astype(BF)
+            msg[pl.ds(base + n * PER, PER), :] = rows
             msg[pl.ds(base + 3 * PER + n * NBQ, NBQ), :] = wires[n]
 
 
@@ -330,14 +335,14 @@
     for k, msg in enumerate((near, far, cross)):
         rows = sends[k]
         if k == 1:
-            passed = near3b[pl.ds(INROWS // 2 + 2 * PER, PER), :]
+            passed = near3b[pl.ds(INROWS // 2 + PER, PER), :]
             rows = (rows.astype(F32) + passed.astype(F32)).astype(BF)
         msg[pl.ds(0, PER), :] = rows
         msg[pl.ds(PER, NBQ), :] = wire
         at = pl.multiple_of((index ^ (k + 1)) * QUARTER, QUARTER)
         msg[pl.ds(PER + NBQ, QUARTER), :] = split_wire(whole[pl.ds(at, QUARTER), :])
-    far[pl.ds(LAST, 2 * PER), :] = near3b[pl.ds(INROWS // 2, 2 * PER), :]
-    far[pl.ds(LAST + 2 * PER, 3 * NBQ), :] = near3[pl.ds(INROWS // 2 + 3 * PER, 3 * NBQ), :]
+    far[pl.ds(LAST, PER), :] = near3b[pl.ds(INROWS // 2, PER), :]
+    far[pl.ds(LAST + PER, 3 * NBQ), :] = near3[pl.ds(INROWS // 2 + 3 * PER, 3 * NBQ), :]
 
 
 def coulomb_kernel(
@@ -357,11 +362,11 @@
             if n == 3:
                 at, dens_at = 0, PER
             elif k == 3:
-                at, dens_at = LAST + n * PER, LAST + 2 * PER + n * NBQ
+                at, dens_at = LAST, LAST + PER + n * NBQ
             else:
                 base = INROWS // 2 if k == 1 else 0
                 at, dens_at = base + n * PER, base + 3 * PER + n * NBQ
-            if not (k == 3 and n == 2):
+            if not (k == 3 and n in (0, 2)):
                 rows = rows + msg[pl.ds(at, PER), :].astype(F32)
             d = d + joined(msg[pl.ds(dens_at, NBQ), :])
         act[pl.ds(m * PER, PER), :] = rows
@@ -455,7 +460,7 @@
         first_kernel,
         "slabs_first",
         [SM, HB, HB, SM, HB, HB],
-        weights + (shape((INROWS, LANES), BF),) + kept + (loaded,) * 3,
+        weights + (shape((INROWS + PER, LANES), BF),) + kept + (loaded,) * 3,
         [
             pltpu.SMEM((nslab,), jnp.int32), pltpu.SMEM((nslab,), jnp.int32),
             pltpu.VMEM(orbitals.T.shape, BF), pltpu.SemaphoreType.DMA((8,)),
@@ -477,20 +482,20 @@
         (where, slabs2, lt, r, bd, d),
         work,
     )
-    out2 = (keep_in2 + near1.astype(F32)).astype(BF)
+    out2 = (keep_in2 + near1[:INROWS].astype(F32)).astype(BF)
     out2, lt = lax.optimization_barrier((out2, lt))
     far1 = to_peer(2, out2)
     news = 3 * PER + 3 * NBQ
     msg3, msg3b, msg3x, keep3, dens3 = call(
         third_kernel,
         "slabs_third",
-        [SM] + [VM] * 9,
+        [SM] + [VM] * 10,
         (
-            shape((INROWS // 2 + news, LANES), BF), shape((INROWS // 2 + 3 * PER, LANES), BF),
+            shape((INROWS // 2 + news, LANES), BF), shape((INROWS // 2 + 2 * PER, LANES), BF),
             shape((news, LANES), BF), kept[0], kept[2],
         ),
         [pltpu.VMEM((3, PER, LANES), BF)] + scratch,
-        (where, slabs3, lt, r, bd, d, sends1, sends2, dens1, dens2),
+        (where, slabs3, lt, r, bd, d, sends1, sends2, dens1, dens2, near1),
         work,
     )
     near3, near3b = to_peer(1, msg3), to_peer(1, msg3b)
@@ -505,7 +510,7 @@
         LAST_WORK,
     )
     last = shape((LAST, LANES), BF)
-    last_far = shape((LAST + 2 * PER + 3 * NBQ, LANES), BF)
+    last_far = shape((LAST + PER + 3 * NBQ, LANES), BF)
     near4, far4, cross4, exch = call(
         exchange_kernel,
         "exchange",

time: 40.8 us -> 40.4 us (level)
    ppermute x8, waiting for transfers between devices: 3.79 us -> 3.32 us  [to_peer(): return lax.ppermute(array, 'pair', [(p, p ^ k) for p in range(4)])]
where the time goes in v18:
time: 40.4 us; the launch traced here: 40.2 us
  Pallas kernels  22.1 us (55%)
  starting transfers between devices  10.1 us (25%)
  waiting for transfers between devices  5.88 us (15%)
  between operations  1.37 us (3%)
  other arithmetic  0.74 us (2%)
    pallas_call x7, Pallas kernels, call(): pl.pallas_call(kernel, name=name, in_specs=inputs, out_specs=[VM] * len(o...  22.1 us
    ppermute x8, starting transfers between devices, to_peer(): return lax.ppermute(array, 'pair', [(p, p ^ k) for p in range(4)])  5.89 us
    ppermute x2, starting transfers between devices, sum_over_aux(): part = part + lax.ppermute(part, 'aux', [(z, z ^ k) for z in range(n)])  4.19 us
    ppermute x8, waiting for transfers between devices, to_peer(): return lax.ppermute(array, 'pair', [(p, p ^ k) for p in range(4)])  3.32 us
    ppermute x2, waiting for transfers between devices, sum_over_aux(): part = part + lax.ppermute(part, 'aux', [(z, z ^ k) for z in range(n)])  2.56 us
  transfers between devices with their start and end apart: 10, of which 5 were waited for; matrix products, arithmetic and copies ran while one was open for 0% of the time, Pallas kernels for 36%

profile of v18, /device:TPU:0, one launch (start us, length us, event | category | flops | bytes accessed | tf_op | source)
XLA Modules:
  0.0 40.2 jit_solution(11046898936290971597)
XLA Ops:
  1.3 0.1 pad_add_fusion.where
  1.4 7.4 %slabs_first.1 = (bf16[192,1024]{1,0:T(8,128)(2,1)S(1)}, bf16[1024,256]{1,0:T(8,128)(2,1)S(1)}, bf16[4,256,256]{2,1,0:T(8,128)(2,1)S(1)}, f32[8,64,128]{2,1,0:T(...) custom-call(s32[2]{0:T(128)S(1)} %pad_add_fusion.where, ...), custom_call_target="tpu_custom_call" | custom-call | flops 5000000000 | bytes 100000 | tf_op jit(solution)/shard_map/slabs_first/pallas_call | solution.py:421
  8.8 0.5 %collective-permute-start = (bf16[1152,128]{1,0:T(8,128)(2,1)S(1)}, bf16[1152,128]{1,0:T(8,128)(2,1)S(1)}, u32[]{:S(2)}, u32[]{:S(2)}) collective-permute-start(bf16[1152,128]{1,0:T(8,128)(2,1)S(1)} %get-tuple-element.45), channel_id=1, source_target_pairs={{0,4},{4,0},{8,12},{12,8},{1,5},{5,1},{9,13},{13,9},{2,6},{6,2},{1... | collective-permute-start | bytes 884744 | tf_op jit(solution)/shard_map/ppermute | solution.py:441
  9.3 4.1 %slabs_second.1 = (f32[1024,128]{1,0:T(8,128)S(1)}, f32[128,128]{1,0:T(8,128)S(1)}, bf16[3,128,128]{2,1,0:T(8,128)(2,1)S(1)}, f32[16,128]{1,0:T(8,128)S(1)}) custom-call(s32[2]{0:T(128)S(1)} %pad_add_fusion.where, bf16[8,2,16,4096]{3,2,1,0:T(8,128)(2,1)S(1)} %get-tuple-element.37.sbuf, bf16[192,1024]{1,0:T(8,128)(2,1)S(1)} %get-tuple-element.46.lt_ref, ...), custom_call_target="tpu_custom_call" | custom-call | flops 5000000000 | bytes 100000 | tf_op jit(solution)/shard_map/slabs_second/pallas_call | solution.py:421
  13.4 0.1 add_convert_fusion
  13.5 2.6 %collective-permute-start.3 = (bf16[1024,128]{1,0:T(8,128)(2,1)S(1)}, bf16[1024,128]{1,0:T(8,128)(2,1)S(1)}, u32[]{:S(2)}, u32[]{:S(2)}) collective-permute-start(bf16[1024,128]{1,0:T(8,128)(2,1)S(1)} %add_convert_fusion), channel_id=1, source_target_pairs={{0,8},{4,12},{8,0},{12,4},{1,9},{5,13},{9,1},{13,5},{2,10},{6,14},... | collective-permute-start | bytes 786440 | tf_op jit(solution)/shard_map/ppermute | solution.py:441
  16.0 4.1 %slabs_third.1 = (bf16[944,128]{1,0:T(8,128)(2,1)S(1)}, bf16[768,128]{1,0:T(8,128)(2,1)S(1)}, bf16[432,128]{1,0:T(8,128)(2,1)S(1)}, f32[128,128]{1,0:T(8,128)S(1)}, f32[16,128]{1,0:T(8,128)S(1)}) custom-call(s32[2]{0:T(128)S(1)} %pad_add_fusion.where, bf16[8,2,16,4096]{3,2,1,0:T(8,128)(2,1)S(1)} %get-tuple-element.43.sbuf, ...), custom_call_target="tpu_custom_call" | custom-call | flops 5000000000 | bytes 100000 | tf_op jit(solution)/shard_map/slabs_third/pallas_call | solution.py:421
  20.1 0.3 collective-permute-start.1
  20.4 0.3 collective-permute-start.2
  20.7 0.1 collective-permute-start.4
  20.8 4.1 %slabs_fourth.1 = (f32[1024,128]{1,0:T(8,128)S(1)}, f32[128,128]{1,0:T(8,128)S(1)}, bf16[3,128,128]{2,1,0:T(8,128)(2,1)S(1)}, f32[16,128]{1,0:T(8,128)S(1)}) custom-call(s32[2]{0:T(128)S(1)} %pad_add_fusion.where, bf16[8,2,16,4096]{3,2,1,0:T(8,128)(2,1)S(1)} %get-tuple-element.52.sbuf, bf16[192,1024]{1,0:T(8,128)(2,1)S(1)} %get-tuple-element.46.lt_ref, ...), custom_call_target="tpu_custom_call" | custom-call | flops 1000000000 | bytes 100000 | tf_op jit(solution)/shard_map/slabs_fourth/pallas_call | solution.py:421
  24.9 0.9 %exchange.1 = (bf16[160,128]{1,0:T(8,128)(2,1)S(1)}, bf16[336,128]{1,0:T(8,128)(2,1)S(1)}, bf16[160,128]{1,0:T(8,128)(2,1)S(1)}, f32[16,128]{1,0:T(8,128)S(1)}) custom-call(s32[2]{0:T(128)S(1)} %pad_add_fusion.where, f32[1024,128]{1,0:T(8,128)S(1)} %get-tuple-element.56.mine, bf16[944,128]{1,0:T(8,128)(2,1)S(1)} %collective-permute-done.1.near3, ...), custom_call_target="tpu_custom_call" | custom-call | bytes 100000 | tf_op jit(solution)/shard_map/exchange/pallas_call | solution.py:421
  25.7 0.1 collective-permute-done.4.far3
  25.8 1.9 %collective-permute-start.6 = (bf16[336,128]{1,0:T(8,128)(2,1)S(1)}, bf16[336,128]{1,0:T(8,128)(2,1)S(1)}, u32[]{:S(2)}, u32[]{:S(2)}) collective-permute-start(bf16[336,128]{1,0:T(8,128)(2,1)S(1)} %get-tuple-element.66), channel_id=1, source_target_pairs={{0,8},{4,12},{8,0},{12,4},{1,9},{5,13},{9,1},{13,5},{2,10},{6,14},... | collective-permute-start | bytes 258056 | tf_op jit(solution)/shard_map/ppermute | solution.py:441
  27.7 0.2 collective-permute-start.7
  28.0 1.0 %collective-permute-done.5.near4 = bf16[160,128]{1,0:T(8,128)(2,1)S(1)} collective-permute-done((bf16[160,128]{1,0:T(8,128)(2,1)S(1)}, bf16[160,128]{1,0:T(8,128)(2,1)S(1)}, u32[]{:S(2)}, u32[]{:S(2)}) %collective-permute-start.5) | collective-permute-done | bytes 40992 | tf_op jit(solution)/shard_map/ppermute | solution.py:441
  29.0 2.2 %collective-permute-done.7.cross4 = bf16[160,128]{1,0:T(8,128)(2,1)S(1)} collective-permute-done((bf16[160,128]{1,0:T(8,128)(2,1)S(1)}, bf16[160,128]{1,0:T(8,128)(2,1)S(1)}, u32[]{:S(2)}, u32[]{:S(2)}) %collective-permute-start.7) | collective-permute-done | bytes 40992 | tf_op jit(solution)/shard_map/ppermute | solution.py:441
  31.2 0.2 coulomb.1
  31.4 1.6 %collective-permute-start.8 = (f32[16,64]{1,0:T(8,128)S(1)}, f32[16,64]{1,0:T(8,128)S(1)}, u32[]{:S(2)}, u32[]{:S(2)}) collective-permute-start(f32[16,64]{1,0:T(8,128)S(1)} %get-tuple-element.69), channel_id=1, source_target_pairs={{0,1},{1,0},{2,3},{3,2},{4,5},{5,4},{6,7},{7,6},{8,9},{9,8},{10,11... | collective-permute-start | bytes 12296 | tf_op jit(solution)/shard_map/ppermute | solution.py:416
  33.0 2.1 %collective-permute-done.8 = f32[16,64]{1,0:T(8,128)S(1)} collective-permute-done((f32[16,64]{1,0:T(8,128)S(1)}, f32[16,64]{1,0:T(8,128)S(1)}, u32[]{:S(2)}, u32[]{:S(2)}) %collective-permute-start.8) | collective-permute-done | bytes 4128 | tf_op jit(solution)/shard_map/ppermute | solution.py:416
  35.1 2.6 %collective-permute-start.9 = (f32[16,64]{1,0:T(8,128)S(1)}, f32[16,64]{1,0:T(8,128)S(1)}, u32[]{:S(2)}, u32[]{:S(2)}) collective-permute-start(f32[16,64]{1,0:T(8,128)S(1)} %add.14), channel_id=1, source_target_pairs={{0,2},{1,3},{2,0},{3,1},{4,6},{5,7},{6,4},{7,5},{8,10},{9,11},{10,... | collective-permute-start | bytes 12296 | tf_op jit(solution)/shard_map/ppermute | solution.py:416
  37.6 1.5 %own_active.1 = f32[64,16,64]{2,1,0:T(8,128)} custom-call(s32[2]{0:T(128)S(1)} %pad_add_fusion.where, f32[512,128]{1,0:T(8,128)S(1)} %get-tuple-element.68.act), custom_call_target="tpu_custom_call" | custom-call | flops 1000000 | bytes 100000 | tf_op jit(solution)/shard_map/own_active/pallas_call | solution.py:421
  39.1 0.5 %collective-permute-done.9 = f32[16,64]{1,0:T(8,128)S(1)} collective-permute-done((f32[16,64]{1,0:T(8,128)S(1)}, f32[16,64]{1,0:T(8,128)S(1)}, u32[]{:S(2)}, u32[]{:S(2)}) %collective-permute-start.9) | collective-permute-done | bytes 4128 | tf_op jit(solution)/shard_map/ppermute | solution.py:416
  39.6 0.6 %add_add_fusion = f32[16,64]{1,0:T(8,128)} fusion(f32[16,64]{1,0:T(8,128)S(1)} %copy-done, f32[16,64]{1,0:T(8,128)S(1)} %add.14, f32[16,64]{1,0:T(8,128)S(1)} %collective-permute-done.9), kind=kLoop, calls=%fused_computation.1 | loop fusion | flops 2048 | bytes 16384 | tf_op jit(solution)/shard_map/add | solution.py:544
  (9 shorter events, 0.0 us)
Async XLA Ops:
  8.8 4.6 %collective-permute-start = (bf16[1152,128]{1,0:T(8,128)(2,1)S(1)}, bf16[1152,128]{1,0:T(8,128)(2,1)S(1)}, u32[]{:S(2)}, u32[]{:S(2)}) collective-permute-start(bf16[1152,128]{1,0:T(8,128)(2,1)S(1)} %get-tuple-element.45), channel_id=1, source_target_pairs={{0,4},{4,0},{8,12},{12,8},{1,5},{5,1},{9,13},{13,9},{2,6},{6,2},{1... | collective-permute-start | bytes 884744 | tf_op jit(solution)/shard_map/ppermute | solution.py:441
  13.5 11.4 %collective-permute-start.3 = (bf16[1024,128]{1,0:T(8,128)(2,1)S(1)}, bf16[1024,128]{1,0:T(8,128)(2,1)S(1)}, u32[]{:S(2)}, u32[]{:S(2)}) collective-permute-start(bf16[1024,128]{1,0:T(8,128)(2,1)S(1)} %add_convert_fusion), channel_id=1, source_target_pairs={{0,8},{4,12},{8,0},{12,4},{1,9},{5,13},{9,1},{13,5},{2,10},{6,14},... | collective-permute-start | bytes 786440 | tf_op jit(solution)/shard_map/ppermute | solution.py:441
  20.1 4.8 %collective-permute-start.1 = (bf16[944,128]{1,0:T(8,128)(2,1)S(1)}, bf16[944,128]{1,0:T(8,128)(2,1)S(1)}, u32[]{:S(2)}, u32[]{:S(2)}) collective-permute-start(bf16[944,128]{1,0:T(8,128)(2,1)S(1)} %get-tuple-element.57), channel_id=1, source_target_pairs={{0,4},{4,0},{8,12},{12,8},{1,5},{5,1},{9,13},{13,9},{2,6},{6,2},{1... | collective-permute-start | bytes 725000 | tf_op jit(solution)/shard_map/ppermute | solution.py:441
  20.4 4.5 %collective-permute-start.2 = (bf16[768,128]{1,0:T(8,128)(2,1)S(1)}, bf16[768,128]{1,0:T(8,128)(2,1)S(1)}, u32[]{:S(2)}, u32[]{:S(2)}) collective-permute-start(bf16[768,128]{1,0:T(8,128)(2,1)S(1)} %get-tuple-element.58), channel_id=1, source_target_pairs={{0,4},{4,0},{8,12},{12,8},{1,5},{5,1},{9,13},{13,9},{2,6},{6,2},{1... | collective-permute-start | bytes 589832 | tf_op jit(solution)/shard_map/ppermute | solution.py:441
  20.7 5.2 %collective-permute-start.4 = (bf16[432,128]{1,0:T(8,128)(2,1)S(1)}, bf16[432,128]{1,0:T(8,128)(2,1)S(1)}, u32[]{:S(2)}, u32[]{:S(2)}) collective-permute-start(bf16[432,128]{1,0:T(8,128)(2,1)S(1)} %get-tuple-element.62), channel_id=1, source_target_pairs={{0,8},{4,12},{8,0},{12,4},{1,9},{5,13},{9,1},{13,5},{2,10},{6,14},... | collective-permute-start | bytes 331784 | tf_op jit(solution)/shard_map/ppermute | solution.py:441
  24.8 14.8 %copy-start = (f32[16,64]{1,0:T(8,128)S(1)}, f32[16,64]{1,0:T(8,128)}, u32[]{:S(2)}) copy-start(f32[16,64]{1,0:T(8,128)} %param.11) | copy-start | bytes 12292
  25.8 5.3 %collective-permute-start.6 = (bf16[336,128]{1,0:T(8,128)(2,1)S(1)}, bf16[336,128]{1,0:T(8,128)(2,1)S(1)}, u32[]{:S(2)}, u32[]{:S(2)}) collective-permute-start(bf16[336,128]{1,0:T(8,128)(2,1)S(1)} %get-tuple-element.66), channel_id=1, source_target_pairs={{0,8},{4,12},{8,0},{12,4},{1,9},{5,13},{9,1},{13,5},{2,10},{6,14},... | collective-permute-start | bytes 258056 | tf_op jit(solution)/shard_map/ppermute | solution.py:441
  27.7 1.2 %collective-permute-start.5 = (bf16[160,128]{1,0:T(8,128)(2,1)S(1)}, bf16[160,128]{1,0:T(8,128)(2,1)S(1)}, u32[]{:S(2)}, u32[]{:S(2)}) collective-permute-start(bf16[160,128]{1,0:T(8,128)(2,1)S(1)} %get-tuple-element.65), channel_id=1, source_target_pairs={{0,4},{4,0},{8,12},{12,8},{1,5},{5,1},{9,13},{13,9},{2,6},{6,2},{1... | collective-permute-start | bytes 122888 | tf_op jit(solution)/shard_map/ppermute | solution.py:441
  27.7 3.4 %collective-permute-start.7 = (bf16[160,128]{1,0:T(8,128)(2,1)S(1)}, bf16[160,128]{1,0:T(8,128)(2,1)S(1)}, u32[]{:S(2)}, u32[]{:S(2)}) collective-permute-start(bf16[160,128]{1,0:T(8,128)(2,1)S(1)} %get-tuple-element.67), channel_id=1, source_target_pairs={{0,12},{4,8},{8,4},{12,0},{1,13},{5,9},{9,5},{13,1},{2,14},{6,10},... | collective-permute-start | bytes 122888 | tf_op jit(solution)/shard_map/ppermute | solution.py:441
  31.4 3.7 %collective-permute-start.8 = (f32[16,64]{1,0:T(8,128)S(1)}, f32[16,64]{1,0:T(8,128)S(1)}, u32[]{:S(2)}, u32[]{:S(2)}) collective-permute-start(f32[16,64]{1,0:T(8,128)S(1)} %get-tuple-element.69), channel_id=1, source_target_pairs={{0,1},{1,0},{2,3},{3,2},{4,5},{5,4},{6,7},{7,6},{8,9},{9,8},{10,11... | collective-permute-start | bytes 12296 | tf_op jit(solution)/shard_map/ppermute | solution.py:416
  35.1 4.5 %collective-permute-start.9 = (f32[16,64]{1,0:T(8,128)S(1)}, f32[16,64]{1,0:T(8,128)S(1)}, u32[]{:S(2)}, u32[]{:S(2)}) collective-permute-start(f32[16,64]{1,0:T(8,128)S(1)} %add.14), channel_id=1, source_target_pairs={{0,2},{1,3},{2,0},{3,1},{4,6},{5,7},{6,4},{7,5},{8,10},{9,11},{10,... | collective-permute-start | bytes 12296 | tf_op jit(solution)/shard_map/ppermute | solution.py:416

commit v19 on v18

--- a/solution.py
+++ b/solution.py
@@ -347,7 +347,7 @@
 
 def coulomb_kernel(
     keep1, keep2, keep3, keep4, dens1, dens2, dens3, dens4, exch,
-    near3, far3, near4, far4, cross4, act, partial,
+    near3, far3, cross4, far4, near4, act, partial,
 ):
     first = low_half(QUARTER)
     early, late = (near3, far3, far4), (near4, far4, cross4)
@@ -519,8 +519,8 @@
         [pltpu.VMEM((NACT, LANES), F32)],
         (where, keep_in4, near3, near3b, far1, sends4, dens4),
     )
-    far3, far4 = lax.optimization_barrier((far3, far4))
-    far4, cross4, near4 = to_peer(2, far4), to_peer(3, cross4), to_peer(1, near4)
+    far3, cross4 = lax.optimization_barrier((far3, cross4))
+    cross4, far4, near4 = to_peer(3, cross4), to_peer(2, far4), to_peer(1, near4)
     act, partial = call(
         coulomb_kernel,
         "coulomb",
@@ -529,7 +529,7 @@
         [],
         (
             keep1, keep2, keep3, keep4, dens1, dens2, dens3, dens4, exch,
-            near3, far3, near4, far4, cross4,
+            near3, far3, cross4, far4, near4,
         ),
     )
     (active,) = call(

time: 40.4 us -> 40.7 us (level)
  transfers between devices with their start and end apart: 10 -> 10, of which waited for: 5 -> 3; matrix products, arithmetic and copies ran while one was open for 0% -> 0% of each run, Pallas kernels for 36% -> 36%
where the time goes in v19:
time: 40.7 us; the launch traced here: 40.5 us
  Pallas kernels  22.1 us (54%)
  starting transfers between devices  10.4 us (26%)
  waiting for transfers between devices  5.77 us (14%)
  between operations  1.37 us (3%)
  other arithmetic  0.74 us (2%)
    pallas_call x7, Pallas kernels, call(): pl.pallas_call(kernel, name=name, in_specs=inputs, out_specs=[VM] * len(o...  22.1 us
    ppermute x8, starting transfers between devices, to_peer(): return lax.ppermute(array, 'pair', [(p, p ^ k) for p in range(4)])  5.96 us
    ppermute x2, starting transfers between devices, sum_over_aux(): part = part + lax.ppermute(part, 'aux', [(z, z ^ k) for z in range(n)])  4.49 us
    ppermute x8, waiting for transfers between devices, to_peer(): return lax.ppermute(array, 'pair', [(p, p ^ k) for p in range(4)])  3.51 us
    ppermute x2, waiting for transfers between devices, sum_over_aux(): part = part + lax.ppermute(part, 'aux', [(z, z ^ k) for z in range(n)])  2.26 us
  transfers between devices with their start and end apart: 10, of which 3 were waited for; matrix products, arithmetic and copies ran while one was open for 0% of the time, Pallas kernels for 36%

profile of v19, /device:TPU:0, one launch (start us, length us, event | category | flops | bytes accessed | tf_op | source)
XLA Modules:
  0.0 40.5 jit_solution(7046096373453113786)
XLA Ops:
  1.3 0.1 pad_add_fusion.where
  1.4 7.4 %slabs_first.1 = (bf16[192,1024]{1,0:T(8,128)(2,1)S(1)}, bf16[1024,256]{1,0:T(8,128)(2,1)S(1)}, bf16[4,256,256]{2,1,0:T(8,128)(2,1)S(1)}, f32[8,64,128]{2,1,0:T(...) custom-call(s32[2]{0:T(128)S(1)} %pad_add_fusion.where, ...), custom_call_target="tpu_custom_call" | custom-call | flops 5000000000 | bytes 100000 | tf_op jit(solution)/shard_map/slabs_first/pallas_call | solution.py:421
  8.8 0.5 %collective-permute-start = (bf16[1152,128]{1,0:T(8,128)(2,1)S(1)}, bf16[1152,128]{1,0:T(8,128)(2,1)S(1)}, u32[]{:S(2)}, u32[]{:S(2)}) collective-permute-start(bf16[1152,128]{1,0:T(8,128)(2,1)S(1)} %get-tuple-element.45), channel_id=1, source_target_pairs={{0,4},{4,0},{8,12},{12,8},{1,5},{5,1},{9,13},{13,9},{2,6},{6,2},{1... | collective-permute-start | bytes 884744 | tf_op jit(solution)/shard_map/ppermute | solution.py:441
  9.3 4.1 %slabs_second.1 = (f32[1024,128]{1,0:T(8,128)S(1)}, f32[128,128]{1,0:T(8,128)S(1)}, bf16[3,128,128]{2,1,0:T(8,128)(2,1)S(1)}, f32[16,128]{1,0:T(8,128)S(1)}) custom-call(s32[2]{0:T(128)S(1)} %pad_add_fusion.where, bf16[8,2,16,4096]{3,2,1,0:T(8,128)(2,1)S(1)} %get-tuple-element.37.sbuf, bf16[192,1024]{1,0:T(8,128)(2,1)S(1)} %get-tuple-element.46.lt_ref, ...), custom_call_target="tpu_custom_call" | custom-call | flops 5000000000 | bytes 100000 | tf_op jit(solution)/shard_map/slabs_second/pallas_call | solution.py:421
  13.4 0.1 add_convert_fusion
  13.5 2.6 %collective-permute-start.3 = (bf16[1024,128]{1,0:T(8,128)(2,1)S(1)}, bf16[1024,128]{1,0:T(8,128)(2,1)S(1)}, u32[]{:S(2)}, u32[]{:S(2)}) collective-permute-start(bf16[1024,128]{1,0:T(8,128)(2,1)S(1)} %add_convert_fusion), channel_id=1, source_target_pairs={{0,8},{4,12},{8,0},{12,4},{1,9},{5,13},{9,1},{13,5},{2,10},{6,14},... | collective-permute-start | bytes 786440 | tf_op jit(solution)/shard_map/ppermute | solution.py:441
  16.0 4.1 %slabs_third.1 = (bf16[944,128]{1,0:T(8,128)(2,1)S(1)}, bf16[768,128]{1,0:T(8,128)(2,1)S(1)}, bf16[432,128]{1,0:T(8,128)(2,1)S(1)}, f32[128,128]{1,0:T(8,128)S(1)}, f32[16,128]{1,0:T(8,128)S(1)}) custom-call(s32[2]{0:T(128)S(1)} %pad_add_fusion.where, bf16[8,2,16,4096]{3,2,1,0:T(8,128)(2,1)S(1)} %get-tuple-element.43.sbuf, ...), custom_call_target="tpu_custom_call" | custom-call | flops 5000000000 | bytes 100000 | tf_op jit(solution)/shard_map/slabs_third/pallas_call | solution.py:421
  20.1 0.3 collective-permute-start.1
  20.4 0.3 collective-permute-start.2
  20.7 0.1 collective-permute-start.4
  20.7 4.1 %slabs_fourth.1 = (f32[1024,128]{1,0:T(8,128)S(1)}, f32[128,128]{1,0:T(8,128)S(1)}, bf16[3,128,128]{2,1,0:T(8,128)(2,1)S(1)}, f32[16,128]{1,0:T(8,128)S(1)}) custom-call(s32[2]{0:T(128)S(1)} %pad_add_fusion.where, bf16[8,2,16,4096]{3,2,1,0:T(8,128)(2,1)S(1)} %get-tuple-element.52.sbuf, bf16[192,1024]{1,0:T(8,128)(2,1)S(1)} %get-tuple-element.46.lt_ref, ...), custom_call_target="tpu_custom_call" | custom-call | flops 1000000000 | bytes 100000 | tf_op jit(solution)/shard_map/slabs_fourth/pallas_call | solution.py:421
  24.8 0.0 copy-start
  24.8 0.0 collective-permute-done.2.near3b
  24.9 0.9 %exchange.1 = (bf16[160,128]{1,0:T(8,128)(2,1)S(1)}, bf16[336,128]{1,0:T(8,128)(2,1)S(1)}, bf16[160,128]{1,0:T(8,128)(2,1)S(1)}, f32[16,128]{1,0:T(8,128)S(1)}) custom-call(s32[2]{0:T(128)S(1)} %pad_add_fusion.where, f32[1024,128]{1,0:T(8,128)S(1)} %get-tuple-element.56.mine, bf16[944,128]{1,0:T(8,128)(2,1)S(1)} %collective-permute-done.1.near3, ...), custom_call_target="tpu_custom_call" | custom-call | bytes 100000 | tf_op jit(solution)/shard_map/exchange/pallas_call | solution.py:421
  25.7 2.0 %collective-permute-start.6 = (bf16[336,128]{1,0:T(8,128)(2,1)S(1)}, bf16[336,128]{1,0:T(8,128)(2,1)S(1)}, u32[]{:S(2)}, u32[]{:S(2)}) collective-permute-start(bf16[336,128]{1,0:T(8,128)(2,1)S(1)} %get-tuple-element.66), channel_id=1, source_target_pairs={{0,8},{4,12},{8,0},{12,4},{1,9},{5,13},{9,1},{13,5},{2,10},{6,14},... | collective-permute-start | bytes 258056 | tf_op jit(solution)/shard_map/ppermute | solution.py:441
  27.7 0.2 collective-permute-start.7
  27.9 3.5 %collective-permute-done.5.cross4 = bf16[160,128]{1,0:T(8,128)(2,1)S(1)} collective-permute-done((bf16[160,128]{1,0:T(8,128)(2,1)S(1)}, bf16[160,128]{1,0:T(8,128)(2,1)S(1)}, u32[]{:S(2)}, u32[]{:S(2)}) %collective-permute-start.5) | collective-permute-done | bytes 40992 | tf_op jit(solution)/shard_map/ppermute | solution.py:441
  31.4 0.2 coulomb.1
  31.6 1.8 %collective-permute-start.8 = (f32[16,64]{1,0:T(8,128)S(1)}, f32[16,64]{1,0:T(8,128)S(1)}, u32[]{:S(2)}, u32[]{:S(2)}) collective-permute-start(f32[16,64]{1,0:T(8,128)S(1)} %get-tuple-element.69), channel_id=1, source_target_pairs={{0,1},{1,0},{2,3},{3,2},{4,5},{5,4},{6,7},{7,6},{8,9},{9,8},{10,11... | collective-permute-start | bytes 12296 | tf_op jit(solution)/shard_map/ppermute | solution.py:416
  33.4 1.9 %collective-permute-done.8 = f32[16,64]{1,0:T(8,128)S(1)} collective-permute-done((f32[16,64]{1,0:T(8,128)S(1)}, f32[16,64]{1,0:T(8,128)S(1)}, u32[]{:S(2)}, u32[]{:S(2)}) %collective-permute-start.8) | collective-permute-done | bytes 4128 | tf_op jit(solution)/shard_map/ppermute | solution.py:416
  35.3 2.7 %collective-permute-start.9 = (f32[16,64]{1,0:T(8,128)S(1)}, f32[16,64]{1,0:T(8,128)S(1)}, u32[]{:S(2)}, u32[]{:S(2)}) collective-permute-start(f32[16,64]{1,0:T(8,128)S(1)} %add.14), channel_id=1, source_target_pairs={{0,2},{1,3},{2,0},{3,1},{4,6},{5,7},{6,4},{7,5},{8,10},{9,11},{10,... | collective-permute-start | bytes 12296 | tf_op jit(solution)/shard_map/ppermute | solution.py:416
  38.1 1.5 %own_active.1 = f32[64,16,64]{2,1,0:T(8,128)} custom-call(s32[2]{0:T(128)S(1)} %pad_add_fusion.where, f32[512,128]{1,0:T(8,128)S(1)} %get-tuple-element.68.act), custom_call_target="tpu_custom_call" | custom-call | flops 1000000 | bytes 100000 | tf_op jit(solution)/shard_map/own_active/pallas_call | solution.py:421
  39.5 0.3 collective-permute-done.9
  39.9 0.6 %add_add_fusion = f32[16,64]{1,0:T(8,128)} fusion(f32[16,64]{1,0:T(8,128)S(1)} %copy-done, f32[16,64]{1,0:T(8,128)S(1)} %add.14, f32[16,64]{1,0:T(8,128)S(1)} %collective-permute-done.9), kind=kLoop, calls=%fused_computation.1 | loop fusion | flops 2048 | bytes 16384 | tf_op jit(solution)/shard_map/add | solution.py:544
  (9 shorter events, 0.0 us)
Async XLA Ops:
  8.8 4.6 %collective-permute-start = (bf16[1152,128]{1,0:T(8,128)(2,1)S(1)}, bf16[1152,128]{1,0:T(8,128)(2,1)S(1)}, u32[]{:S(2)}, u32[]{:S(2)}) collective-permute-start(bf16[1152,128]{1,0:T(8,128)(2,1)S(1)} %get-tuple-element.45), channel_id=1, source_target_pairs={{0,4},{4,0},{8,12},{12,8},{1,5},{5,1},{9,13},{13,9},{2,6},{6,2},{1... | collective-permute-start | bytes 884744 | tf_op jit(solution)/shard_map/ppermute | solution.py:441
  13.5 11.4 %collective-permute-start.3 = (bf16[1024,128]{1,0:T(8,128)(2,1)S(1)}, bf16[1024,128]{1,0:T(8,128)(2,1)S(1)}, u32[]{:S(2)}, u32[]{:S(2)}) collective-permute-start(bf16[1024,128]{1,0:T(8,128)(2,1)S(1)} %add_convert_fusion), channel_id=1, source_target_pairs={{0,8},{4,12},{8,0},{12,4},{1,9},{5,13},{9,1},{13,5},{2,10},{6,14},... | collective-permute-start | bytes 786440 | tf_op jit(solution)/shard_map/ppermute | solution.py:441
  20.1 4.7 %collective-permute-start.1 = (bf16[944,128]{1,0:T(8,128)(2,1)S(1)}, bf16[944,128]{1,0:T(8,128)(2,1)S(1)}, u32[]{:S(2)}, u32[]{:S(2)}) collective-permute-start(bf16[944,128]{1,0:T(8,128)(2,1)S(1)} %get-tuple-element.57), channel_id=1, source_target_pairs={{0,4},{4,0},{8,12},{12,8},{1,5},{5,1},{9,13},{13,9},{2,6},{6,2},{1... | collective-permute-start | bytes 725000 | tf_op jit(solution)/shard_map/ppermute | solution.py:441
  20.4 4.5 %collective-permute-start.2 = (bf16[768,128]{1,0:T(8,128)(2,1)S(1)}, bf16[768,128]{1,0:T(8,128)(2,1)S(1)}, u32[]{:S(2)}, u32[]{:S(2)}) collective-permute-start(bf16[768,128]{1,0:T(8,128)(2,1)S(1)} %get-tuple-element.58), channel_id=1, source_target_pairs={{0,4},{4,0},{8,12},{12,8},{1,5},{5,1},{9,13},{13,9},{2,6},{6,2},{1... | collective-permute-start | bytes 589832 | tf_op jit(solution)/shard_map/ppermute | solution.py:441
  20.7 7.1 %collective-permute-start.4 = (bf16[432,128]{1,0:T(8,128)(2,1)S(1)}, bf16[432,128]{1,0:T(8,128)(2,1)S(1)}, u32[]{:S(2)}, u32[]{:S(2)}) collective-permute-start(bf16[432,128]{1,0:T(8,128)(2,1)S(1)} %get-tuple-element.62), channel_id=1, source_target_pairs={{0,8},{4,12},{8,0},{12,4},{1,9},{5,13},{9,1},{13,5},{2,10},{6,14},... | collective-permute-start | bytes 331784 | tf_op jit(solution)/shard_map/ppermute | solution.py:441
  24.8 15.1 %copy-start = (f32[16,64]{1,0:T(8,128)S(1)}, f32[16,64]{1,0:T(8,128)}, u32[]{:S(2)}) copy-start(f32[16,64]{1,0:T(8,128)} %param.11) | copy-start | bytes 12292
  25.7 5.7 %collective-permute-start.6 = (bf16[336,128]{1,0:T(8,128)(2,1)S(1)}, bf16[336,128]{1,0:T(8,128)(2,1)S(1)}, u32[]{:S(2)}, u32[]{:S(2)}) collective-permute-start(bf16[336,128]{1,0:T(8,128)(2,1)S(1)} %get-tuple-element.66), channel_id=1, source_target_pairs={{0,8},{4,12},{8,0},{12,4},{1,9},{5,13},{9,1},{13,5},{2,10},{6,14},... | collective-permute-start | bytes 258056 | tf_op jit(solution)/shard_map/ppermute | solution.py:441
  27.7 3.7 %collective-permute-start.5 = (bf16[160,128]{1,0:T(8,128)(2,1)S(1)}, bf16[160,128]{1,0:T(8,128)(2,1)S(1)}, u32[]{:S(2)}, u32[]{:S(2)}) collective-permute-start(bf16[160,128]{1,0:T(8,128)(2,1)S(1)} %get-tuple-element.65), channel_id=1, source_target_pairs={{0,12},{4,8},{8,4},{12,0},{1,13},{5,9},{9,5},{13,1},{2,14},{6,10},... | collective-permute-start | bytes 122888 | tf_op jit(solution)/shard_map/ppermute | solution.py:441
  27.7 3.7 %collective-permute-start.7 = (bf16[160,128]{1,0:T(8,128)(2,1)S(1)}, bf16[160,128]{1,0:T(8,128)(2,1)S(1)}, u32[]{:S(2)}, u32[]{:S(2)}) collective-permute-start(bf16[160,128]{1,0:T(8,128)(2,1)S(1)} %get-tuple-element.67), channel_id=1, source_target_pairs={{0,4},{4,0},{8,12},{12,8},{1,5},{5,1},{9,13},{13,9},{2,6},{6,2},{1... | collective-permute-start | bytes 122888 | tf_op jit(solution)/shard_map/ppermute | solution.py:441
  31.6 3.7 %collective-permute-start.8 = (f32[16,64]{1,0:T(8,128)S(1)}, f32[16,64]{1,0:T(8,128)S(1)}, u32[]{:S(2)}, u32[]{:S(2)}) collective-permute-start(f32[16,64]{1,0:T(8,128)S(1)} %get-tuple-element.69), channel_id=1, source_target_pairs={{0,1},{1,0},{2,3},{3,2},{4,5},{5,4},{6,7},{7,6},{8,9},{9,8},{10,11... | collective-permute-start | bytes 12296 | tf_op jit(solution)/shard_map/ppermute | solution.py:416
  35.3 4.5 %collective-permute-start.9 = (f32[16,64]{1,0:T(8,128)S(1)}, f32[16,64]{1,0:T(8,128)S(1)}, u32[]{:S(2)}, u32[]{:S(2)}) collective-permute-start(f32[16,64]{1,0:T(8,128)S(1)} %add.14), channel_id=1, source_target_pairs={{0,2},{1,3},{2,0},{3,1},{4,6},{5,7},{6,4},{7,5},{8,10},{9,11},{10,... | collective-permute-start | bytes 12296 | tf_op jit(solution)/shard_map/ppermute | solution.py:416

commit v20 on v18

--- a/solution.py
+++ b/solution.py
@@ -111,23 +111,23 @@
                     )
 
     def second_transform(g):
-        rows = pt_ref[4 * g : 4 * g + 4].reshape(4 * NACT, pt_ref.shape[2])
+        rows = pt_ref[group * g : group * (g + 1)].reshape(group * NACT, pt_ref.shape[2])
         one = jnp.dot(rows, r_ref[...], preferred_element_type=F32)
         two = jnp.dot(
-            lt_ref[...], q_ref[:, 4 * g * BS : (4 * g + 4) * BS], preferred_element_type=F32
+            lt_ref[...], q_ref[:, group * g * BS : group * (g + 1) * BS], preferred_element_type=F32
         )
         return one, two
 
     def assemble(g, both):
         one, two = both
-        for p in range(2):
+        for p in range(group // 2):
             w0 = one[2 * p * NACT : (2 * p + 1) * NACT]
             w1 = one[(2 * p + 1) * NACT : (2 * p + 2) * NACT]
             turned = two[:, p * LANES : (p + 1) * LANES]
             across = turned[:NIN].T
             square = jnp.concatenate([turned[NIN:], turned[NIN:]], axis=0).T
             emit(
-                2 * g + p,
+                group // 2 * g + p,
                 w0[:, :NIN] + across[:NACT],
                 w1[:, :NIN] + across[NACT:],
                 jnp.where(first_s, w0[:, NIN:] + square[:NACT], w1[:, NIN:] + square[NACT:]),
@@ -158,8 +158,8 @@
                 load(g + 1, scratch[2 * ((g + 1) % 2) : 2 * ((g + 1) % 2) + 2])
             transform(g, scratch[2 * (g % 2) : 2 * (g % 2) + 2])
     whole = second_transform(0)
-    for g in range(NBQ // 4):
-        following = second_transform(g + 1) if g + 1 < NBQ // 4 else None
+    for g in range(NBQ // group):
+        following = second_transform(g + 1) if g + 1 < NBQ // group else None
         assemble(g, whole)
         whole = following
 

time: 40.4 us -> 40.1 us (level)
  no operation moved by 1% of the time
where the time goes in v20:
time: 40.1 us; the launch traced here: 39.9 us
  Pallas kernels  21.9 us (55%)
  starting transfers between devices  10.1 us (25%)
  waiting for transfers between devices  5.89 us (15%)
  between operations  1.37 us (3%)
  other arithmetic  0.74 us (2%)
    pallas_call x7, Pallas kernels, call(): pl.pallas_call(kernel, name=name, in_specs=inputs, out_specs=[VM] * len(o...  21.9 us
    ppermute x8, starting transfers between devices, to_peer(): return lax.ppermute(array, 'pair', [(p, p ^ k) for p in range(4)])  5.89 us
    ppermute x2, starting transfers between devices, sum_over_aux(): part = part + lax.ppermute(part, 'aux', [(z, z ^ k) for z in range(n)])  4.19 us
    ppermute x8, waiting for transfers between devices, to_peer(): return lax.ppermute(array, 'pair', [(p, p ^ k) for p in range(4)])  3.32 us
    ppermute x2, waiting for transfers between devices, sum_over_aux(): part = part + lax.ppermute(part, 'aux', [(z, z ^ k) for z in range(n)])  2.57 us
  transfers between devices with their start and end apart: 10, of which 5 were waited for; matrix products, arithmetic and copies ran while one was open for 0% of the time, Pallas kernels for 36%

profile of v20, /device:TPU:0, one launch (start us, length us, event | category | flops | bytes accessed | tf_op | source)
XLA Modules:
  0.0 39.9 jit_solution(11646061130518590218)
XLA Ops:
  1.3 0.1 pad_add_fusion.where
  1.4 7.4 %slabs_first.1 = (bf16[192,1024]{1,0:T(8,128)(2,1)S(1)}, bf16[1024,256]{1,0:T(8,128)(2,1)S(1)}, bf16[4,256,256]{2,1,0:T(8,128)(2,1)S(1)}, f32[8,64,128]{2,1,0:T(...) custom-call(s32[2]{0:T(128)S(1)} %pad_add_fusion.where, ...), custom_call_target="tpu_custom_call" | custom-call | flops 5000000000 | bytes 100000 | tf_op jit(solution)/shard_map/slabs_first/pallas_call | solution.py:421
  8.8 0.5 %collective-permute-start = (bf16[1152,128]{1,0:T(8,128)(2,1)S(1)}, bf16[1152,128]{1,0:T(8,128)(2,1)S(1)}, u32[]{:S(2)}, u32[]{:S(2)}) collective-permute-start(bf16[1152,128]{1,0:T(8,128)(2,1)S(1)} %get-tuple-element.45), channel_id=1, source_target_pairs={{0,4},{4,0},{8,12},{12,8},{1,5},{5,1},{9,13},{13,9},{2,6},{6,2},{1... | collective-permute-start | bytes 884744 | tf_op jit(solution)/shard_map/ppermute | solution.py:441
  9.3 4.0 %slabs_second.1 = (f32[1024,128]{1,0:T(8,128)S(1)}, f32[128,128]{1,0:T(8,128)S(1)}, bf16[3,128,128]{2,1,0:T(8,128)(2,1)S(1)}, f32[16,128]{1,0:T(8,128)S(1)}) custom-call(s32[2]{0:T(128)S(1)} %pad_add_fusion.where, bf16[8,2,16,4096]{3,2,1,0:T(8,128)(2,1)S(1)} %get-tuple-element.37.sbuf, bf16[192,1024]{1,0:T(8,128)(2,1)S(1)} %get-tuple-element.46.lt_ref, ...), custom_call_target="tpu_custom_call" | custom-call | flops 5000000000 | bytes 100000 | tf_op jit(solution)/shard_map/slabs_second/pallas_call | solution.py:421
  13.3 0.1 add_convert_fusion
  13.4 2.6 %collective-permute-start.3 = (bf16[1024,128]{1,0:T(8,128)(2,1)S(1)}, bf16[1024,128]{1,0:T(8,128)(2,1)S(1)}, u32[]{:S(2)}, u32[]{:S(2)}) collective-permute-start(bf16[1024,128]{1,0:T(8,128)(2,1)S(1)} %add_convert_fusion), channel_id=1, source_target_pairs={{0,8},{4,12},{8,0},{12,4},{1,9},{5,13},{9,1},{13,5},{2,10},{6,14},... | collective-permute-start | bytes 786440 | tf_op jit(solution)/shard_map/ppermute | solution.py:441
  15.9 4.0 %slabs_third.1 = (bf16[944,128]{1,0:T(8,128)(2,1)S(1)}, bf16[768,128]{1,0:T(8,128)(2,1)S(1)}, bf16[432,128]{1,0:T(8,128)(2,1)S(1)}, f32[128,128]{1,0:T(8,128)S(1)}, f32[16,128]{1,0:T(8,128)S(1)}) custom-call(s32[2]{0:T(128)S(1)} %pad_add_fusion.where, bf16[8,2,16,4096]{3,2,1,0:T(8,128)(2,1)S(1)} %get-tuple-element.43.sbuf, ...), custom_call_target="tpu_custom_call" | custom-call | flops 5000000000 | bytes 100000 | tf_op jit(solution)/shard_map/slabs_third/pallas_call | solution.py:421
  19.9 0.3 collective-permute-start.1
  20.2 0.3 collective-permute-start.2
  20.5 0.1 collective-permute-start.4
  20.6 4.0 %slabs_fourth.1 = (f32[1024,128]{1,0:T(8,128)S(1)}, f32[128,128]{1,0:T(8,128)S(1)}, bf16[3,128,128]{2,1,0:T(8,128)(2,1)S(1)}, f32[16,128]{1,0:T(8,128)S(1)}) custom-call(s32[2]{0:T(128)S(1)} %pad_add_fusion.where, bf16[8,2,16,4096]{3,2,1,0:T(8,128)(2,1)S(1)} %get-tuple-element.52.sbuf, bf16[192,1024]{1,0:T(8,128)(2,1)S(1)} %get-tuple-element.46.lt_ref, ...), custom_call_target="tpu_custom_call" | custom-call | flops 1000000000 | bytes 100000 | tf_op jit(solution)/shard_map/slabs_fourth/pallas_call | solution.py:421
  24.6 0.9 %exchange.1 = (bf16[160,128]{1,0:T(8,128)(2,1)S(1)}, bf16[336,128]{1,0:T(8,128)(2,1)S(1)}, bf16[160,128]{1,0:T(8,128)(2,1)S(1)}, f32[16,128]{1,0:T(8,128)S(1)}) custom-call(s32[2]{0:T(128)S(1)} %pad_add_fusion.where, f32[1024,128]{1,0:T(8,128)S(1)} %get-tuple-element.56.mine, bf16[944,128]{1,0:T(8,128)(2,1)S(1)} %collective-permute-done.1.near3, ...), custom_call_target="tpu_custom_call" | custom-call | bytes 100000 | tf_op jit(solution)/shard_map/exchange/pallas_call | solution.py:421
  25.5 0.2 collective-permute-done.4.far3
  25.7 1.8 %collective-permute-start.6 = (bf16[336,128]{1,0:T(8,128)(2,1)S(1)}, bf16[336,128]{1,0:T(8,128)(2,1)S(1)}, u32[]{:S(2)}, u32[]{:S(2)}) collective-permute-start(bf16[336,128]{1,0:T(8,128)(2,1)S(1)} %get-tuple-element.66), channel_id=1, source_target_pairs={{0,8},{4,12},{8,0},{12,4},{1,9},{5,13},{9,1},{13,5},{2,10},{6,14},... | collective-permute-start | bytes 258056 | tf_op jit(solution)/shard_map/ppermute | solution.py:441
  27.5 0.3 collective-permute-start.7
  27.8 0.9 %collective-permute-done.5.near4 = bf16[160,128]{1,0:T(8,128)(2,1)S(1)} collective-permute-done((bf16[160,128]{1,0:T(8,128)(2,1)S(1)}, bf16[160,128]{1,0:T(8,128)(2,1)S(1)}, u32[]{:S(2)}, u32[]{:S(2)}) %collective-permute-start.5) | collective-permute-done | bytes 40992 | tf_op jit(solution)/shard_map/ppermute | solution.py:441
  28.7 2.2 %collective-permute-done.7.cross4 = bf16[160,128]{1,0:T(8,128)(2,1)S(1)} collective-permute-done((bf16[160,128]{1,0:T(8,128)(2,1)S(1)}, bf16[160,128]{1,0:T(8,128)(2,1)S(1)}, u32[]{:S(2)}, u32[]{:S(2)}) %collective-permute-start.7) | collective-permute-done | bytes 40992 | tf_op jit(solution)/shard_map/ppermute | solution.py:441
  30.9 0.2 coulomb.1
  31.1 1.6 %collective-permute-start.8 = (f32[16,64]{1,0:T(8,128)S(1)}, f32[16,64]{1,0:T(8,128)S(1)}, u32[]{:S(2)}, u32[]{:S(2)}) collective-permute-start(f32[16,64]{1,0:T(8,128)S(1)} %get-tuple-element.69), channel_id=1, source_target_pairs={{0,1},{1,0},{2,3},{3,2},{4,5},{5,4},{6,7},{7,6},{8,9},{9,8},{10,11... | collective-permute-start | bytes 12296 | tf_op jit(solution)/shard_map/ppermute | solution.py:416
  32.7 2.1 %collective-permute-done.8 = f32[16,64]{1,0:T(8,128)S(1)} collective-permute-done((f32[16,64]{1,0:T(8,128)S(1)}, f32[16,64]{1,0:T(8,128)S(1)}, u32[]{:S(2)}, u32[]{:S(2)}) %collective-permute-start.8) | collective-permute-done | bytes 4128 | tf_op jit(solution)/shard_map/ppermute | solution.py:416
  34.8 2.6 %collective-permute-start.9 = (f32[16,64]{1,0:T(8,128)S(1)}, f32[16,64]{1,0:T(8,128)S(1)}, u32[]{:S(2)}, u32[]{:S(2)}) collective-permute-start(f32[16,64]{1,0:T(8,128)S(1)} %add.14), channel_id=1, source_target_pairs={{0,2},{1,3},{2,0},{3,1},{4,6},{5,7},{6,4},{7,5},{8,10},{9,11},{10,... | collective-permute-start | bytes 12296 | tf_op jit(solution)/shard_map/ppermute | solution.py:416
  37.4 1.5 %own_active.1 = f32[64,16,64]{2,1,0:T(8,128)} custom-call(s32[2]{0:T(128)S(1)} %pad_add_fusion.where, f32[512,128]{1,0:T(8,128)S(1)} %get-tuple-element.68.act), custom_call_target="tpu_custom_call" | custom-call | flops 1000000 | bytes 100000 | tf_op jit(solution)/shard_map/own_active/pallas_call | solution.py:421
  38.8 0.5 %collective-permute-done.9 = f32[16,64]{1,0:T(8,128)S(1)} collective-permute-done((f32[16,64]{1,0:T(8,128)S(1)}, f32[16,64]{1,0:T(8,128)S(1)}, u32[]{:S(2)}, u32[]{:S(2)}) %collective-permute-start.9) | collective-permute-done | bytes 4128 | tf_op jit(solution)/shard_map/ppermute | solution.py:416
  39.3 0.6 %add_add_fusion = f32[16,64]{1,0:T(8,128)} fusion(f32[16,64]{1,0:T(8,128)S(1)} %copy-done, f32[16,64]{1,0:T(8,128)S(1)} %add.14, f32[16,64]{1,0:T(8,128)S(1)} %collective-permute-done.9), kind=kLoop, calls=%fused_computation.1 | loop fusion | flops 2048 | bytes 16384 | tf_op jit(solution)/shard_map/add | solution.py:544
  (9 shorter events, 0.0 us)
Async XLA Ops:
  8.8 4.5 %collective-permute-start = (bf16[1152,128]{1,0:T(8,128)(2,1)S(1)}, bf16[1152,128]{1,0:T(8,128)(2,1)S(1)}, u32[]{:S(2)}, u32[]{:S(2)}) collective-permute-start(bf16[1152,128]{1,0:T(8,128)(2,1)S(1)} %get-tuple-element.45), channel_id=1, source_target_pairs={{0,4},{4,0},{8,12},{12,8},{1,5},{5,1},{9,13},{13,9},{2,6},{6,2},{1... | collective-permute-start | bytes 884744 | tf_op jit(solution)/shard_map/ppermute | solution.py:441
  13.4 11.2 %collective-permute-start.3 = (bf16[1024,128]{1,0:T(8,128)(2,1)S(1)}, bf16[1024,128]{1,0:T(8,128)(2,1)S(1)}, u32[]{:S(2)}, u32[]{:S(2)}) collective-permute-start(bf16[1024,128]{1,0:T(8,128)(2,1)S(1)} %add_convert_fusion), channel_id=1, source_target_pairs={{0,8},{4,12},{8,0},{12,4},{1,9},{5,13},{9,1},{13,5},{2,10},{6,14},... | collective-permute-start | bytes 786440 | tf_op jit(solution)/shard_map/ppermute | solution.py:441
  19.9 4.7 %collective-permute-start.1 = (bf16[944,128]{1,0:T(8,128)(2,1)S(1)}, bf16[944,128]{1,0:T(8,128)(2,1)S(1)}, u32[]{:S(2)}, u32[]{:S(2)}) collective-permute-start(bf16[944,128]{1,0:T(8,128)(2,1)S(1)} %get-tuple-element.57), channel_id=1, source_target_pairs={{0,4},{4,0},{8,12},{12,8},{1,5},{5,1},{9,13},{13,9},{2,6},{6,2},{1... | collective-permute-start | bytes 725000 | tf_op jit(solution)/shard_map/ppermute | solution.py:441
  20.2 4.4 %collective-permute-start.2 = (bf16[768,128]{1,0:T(8,128)(2,1)S(1)}, bf16[768,128]{1,0:T(8,128)(2,1)S(1)}, u32[]{:S(2)}, u32[]{:S(2)}) collective-permute-start(bf16[768,128]{1,0:T(8,128)(2,1)S(1)} %get-tuple-element.58), channel_id=1, source_target_pairs={{0,4},{4,0},{8,12},{12,8},{1,5},{5,1},{9,13},{13,9},{2,6},{6,2},{1... | collective-permute-start | bytes 589832 | tf_op jit(solution)/shard_map/ppermute | solution.py:441
  20.5 5.2 %collective-permute-start.4 = (bf16[432,128]{1,0:T(8,128)(2,1)S(1)}, bf16[432,128]{1,0:T(8,128)(2,1)S(1)}, u32[]{:S(2)}, u32[]{:S(2)}) collective-permute-start(bf16[432,128]{1,0:T(8,128)(2,1)S(1)} %get-tuple-element.62), channel_id=1, source_target_pairs={{0,8},{4,12},{8,0},{12,4},{1,9},{5,13},{9,1},{13,5},{2,10},{6,14},... | collective-permute-start | bytes 331784 | tf_op jit(solution)/shard_map/ppermute | solution.py:441
  24.5 14.8 %copy-start = (f32[16,64]{1,0:T(8,128)S(1)}, f32[16,64]{1,0:T(8,128)}, u32[]{:S(2)}) copy-start(f32[16,64]{1,0:T(8,128)} %param.11) | copy-start | bytes 12292
  25.7 5.2 %collective-permute-start.6 = (bf16[336,128]{1,0:T(8,128)(2,1)S(1)}, bf16[336,128]{1,0:T(8,128)(2,1)S(1)}, u32[]{:S(2)}, u32[]{:S(2)}) collective-permute-start(bf16[336,128]{1,0:T(8,128)(2,1)S(1)} %get-tuple-element.66), channel_id=1, source_target_pairs={{0,8},{4,12},{8,0},{12,4},{1,9},{5,13},{9,1},{13,5},{2,10},{6,14},... | collective-permute-start | bytes 258056 | tf_op jit(solution)/shard_map/ppermute | solution.py:441
  27.5 1.2 %collective-permute-start.5 = (bf16[160,128]{1,0:T(8,128)(2,1)S(1)}, bf16[160,128]{1,0:T(8,128)(2,1)S(1)}, u32[]{:S(2)}, u32[]{:S(2)}) collective-permute-start(bf16[160,128]{1,0:T(8,128)(2,1)S(1)} %get-tuple-element.65), channel_id=1, source_target_pairs={{0,4},{4,0},{8,12},{12,8},{1,5},{5,1},{9,13},{13,9},{2,6},{6,2},{1... | collective-permute-start | bytes 122888 | tf_op jit(solution)/shard_map/ppermute | solution.py:441
  27.5 3.4 %collective-permute-start.7 = (bf16[160,128]{1,0:T(8,128)(2,1)S(1)}, bf16[160,128]{1,0:T(8,128)(2,1)S(1)}, u32[]{:S(2)}, u32[]{:S(2)}) collective-permute-start(bf16[160,128]{1,0:T(8,128)(2,1)S(1)} %get-tuple-element.67), channel_id=1, source_target_pairs={{0,12},{4,8},{8,4},{12,0},{1,13},{5,9},{9,5},{13,1},{2,14},{6,10},... | collective-permute-start | bytes 122888 | tf_op jit(solution)/shard_map/ppermute | solution.py:441
  31.1 3.7 %collective-permute-start.8 = (f32[16,64]{1,0:T(8,128)S(1)}, f32[16,64]{1,0:T(8,128)S(1)}, u32[]{:S(2)}, u32[]{:S(2)}) collective-permute-start(f32[16,64]{1,0:T(8,128)S(1)} %get-tuple-element.69), channel_id=1, source_target_pairs={{0,1},{1,0},{2,3},{3,2},{4,5},{5,4},{6,7},{7,6},{8,9},{9,8},{10,11... | collective-permute-start | bytes 12296 | tf_op jit(solution)/shard_map/ppermute | solution.py:416
  34.8 4.5 %collective-permute-start.9 = (f32[16,64]{1,0:T(8,128)S(1)}, f32[16,64]{1,0:T(8,128)S(1)}, u32[]{:S(2)}, u32[]{:S(2)}) collective-permute-start(f32[16,64]{1,0:T(8,128)S(1)} %add.14), channel_id=1, source_target_pairs={{0,2},{1,3},{2,0},{3,1},{4,6},{5,7},{6,4},{7,5},{8,10},{9,11},{10,... | collective-permute-start | bytes 12296 | tf_op jit(solution)/shard_map/ppermute | solution.py:416
